TPU v7x, 32 devices: a whole 2x2x4 slice. The times are simulated.
32 devices in a mesh: seq: 8 (over y, x, core), dp: 4 (over z).
Axes of the slice: x: 2, y: 2, z: 4, core: 2. Of those that a mesh axis runs over, the one named last changes fastest.
Arguments:
- bases: int32 [4, 1024], P('dp', 'seq'), may hold values from 0 to 3
- lengths: int32 [4, 8], P('dp', 'seq'), may hold values from 64 to 128, as said below
- cotangent: bfloat16 [4, 1024, 768], P('dp', 'seq'), may hold values from -6 to 6
- first_conv_taps: bfloat16 [3, 768, 384], P(None, 'seq'), may hold values from -0.125 to 0.125
- first_projection: bfloat16 [384, 768], P('seq'), may hold values from -0.3125 to 0.3125
- second_conv_taps: bfloat16 [3, 768, 384], P(None, 'seq'), may hold values from -0.125 to 0.125
- second_projection: bfloat16 [384, 768], P('seq'), may hold values from -0.3125 to 0.3125
- embed: float32 [4, 768], replicated, may hold values from -6 to 6
Outputs:
- saliency: float32 [4, 4, 1024], P('dp', None, 'seq')
- grad_proj: float32 [589824], P(('seq', 'dp'))
Inputs may be any that keep to these rules, and one draw needn't show every extreme that they name: `lengths`: every block holds between 64 and 128 live rows; in each window one block holds exactly 128 and another exactly 64.
All inputs are finite; a program needn't handle non-finite values.
Results may differ from a plain program's by a relative error of at most 0.0042.
Values may be sent and summed in bfloat16 or wider, within the bound.
No kernel may reach another device: no remote copies, remote signals or barrier semaphores. Data moves between devices by JAX's collectives and lax.ppermute only.
A program may use at most 64 MiB of HBM per device.

v0:
```python
import math

import jax
import jax.numpy as jnp
from jax import lax
from jax.sharding import PartitionSpec as P

FIRST_DILATION = 16
SECOND_DILATION = 64


SQRT_HALF = 0.7071067811865476
INV_SQRT_TWO_PI = 0.3989422804014327


def extended_2(block, sides, width):
    for axis, dim in sides:
        count = lax.axis_size(axis)
        forward = [(i, i + 1) for i in range(count - 1)]
        backward = [(target, source) for source, target in forward]
        low = lax.ppermute(
            lax.slice_in_dim(block, block.shape[dim] - width, None, axis=dim), axis, forward
        )
        high = lax.ppermute(lax.slice_in_dim(block, 0, width, axis=dim), axis, backward)
        block = jnp.concatenate([low, block, high], axis=dim)
    return block


def from_partner(array, axis, bit):
    return lax.ppermute(array, axis, [(i, i ^ 1 << bit) for i in range(lax.axis_size(axis))])


def gelu_value(values):
    return 0.5 * values * (1.0 + lax.erf(values * SQRT_HALF))


def gelu_slope(values):
    return (
        0.5 * (1.0 + lax.erf(values * SQRT_HALF))
        + values * jnp.exp(-0.5 * values * values) * INV_SQRT_TWO_PI
    )


def flip_live(values, live_count, axis_idx):
    return jnp.roll(jnp.flip(values, axis_idx), live_count - values.shape[axis_idx], axis=axis_idx)


def fetch(conv_shard, proj_shard):
    return (
        lax.all_gather(conv_shard, "seq", axis=1, tiled=True),
        lax.all_gather(proj_shard, "seq", axis=0, tiled=True),
    )


def widen(values, counts, dilation):
    head_rows = values[:, :dilation]
    tail_rows = jnp.stack(
        [
            lax.dynamic_slice_in_dim(values[member], counts[member] - dilation, dilation, 0)
            for member in range(2)
        ]
    )
    rim_rows = jnp.concatenate([head_rows, tail_rows], axis=1)
    padded = extended_2(rim_rows, (("seq", 1),), dilation)
    left_rim = padded[:, :dilation]
    right_rim = padded[:, 3 * dilation :]
    zero_rows = jnp.zeros((2, dilation, values.shape[2]), values.dtype)
    extended = jnp.concatenate([left_rim, values, zero_rows], axis=1)
    return jnp.stack(
        [
            lax.dynamic_update_slice_in_dim(
                extended[member], right_rim[member], counts[member] + dilation, 0
            )
            for member in range(2)
        ]
    )


def taps_forward(extended, weights, dilation, capacity, tap_order):
    results = []
    for member in range(2):
        summed = jnp.zeros((capacity, weights.shape[2]), jnp.float32)
        for offset in range(3):
            window_rows = extended[member, offset * dilation : offset * dilation + capacity]
            summed = summed + jnp.dot(
                window_rows, weights[tap_order[member][offset]], preferred_element_type=jnp.float32
            )
        results.append(summed)
    return jnp.stack(results)


def taps_backward(extended, weights, dilation, capacity, tap_order):
    results = []
    for member in range(2):
        summed = jnp.zeros((capacity, weights.shape[1]), jnp.float32)
        for offset in range(3):
            window_rows = extended[member, offset * dilation : offset * dilation + capacity]
            weight_idx = tap_order[member][2 - offset]
            summed = summed + lax.dot_general(
                window_rows,
                weights[weight_idx],
                (((1,), (1,)), ((), ())),
                preferred_element_type=jnp.float32,
            )
        results.append(summed)
    return jnp.stack(results)


def shards(
    bases,
    lengths,
    cotangent,
    first_conv_taps,
    first_projection,
    second_conv_taps,
    second_projection,
    embed,
):
    capacity = bases.shape[1]
    channels = embed.shape[1]
    own_count = lengths[0, 0]
    own_bases = bases[0]
    own_cot = cotangent[0]
    positions = jnp.arange(capacity, dtype=jnp.int32)
    own_live = positions < own_count
    mirror_bits = lax.axis_size("seq").bit_length() - 1
    flipped_cot = jnp.where(
        own_live[:, None], flip_live(own_cot, own_count, 0), jnp.zeros_like(own_cot)
    )
    flipped_codes = (3 - flip_live(own_bases, own_count, 0)).astype(jnp.bfloat16)
    partner_info = jnp.stack(
        [
            jnp.where(own_live, flipped_codes, jnp.zeros_like(flipped_codes)),
            own_live.astype(jnp.bfloat16),
        ]
    )
    for bit_index in range(mirror_bits):
        flipped_cot, partner_info = from_partner((flipped_cot, partner_info), "seq", bit_index)
    other_count = jnp.sum(partner_info[1].astype(jnp.float32)).astype(jnp.int32)
    other_bases = partner_info[0].astype(jnp.int32)
    tap_order = ((0, 1, 2), (0, 1, 2))
    counts = jnp.stack([own_count, other_count])
    live = (positions[None, :] < counts[:, None]).astype(jnp.float32)[:, :, None]
    codes = jnp.stack([own_bases, other_bases])
    stream = jnp.zeros((2, capacity, channels), jnp.float32)
    for code_value in range(4):
        stream = stream + jnp.where(
            (codes == code_value)[:, :, None], embed[code_value][None, None, :], 0.0
        )
    stream = stream * live
    cot_half = 0.5 * jnp.stack([own_cot, flipped_cot]).astype(jnp.float32) * live
    residual_blocks = [
        (first_conv_taps, first_projection, FIRST_DILATION),
        (second_conv_taps, second_projection, SECOND_DILATION),
    ]
    kept = []
    saved = []
    for conv_shard, proj_shard, dilation in residual_blocks:
        conv_full, proj_full = fetch(conv_shard, proj_shard)
        kept.append((conv_full, proj_full))
        active = gelu_value(stream).astype(jnp.bfloat16)
        extended = widen(active, counts, dilation)
        before = taps_forward(extended, conv_full, dilation, capacity, tap_order) * live
        middle = gelu_value(before).astype(jnp.bfloat16)
        saved.append((stream, before, middle))
        stream = stream + jnp.einsum(
            "srb,bc->src", middle, proj_full, preferred_element_type=jnp.float32
        )
    grad_rows = cot_half
    proj_grads = [None, None]
    for block_idx in (1, 0):
        conv_shard, proj_shard, dilation = residual_blocks[block_idx]
        conv_full, proj_full = fetch(conv_shard, proj_shard)
        stream_in, before, middle = saved[block_idx]
        grad_low = grad_rows.astype(jnp.bfloat16)
        proj_grads[block_idx] = jnp.einsum(
            "srb,src->bc", middle, grad_low, preferred_element_type=jnp.float32
        )
        back_mid = jnp.einsum(
            "src,bc->srb", grad_low, proj_full, preferred_element_type=jnp.float32
        )
        grad_before = (back_mid * gelu_slope(before) * live).astype(jnp.bfloat16)
        extended = widen(grad_before, counts, dilation)
        grad_active = taps_backward(extended, conv_full, dilation, capacity, tap_order)
        grad_rows = grad_rows + grad_active * gelu_slope(stream_in) * live
    own_sal = jnp.einsum("bc,rc->br", embed, grad_rows[0], precision=lax.Precision.HIGHEST)
    other_sal = jnp.einsum("bc,rc->br", embed[::-1], grad_rows[1], precision=lax.Precision.HIGHEST)
    other_live = (positions < other_count).astype(jnp.float32)[None, :]
    other_sal = flip_live(other_sal, other_count, 1) * other_live
    for bit_index in range(mirror_bits):
        other_sal = from_partner(other_sal, "seq", bit_index)
    saliency = (own_sal + other_sal) * own_live.astype(jnp.float32)[None, :] / math.sqrt(channels)
    device_count = lax.axis_size("seq") * lax.axis_size("dp")
    scale = 1.0 / math.sqrt(device_count * capacity)
    terms = jnp.concatenate([proj_grads[0].reshape(-1), proj_grads[1].reshape(-1)]) * scale
    grad_part = lax.psum_scatter(terms, ("seq", "dp"), scatter_dimension=0, tiled=True)
    return (saliency[None], grad_part)


def solution(mesh):
    in_specs = (
        P("dp", "seq"),
        P("dp", "seq"),
        P("dp", "seq", None),
        P(None, "seq", None),
        P("seq", None),
        P(None, "seq", None),
        P("seq", None),
        P(),
    )
    out_specs = (P("dp", None, "seq"), P(("seq", "dp")))
    return jax.shard_map(shards, mesh=mesh, in_specs=in_specs, out_specs=out_specs, check_vma=False)
```

profile of v0, /device:TPU:0, one launch (start us, length us, event | category | flops | bytes accessed | tf_op | source)
XLA Modules:
  0.0 266.8 jit_solution(5800398627473177468)
XLA Ops:
  10.0 2.4 rev.15
  12.8 2.1 rev.17
  14.9 0.9 slice_reduce_fusion.3
  15.9 12.3 %all_gather.17 = bf16[384,768]{1,0:T(8,128)(2,1)S(1)} all-gather(bf16[48,768]{1,0:T(8,128)(2,1)} %param.12), channel_id=1, replica_groups=mesh['seq'=8,'dp'=4] {'seq'}, dimensions={0}, use_global_device_ids=true | all-gather | bytes 663552 | tf_op jit(solution)/shard_map/all_gather | solution.py:51
  28.2 12.8 %all_gather.15 = bf16[384,768]{1,0:T(8,128)(2,1)} all-gather(bf16[48,768]{1,0:T(8,128)(2,1)S(1)} %copy-done.26), channel_id=1, replica_groups=mesh['seq'=8,'dp'=4] {'seq'}, dimensions={0}, use_global_device_ids=true | all-gather | bytes 663552 | tf_op jit(solution)/shard_map/all_gather | solution.py:51
  41.7 2.9 %collective-permute-done.4 = bf16[2,128]{1,0:T(2,128)(2,1)S(1)} collective-permute-done((bf16[2,128]{1,0:T(2,128)(2,1)S(1)}, bf16[2,128]{1,0:T(2,128)(2,1)S(1)}, u32[]{:S(2)}, u32[]{:S(2)}) %collective-permute-start.4) | collective-permute-done | bytes 544 | tf_op jit(solution)/shard_map/ppermute | solution.py:30
  45.1 3.0 %collective-permute-done.5 = bf16[2,128]{1,0:T(2,128)(2,1)S(1)} collective-permute-done((bf16[2,128]{1,0:T(2,128)(2,1)S(1)}, bf16[2,128]{1,0:T(2,128)(2,1)S(1)}, u32[]{:S(2)}, u32[]{:S(2)}) %collective-permute-start.5) | collective-permute-done | bytes 544 | tf_op jit(solution)/shard_map/ppermute | solution.py:30
  50.7 1.3 collective-permute-start.6
  52.5 1.3 collective-permute-start.7
  54.0 3.5 %collective-permute-start.1 = (bf16[128,768]{1,0:T(8,128)(2,1)S(1)}, bf16[128,768]{1,0:T(8,128)(2,1)}, u32[]{:S(2)}, u32[]{:S(2)}) collective-permute-start(bf16[128,768]{1,0:T(8,128)(2,1)S(1)} %collective-permute-done), channel_id=1, source_target_pairs={{0,8},{4,12},{8,0},{12,4},{16,24},{20,28},{24,16},{28,20},{1,9},{5... | collective-permute-start | bytes 589832 | tf_op jit(solution)/shard_map/ppermute | solution.py:30
  58.2 5.2 %collective-permute-done.1 = bf16[128,768]{1,0:T(8,128)(2,1)} collective-permute-done((bf16[128,768]{1,0:T(8,128)(2,1)S(1)}, bf16[128,768]{1,0:T(8,128)(2,1)}, u32[]{:S(2)}, u32[]{:S(2)}) %collective-permute-start.1) | collective-permute-done | bytes 196640 | tf_op jit(solution)/shard_map/ppermute | solution.py:30
  63.4 1.5 collective-permute-start.2
  64.9 1.5 fusion.40
  66.4 1.3 convolution_add_fusion.14
  68.9 1.5 multiply_convert_fusion
  70.5 1.3 collective-permute-start.9
  72.0 3.0 %collective-permute-start.8 = (bf16[2,64,768]{2,1,0:T(8,128)(2,1)S(1)}, bf16[2,64,768]{2,1,0:T(8,128)(2,1)S(1)}, u32[]{:S(2)}, u32[]{:S(2)}) collective-permute-start(bf16[2,64,768]{2,1,0:T(8,128)(2,1)S(1)} %pad_maximum_fusion.1), channel_id=1, source_target_pairs={{0,4},{4,8},{8,12},{12,16},{16,20},{20,24},{24,28},{1,5},{5,9},{9,... | collective-permute-start | bytes 589832 | tf_op jit(solution)/shard_map/ppermute | solution.py:21
  75.0 1.0 collective-permute-done.8
  76.3 0.9 dynamic_update_slice.34
  78.7 1.6 fusion.44
  80.3 1.5 convolution_add_fusion.10
  83.2 1.4 fusion.6
  85.4 1.3 collective-permute-start.11
  87.4 4.8 %collective-permute-start.10 = (bf16[2,64,384]{2,1,0:T(8,128)(2,1)}, bf16[2,64,384]{2,1,0:T(8,128)(2,1)}, u32[]{:S(2)}, u32[]{:S(2)}) collective-permute-start(bf16[2,64,384]{2,1,0:T(8,128)(2,1)} %pad_maximum_fusion.4), channel_id=1, source_target_pairs={{0,4},{4,8},{8,12},{12,16},{16,20},{20,24},{24,28},{1,5},{5,9},{9,... | collective-permute-start | bytes 294920 | tf_op jit(solution)/shard_map/ppermute | solution.py:21
  92.2 2.4 convolution_bitcast_fusion
  94.6 2.3 reshape.168
  96.9 1.1 maximum_maximum_fusion.2
  98.1 0.8 fusion.65
  98.9 1.5 fusion.72
  100.3 1.5 dynamic_update_slice.36
  101.9 1.5 dynamic_update_slice.37
  103.4 1.3 fusion.42
  104.7 1.2 convolution_add_fusion.6
  107.5 1.3 fusion.18
  109.9 1.1 reshape.167
  111.0 1.3 collective-permute-start.13
  112.4 4.3 %collective-permute-start.12 = (bf16[2,16,384]{2,1,0:T(8,128)(2,1)S(1)}, bf16[2,16,384]{2,1,0:T(8,128)(2,1)S(1)}, u32[]{:S(2)}, u32[]{:S(2)}) collective-permute-start(bf16[2,16,384]{2,1,0:T(8,128)(2,1)S(1)} %pad_maximum_fusion.6), channel_id=1, source_target_pairs={{0,4},{4,8},{8,12},{12,16},{16,20},{20,24},{24,28},{1,5},{5,9},{9,... | collective-permute-start | bytes 73736 | tf_op jit(solution)/shard_map/ppermute | solution.py:21
  116.7 3.2 %maximum_multiply_fusion = f32[589824]{0:T(1024)} fusion(f32[294912]{0:T(1024)} %reshape.168, f32[294912]{0:T(1024)} %reshape.167), kind=kLoop, calls=%fused_computation | loop fusion | flops 1179648 | bytes 4718592 | tf_op jit(solution)/shard_map/mul | solution.py:195
  123.6 2.0 fusion.25
  126.3 1.7 collective-permute-start.14
  128.0 0.8 collective-permute-done.14
  128.8 3.7 %collective-permute-start.15 = (f32[4,128]{1,0:T(4,128)S(1)}, f32[4,128]{1,0:T(4,128)S(1)}, u32[]{:S(2)}, u32[]{:S(2)}) collective-permute-start(f32[4,128]{1,0:T(4,128)S(1)} %collective-permute-done.14), channel_id=1, source_target_pairs={{0,8},{4,12},{8,0},{12,4},{16,24},{20,28},{24,16},{28,20},{1,9},{5... | collective-permute-start | bytes 6152 | tf_op jit(solution)/shard_map/ppermute | solution.py:30
  132.5 1.6 collective-permute-done.15
  134.1 1.0 collective-permute-start.16
  135.0 2.6 collective-permute-done.16
  137.7 1.0 multiply_bitcast_fusion
  138.7 120.1 %all-reduce.3.cloned.1.call-done = f32[589824]{0:T(1024)} async-done(((f32[589824]{0:T(1024)}), f32[589824]{0:T(1024)}) %all-reduce.3.cloned.1.call-update) | async-done | bytes 2359312
  258.8 1.5 dynamic-slice.8
  (204 shorter events, 19.4 us)
Async XLA Ops:
  7.2 43.0 %copy-start.52 = (s32[1,128]{1,0:T(1,128)S(1)}, s32[1,128]{1,0:T(1,128)}, u32[]{:S(2)}) copy-start(s32[1,128]{1,0:T(1,128)} %param.8) | copy-start | bytes 1540
  7.2 21.0 %copy-start.26 = (bf16[48,768]{1,0:T(8,128)(2,1)S(1)}, bf16[48,768]{1,0:T(8,128)(2,1)}, u32[]{:S(2)}) copy-start(bf16[48,768]{1,0:T(8,128)(2,1)} %param.14) | copy-start | bytes 221188
  7.2 57.8 %all-gather.3.cloned.1.call-start = ((), (), s32[]{:S(2)}) async-start(), calls=%async_computation | async-start | bytes 1990656 | tf_op jit(solution)/shard_map/all_gather | solution.py:50
  7.9 70.8 %all-gather.5.cloned.1.call-start = ((), (), s32[]{:S(2)}) async-start(), calls=%async_computation.1 | async-start | bytes 1990656 | tf_op jit(solution)/shard_map/all_gather | solution.py:50
  9.5 31.5 %collective-permute-start.3 = (bf16[2,128]{1,0:T(2,128)(2,1)S(1)}, bf16[2,128]{1,0:T(2,128)(2,1)S(1)}, u32[]{:S(2)}, u32[]{:S(2)}) collective-permute-start(bf16[2,128]{1,0:T(2,128)(2,1)S(1)} %pad_maximum_fusion.7), channel_id=1, source_target_pairs={{0,4},{4,0},{8,12},{12,8},{16,20},{20,16},{24,28},{28,24},{1,5},{5... | collective-permute-start | bytes 1544 | tf_op jit(solution)/shard_map/ppermute | solution.py:30
  12.6 41.4 %collective-permute-start = (bf16[128,768]{1,0:T(8,128)(2,1)S(1)}, bf16[128,768]{1,0:T(8,128)(2,1)S(1)}, u32[]{:S(2)}, u32[]{:S(2)}) collective-permute-start(bf16[128,768]{1,0:T(8,128)(2,1)S(1)} %fusion.49), channel_id=1, source_target_pairs={{0,4},{4,0},{8,12},{12,8},{16,20},{20,16},{24,28},{28,24},{1,5},{5... | collective-permute-start | bytes 589832 | tf_op jit(solution)/shard_map/ppermute | solution.py:30
  12.7 246.0 %all-reduce.3.cloned.1.call-start = ((), (), s32[]{:S(2)}) async-start(), calls=%async_computation.2 | async-start | bytes 4718592
  15.8 53.0 %copy-start.27 = (f32[768]{0:T(1024)}, f32[768]{0:T(1024)S(1)}, u32[]{:S(2)}) copy-start(f32[768]{0:T(1024)S(1)} %get-tuple-element.3) | copy-start | bytes 9220
  15.8 53.0 %copy-start.29 = (f32[768]{0:T(1024)}, f32[768]{0:T(1024)S(1)}, u32[]{:S(2)}) copy-start(f32[768]{0:T(1024)S(1)} %get-tuple-element.4) | copy-start | bytes 9220
  15.8 53.0 %copy-start.31 = (f32[768]{0:T(1024)}, f32[768]{0:T(1024)S(1)}, u32[]{:S(2)}) copy-start(f32[768]{0:T(1024)S(1)} %get-tuple-element.5) | copy-start | bytes 9220
  28.2 40.7 %copy-start.22 = (bf16[384,768]{1,0:T(8,128)(2,1)}, bf16[384,768]{1,0:T(8,128)(2,1)S(1)}, u32[]{:S(2)}) copy-start(bf16[384,768]{1,0:T(8,128)(2,1)S(1)} %all_gather.17) | copy-start | bytes 1769476
  41.0 3.5 %collective-permute-start.4 = (bf16[2,128]{1,0:T(2,128)(2,1)S(1)}, bf16[2,128]{1,0:T(2,128)(2,1)S(1)}, u32[]{:S(2)}, u32[]{:S(2)}) collective-permute-start(bf16[2,128]{1,0:T(2,128)(2,1)S(1)} %collective-permute-done.3), channel_id=1, source_target_pairs={{0,8},{4,12},{8,0},{12,4},{16,24},{20,28},{24,16},{28,20},{1,9},{5... | collective-permute-start | bytes 1544 | tf_op jit(solution)/shard_map/ppermute | solution.py:30
  41.6 34.4 %copy-start.48 = (bf16[256]{0:T(256)(128)(2,1)}, bf16[256]{0:T(256)(128)(2,1)S(1)}, u32[]{:S(2)}) copy-start(bf16[256]{0:T(256)(128)(2,1)S(1)} %pad.22.clone) | copy-start | bytes 1540
  41.7 15.9 %copy-start.49 = (bf16[160]{0:T(256)(128)(2,1)}, bf16[160]{0:T(256)(128)(2,1)S(1)}, u32[]{:S(2)}) copy-start(bf16[160]{0:T(256)(128)(2,1)S(1)} %pad.29.clone) | copy-start | bytes 964
  44.6 3.5 %collective-permute-start.5 = (bf16[2,128]{1,0:T(2,128)(2,1)S(1)}, bf16[2,128]{1,0:T(2,128)(2,1)S(1)}, u32[]{:S(2)}, u32[]{:S(2)}) collective-permute-start(bf16[2,128]{1,0:T(2,128)(2,1)S(1)} %collective-permute-done.4), channel_id=1, source_target_pairs={{0,16},{4,20},{8,24},{12,28},{16,0},{20,4},{24,8},{28,12},{1,17},{... | collective-permute-start | bytes 1544 | tf_op jit(solution)/shard_map/ppermute | solution.py:30
  49.5 19.4 %copy-start.33 = (f32[2,128]{1,0:T(2,128)}, f32[2,128]{1,0:T(2,128)S(1)}, u32[]{:S(2)}) copy-start(f32[2,128]{1,0:T(2,128)S(1)} %fusion.56) | copy-start | bytes 3076
  50.2 18.7 %copy-start.40 = (pred[2,128]{1,0:T(4,128)(4,1)}, pred[2,128]{1,0:T(4,128)(4,1)S(1)}, u32[]{:S(2)}) copy-start(pred[2,128]{1,0:T(4,128)(4,1)S(1)} %get-tuple-element.30) | copy-start | bytes 772
  50.2 18.7 %copy-start.42 = (pred[2,128]{1,0:T(4,128)(4,1)}, pred[2,128]{1,0:T(4,128)(4,1)S(1)}, u32[]{:S(2)}) copy-start(pred[2,128]{1,0:T(4,128)(4,1)S(1)} %get-tuple-element.31) | copy-start | bytes 772
  50.2 18.7 %copy-start.44 = (pred[2,128]{1,0:T(4,128)(4,1)}, pred[2,128]{1,0:T(4,128)(4,1)S(1)}, u32[]{:S(2)}) copy-start(pred[2,128]{1,0:T(4,128)(4,1)S(1)} %get-tuple-element.32) | copy-start | bytes 772
  50.2 18.7 %copy-start.46 = (pred[2,128]{1,0:T(4,128)(4,1)}, pred[2,128]{1,0:T(4,128)(4,1)S(1)}, u32[]{:S(2)}) copy-start(pred[2,128]{1,0:T(4,128)(4,1)S(1)} %get-tuple-element.33) | copy-start | bytes 772
  50.7 3.1 %collective-permute-start.6 = (bf16[2,16,768]{2,1,0:T(8,128)(2,1)S(1)}, bf16[2,16,768]{2,1,0:T(8,128)(2,1)S(1)}, u32[]{:S(2)}, u32[]{:S(2)}) collective-permute-start(bf16[2,16,768]{2,1,0:T(8,128)(2,1)S(1)} %pad_maximum_fusion.5), channel_id=1, source_target_pairs={{0,4},{4,8},{8,12},{12,16},{16,20},{20,24},{24,28},{1,5},{5,9},{9,... | collective-permute-start | bytes 147464 | tf_op jit(solution)/shard_map/ppermute | solution.py:21
  52.5 5.1 %collective-permute-start.7 = (bf16[2,16,768]{2,1,0:T(8,128)(2,1)S(1)}, bf16[2,16,768]{2,1,0:T(8,128)(2,1)S(1)}, u32[]{:S(2)}, u32[]{:S(2)}) collective-permute-start(bf16[2,16,768]{2,1,0:T(8,128)(2,1)S(1)} %slice.285), channel_id=1, source_target_pairs={{4,0},{8,4},{12,8},{16,12},{20,16},{24,20},{28,24},{5,1},{9,5},{13... | collective-permute-start | bytes 147464 | tf_op jit(solution)/shard_map/ppermute | solution.py:24
  54.0 9.4 %collective-permute-start.1 = (bf16[128,768]{1,0:T(8,128)(2,1)S(1)}, bf16[128,768]{1,0:T(8,128)(2,1)}, u32[]{:S(2)}, u32[]{:S(2)}) collective-permute-start(bf16[128,768]{1,0:T(8,128)(2,1)S(1)} %collective-permute-done), channel_id=1, source_target_pairs={{0,8},{4,12},{8,0},{12,4},{16,24},{20,28},{24,16},{28,20},{1,9},{5... | collective-permute-start | bytes 589832 | tf_op jit(solution)/shard_map/ppermute | solution.py:30
  63.4 19.5 %collective-permute-start.2 = (bf16[128,768]{1,0:T(8,128)(2,1)}, bf16[128,768]{1,0:T(8,128)(2,1)}, u32[]{:S(2)}, u32[]{:S(2)}) collective-permute-start(bf16[128,768]{1,0:T(8,128)(2,1)} %collective-permute-done.1), channel_id=1, source_target_pairs={{0,16},{4,20},{8,24},{12,28},{16,0},{20,4},{24,8},{28,12},{1,17},{... | collective-permute-start | bytes 589832 | tf_op jit(solution)/shard_map/ppermute | solution.py:30
  64.9 2.8 %copy-start = (bf16[3,768,384]{2,1,0:T(8,128)(2,1)S(1)}, bf16[3,768,384]{2,1,0:T(8,128)(2,1)}, u32[]{:S(2)}) copy-start(bf16[3,768,384]{2,1,0:T(8,128)(2,1)} %all-gather.3.cloned.1.call-done) | copy-start | bytes 5308420
  68.0 2.5 copy-start.18
  68.9 1.6 copy-start.20
  70.5 4.5 %collective-permute-start.9 = (bf16[2,64,768]{2,1,0:T(8,128)(2,1)S(1)}, bf16[2,64,768]{2,1,0:T(8,128)(2,1)S(1)}, u32[]{:S(2)}, u32[]{:S(2)}) collective-permute-start(bf16[2,64,768]{2,1,0:T(8,128)(2,1)S(1)} %slice.301), channel_id=1, source_target_pairs={{4,0},{8,4},{12,8},{16,12},{20,16},{24,20},{28,24},{5,1},{9,5},{13... | collective-permute-start | bytes 589832 | tf_op jit(solution)/shard_map/ppermute | solution.py:24
  72.0 4.1 %collective-permute-start.8 = (bf16[2,64,768]{2,1,0:T(8,128)(2,1)S(1)}, bf16[2,64,768]{2,1,0:T(8,128)(2,1)S(1)}, u32[]{:S(2)}, u32[]{:S(2)}) collective-permute-start(bf16[2,64,768]{2,1,0:T(8,128)(2,1)S(1)} %pad_maximum_fusion.1), channel_id=1, source_target_pairs={{0,4},{4,8},{8,12},{12,16},{16,20},{20,24},{24,28},{1,5},{5,9},{9,... | collective-permute-start | bytes 589832 | tf_op jit(solution)/shard_map/ppermute | solution.py:21
  78.7 3.1 %copy-start.1 = (bf16[3,768,384]{2,1,0:T(8,128)(2,1)S(1)}, bf16[3,768,384]{2,1,0:T(8,128)(2,1)}, u32[]{:S(2)}) copy-start(bf16[3,768,384]{2,1,0:T(8,128)(2,1)} %all-gather.5.cloned.1.call-done) | copy-start | bytes 5308420
  78.7 3.1 %copy-start.14 = (bf16[1,256,768]{2,1,0:T(8,128)(2,1)S(1)}, bf16[1,256,768]{2,1,0:T(8,128)(2,1)}, u32[]{:S(2)}) copy-start(bf16[1,256,768]{2,1,0:T(8,128)(2,1)} %copy-done.13) | copy-start | bytes 1179652
  80.3 2.1 copy-start.12
  85.4 13.5 %collective-permute-start.11 = (bf16[2,64,384]{2,1,0:T(8,128)(2,1)}, bf16[2,64,384]{2,1,0:T(8,128)(2,1)}, u32[]{:S(2)}, u32[]{:S(2)}) collective-permute-start(bf16[2,64,384]{2,1,0:T(8,128)(2,1)} %slice.317), channel_id=1, source_target_pairs={{4,0},{8,4},{12,8},{16,12},{20,16},{24,20},{28,24},{5,1},{9,5},{13... | collective-permute-start | bytes 294920 | tf_op jit(solution)/shard_map/ppermute | solution.py:24
  87.4 9.5 %collective-permute-start.10 = (bf16[2,64,384]{2,1,0:T(8,128)(2,1)}, bf16[2,64,384]{2,1,0:T(8,128)(2,1)}, u32[]{:S(2)}, u32[]{:S(2)}) collective-permute-start(bf16[2,64,384]{2,1,0:T(8,128)(2,1)} %pad_maximum_fusion.4), channel_id=1, source_target_pairs={{0,4},{4,8},{8,12},{12,16},{16,20},{20,24},{24,28},{1,5},{5,9},{9,... | collective-permute-start | bytes 294920 | tf_op jit(solution)/shard_map/ppermute | solution.py:21
  103.4 2.5 copy-start.15
  103.4 2.8 %copy-start.16 = (bf16[1,256,384]{2,1,0:T(8,128)(2,1)S(1)}, bf16[1,256,384]{2,1,0:T(8,128)(2,1)}, u32[]{:S(2)}) copy-start(bf16[1,256,384]{2,1,0:T(8,128)(2,1)} %dynamic_update_slice.36) | copy-start | bytes 589828
  106.9 2.0 copy-start.19
  106.9 2.0 copy-start.21
  106.9 2.0 copy-start.23
  107.3 2.1 copy-start.4
  111.0 9.6 %collective-permute-start.13 = (bf16[2,16,384]{2,1,0:T(8,128)(2,1)S(1)}, bf16[2,16,384]{2,1,0:T(8,128)(2,1)S(1)}, u32[]{:S(2)}, u32[]{:S(2)}) collective-permute-start(bf16[2,16,384]{2,1,0:T(8,128)(2,1)S(1)} %slice.330), channel_id=1, source_target_pairs={{4,0},{8,4},{12,8},{16,12},{20,16},{24,20},{28,24},{5,1},{9,5},{13... | collective-permute-start | bytes 73736 | tf_op jit(solution)/shard_map/ppermute | solution.py:24
  112.4 7.5 %collective-permute-start.12 = (bf16[2,16,384]{2,1,0:T(8,128)(2,1)S(1)}, bf16[2,16,384]{2,1,0:T(8,128)(2,1)S(1)}, u32[]{:S(2)}, u32[]{:S(2)}) collective-permute-start(bf16[2,16,384]{2,1,0:T(8,128)(2,1)S(1)} %pad_maximum_fusion.6), channel_id=1, source_target_pairs={{0,4},{4,8},{8,12},{12,16},{16,20},{20,24},{24,28},{1,5},{5,9},{9,... | collective-permute-start | bytes 73736 | tf_op jit(solution)/shard_map/ppermute | solution.py:21
  122.2 1.4 copy-start.10
  123.6 2.6 copy-start.51
  123.6 14.0 %copy-start.25 = (f32[4,768]{1,0:T(4,128)S(1)}, f32[4,768]{1,0:T(4,128)}, u32[]{:S(2)}) copy-start(f32[4,768]{1,0:T(4,128)} %param.15) | copy-start | bytes 36868
  126.3 2.6 collective-permute-start.14
  128.8 5.2 %collective-permute-start.15 = (f32[4,128]{1,0:T(4,128)S(1)}, f32[4,128]{1,0:T(4,128)S(1)}, u32[]{:S(2)}, u32[]{:S(2)}) collective-permute-start(f32[4,128]{1,0:T(4,128)S(1)} %collective-permute-done.14), channel_id=1, source_target_pairs={{0,8},{4,12},{8,0},{12,4},{16,24},{20,28},{24,16},{28,20},{1,9},{5... | collective-permute-start | bytes 6152 | tf_op jit(solution)/shard_map/ppermute | solution.py:30
  134.1 3.6 %collective-permute-start.16 = (f32[4,128]{1,0:T(4,128)S(1)}, f32[4,128]{1,0:T(4,128)S(1)}, u32[]{:S(2)}, u32[]{:S(2)}) collective-permute-start(f32[4,128]{1,0:T(4,128)S(1)} %collective-permute-done.15), channel_id=1, source_target_pairs={{0,16},{4,20},{8,24},{12,28},{16,0},{20,4},{24,8},{28,12},{1,17},{... | collective-permute-start | bytes 6152 | tf_op jit(solution)/shard_map/ppermute | solution.py:30
  (25 other events, 29.2 us)
Sparse Core Ops, SparseCore 0:
  9.9 31.9 all-gather.2
  43.8 30.7 all-gather.4
  120.0 138.7 all-reduce.2
where the time goes:
time: 268 us; the launch traced here: 267 us
  waiting for transfers between devices  138 us (51%)
  starting transfers between devices  31.8 us (12%)
  blocking collectives  25.1 us (9%)
  local copies, waits for them, and re-layouts  23 us (9%)
  matrix products  21.3 us (8%)
  between operations  16.2 us (6%)
  other arithmetic  11.5 us (4%)
    unnamed x4, waiting for transfers between devices  121 us
    all_gather x2, blocking collectives, fetch(): lax.all_gather(proj_shard, 'seq', axis=0, tiled=True)  25.1 us
    ppermute x9, waiting for transfers between devices, from_partner(): lax.ppermute(array, axis, [(i, i ^ 1 << bit) for i in range(lax.axis_size...  16.1 us
    ppermute x4, starting transfers between devices, extended_2(): lax.ppermute(lax.slice_in_dim(block, block.shape[dim] - width, None, axis...  13.4 us
    ppermute x9, starting transfers between devices, from_partner(): lax.ppermute(array, axis, [(i, i ^ 1 << bit) for i in range(lax.axis_size...  13.1 us
    dot_general x12, matrix products, taps_forward(): jnp.dot(window_rows, weights[tap_order[member][offset]], preferred_elemen...  7.94 us
    dynamic_update_slice x8, local copies, waits for them, and re-layouts, widen(): lax.dynamic_update_slice_in_dim(extended[member], right_rim[member], coun...  5.75 us
    dot_general x12, matrix products, taps_backward(): lax.dot_general(window_rows, weights[weight_idx], (((1,), (1,)), ((), ())...  5.69 us
  transfers between devices with their start and end apart: 20, of which 8 were waited for; matrix products, arithmetic and copies ran while one was open for 14% of the time, Pallas kernels for 0%

commit v1 on v0

v1 whole, which is shorter than its diff:
```python
import functools
import math

import jax
import jax.numpy as jnp
from jax import lax
from jax.experimental import pallas as pl
from jax.experimental.pallas import tpu as pltpu
from jax.sharding import PartitionSpec as P

FIRST_DILATION = 16
SECOND_DILATION = 64
HALO = FIRST_DILATION + SECOND_DILATION
SPILL = 16
REACH = 3
TABLE = 128
SQRT_HALF = 0.7071067811865476
INV_SQRT_TWO_PI = 0.3989422804014327
F32 = jnp.float32
BF16 = jnp.bfloat16
FAR = -100000.0


def gelu_pair(v):
    half = 0.5 * (1.0 + lax.erf(v * SQRT_HALF))
    return v * half, half + v * jnp.exp(-0.5 * v * v) * INV_SQRT_TWO_PI


def split(v):
    high = v.astype(BF16)
    return high, (v - high.astype(F32)).astype(BF16)


def mm(a, b):
    return lax.dot_general(a, b, (((1,), (0,)), ((), ())), preferred_element_type=F32)


def mm_nt(a, b):
    return lax.dot_general(a, b, (((1,), (1,)), ((), ())), preferred_element_type=F32)


def mm_tn(a, b):
    return lax.dot_general(a, b, (((0,), (0,)), ((), ())), preferred_element_type=F32)


def iota(shape, dim):
    return lax.broadcasted_iota(jnp.int32, shape, dim)


def spread(rows, index):
    out = jnp.broadcast_to(rows[0:1], (index.shape[0], rows.shape[1]))
    for q in range(1, 4):
        out = jnp.where(index == q, rows[q : q + 1], out)
    return out


def call(body, out_shapes, args, scratch=(), limit=24, cost=None):
    in_specs = [
        pl.BlockSpec(memory_space=pltpu.SMEM if a.dtype == jnp.int32 and a.ndim == 1 else pltpu.VMEM)
        for a in args
    ]
    return pl.pallas_call(
        body,
        out_shape=[jax.ShapeDtypeStruct(s, d) for s, d in out_shapes],
        in_specs=in_specs,
        out_specs=[pl.BlockSpec(memory_space=pltpu.VMEM)] * len(out_shapes),
        scratch_shapes=list(scratch),
        compiler_params=pltpu.CompilerParams(vmem_limit_bytes=limit * 1024 * 1024),
        cost_estimate=cost,
    )(*args)


def base_tables(embed_ref, pick, conv, shard):
    row = iota((16, 1), 0)
    low, high = row & 3, row >> 2
    emb = embed_ref[...]
    by_low = spread(emb, low)
    by_high = spread(emb, high)
    act = gelu_pair(by_low)[0].astype(BF16)
    prod_high, prod_low = split(gelu_pair(by_high)[1] * by_low)
    own = mm(jnp.concatenate([act, prod_high, prod_low], axis=0), pick).astype(BF16)
    first = jnp.zeros((16, conv.shape[2]), F32)
    second = []
    for k in range(3):
        res = mm(own, conv[k])
        first = jnp.where(high == k, res[0:16], first)
        second.append(res[16:32] + res[32:48])
    return first, jnp.concatenate(second, axis=0)


def prep_kernel(
    where_ref, bases_ref, cot_ref, c1_ref, p1_ref, c2_ref, p2_ref, embed_ref,
    m1_ref, m2_ref, r1_ref, r2_ref, l1_ref, l2_ref,
):
    me, count = where_ref[0], where_ref[2]
    shard = c1_ref.shape[1]
    chans = embed_ref.shape[1]
    width = c1_ref.shape[2]
    pick = (iota((chans, shard), 0) == iota((chans, shard), 1) + me * shard).astype(BF16)
    first, second = base_tables(embed_ref, pick, c1_ref, shard)
    prows = p1_ref.shape[0]
    m1_ref[0:prows] = p1_ref[...]
    f_high, f_low = split(first)
    cap = bases_ref.shape[1]
    info = jnp.concatenate(
        [
            bases_ref[...].astype(F32),
            jnp.full((1, 128), count, jnp.int32).astype(F32),
            jnp.zeros((1, chans - cap - 128), F32),
        ],
        axis=1,
    )
    tail = jnp.concatenate([f_high.astype(F32), f_low.astype(F32)], axis=1)
    tail = jnp.where(iota((16, 1), 0) == 12, info, tail)
    m1_ref[prows : prows + 16] = tail.astype(BF16)
    half = 3 * shard // 2
    flat = c2_ref[...].reshape(3 * shard, width)
    m2_ref[0:half, 0:width] = flat[0:half]
    m2_ref[0:half, width : 2 * width] = flat[half : 2 * half]
    m2_ref[half : half + prows] = p2_ref[...]
    s_high, s_low = split(second)
    m2_ref[half + prows : half + prows + 48, 0:width] = s_high
    m2_ref[half + prows : half + prows + 48, width : 2 * width] = s_low
    cot = cot_ref[...]
    take = (iota((HALO, cap), 1) == iota((HALO, cap), 0) + (count - HALO)).astype(BF16)
    last = mm(take, cot).astype(BF16)
    r1_ref[...] = last
    r2_ref[...] = last[HALO - SPILL :]
    l1_ref[...] = cot[0:HALO]
    l2_ref[...] = cot[0:SPILL]


def table_body(
    first, project, info_at, cot_ref, r1_ref, r2_ref, l1_ref, l2_ref, embed_ref,
    b1_ref, s1_ref, a2_ref, s2_ref, hot_f_ref, hot_r_ref, cx_ref,
):
    cap = cot_ref.shape[0]
    outer = HALO + SECOND_DILATION + FIRST_DILATION
    span = cap + 2 * outer
    counts = [info_at(o)[0:1, cap : cap + 128] for o in range(-REACH, REACH + 1)]
    begin = [None] * (2 * REACH + 1)
    begin[REACH] = jnp.zeros((1, 128), F32)
    for o in range(1, REACH + 1):
        begin[REACH + o] = begin[REACH + o - 1] + counts[REACH + o - 1]
        begin[REACH - o] = begin[REACH - o + 1] - counts[REACH - o]
    lane = iota((1, 128), 1).astype(F32)
    rowpos = (iota((span, 128), 0) - outer).astype(F32)
    total = jnp.zeros((span, 128), F32)
    for o in range(-REACH, REACH + 1):
        code = info_at(o)[0:1, 0:cap] + 1.0
        pos = jnp.where(lane < counts[REACH + o], begin[REACH + o] + lane, FAR)
        total = total + jnp.where(rowpos == pos, code, 0.0)
    codes = jnp.sum(total, axis=1, keepdims=True)
    d = FIRST_DILATION
    left, mid, right = codes[0 : span - 2 * d], codes[d : span - d], codes[2 * d : span]
    rows = span - 2 * d
    lanes = iota((rows, TABLE), 1).astype(F32)
    flip = lambda c: jnp.where(c == 0.0, 0.0, 5.0 - c)
    idx = jnp.where(mid == 0.0, -1.0, (mid - 1.0) * 25.0 + left * 5.0 + right)
    hot_f_ref[...] = (lanes == idx).astype(BF16)
    idx = jnp.where(mid == 0.0, -1.0, (4.0 - mid) * 25.0 + flip(right) * 5.0 + flip(left))
    hot_r_ref[...] = (lanes == idx).astype(BF16)

    entry = iota((TABLE, 1), 0)
    by25 = (entry * 1311) >> 15
    by5 = (entry * 6554) >> 15
    in_left = by5 - 5 * by25
    in_right = entry - 5 * by5
    sums = jnp.zeros((TABLE, first.shape[1]), F32)
    for q in range(4):
        sums = jnp.where(in_left == q + 1, first[q : q + 1], sums)
    sums = sums + spread(first[4:8], by25)
    after = jnp.zeros((TABLE, first.shape[1]), F32)
    for q in range(4):
        after = jnp.where(in_right == q + 1, first[8 + q : 9 + q], after)
    value, slope = gelu_pair(sums + after)
    b1 = value.astype(BF16)
    b1_ref[...] = b1
    high, low = split(slope)
    s1_ref[0:TABLE] = high
    s1_ref[TABLE : 2 * TABLE] = low
    stream = spread(embed_ref[...], by25) + mm(b1, project)
    value, slope = gelu_pair(stream)
    a2_ref[...] = value.astype(BF16)
    high, low = split(slope)
    s2_ref[0:TABLE] = high
    s2_ref[TABLE : 2 * TABLE] = low

    own_n = counts[REACH]
    before_n, after_n = counts[REACH - 1], counts[REACH + 1]
    grow = cap + 2 * HALO
    lane_h = iota((1, HALO), 1).astype(F32)
    lane_s = iota((1, SPILL), 1).astype(F32)
    row_h = (iota((grow, HALO), 0) - HALO).astype(F32)
    row_s = (iota((grow, SPILL), 0) - HALO).astype(F32)
    row_o = (iota((grow, cap), 0) - HALO).astype(F32)
    own_pos = jnp.where(lane < own_n, lane, FAR)
    acc = mm((row_o == own_pos).astype(BF16), cot_ref[...])
    pos = jnp.where(lane_h >= HALO - before_n[:, 0:HALO], lane_h - HALO, FAR)
    acc = acc + mm((row_h == pos).astype(BF16), r1_ref[...])
    pos = jnp.where(
        counts[REACH - 2][:, 0:SPILL] > 0.0, lane_s - SPILL - before_n[:, 0:SPILL], FAR
    )
    acc = acc + mm((row_s == pos).astype(BF16), r2_ref[...])
    pos = jnp.where(lane_h < after_n[:, 0:HALO], lane_h + own_n[:, 0:HALO], FAR)
    acc = acc + mm((row_h == pos).astype(BF16), l1_ref[...])
    pos = jnp.where(
        (counts[REACH + 2][:, 0:SPILL] > 0.0) & (after_n[:, 0:SPILL] < HALO),
        lane_s + own_n[:, 0:SPILL] + after_n[:, 0:SPILL],
        FAR,
    )
    acc = acc + mm((row_s == pos).astype(BF16), l2_ref[...])
    cx_ref[...] = (0.5 * acc).astype(BF16)


def table_kernel_packed(rels, where_ref, *refs):
    parts = refs[: len(rels)]
    rest = refs[len(rels) : len(rels) + 6]
    outs = refs[len(rels) + 6 :]
    p1_ref = outs[7]
    info_ref = outs[8]
    me = where_ref[0]
    shard = parts[0].shape[0] - 16
    width = parts[0].shape[1] // 2
    info_ref[...] = jnp.zeros(info_ref.shape, F32)
    first = jnp.zeros((16, width), F32)
    for rel, part in zip(rels, parts):
        peer = me ^ rel
        p1_ref[pl.ds(pl.multiple_of(peer * shard, 16), shard), :] = part[0:shard]
        tail = part[shard : shard + 16].astype(F32)
        first = first + tail[:, 0:width] + tail[:, width : 2 * width]
        info_ref[REACH + peer] = jnp.broadcast_to(tail[12:13, 0:256], (8, 256))
    table_body(
        first, p1_ref[...], lambda o: info_ref[me + (REACH + o)], *rest, *outs[:7]
    )


def table_kernel_plain(first_ref, project_ref, info_ref, *refs):
    table_body(first_ref[...], project_ref[...], lambda o: info_ref[REACH + o], *refs)


def tower_body(
    conv, p2, second, p1, count, bases_ref, cx_ref, b1_ref, s1_ref, a2_ref, s2_ref,
    hot_f_ref, hot_r_ref, embed_ref, sal_ref, put,
):
    cap = bases_ref.shape[1]
    grow = cap + 2 * HALO
    inner = cap + 2 * FIRST_DILATION
    d, D = FIRST_DILATION, SECOND_DILATION
    cx = cx_ref[...]
    a2 = a2_ref[...]
    taps = []
    for k in range(3):
        high, low = split(mm(a2, conv(k)))
        taps.append(jnp.concatenate([high, low], axis=0))
    back_mid = mm_nt(cx, p2)
    own_col = (iota((cap, 1), 0) < count).astype(F32)
    own_cx = cx[HALO : HALO + cap]
    own_gb = (own_cx.astype(F32) * own_col).astype(BF16)
    grads = []
    mids = []
    for hot_ref, order in ((hot_f_ref, (0, 1, 2)), (hot_r_ref, (2, 1, 0))):
        before = jnp.zeros((grow, a2_ref.shape[1] // 2), F32)
        for place in range(3):
            hot = hot_ref[place * D : place * D + grow]
            before = before + mm(jnp.concatenate([hot, hot], axis=1), taps[order[place]])
        value, slope = gelu_pair(before)
        mids.append(value[HALO : HALO + cap].astype(BF16))
        grads.append((back_mid * slope).astype(BF16))
    dproj2 = mm_tn(mids[0], own_gb) + mm_tn(mids[1], own_gb)
    put(1, dproj2)
    base_g = cx[D : D + inner].astype(F32)
    b1 = b1_ref[...]
    s1 = s1_ref[...]
    s2 = s2_ref[...]
    sal = jnp.zeros((8, cap), F32)
    emb = embed_ref[...]
    emb8 = jnp.concatenate([emb, emb], axis=0)
    flipped = jnp.concatenate(
        [emb[3 - c : 4 - c] for c in range(4)] * 2, axis=0
    )
    sec_high, sec_low = split(second)
    bases = bases_ref[...]
    dproj1 = None
    for pass_idx, (hot_ref, order) in enumerate(((hot_f_ref, (0, 1, 2)), (hot_r_ref, (2, 1, 0)))):
        grad = grads[pass_idx]
        ga = jnp.zeros((inner, cx.shape[1]), F32)
        for place in range(3):
            ga = ga + mm_nt(grad[place * D : place * D + inner], conv(order[2 - place]))
        hot = hot_ref[2 * D : 2 * D + inner]
        hot2 = jnp.concatenate([hot, hot], axis=1)
        g = base_g + ga * mm(hot2, s2)
        gb = g.astype(BF16)
        own_hot = (hot[d : d + cap].astype(F32) * own_col).astype(BF16)
        own_b1 = mm(own_hot, b1).astype(BF16)
        piece = mm_tn(own_b1, gb[d : d + cap])
        dproj1 = piece if dproj1 is None else dproj1 + piece
        gh = (mm_nt(gb, p1) * mm(hot2, s1)).astype(BF16)
        g_high, g_low = split(g[d : d + cap])
        e_high, e_low = split(emb8 if pass_idx == 0 else flipped)
        sal = sal + mm_nt(e_high, g_high) + mm_nt(e_high, g_low) + mm_nt(e_low, g_high)
        table = jnp.zeros((16, cap), F32)
        for place in range(3):
            k = order[2 - place]
            rows = gh[place * d : place * d + cap]
            table = table + mm_nt(sec_high[16 * k : 16 * k + 16], rows)
            table = table + mm_nt(sec_low[16 * k : 16 * k + 16], rows)
        got = jnp.zeros((4, cap), F32)
        for q in range(4):
            match = bases == (q if pass_idx == 0 else 3 - q)
            got = got + jnp.where(match, table[4 * q : 4 * q + 4], 0.0)
        if pass_idx == 1:
            got = jnp.concatenate([got[3 - c : 4 - c] for c in range(4)], axis=0)
        sal = sal + jnp.concatenate([got, got], axis=0)
    put(0, dproj1)
    live = iota((1, cap), 1) < count
    sal_ref[...] = jnp.where(live, sal[0:4] * (1.0 / math.sqrt(cx.shape[1])), 0.0)


def tower_kernel_packed(rels, where_ref, *refs):
    parts = refs[: len(rels)]
    bases_ref, cx_ref, b1_ref, s1_ref, a2_ref, s2_ref, hf, hr, p1_ref, emb = refs[len(rels) : len(rels) + 10]
    sal_ref, keep_ref, send_ref, conv_ref, p2_ref, all_ref = refs[len(rels) + 10 :]
    me, count = where_ref[0], where_ref[2]
    chans = cx_ref.shape[1]
    width = chans // 2
    shard = chans // 8
    prow = width // 8
    half = 3 * shard // 2
    second = jnp.zeros((48, width), F32)
    for rel, part in zip(rels, parts):
        peer = me ^ rel
        at = pl.multiple_of(peer * shard, 16)
        conv_ref[0, pl.ds(at, shard), :] = part[0:shard, 0:width]
        conv_ref[1, pl.ds(at, half - shard), :] = part[shard:half, 0:width]
        at_half = pl.multiple_of(peer * shard + (half - shard), 16)
        conv_ref[1, pl.ds(at_half, half - shard), :] = part[0 : half - shard, width : 2 * width]
        conv_ref[2, pl.ds(at, shard), :] = part[half - shard : half, width : 2 * width]
        p2_ref[pl.ds(pl.multiple_of(peer * prow, 16), prow), :] = part[half : half + prow]
        tail = part[half + prow : half + prow + 48].astype(F32)
        second = second + tail[:, 0:width] + tail[:, width : 2 * width]

    def put(block, value):
        rows = value.shape[0] // 4
        for c in range(4):
            all_ref[(4 * block + c) ^ me] = value[c * rows : (c + 1) * rows]

    tower_body(
        lambda k: conv_ref[k], p2_ref[...], second, p1_ref[...], count, bases_ref, cx_ref,
        b1_ref, s1_ref, a2_ref, s2_ref, hf, hr, emb, sal_ref, put,
    )
    for rel in range(4):
        keep_ref[rel] = all_ref[2 * rel]
        send_ref[rel] = all_ref[2 * rel + 1].astype(BF16)


def tower_kernel_plain(
    where_ref, conv_ref, p2_ref, second_ref, p1_ref, bases_ref, cx_ref, b1_ref, s1_ref,
    a2_ref, s2_ref, hf, hr, emb, sal_ref, grad_ref,
):
    def put(block, value):
        rows = value.shape[0]
        grad_ref[block * rows : (block + 1) * rows] = value

    tower_body(
        lambda k: conv_ref[k], p2_ref[...], second_ref[...], p1_ref[...], where_ref[2],
        bases_ref, cx_ref, b1_ref, s1_ref, a2_ref, s2_ref, hf, hr, emb, sal_ref, put,
    )


def core_sum_kernel(keep_ref, recv_ref, own_ref, x_ref, y_ref, d_ref):
    own_ref[...] = keep_ref[0] + recv_ref[0].astype(F32)
    for rel, out in ((1, x_ref), (2, y_ref), (3, d_ref)):
        out[...] = (keep_ref[rel] + recv_ref[rel].astype(F32)).astype(BF16)


def plane_sum_kernel(where_ref, own_ref, x_ref, y_ref, d_ref, *refs):
    outs, sum_ref = refs[:-1], refs[-1]
    sum_ref[...] = (
        own_ref[...] + x_ref[...].astype(F32) + y_ref[...].astype(F32) + d_ref[...].astype(F32)
    )
    z = where_ref[1]
    rows = own_ref.shape[0] // len(outs)
    width = own_ref.shape[1] // 2
    for rel, out in enumerate(outs):
        value = sum_ref[pl.ds(pl.multiple_of((z ^ rel) * rows, 8), rows), :]
        if rel == 0:
            out[...] = value
        else:
            out[...] = jnp.concatenate(
                [value[:, 0:width], value[:, width : 2 * width]], axis=0
            ).astype(BF16)


def last_sum_kernel(scale, own_ref, *refs):
    out_ref = refs[-1]
    total = own_ref[...]
    rows = total.shape[0]
    for ref in refs[:-1]:
        value = ref[...].astype(F32)
        total = total + jnp.concatenate([value[0:rows], value[rows : 2 * rows]], axis=1)
    out_ref[...] = total * scale


def xor_move(array, axis, bits):
    return lax.ppermute(array, axis, [(i, i ^ bits) for i in range(lax.axis_size(axis))])


def shift_move(array, axis, by):
    size = lax.axis_size(axis)
    return lax.ppermute(array, axis, [(i, i + by) for i in range(size) if 0 <= i + by < size])


def table_shapes(cap, chans, width):
    rows = cap + 2 * (HALO + SECOND_DILATION)
    return [
        ((TABLE, width), BF16),
        ((2 * TABLE, width), BF16),
        ((TABLE, chans), BF16),
        ((2 * TABLE, chans), BF16),
        ((rows, TABLE), BF16),
        ((rows, TABLE), BF16),
        ((cap + 2 * HALO, chans), BF16),
    ]


def fast_shards(bases, where, cot, c1, p1, c2, p2, embed):
    cap, chans = cot.shape
    width = c1.shape[2]
    n_dp = lax.axis_size("dp")
    m1, m2, r1, r2, l1, l2 = call(
        prep_kernel,
        [
            ((p1.shape[0] + 16, chans), BF16),
            ((3 * c2.shape[1] // 2 + p2.shape[0] + 48, chans), BF16),
            ((HALO, chans), BF16),
            ((SPILL, chans), BF16),
            ((HALO, chans), BF16),
            ((SPILL, chans), BF16),
        ],
        [where, bases, cot, c1, p1, c2, p2, embed],
    )

    def gather(m):
        near = [m] + [xor_move(m, "seq", bits) for bits in (2, 4, 6)]
        return near + [xor_move(a, "seq", 1) for a in near]

    rels = (0, 2, 4, 6, 1, 3, 5, 7)
    g1 = gather(m1)
    halos = [
        shift_move(r1, "seq", 1),
        shift_move(r2, "seq", 2),
        shift_move(l1, "seq", -1),
        shift_move(l2, "seq", -2),
    ]
    g2 = gather(m2)
    tables = call(
        functools.partial(table_kernel_packed, rels),
        table_shapes(cap, chans, width) + [((width, chans), BF16)],
        [where, *g1, cot, *halos, embed],
        scratch=[pltpu.VMEM((8 + 2 * REACH, 8, 256), F32)],
        cost=pl.CostEstimate(flops=3 * 10**8, bytes_accessed=4 * 10**6, transcendentals=0),
    )
    b1, s1, a2, s2, hf, hr, cx, p1_full = tables
    rows = chans // 8
    sal, keep, send = call(
        functools.partial(tower_kernel_packed, rels),
        [((4, cap), F32), ((4, rows, chans), F32), ((4, rows, chans), BF16)],
        [where, *g2, bases, cx, b1, s1, a2, s2, hf, hr, p1_full, embed],
        scratch=[
            pltpu.VMEM((3, chans, width), BF16),
            pltpu.VMEM((width, chans), BF16),
            pltpu.VMEM((8, rows, chans), F32),
        ],
        limit=40,
    )
    recv = xor_move(send, "seq", 1)
    own, sx, sy, sd = call(
        core_sum_kernel,
        [((rows, chans), F32)] + [((rows, chans), BF16)] * 3,
        [keep, recv],
    )
    got = [xor_move(a, "seq", bits) for a, bits in ((sx, 2), (sy, 4), (sd, 6))]
    part = rows // n_dp
    outs = call(
        plane_sum_kernel,
        [((part, chans), F32)] + [((2 * part, width), BF16)] * (n_dp - 1),
        [where, own, *got],
        scratch=[pltpu.VMEM((rows, chans), F32)],
    )
    far = [xor_move(a, "dp", rel + 1) for rel, a in enumerate(outs[1:])]
    scale = 1.0 / math.sqrt(8 * n_dp * cap)
    (grad,) = call(
        functools.partial(last_sum_kernel, scale), [((part, chans), F32)], [outs[0], *far]
    )
    return sal[None], grad.reshape(-1)


def plain_shards(bases, where, cot, c1, p1, c2, p2, embed):
    cap, chans = cot.shape
    width = c1.shape[2]
    me, count = where[0], where[2]
    shard = c1.shape[1]
    own = lax.dynamic_slice_in_dim(embed, me * shard, shard, 1)
    act, slope = gelu_pair(own)
    taps = c1.astype(F32)
    high = lax.Precision.HIGHEST
    first = jnp.einsum("qc,kcb->kqb", act.astype(BF16).astype(F32), taps, precision=high)
    second = jnp.einsum("qc,dc,kcb->kqdb", slope, own, taps, precision=high)
    first = lax.psum(first.reshape(12, width), "seq")
    second = lax.psum(second.reshape(48, width), "seq")
    first = jnp.concatenate([first, jnp.zeros((4, width), F32)], axis=0)
    p1_full = lax.all_gather(p1, "seq", axis=0, tiled=True)
    p2_full = lax.all_gather(p2, "seq", axis=0, tiled=True)
    conv = lax.all_gather(c2, "seq", axis=1, tiled=True)
    info = jnp.concatenate(
        [bases.astype(F32), jnp.broadcast_to(count.astype(F32), (1, 128))], axis=1
    )
    info = lax.all_gather(info, "seq", axis=0, tiled=True)
    info = jnp.pad(info, ((REACH, REACH), (0, 0)))
    info = lax.dynamic_slice_in_dim(info, me, 2 * REACH + 1, 0)
    info = jnp.broadcast_to(info[:, None, :], (2 * REACH + 1, 8, cap + 128))
    padded = jnp.pad(cot, ((HALO, 0), (0, 0)))
    last = lax.dynamic_slice_in_dim(padded, count, HALO, 0)
    halos = [
        shift_move(last, "seq", 1),
        shift_move(last[HALO - SPILL :], "seq", 2),
        shift_move(cot[:HALO], "seq", -1),
        shift_move(cot[:SPILL], "seq", -2),
    ]
    b1, s1, a2, s2, hf, hr, cx = call(
        table_kernel_plain,
        table_shapes(cap, chans, width),
        [first, p1_full, info, cot, *halos, embed],
    )
    sal, grad = call(
        tower_kernel_plain,
        [((4, cap), F32), ((2 * width, chans), F32)],
        [where, conv, p2_full, second, p1_full, bases, cx, b1, s1, a2, s2, hf, hr, embed],
        limit=40,
    )
    scale = 1.0 / math.sqrt(lax.axis_size("seq") * lax.axis_size("dp") * cap)
    grad = lax.psum_scatter(
        grad.reshape(-1) * scale, ("seq", "dp"), scatter_dimension=0, tiled=True
    )
    return sal[None], grad


def shards(
    bases,
    lengths,
    cotangent,
    first_conv_taps,
    first_projection,
    second_conv_taps,
    second_projection,
    embed,
):
    where = jnp.stack(
        [
            lax.axis_index("seq").astype(jnp.int32),
            lax.axis_index("dp").astype(jnp.int32),
            lengths[0, 0],
        ]
    )
    run = fast_shards if lax.axis_size("seq") == 8 and lax.axis_size("dp") == 4 else plain_shards
    return run(
        bases, where, cotangent[0], first_conv_taps, first_projection, second_conv_taps,
        second_projection, embed,
    )


def solution(mesh):
    in_specs = (
        P("dp", "seq"),
        P("dp", "seq"),
        P("dp", "seq", None),
        P(None, "seq", None),
        P("seq", None),
        P(None, "seq", None),
        P("seq", None),
        P(),
    )
    out_specs = (P("dp", None, "seq"), P(("seq", "dp")))
    return jax.shard_map(shards, mesh=mesh, in_specs=in_specs, out_specs=out_specs, check_vma=False)
```

time: 268 us -> 91 us (0.34)
  waiting for transfers between devices: 138 us -> 36.6 us
  blocking collectives: 25.1 us -> 0 us
  matrix products: 21.3 us -> 0 us
  local copies, waits for them, and re-layouts: 23 us -> 8.21 us
  between operations: 16.2 us -> 1.46 us
  other arithmetic: 11.5 us -> 0.08 us
  Pallas kernels: 0 us -> 10.1 us
    unnamed x4 -> x0, waiting for transfers between devices: 121 us -> none
    all_gather x2 -> x0, blocking collectives: 25.1 us -> none  [fetch(): lax.all_gather(proj_shard, 'seq', axis=0, tiled=True)]
    dot_general x31 -> x0, matrix products: 21.3 us -> none  [the longest x12 7.94 us: taps_forward(): jnp.dot(window_rows, weights[tap_order[member][offset]], preferred_elemen...]
    ppermute x17 -> x25, waiting for transfers between devices: 17.1 us -> 36.6 us  [the longest x21 19.8 us: xor_move(): lax.ppermute(array, axis, [(i, i ^ bits) for i in range(lax.axis_size(axi...]
    pallas_call x0 -> x6, Pallas kernels: none -> 10.1 us  [call(): pl.pallas_call(body, out_shape=[jax.ShapeDtypeStruct(s, d) for s, d in ou...]
    dynamic_update_slice x8 -> x0, local copies, waits for them, and re-layouts: 5.75 us -> none  [widen(): lax.dynamic_update_slice_in_dim(extended[member], right_rim[member], coun...]
    rev x4 -> x0, local copies, waits for them, and re-layouts: 5.37 us -> none  [the longest x3 3.23 us: flip_live(): jnp.flip(values, axis_idx)]
    slice x17 -> x0, local copies, waits for them, and re-layouts: 4.12 us -> none  [the longest x4 1.48 us: widen(): right_rim[member]]
  transfers between devices with their start and end apart: 20 -> 25, of which waited for: 8 -> 13; matrix products, arithmetic and copies ran while one was open for 14% -> 0% of each run, Pallas kernels for 0% -> 2%
where the time goes in v1:
time: 91 us; the launch traced here: 90.4 us
  waiting for transfers between devices  36.6 us (40%)
  starting transfers between devices  34 us (37%)
  Pallas kernels  10.1 us (11%)
  local copies, waits for them, and re-layouts  8.21 us (9%)
  between operations  1.46 us (2%)
    ppermute x21, starting transfers between devices, xor_move(): lax.ppermute(array, axis, [(i, i ^ bits) for i in range(lax.axis_size(axi...  26.3 us
    ppermute x21, waiting for transfers between devices, xor_move(): lax.ppermute(array, axis, [(i, i ^ bits) for i in range(lax.axis_size(axi...  19.8 us
    ppermute x4, waiting for transfers between devices, shift_move(): lax.ppermute(array, axis, [(i, i + by) for i in range(size) if 0 <= i + b...  16.8 us
    pallas_call x6, Pallas kernels, call(): pl.pallas_call(body, out_shape=[jax.ShapeDtypeStruct(s, d) for s, d in ou...  10.1 us
    ppermute x4, starting transfers between devices, shift_move(): lax.ppermute(array, axis, [(i, i + by) for i in range(size) if 0 <= i + b...  7.63 us
    unnamed x22, local copies, waits for them, and re-layouts  7.57 us
  transfers between devices with their start and end apart: 25, of which 13 were waited for; matrix products, arithmetic and copies ran while one was open for 0% of the time, Pallas kernels for 2%

profile of v1, /device:TPU:0, one launch (start us, length us, event | category | flops | bytes accessed | tf_op | source)
XLA Modules:
  0.0 90.4 jit_solution(15353453483553135796)
XLA Ops:
  1.4 0.9 %copy-done = bf16[1,128,768]{2,1,0:T(8,128)(2,1)S(1)} copy-done((bf16[1,128,768]{2,1,0:T(8,128)(2,1)S(1)}, bf16[1,128,768]{2,1,0:T(8,128)(2,1)}, u32[]{:S(2)}) %copy-start) | copy-done | bytes 196632
  2.3 0.9 %copy-done.2 = bf16[3,96,384]{2,1,0:T(8,128)(2,1)S(1)} copy-done((bf16[3,96,384]{2,1,0:T(8,128)(2,1)S(1)}, bf16[3,96,384]{2,1,0:T(8,128)(2,1)}, u32[]{:S(2)}) %copy-start.2) | copy-done | bytes 221208
  3.3 0.9 %copy-done.3 = bf16[3,96,384]{2,1,0:T(8,128)(2,1)S(1)} copy-done((bf16[3,96,384]{2,1,0:T(8,128)(2,1)S(1)}, bf16[3,96,384]{2,1,0:T(8,128)(2,1)}, u32[]{:S(2)}) %copy-start.3) | copy-done | bytes 221208
  4.2 0.7 copy-done.4
  4.9 0.9 copy-done.7
  5.8 0.9 copy-done.8
  6.7 0.7 copy-done.9
  7.3 0.9 %shard_map.95 = (bf16[64,768]{1,0:T(8,128)(2,1)S(1)}, bf16[240,768]{1,0:T(8,128)(2,1)S(1)}, bf16[80,768]{1,0:T(8,128)(2,1)S(1)}, bf16[16,768]{1,0:T(8,128)(2,1)S...) custom-call(s32[3]{0:T(128)S(1)} %pad_add_fusion.where_ref, s32[1,128]{1,0:T(1,128)S(1)} %copy-done.9, ...), custom_call_target="tpu_custom_call" | custom-call | tf_op jit(solution)/shard_map/pallas_call | solution.py:62
  8.3 4.0 %collective-permute-start.2 = (bf16[240,768]{1,0:T(8,128)(2,1)S(1)}, bf16[240,768]{1,0:T(8,128)(2,1)S(1)}, u32[]{:S(2)}, u32[]{:S(2)}) collective-permute-start(bf16[240,768]{1,0:T(8,128)(2,1)S(1)} %get-tuple-element.27.refs_0_), channel_id=1, source_target_pairs={{0,24},{4,28},{8,16},{12,20},{16,8},{20,12},{24,0},{28,4},{1,25},{... | collective-permute-start | bytes 1105928 | tf_op jit(solution)/shard_map/ppermute | solution.py:406
  12.2 0.5 collective-permute-start.1
  12.7 0.1 collective-permute-start
  12.9 3.8 %collective-permute-start.15 = (bf16[16,768]{1,0:T(8,128)(2,1)S(1)}, bf16[16,768]{1,0:T(8,128)(2,1)S(1)}, u32[]{:S(2)}, u32[]{:S(2)}) collective-permute-start(bf16[16,768]{1,0:T(8,128)(2,1)S(1)} %get-tuple-element.30), channel_id=1, source_target_pairs={{0,8},{4,12},{8,16},{12,20},{16,24},{20,28},{1,9},{5,13},{9,17},{1... | collective-permute-start | bytes 73736 | tf_op jit(solution)/shard_map/ppermute | solution.py:411
  16.7 11.8 %collective-permute-done.15.refs_10_ = bf16[16,768]{1,0:T(8,128)(2,1)S(1)} collective-permute-done((bf16[16,768]{1,0:T(8,128)(2,1)S(1)}, bf16[16,768]{1,0:T(8,128)(2,1)S(1)}, u32[]{:S(2)}, u32[]{:S(2)}) %collective-permute-start.15) | collective-permute-done | bytes 24608 | tf_op jit(solution)/shard_map/ppermute | solution.py:411
  28.5 1.3 %collective-permute-start.17 = (bf16[16,768]{1,0:T(8,128)(2,1)S(1)}, bf16[16,768]{1,0:T(8,128)(2,1)S(1)}, u32[]{:S(2)}, u32[]{:S(2)}) collective-permute-start(bf16[16,768]{1,0:T(8,128)(2,1)S(1)} %get-tuple-element.32), channel_id=1, source_target_pairs={{8,0},{12,4},{16,8},{20,12},{24,16},{28,20},{9,1},{13,5},{17,9},{2... | collective-permute-start | bytes 73736 | tf_op jit(solution)/shard_map/ppermute | solution.py:411
  29.8 4.9 %collective-permute-done.17.refs_12_ = bf16[16,768]{1,0:T(8,128)(2,1)S(1)} collective-permute-done((bf16[16,768]{1,0:T(8,128)(2,1)S(1)}, bf16[16,768]{1,0:T(8,128)(2,1)S(1)}, u32[]{:S(2)}, u32[]{:S(2)}) %collective-permute-start.17) | collective-permute-done | bytes 24608 | tf_op jit(solution)/shard_map/ppermute | solution.py:411
  34.7 1.1 %collective-permute-start.9 = (bf16[64,768]{1,0:T(8,128)(2,1)S(1)}, bf16[64,768]{1,0:T(8,128)(2,1)S(1)}, u32[]{:S(2)}, u32[]{:S(2)}) collective-permute-start(bf16[64,768]{1,0:T(8,128)(2,1)S(1)} %get-tuple-element.28.refs_0_), channel_id=1, source_target_pairs={{0,24},{4,28},{8,16},{12,20},{16,8},{20,12},{24,0},{28,4},{1,25},{... | collective-permute-start | bytes 294920 | tf_op jit(solution)/shard_map/ppermute | solution.py:406
  35.9 3.2 %collective-permute-start.8 = (bf16[64,768]{1,0:T(8,128)(2,1)S(1)}, bf16[64,768]{1,0:T(8,128)(2,1)S(1)}, u32[]{:S(2)}, u32[]{:S(2)}) collective-permute-start(bf16[64,768]{1,0:T(8,128)(2,1)S(1)} %get-tuple-element.28.refs_0_), channel_id=1, source_target_pairs={{0,16},{4,20},{8,24},{12,28},{16,0},{20,4},{24,8},{28,12},{1,17},{... | collective-permute-start | bytes 294920 | tf_op jit(solution)/shard_map/ppermute | solution.py:406
  39.1 1.1 %collective-permute-done.9.refs_3_ = bf16[64,768]{1,0:T(8,128)(2,1)S(1)} collective-permute-done((bf16[64,768]{1,0:T(8,128)(2,1)S(1)}, bf16[64,768]{1,0:T(8,128)(2,1)S(1)}, u32[]{:S(2)}, u32[]{:S(2)}) %collective-permute-start.9) | collective-permute-done | bytes 98336 | tf_op jit(solution)/shard_map/ppermute | solution.py:406
  40.2 3.0 %collective-permute-start.7 = (bf16[64,768]{1,0:T(8,128)(2,1)S(1)}, bf16[64,768]{1,0:T(8,128)(2,1)S(1)}, u32[]{:S(2)}, u32[]{:S(2)}) collective-permute-start(bf16[64,768]{1,0:T(8,128)(2,1)S(1)} %get-tuple-element.28.refs_0_), channel_id=1, source_target_pairs={{0,8},{4,12},{8,0},{12,4},{16,24},{20,28},{24,16},{28,20},{1,9},{5... | collective-permute-start | bytes 294920 | tf_op jit(solution)/shard_map/ppermute | solution.py:406
  43.3 1.3 %collective-permute-start.14 = (bf16[80,768]{1,0:T(8,128)(2,1)S(1)}, bf16[80,768]{1,0:T(8,128)(2,1)S(1)}, u32[]{:S(2)}, u32[]{:S(2)}) collective-permute-start(bf16[80,768]{1,0:T(8,128)(2,1)S(1)} %get-tuple-element.29), channel_id=1, source_target_pairs={{0,4},{4,8},{8,12},{12,16},{16,20},{20,24},{24,28},{1,5},{5,9},{9,... | collective-permute-start | bytes 368648 | tf_op jit(solution)/shard_map/ppermute | solution.py:411
  44.6 1.3 %collective-permute-done.7.refs_1_ = bf16[64,768]{1,0:T(8,128)(2,1)S(1)} collective-permute-done((bf16[64,768]{1,0:T(8,128)(2,1)S(1)}, bf16[64,768]{1,0:T(8,128)(2,1)S(1)}, u32[]{:S(2)}, u32[]{:S(2)}) %collective-permute-start.7) | collective-permute-done | bytes 98336 | tf_op jit(solution)/shard_map/ppermute | solution.py:406
  45.9 1.3 %collective-permute-start.16 = (bf16[80,768]{1,0:T(8,128)(2,1)S(1)}, bf16[80,768]{1,0:T(8,128)(2,1)S(1)}, u32[]{:S(2)}, u32[]{:S(2)}) collective-permute-start(bf16[80,768]{1,0:T(8,128)(2,1)S(1)} %get-tuple-element.31), channel_id=1, source_target_pairs={{4,0},{8,4},{12,8},{16,12},{20,16},{24,20},{28,24},{5,1},{9,5},{13... | collective-permute-start | bytes 368648 | tf_op jit(solution)/shard_map/ppermute | solution.py:411
  47.2 1.2 %collective-permute-start.3 = (bf16[240,768]{1,0:T(8,128)(2,1)S(1)}, bf16[240,768]{1,0:T(8,128)(2,1)S(1)}, u32[]{:S(2)}, u32[]{:S(2)}) collective-permute-start(bf16[240,768]{1,0:T(8,128)(2,1)S(1)} %get-tuple-element.27.refs_0_), channel_id=1, source_target_pairs={{0,4},{4,0},{8,12},{12,8},{16,20},{20,16},{24,28},{28,24},{1,5},{5... | collective-permute-start | bytes 1105928 | tf_op jit(solution)/shard_map/ppermute | solution.py:406
  48.4 0.4 collective-permute-start.5
  49.1 3.4 %collective-permute-start.13 = (bf16[64,768]{1,0:T(8,128)(2,1)S(1)}, bf16[64,768]{1,0:T(8,128)(2,1)S(1)}, u32[]{:S(2)}, u32[]{:S(2)}) collective-permute-start(bf16[64,768]{1,0:T(8,128)(2,1)S(1)} %collective-permute-done.9.refs_3_), channel_id=1, source_target_pairs={{0,4},{4,0},{8,12},{12,8},{16,20},{20,16},{24,28},{28,24},{1,5},{5... | collective-permute-start | bytes 294920 | tf_op jit(solution)/shard_map/ppermute | solution.py:406
  52.5 0.9 %collective-permute-done.13.refs_7_ = bf16[64,768]{1,0:T(8,128)(2,1)S(1)} collective-permute-done((bf16[64,768]{1,0:T(8,128)(2,1)S(1)}, bf16[64,768]{1,0:T(8,128)(2,1)S(1)}, u32[]{:S(2)}, u32[]{:S(2)}) %collective-permute-start.13) | collective-permute-done | bytes 98336 | tf_op jit(solution)/shard_map/ppermute | solution.py:406
  53.4 0.4 collective-permute-start.12
  53.8 0.9 %collective-permute-done.12.refs_6_ = bf16[64,768]{1,0:T(8,128)(2,1)S(1)} collective-permute-done((bf16[64,768]{1,0:T(8,128)(2,1)S(1)}, bf16[64,768]{1,0:T(8,128)(2,1)S(1)}, u32[]{:S(2)}, u32[]{:S(2)}) %collective-permute-start.12) | collective-permute-done | bytes 98336 | tf_op jit(solution)/shard_map/ppermute | solution.py:406
  54.7 0.4 collective-permute-start.11
  55.1 0.9 %collective-permute-done.11.refs_5_ = bf16[64,768]{1,0:T(8,128)(2,1)S(1)} collective-permute-done((bf16[64,768]{1,0:T(8,128)(2,1)S(1)}, bf16[64,768]{1,0:T(8,128)(2,1)S(1)}, u32[]{:S(2)}, u32[]{:S(2)}) %collective-permute-start.11) | collective-permute-done | bytes 98336 | tf_op jit(solution)/shard_map/ppermute | solution.py:406
  56.0 0.9 %copy-done.1 = bf16[1,128,768]{2,1,0:T(8,128)(2,1)S(1)} copy-done((bf16[1,128,768]{2,1,0:T(8,128)(2,1)S(1)}, bf16[1,128,768]{2,1,0:T(8,128)(2,1)}, u32[]{:S(2)}) %copy-start.1) | copy-done | bytes 196632
  56.9 0.7 copy-done.5
  57.6 2.0 %shard_map.96 = (bf16[128,384]{1,0:T(8,128)(2,1)S(1)}, bf16[256,384]{1,0:T(8,128)(2,1)S(1)}, bf16[128,768]{1,0:T(8,128)(2,1)S(1)}, bf16[256,768]{1,0:T(8,128)(2,...) custom-call(s32[3]{0:T(128)S(1)} %pad_add_fusion.where_ref, ...), custom_call_target="tpu_custom_call" | custom-call | flops 300000000 | bytes 4000000 | tf_op jit(solution)/shard_map/pallas_call | solution.py:62
  59.7 6.4 %shard_map.97 = (f32[4,128]{1,0:T(4,128)}, f32[4,96,768]{2,1,0:T(8,128)S(1)}, bf16[4,96,768]{2,1,0:T(8,128)(2,1)S(1)}) custom-call(s32[3]{0:T(128)S(1)} %pad_add_fusion.where_ref, bf16[240,768]{1,0:T(8,128)(2,1)S(1)} %get-tuple-element.27.refs_0_, bf16[240,768]{1,0:T(8,128)(2,1)S(1)} %collective-permute-done.refs_1_, ...), custom_call_target="tpu_custom_call" | custom-call | tf_op jit(solution)/shard_map/pallas_call | solution.py:62
  66.1 0.4 collective-permute-start.18
  66.5 1.6 %collective-permute-done.18.recv_ref = bf16[4,96,768]{2,1,0:T(8,128)(2,1)S(1)} collective-permute-done((bf16[4,96,768]{2,1,0:T(8,128)(2,1)S(1)}, bf16[4,96,768]{2,1,0:T(8,128)(2,1)S(1)}, u32[]{:S(2)}, u32[]{:S(2)}) %collective-permute-start.18) | collective-permute-done | bytes 589856 | tf_op jit(solution)/shard_map/ppermute | solution.py:406
  68.1 0.1 shard_map.98
  68.2 1.9 %collective-permute-start.19 = (bf16[96,768]{1,0:T(8,128)(2,1)S(1)}, bf16[96,768]{1,0:T(8,128)(2,1)S(1)}, u32[]{:S(2)}, u32[]{:S(2)}) collective-permute-start(bf16[96,768]{1,0:T(8,128)(2,1)S(1)} %get-tuple-element.45), channel_id=1, source_target_pairs={{0,8},{4,12},{8,0},{12,4},{16,24},{20,28},{24,16},{28,20},{1,9},{5... | collective-permute-start | bytes 442376 | tf_op jit(solution)/shard_map/ppermute | solution.py:406
  70.2 1.6 %collective-permute-start.21 = (bf16[96,768]{1,0:T(8,128)(2,1)S(1)}, bf16[96,768]{1,0:T(8,128)(2,1)S(1)}, u32[]{:S(2)}, u32[]{:S(2)}) collective-permute-start(bf16[96,768]{1,0:T(8,128)(2,1)S(1)} %get-tuple-element.47), channel_id=1, source_target_pairs={{0,24},{4,28},{8,16},{12,20},{16,8},{20,12},{24,0},{28,4},{1,25},{... | collective-permute-start | bytes 442376 | tf_op jit(solution)/shard_map/ppermute | solution.py:406
  71.8 3.2 %collective-permute-done.19.x_ref = bf16[96,768]{1,0:T(8,128)(2,1)S(1)} collective-permute-done((bf16[96,768]{1,0:T(8,128)(2,1)S(1)}, bf16[96,768]{1,0:T(8,128)(2,1)S(1)}, u32[]{:S(2)}, u32[]{:S(2)}) %collective-permute-start.19) | collective-permute-done | bytes 147488 | tf_op jit(solution)/shard_map/ppermute | solution.py:406
  75.0 4.2 %collective-permute-done.20.y_ref = bf16[96,768]{1,0:T(8,128)(2,1)S(1)} collective-permute-done((bf16[96,768]{1,0:T(8,128)(2,1)S(1)}, bf16[96,768]{1,0:T(8,128)(2,1)S(1)}, u32[]{:S(2)}, u32[]{:S(2)}) %collective-permute-start.20) | collective-permute-done | bytes 147488 | tf_op jit(solution)/shard_map/ppermute | solution.py:406
  79.2 0.6 shard_map.99
  79.8 1.6 %collective-permute-start.22 = (bf16[48,384]{1,0:T(8,128)(2,1)S(1)}, bf16[48,384]{1,0:T(8,128)(2,1)S(1)}, u32[]{:S(2)}, u32[]{:S(2)}) collective-permute-start(bf16[48,384]{1,0:T(8,128)(2,1)S(1)} %get-tuple-element.49), channel_id=1, source_target_pairs={{0,1},{1,0},{2,3},{3,2},{4,5},{5,4},{6,7},{7,6},{8,9},{9,8},{10,11... | collective-permute-start | bytes 110600 | tf_op jit(solution)/shard_map/ppermute | solution.py:406
  81.4 2.6 %collective-permute-start.23 = (bf16[48,384]{1,0:T(8,128)(2,1)S(1)}, bf16[48,384]{1,0:T(8,128)(2,1)S(1)}, u32[]{:S(2)}, u32[]{:S(2)}) collective-permute-start(bf16[48,384]{1,0:T(8,128)(2,1)S(1)} %get-tuple-element.50), channel_id=1, source_target_pairs={{0,2},{1,3},{2,0},{3,1},{4,6},{5,7},{6,4},{7,5},{8,10},{9,11},{10,... | collective-permute-start | bytes 110600 | tf_op jit(solution)/shard_map/ppermute | solution.py:406
  84.0 0.2 collective-permute-start.24
  84.3 2.4 %collective-permute-done.23.refs_1_ = bf16[48,384]{1,0:T(8,128)(2,1)S(1)} collective-permute-done((bf16[48,384]{1,0:T(8,128)(2,1)S(1)}, bf16[48,384]{1,0:T(8,128)(2,1)S(1)}, u32[]{:S(2)}, u32[]{:S(2)}) %collective-permute-start.23) | collective-permute-done | bytes 36896 | tf_op jit(solution)/shard_map/ppermute | solution.py:406
  86.6 3.1 %collective-permute-done.24.refs_2_ = bf16[48,384]{1,0:T(8,128)(2,1)S(1)} collective-permute-done((bf16[48,384]{1,0:T(8,128)(2,1)S(1)}, bf16[48,384]{1,0:T(8,128)(2,1)S(1)}, u32[]{:S(2)}, u32[]{:S(2)}) %collective-permute-start.24) | collective-permute-done | bytes 36896 | tf_op jit(solution)/shard_map/ppermute | solution.py:406
  89.8 0.6 reshape.7
  (32 shorter events, 0.5 us)
Async XLA Ops:
  0.6 59.0 %copy-start.6 = (f32[4,768]{1,0:T(4,128)S(1)}, f32[4,768]{1,0:T(4,128)}, u32[]{:S(2)}) copy-start(f32[4,768]{1,0:T(4,128)} %refs_17_.1) | copy-start | bytes 36868
  0.6 59.0 %copy-start.10 = (s32[1,128]{1,0:T(1,128)S(1)}, s32[1,128]{1,0:T(1,128)}, u32[]{:S(2)}) copy-start(s32[1,128]{1,0:T(1,128)} %refs_8_.1) | copy-start | bytes 1540
  1.4 0.9 %copy-start = (bf16[1,128,768]{2,1,0:T(8,128)(2,1)S(1)}, bf16[1,128,768]{2,1,0:T(8,128)(2,1)}, u32[]{:S(2)}) copy-start(bf16[1,128,768]{2,1,0:T(8,128)(2,1)} %param.10) | copy-start | bytes 589828
  2.3 0.9 %copy-start.2 = (bf16[3,96,384]{2,1,0:T(8,128)(2,1)S(1)}, bf16[3,96,384]{2,1,0:T(8,128)(2,1)}, u32[]{:S(2)}) copy-start(bf16[3,96,384]{2,1,0:T(8,128)(2,1)} %c1_ref.1) | copy-start | bytes 663556
  3.3 0.9 %copy-start.3 = (bf16[3,96,384]{2,1,0:T(8,128)(2,1)S(1)}, bf16[3,96,384]{2,1,0:T(8,128)(2,1)}, u32[]{:S(2)}) copy-start(bf16[3,96,384]{2,1,0:T(8,128)(2,1)} %c2_ref.1) | copy-start | bytes 663556
  4.2 0.7 copy-start.4
  4.9 0.9 copy-start.7
  5.8 0.9 copy-start.8
  6.7 0.7 copy-start.9
  8.3 40.1 %collective-permute-start.2 = (bf16[240,768]{1,0:T(8,128)(2,1)S(1)}, bf16[240,768]{1,0:T(8,128)(2,1)S(1)}, u32[]{:S(2)}, u32[]{:S(2)}) collective-permute-start(bf16[240,768]{1,0:T(8,128)(2,1)S(1)} %get-tuple-element.27.refs_0_), channel_id=1, source_target_pairs={{0,24},{4,28},{8,16},{12,20},{16,8},{20,12},{24,0},{28,4},{1,25},{... | collective-permute-start | bytes 1105928 | tf_op jit(solution)/shard_map/ppermute | solution.py:406
  12.2 36.2 %collective-permute-start.1 = (bf16[240,768]{1,0:T(8,128)(2,1)S(1)}, bf16[240,768]{1,0:T(8,128)(2,1)S(1)}, u32[]{:S(2)}, u32[]{:S(2)}) collective-permute-start(bf16[240,768]{1,0:T(8,128)(2,1)S(1)} %get-tuple-element.27.refs_0_), channel_id=1, source_target_pairs={{0,16},{4,20},{8,24},{12,28},{16,0},{20,4},{24,8},{28,12},{1,17},{... | collective-permute-start | bytes 1105928 | tf_op jit(solution)/shard_map/ppermute | solution.py:406
  12.7 36.1 %collective-permute-start = (bf16[240,768]{1,0:T(8,128)(2,1)S(1)}, bf16[240,768]{1,0:T(8,128)(2,1)S(1)}, u32[]{:S(2)}, u32[]{:S(2)}) collective-permute-start(bf16[240,768]{1,0:T(8,128)(2,1)S(1)} %get-tuple-element.27.refs_0_), channel_id=1, source_target_pairs={{0,8},{4,12},{8,0},{12,4},{16,24},{20,28},{24,16},{28,20},{1,9},{5... | collective-permute-start | bytes 1105928 | tf_op jit(solution)/shard_map/ppermute | solution.py:406
  12.9 15.7 %collective-permute-start.15 = (bf16[16,768]{1,0:T(8,128)(2,1)S(1)}, bf16[16,768]{1,0:T(8,128)(2,1)S(1)}, u32[]{:S(2)}, u32[]{:S(2)}) collective-permute-start(bf16[16,768]{1,0:T(8,128)(2,1)S(1)} %get-tuple-element.30), channel_id=1, source_target_pairs={{0,8},{4,12},{8,16},{12,20},{16,24},{20,28},{1,9},{5,13},{9,17},{1... | collective-permute-start | bytes 73736 | tf_op jit(solution)/shard_map/ppermute | solution.py:411
  16.7 19.2 %collective-permute-start.10 = (bf16[64,768]{1,0:T(8,128)(2,1)S(1)}, bf16[64,768]{1,0:T(8,128)(2,1)S(1)}, u32[]{:S(2)}, u32[]{:S(2)}) collective-permute-start(bf16[64,768]{1,0:T(8,128)(2,1)S(1)} %get-tuple-element.28.refs_0_), channel_id=1, source_target_pairs={{0,4},{4,0},{8,12},{12,8},{16,20},{20,16},{24,28},{28,24},{1,5},{5... | collective-permute-start | bytes 294920 | tf_op jit(solution)/shard_map/ppermute | solution.py:406
  28.5 6.2 %collective-permute-start.17 = (bf16[16,768]{1,0:T(8,128)(2,1)S(1)}, bf16[16,768]{1,0:T(8,128)(2,1)S(1)}, u32[]{:S(2)}, u32[]{:S(2)}) collective-permute-start(bf16[16,768]{1,0:T(8,128)(2,1)S(1)} %get-tuple-element.32), channel_id=1, source_target_pairs={{8,0},{12,4},{16,8},{20,12},{24,16},{28,20},{9,1},{13,5},{17,9},{2... | collective-permute-start | bytes 73736 | tf_op jit(solution)/shard_map/ppermute | solution.py:411
  34.7 5.5 %collective-permute-start.9 = (bf16[64,768]{1,0:T(8,128)(2,1)S(1)}, bf16[64,768]{1,0:T(8,128)(2,1)S(1)}, u32[]{:S(2)}, u32[]{:S(2)}) collective-permute-start(bf16[64,768]{1,0:T(8,128)(2,1)S(1)} %get-tuple-element.28.refs_0_), channel_id=1, source_target_pairs={{0,24},{4,28},{8,16},{12,20},{16,8},{20,12},{24,0},{28,4},{1,25},{... | collective-permute-start | bytes 294920 | tf_op jit(solution)/shard_map/ppermute | solution.py:406
  35.9 7.4 %collective-permute-start.8 = (bf16[64,768]{1,0:T(8,128)(2,1)S(1)}, bf16[64,768]{1,0:T(8,128)(2,1)S(1)}, u32[]{:S(2)}, u32[]{:S(2)}) collective-permute-start(bf16[64,768]{1,0:T(8,128)(2,1)S(1)} %get-tuple-element.28.refs_0_), channel_id=1, source_target_pairs={{0,16},{4,20},{8,24},{12,28},{16,0},{20,4},{24,8},{28,12},{1,17},{... | collective-permute-start | bytes 294920 | tf_op jit(solution)/shard_map/ppermute | solution.py:406
  40.2 5.6 %collective-permute-start.7 = (bf16[64,768]{1,0:T(8,128)(2,1)S(1)}, bf16[64,768]{1,0:T(8,128)(2,1)S(1)}, u32[]{:S(2)}, u32[]{:S(2)}) collective-permute-start(bf16[64,768]{1,0:T(8,128)(2,1)S(1)} %get-tuple-element.28.refs_0_), channel_id=1, source_target_pairs={{0,8},{4,12},{8,0},{12,4},{16,24},{20,28},{24,16},{28,20},{1,9},{5... | collective-permute-start | bytes 294920 | tf_op jit(solution)/shard_map/ppermute | solution.py:406
  43.3 3.9 %collective-permute-start.14 = (bf16[80,768]{1,0:T(8,128)(2,1)S(1)}, bf16[80,768]{1,0:T(8,128)(2,1)S(1)}, u32[]{:S(2)}, u32[]{:S(2)}) collective-permute-start(bf16[80,768]{1,0:T(8,128)(2,1)S(1)} %get-tuple-element.29), channel_id=1, source_target_pairs={{0,4},{4,8},{8,12},{12,16},{16,20},{20,24},{24,28},{1,5},{5,9},{9,... | collective-permute-start | bytes 368648 | tf_op jit(solution)/shard_map/ppermute | solution.py:411
  45.9 3.2 %collective-permute-start.16 = (bf16[80,768]{1,0:T(8,128)(2,1)S(1)}, bf16[80,768]{1,0:T(8,128)(2,1)S(1)}, u32[]{:S(2)}, u32[]{:S(2)}) collective-permute-start(bf16[80,768]{1,0:T(8,128)(2,1)S(1)} %get-tuple-element.31), channel_id=1, source_target_pairs={{4,0},{8,4},{12,8},{16,12},{20,16},{24,20},{28,24},{5,1},{9,5},{13... | collective-permute-start | bytes 368648 | tf_op jit(solution)/shard_map/ppermute | solution.py:411
  47.2 12.4 %collective-permute-start.3 = (bf16[240,768]{1,0:T(8,128)(2,1)S(1)}, bf16[240,768]{1,0:T(8,128)(2,1)S(1)}, u32[]{:S(2)}, u32[]{:S(2)}) collective-permute-start(bf16[240,768]{1,0:T(8,128)(2,1)S(1)} %get-tuple-element.27.refs_0_), channel_id=1, source_target_pairs={{0,4},{4,0},{8,12},{12,8},{16,20},{20,16},{24,28},{28,24},{1,5},{5... | collective-permute-start | bytes 1105928 | tf_op jit(solution)/shard_map/ppermute | solution.py:406
  48.4 11.3 %collective-permute-start.6 = (bf16[240,768]{1,0:T(8,128)(2,1)S(1)}, bf16[240,768]{1,0:T(8,128)(2,1)S(1)}, u32[]{:S(2)}, u32[]{:S(2)}) collective-permute-start(bf16[240,768]{1,0:T(8,128)(2,1)S(1)} %collective-permute-done.2.refs_3_), channel_id=1, source_target_pairs={{0,4},{4,0},{8,12},{12,8},{16,20},{20,16},{24,28},{28,24},{1,5},{5... | collective-permute-start | bytes 1105928 | tf_op jit(solution)/shard_map/ppermute | solution.py:406
  48.4 11.2 %collective-permute-start.5 = (bf16[240,768]{1,0:T(8,128)(2,1)S(1)}, bf16[240,768]{1,0:T(8,128)(2,1)S(1)}, u32[]{:S(2)}, u32[]{:S(2)}) collective-permute-start(bf16[240,768]{1,0:T(8,128)(2,1)S(1)} %collective-permute-done.1.refs_2_), channel_id=1, source_target_pairs={{0,4},{4,0},{8,12},{12,8},{16,20},{20,16},{24,28},{28,24},{1,5},{5... | collective-permute-start | bytes 1105928 | tf_op jit(solution)/shard_map/ppermute | solution.py:406
  48.9 10.8 %collective-permute-start.4 = (bf16[240,768]{1,0:T(8,128)(2,1)S(1)}, bf16[240,768]{1,0:T(8,128)(2,1)S(1)}, u32[]{:S(2)}, u32[]{:S(2)}) collective-permute-start(bf16[240,768]{1,0:T(8,128)(2,1)S(1)} %collective-permute-done.refs_1_), channel_id=1, source_target_pairs={{0,4},{4,0},{8,12},{12,8},{16,20},{20,16},{24,28},{28,24},{1,5},{5... | collective-permute-start | bytes 1105928 | tf_op jit(solution)/shard_map/ppermute | solution.py:406
  49.1 4.3 %collective-permute-start.13 = (bf16[64,768]{1,0:T(8,128)(2,1)S(1)}, bf16[64,768]{1,0:T(8,128)(2,1)S(1)}, u32[]{:S(2)}, u32[]{:S(2)}) collective-permute-start(bf16[64,768]{1,0:T(8,128)(2,1)S(1)} %collective-permute-done.9.refs_3_), channel_id=1, source_target_pairs={{0,4},{4,0},{8,12},{12,8},{16,20},{20,16},{24,28},{28,24},{1,5},{5... | collective-permute-start | bytes 294920 | tf_op jit(solution)/shard_map/ppermute | solution.py:406
  53.4 1.3 %collective-permute-start.12 = (bf16[64,768]{1,0:T(8,128)(2,1)S(1)}, bf16[64,768]{1,0:T(8,128)(2,1)S(1)}, u32[]{:S(2)}, u32[]{:S(2)}) collective-permute-start(bf16[64,768]{1,0:T(8,128)(2,1)S(1)} %collective-permute-done.8.refs_2_), channel_id=1, source_target_pairs={{0,4},{4,0},{8,12},{12,8},{16,20},{20,16},{24,28},{28,24},{1,5},{5... | collective-permute-start | bytes 294920 | tf_op jit(solution)/shard_map/ppermute | solution.py:406
  54.7 1.3 %collective-permute-start.11 = (bf16[64,768]{1,0:T(8,128)(2,1)S(1)}, bf16[64,768]{1,0:T(8,128)(2,1)S(1)}, u32[]{:S(2)}, u32[]{:S(2)}) collective-permute-start(bf16[64,768]{1,0:T(8,128)(2,1)S(1)} %collective-permute-done.7.refs_1_), channel_id=1, source_target_pairs={{0,4},{4,0},{8,12},{12,8},{16,20},{20,16},{24,28},{28,24},{1,5},{5... | collective-permute-start | bytes 294920 | tf_op jit(solution)/shard_map/ppermute | solution.py:406
  56.0 0.9 %copy-start.1 = (bf16[1,128,768]{2,1,0:T(8,128)(2,1)S(1)}, bf16[1,128,768]{2,1,0:T(8,128)(2,1)}, u32[]{:S(2)}) copy-start(bf16[1,128,768]{2,1,0:T(8,128)(2,1)} %param.10) | copy-start | bytes 589828
  56.9 0.7 copy-start.5
  66.1 2.0 %collective-permute-start.18 = (bf16[4,96,768]{2,1,0:T(8,128)(2,1)S(1)}, bf16[4,96,768]{2,1,0:T(8,128)(2,1)S(1)}, u32[]{:S(2)}, u32[]{:S(2)}) collective-permute-start(bf16[4,96,768]{2,1,0:T(8,128)(2,1)S(1)} %get-tuple-element.43), channel_id=1, source_target_pairs={{0,4},{4,0},{8,12},{12,8},{16,20},{20,16},{24,28},{28,24},{1,5},{5... | collective-permute-start | bytes 1769480 | tf_op jit(solution)/shard_map/ppermute | solution.py:406
  68.2 6.7 %collective-permute-start.19 = (bf16[96,768]{1,0:T(8,128)(2,1)S(1)}, bf16[96,768]{1,0:T(8,128)(2,1)S(1)}, u32[]{:S(2)}, u32[]{:S(2)}) collective-permute-start(bf16[96,768]{1,0:T(8,128)(2,1)S(1)} %get-tuple-element.45), channel_id=1, source_target_pairs={{0,8},{4,12},{8,0},{12,4},{16,24},{20,28},{24,16},{28,20},{1,9},{5... | collective-permute-start | bytes 442376 | tf_op jit(solution)/shard_map/ppermute | solution.py:406
  70.2 9.0 %collective-permute-start.20 = (bf16[96,768]{1,0:T(8,128)(2,1)S(1)}, bf16[96,768]{1,0:T(8,128)(2,1)S(1)}, u32[]{:S(2)}, u32[]{:S(2)}) collective-permute-start(bf16[96,768]{1,0:T(8,128)(2,1)S(1)} %get-tuple-element.46), channel_id=1, source_target_pairs={{0,16},{4,20},{8,24},{12,28},{16,0},{20,4},{24,8},{28,12},{1,17},{... | collective-permute-start | bytes 442376 | tf_op jit(solution)/shard_map/ppermute | solution.py:406
  70.2 9.0 %collective-permute-start.21 = (bf16[96,768]{1,0:T(8,128)(2,1)S(1)}, bf16[96,768]{1,0:T(8,128)(2,1)S(1)}, u32[]{:S(2)}, u32[]{:S(2)}) collective-permute-start(bf16[96,768]{1,0:T(8,128)(2,1)S(1)} %get-tuple-element.47), channel_id=1, source_target_pairs={{0,24},{4,28},{8,16},{12,20},{16,8},{20,12},{24,0},{28,4},{1,25},{... | collective-permute-start | bytes 442376 | tf_op jit(solution)/shard_map/ppermute | solution.py:406
  79.8 4.5 %collective-permute-start.22 = (bf16[48,384]{1,0:T(8,128)(2,1)S(1)}, bf16[48,384]{1,0:T(8,128)(2,1)S(1)}, u32[]{:S(2)}, u32[]{:S(2)}) collective-permute-start(bf16[48,384]{1,0:T(8,128)(2,1)S(1)} %get-tuple-element.49), channel_id=1, source_target_pairs={{0,1},{1,0},{2,3},{3,2},{4,5},{5,4},{6,7},{7,6},{8,9},{9,8},{10,11... | collective-permute-start | bytes 110600 | tf_op jit(solution)/shard_map/ppermute | solution.py:406
  81.4 5.2 %collective-permute-start.23 = (bf16[48,384]{1,0:T(8,128)(2,1)S(1)}, bf16[48,384]{1,0:T(8,128)(2,1)S(1)}, u32[]{:S(2)}, u32[]{:S(2)}) collective-permute-start(bf16[48,384]{1,0:T(8,128)(2,1)S(1)} %get-tuple-element.50), channel_id=1, source_target_pairs={{0,2},{1,3},{2,0},{3,1},{4,6},{5,7},{6,4},{7,5},{8,10},{9,11},{10,... | collective-permute-start | bytes 110600 | tf_op jit(solution)/shard_map/ppermute | solution.py:406
  84.0 5.8 %collective-permute-start.24 = (bf16[48,384]{1,0:T(8,128)(2,1)S(1)}, bf16[48,384]{1,0:T(8,128)(2,1)S(1)}, u32[]{:S(2)}, u32[]{:S(2)}) collective-permute-start(bf16[48,384]{1,0:T(8,128)(2,1)S(1)} %get-tuple-element.51), channel_id=1, source_target_pairs={{0,3},{1,2},{2,1},{3,0},{4,7},{5,6},{6,5},{7,4},{8,11},{9,10},{10,... | collective-permute-start | bytes 110600 | tf_op jit(solution)/shard_map/ppermute | solution.py:406

commit v2 on v1

--- a/solution.py
+++ b/solution.py
@@ -54,9 +54,9 @@
     return out
 
 
-def call(body, out_shapes, args, scratch=(), limit=24, cost=None):
+def call(body, out_shapes, args, scratch=(), limit=24, cost=None, space=pltpu.VMEM):
     in_specs = [
-        pl.BlockSpec(memory_space=pltpu.SMEM if a.dtype == jnp.int32 and a.ndim == 1 else pltpu.VMEM)
+        pl.BlockSpec(memory_space=pltpu.SMEM if a.dtype == jnp.int32 and a.ndim == 1 else space)
         for a in args
     ]
     return pl.pallas_call(
@@ -88,20 +88,29 @@
     return first, jnp.concatenate(second, axis=0)
 
 
-def prep_kernel(
-    where_ref, bases_ref, cot_ref, c1_ref, p1_ref, c2_ref, p2_ref, embed_ref,
-    m1_ref, m2_ref, r1_ref, r2_ref, l1_ref, l2_ref,
-):
+def prep_kernel(where_ref, *refs):
+    sources = refs[:7]
+    own_ref, x_ref, y_ref, d_ref, cot_out, embed_out, bases_out = refs[7:14]
+    held = refs[14:21]
+    sems = refs[21]
+    moves = [
+        pltpu.make_async_copy(src, dst, sems.at[n])
+        for n, (src, dst) in enumerate(zip(sources, held))
+    ]
+    for move in moves:
+        move.start()
+    for move in moves:
+        move.wait()
+    embed_ref, c1_ref, cot_ref, bases_ref, c2_ref, p2_ref, p1_ref = held
     me, count = where_ref[0], where_ref[2]
     shard = c1_ref.shape[1]
     chans = embed_ref.shape[1]
     width = c1_ref.shape[2]
+    cap = bases_ref.shape[1]
+    prows = p1_ref.shape[0]
     pick = (iota((chans, shard), 0) == iota((chans, shard), 1) + me * shard).astype(BF16)
     first, second = base_tables(embed_ref, pick, c1_ref, shard)
-    prows = p1_ref.shape[0]
-    m1_ref[0:prows] = p1_ref[...]
     f_high, f_low = split(first)
-    cap = bases_ref.shape[1]
     info = jnp.concatenate(
         [
             bases_ref[...].astype(F32),
@@ -112,26 +121,29 @@
     )
     tail = jnp.concatenate([f_high.astype(F32), f_low.astype(F32)], axis=1)
     tail = jnp.where(iota((16, 1), 0) == 12, info, tail)
-    m1_ref[prows : prows + 16] = tail.astype(BF16)
+    wide = jnp.concatenate([second[0:24], second[24:48]], axis=1)
+    tail = jnp.concatenate([wide, tail, jnp.zeros((8, chans), F32)], axis=0).astype(BF16)
     half = 3 * shard // 2
     flat = c2_ref[...].reshape(3 * shard, width)
-    m2_ref[0:half, 0:width] = flat[0:half]
-    m2_ref[0:half, width : 2 * width] = flat[half : 2 * half]
-    m2_ref[half : half + prows] = p2_ref[...]
-    s_high, s_low = split(second)
-    m2_ref[half + prows : half + prows + 48, 0:width] = s_high
-    m2_ref[half + prows : half + prows + 48, width : 2 * width] = s_low
     cot = cot_ref[...]
     take = (iota((HALO, cap), 1) == iota((HALO, cap), 0) + (count - HALO)).astype(BF16)
     last = mm(take, cot).astype(BF16)
-    r1_ref[...] = last
-    r2_ref[...] = last[HALO - SPILL :]
-    l1_ref[...] = cot[0:HALO]
-    l2_ref[...] = cot[0:SPILL]
+    chip = me >> 1
+    for rel, out in enumerate((own_ref, x_ref, y_ref, d_ref)):
+        out[0:half, 0:width] = flat[0:half]
+        out[0:half, width : 2 * width] = flat[half : 2 * half]
+        out[half : half + prows] = p2_ref[...]
+        out[half + prows : half + 2 * prows] = p1_ref[...]
+        out[half + 2 * prows : half + 2 * prows + 48] = tail
+        upward = (me & 1) == 0 if rel == 0 else (chip ^ rel) > chip
+        out[half + 2 * prows + 48 :] = jnp.where(upward, last, cot[0:HALO])
+    cot_out[...] = cot
+    embed_out[...] = embed_ref[...]
+    bases_out[...] = bases_ref[...]
 
 
 def table_body(
-    first, project, info_at, cot_ref, r1_ref, r2_ref, l1_ref, l2_ref, embed_ref,
+    first, project, info_at, cot_ref, r1, r2, l1, l2, embed_ref,
     b1_ref, s1_ref, a2_ref, s2_ref, hot_f_ref, hot_r_ref, cx_ref,
 ):
     cap = cot_ref.shape[0]
@@ -197,46 +209,29 @@
     own_pos = jnp.where(lane < own_n, lane, FAR)
     acc = mm((row_o == own_pos).astype(BF16), cot_ref[...])
     pos = jnp.where(lane_h >= HALO - before_n[:, 0:HALO], lane_h - HALO, FAR)
-    acc = acc + mm((row_h == pos).astype(BF16), r1_ref[...])
+    acc = acc + mm((row_h == pos).astype(BF16), r1)
     pos = jnp.where(
         counts[REACH - 2][:, 0:SPILL] > 0.0, lane_s - SPILL - before_n[:, 0:SPILL], FAR
     )
-    acc = acc + mm((row_s == pos).astype(BF16), r2_ref[...])
+    acc = acc + mm((row_s == pos).astype(BF16), r2)
     pos = jnp.where(lane_h < after_n[:, 0:HALO], lane_h + own_n[:, 0:HALO], FAR)
-    acc = acc + mm((row_h == pos).astype(BF16), l1_ref[...])
+    acc = acc + mm((row_h == pos).astype(BF16), l1)
     pos = jnp.where(
         (counts[REACH + 2][:, 0:SPILL] > 0.0) & (after_n[:, 0:SPILL] < HALO),
         lane_s + own_n[:, 0:SPILL] + after_n[:, 0:SPILL],
         FAR,
     )
-    acc = acc + mm((row_s == pos).astype(BF16), l2_ref[...])
+    acc = acc + mm((row_s == pos).astype(BF16), l2)
     cx_ref[...] = (0.5 * acc).astype(BF16)
 
 
-def table_kernel_packed(rels, where_ref, *refs):
-    parts = refs[: len(rels)]
-    rest = refs[len(rels) : len(rels) + 6]
-    outs = refs[len(rels) + 6 :]
-    p1_ref = outs[7]
-    info_ref = outs[8]
-    me = where_ref[0]
-    shard = parts[0].shape[0] - 16
-    width = parts[0].shape[1] // 2
-    info_ref[...] = jnp.zeros(info_ref.shape, F32)
-    first = jnp.zeros((16, width), F32)
-    for rel, part in zip(rels, parts):
-        peer = me ^ rel
-        p1_ref[pl.ds(pl.multiple_of(peer * shard, 16), shard), :] = part[0:shard]
-        tail = part[shard : shard + 16].astype(F32)
-        first = first + tail[:, 0:width] + tail[:, width : 2 * width]
-        info_ref[REACH + peer] = jnp.broadcast_to(tail[12:13, 0:256], (8, 256))
+def table_kernel_plain(
+    first_ref, project_ref, info_ref, cot_ref, r1_ref, r2_ref, l1_ref, l2_ref, embed_ref, *outs
+):
     table_body(
-        first, p1_ref[...], lambda o: info_ref[me + (REACH + o)], *rest, *outs[:7]
-    )
-
-
-def table_kernel_plain(first_ref, project_ref, info_ref, *refs):
-    table_body(first_ref[...], project_ref[...], lambda o: info_ref[REACH + o], *refs)
+        first_ref[...], project_ref[...], lambda o: info_ref[REACH + o], cot_ref, r1_ref[...],
+        r2_ref[...], l1_ref[...], l2_ref[...], embed_ref, *outs
+    )
 
 
 def tower_body(
@@ -317,18 +312,24 @@
     sal_ref[...] = jnp.where(live, sal[0:4] * (1.0 / math.sqrt(cx.shape[1])), 0.0)
 
 
-def tower_kernel_packed(rels, where_ref, *refs):
-    parts = refs[: len(rels)]
-    bases_ref, cx_ref, b1_ref, s1_ref, a2_ref, s2_ref, hf, hr, p1_ref, emb = refs[len(rels) : len(rels) + 10]
-    sal_ref, keep_ref, send_ref, conv_ref, p2_ref, all_ref = refs[len(rels) + 10 :]
+def tower_kernel_packed(where_ref, *refs):
+    parts = refs[:8]
+    cot_ref, embed_ref, bases_ref, sal_ref, keep_ref, send_ref = refs[8:14]
+    tables = refs[14:21]
+    conv_ref, p1_ref, p2_ref, info_ref, halo_ref, all_ref = refs[21:]
     me, count = where_ref[0], where_ref[2]
-    chans = cx_ref.shape[1]
+    chip, core = me >> 1, me & 1
+    chans = cot_ref.shape[1]
     width = chans // 2
     shard = chans // 8
     prow = width // 8
     half = 3 * shard // 2
-    second = jnp.zeros((48, width), F32)
-    for rel, part in zip(rels, parts):
+    info_ref[0:REACH] = jnp.zeros((REACH, 8, 256), F32)
+    info_ref[REACH + 8 :] = jnp.zeros((REACH, 8, 256), F32)
+    first = jnp.zeros((16, width), F32)
+    wide = jnp.zeros((24, chans), F32)
+    for n, part in enumerate(parts):
+        rel = 2 * (n & 3) + (n >> 2)
         peer = me ^ rel
         at = pl.multiple_of(peer * shard, 16)
         conv_ref[0, pl.ds(at, shard), :] = part[0:shard, 0:width]
@@ -336,22 +337,37 @@
         at_half = pl.multiple_of(peer * shard + (half - shard), 16)
         conv_ref[1, pl.ds(at_half, half - shard), :] = part[0 : half - shard, width : 2 * width]
         conv_ref[2, pl.ds(at, shard), :] = part[half - shard : half, width : 2 * width]
-        p2_ref[pl.ds(pl.multiple_of(peer * prow, 16), prow), :] = part[half : half + prow]
-        tail = part[half + prow : half + prow + 48].astype(F32)
-        second = second + tail[:, 0:width] + tail[:, width : 2 * width]
+        at = pl.multiple_of(peer * prow, 16)
+        p2_ref[pl.ds(at, prow), :] = part[half : half + prow]
+        p1_ref[pl.ds(at, prow), :] = part[half + prow : half + 2 * prow]
+        tail = part[half + 2 * prow : half + 2 * prow + 48].astype(F32)
+        wide = wide + tail[0:24]
+        first = first + tail[24:40, 0:width] + tail[24:40, width : 2 * width]
+        info_ref[REACH + peer] = jnp.broadcast_to(tail[36:37, 0:256], (8, 256))
+        halo_ref[(n >> 2) * 4 + (peer >> 1)] = part[half + 2 * prow + 48 :]
+    r1 = halo_ref[4 + jnp.maximum(chip + core - 1, 0)]
+    l1 = halo_ref[4 + jnp.minimum(chip + core, 3)]
+    r2 = halo_ref[jnp.maximum(chip - 1, 0)]
+    l2 = halo_ref[jnp.minimum(chip + 1, 3)]
+    table_body(
+        first, p1_ref[...], lambda o: info_ref[me + (REACH + o)], cot_ref, r1,
+        r2[HALO - SPILL :], l1, l2[0:SPILL], embed_ref, *tables,
+    )
+    second = jnp.concatenate([wide[:, 0:width], wide[:, width : 2 * width]], axis=0)
 
     def put(block, value):
         rows = value.shape[0] // 4
         for c in range(4):
-            all_ref[(4 * block + c) ^ me] = value[c * rows : (c + 1) * rows]
-
+            peer = 4 * block + c
+            all_ref[((core ^ (peer & 1)) << 2) + (peer >> 1)] = value[c * rows : (c + 1) * rows]
+
+    b1, s1, a2, s2, hf, hr, cx = tables
     tower_body(
-        lambda k: conv_ref[k], p2_ref[...], second, p1_ref[...], count, bases_ref, cx_ref,
-        b1_ref, s1_ref, a2_ref, s2_ref, hf, hr, emb, sal_ref, put,
-    )
-    for rel in range(4):
-        keep_ref[rel] = all_ref[2 * rel]
-        send_ref[rel] = all_ref[2 * rel + 1].astype(BF16)
+        lambda k: conv_ref[k], p2_ref[...], second, p1_ref[...], count, bases_ref, cx,
+        b1, s1, a2, s2, hf, hr, embed_ref, sal_ref, put,
+    )
+    keep_ref[...] = all_ref[0:4]
+    send_ref[...] = all_ref[4:8].astype(BF16)
 
 
 def tower_kernel_plain(
@@ -368,42 +384,43 @@
     )
 
 
-def core_sum_kernel(keep_ref, recv_ref, own_ref, x_ref, y_ref, d_ref):
-    own_ref[...] = keep_ref[0] + recv_ref[0].astype(F32)
-    for rel, out in ((1, x_ref), (2, y_ref), (3, d_ref)):
-        out[...] = (keep_ref[rel] + recv_ref[rel].astype(F32)).astype(BF16)
-
-
-def plane_sum_kernel(where_ref, own_ref, x_ref, y_ref, d_ref, *refs):
-    outs, sum_ref = refs[:-1], refs[-1]
-    sum_ref[...] = (
-        own_ref[...] + x_ref[...].astype(F32) + y_ref[...].astype(F32) + d_ref[...].astype(F32)
-    )
-    z = where_ref[1]
-    rows = own_ref.shape[0] // len(outs)
+def core_sum_kernel(where_ref, keep_ref, recv_ref, own_ref, out_ref):
+    out_ref[...] = (keep_ref[...] + recv_ref[...].astype(F32)).astype(BF16)
+    chip = where_ref[0] >> 1
+    own_ref[...] = keep_ref[chip] + recv_ref[chip].astype(F32)
+
+
+def plane_sum_kernel(where_ref, own_ref, got_ref, mine_ref, out_ref, sum_ref):
+    chip, z = where_ref[0] >> 1, where_ref[1]
+    total = own_ref[...]
+    for c in range(got_ref.shape[0]):
+        total = total + jnp.where(chip == c, 0.0, got_ref[c].astype(F32))
+    sum_ref[...] = total
+    count, rows = out_ref.shape[0], mine_ref.shape[0]
     width = own_ref.shape[1] // 2
-    for rel, out in enumerate(outs):
-        value = sum_ref[pl.ds(pl.multiple_of((z ^ rel) * rows, 8), rows), :]
-        if rel == 0:
-            out[...] = value
-        else:
-            out[...] = jnp.concatenate(
-                [value[:, 0:width], value[:, width : 2 * width]], axis=0
-            ).astype(BF16)
-
-
-def last_sum_kernel(scale, own_ref, *refs):
-    out_ref = refs[-1]
-    total = own_ref[...]
-    rows = total.shape[0]
-    for ref in refs[:-1]:
-        value = ref[...].astype(F32)
-        total = total + jnp.concatenate([value[0:rows], value[rows : 2 * rows]], axis=1)
-    out_ref[...] = total * scale
-
-
-def xor_move(array, axis, bits):
-    return lax.ppermute(array, axis, [(i, i ^ bits) for i in range(lax.axis_size(axis))])
+    for c in range(count):
+        value = total[c * rows : (c + 1) * rows]
+        out_ref[c] = jnp.concatenate([value[:, 0:width], value[:, width:]], axis=0).astype(BF16)
+    mine_ref[...] = sum_ref[pl.ds(pl.multiple_of(z * rows, 8), rows), :]
+
+
+def last_sum_kernel(scale, where_ref, mine_ref, got_ref, out_ref):
+    total = mine_ref[...]
+    rows, chans = total.shape
+    for c in range(got_ref.shape[0]):
+        value = got_ref[c].astype(F32)
+        value = jnp.concatenate([value[0:rows], value[rows : 2 * rows]], axis=1)
+        total = total + jnp.where(where_ref[1] == c, 0.0, value)
+    total = total * scale
+    parts = chans // 128
+    for n in range(parts):
+        out_ref[pl.ds(n, rows, stride=parts), :] = total[:, 128 * n : 128 * n + 128]
+
+
+def flip_move(array, *axes):
+    sizes = [lax.axis_size(a) for a in axes]
+    size = math.prod(sizes)
+    return lax.ppermute(array, axes, [(i, size - 1 - i) for i in range(size)])
 
 
 def shift_move(array, axis, by):
@@ -424,79 +441,79 @@
     ]
 
 
-def fast_shards(bases, where, cot, c1, p1, c2, p2, embed):
+def fast_shards(
+    bases, lengths, cotangent, c1, p1, c2, p2, embed
+):
+    cot = cotangent[0]
+    me = (lax.axis_index("y") * 2 + lax.axis_index("x")) * 2 + lax.axis_index("core")
+    where = jnp.stack([me.astype(jnp.int32), lax.axis_index("dp").astype(jnp.int32), lengths[0, 0]])
     cap, chans = cot.shape
     width = c1.shape[2]
     n_dp = lax.axis_size("dp")
-    m1, m2, r1, r2, l1, l2 = call(
+    height = 3 * c2.shape[1] // 2 + 2 * p1.shape[0] + 48 + HALO
+    sources = [embed, c1, cot, bases, c2, p2, p1]
+    outs = call(
         prep_kernel,
-        [
-            ((p1.shape[0] + 16, chans), BF16),
-            ((3 * c2.shape[1] // 2 + p2.shape[0] + 48, chans), BF16),
-            ((HALO, chans), BF16),
-            ((SPILL, chans), BF16),
-            ((HALO, chans), BF16),
-            ((SPILL, chans), BF16),
-        ],
-        [where, bases, cot, c1, p1, c2, p2, embed],
-    )
-
-    def gather(m):
-        near = [m] + [xor_move(m, "seq", bits) for bits in (2, 4, 6)]
-        return near + [xor_move(a, "seq", 1) for a in near]
-
-    rels = (0, 2, 4, 6, 1, 3, 5, 7)
-    g1 = gather(m1)
-    halos = [
-        shift_move(r1, "seq", 1),
-        shift_move(r2, "seq", 2),
-        shift_move(l1, "seq", -1),
-        shift_move(l2, "seq", -2),
-    ]
-    g2 = gather(m2)
-    tables = call(
-        functools.partial(table_kernel_packed, rels),
-        table_shapes(cap, chans, width) + [((width, chans), BF16)],
-        [where, *g1, cot, *halos, embed],
-        scratch=[pltpu.VMEM((8 + 2 * REACH, 8, 256), F32)],
-        cost=pl.CostEstimate(flops=3 * 10**8, bytes_accessed=4 * 10**6, transcendentals=0),
-    )
-    b1, s1, a2, s2, hf, hr, cx, p1_full = tables
+        [((height, chans), BF16)] * 4
+        + [(cot.shape, BF16), (embed.shape, F32), (bases.shape, jnp.int32)],
+        [where, *sources],
+        scratch=[pltpu.VMEM(a.shape, a.dtype) for a in sources]
+        + [pltpu.SemaphoreType.DMA((len(sources),))],
+        space=pl.ANY,
+    )
+    near = list(outs[:4])
+    for n, axes in ((1, ("x",)), (2, ("y",)), (3, ("y", "x"))):
+        near[n] = flip_move(near[n], *axes)
+    across = [flip_move(a, "core") for a in near]
     rows = chans // 8
     sal, keep, send = call(
-        functools.partial(tower_kernel_packed, rels),
+        tower_kernel_packed,
         [((4, cap), F32), ((4, rows, chans), F32), ((4, rows, chans), BF16)],
-        [where, *g2, bases, cx, b1, s1, a2, s2, hf, hr, p1_full, embed],
-        scratch=[
+        [where, outs[0], *near[1:], *across, *outs[4:]],
+        scratch=[pltpu.VMEM(s, d) for s, d in table_shapes(cap, chans, width)]
+        + [
             pltpu.VMEM((3, chans, width), BF16),
             pltpu.VMEM((width, chans), BF16),
+            pltpu.VMEM((width, chans), BF16),
+            pltpu.VMEM((8 + 2 * REACH, 8, 256), F32),
+            pltpu.VMEM((8, HALO, chans), BF16),
             pltpu.VMEM((8, rows, chans), F32),
         ],
         limit=40,
     )
-    recv = xor_move(send, "seq", 1)
-    own, sx, sy, sd = call(
+    recv = flip_move(send, "core")
+    own, out = call(
         core_sum_kernel,
-        [((rows, chans), F32)] + [((rows, chans), BF16)] * 3,
-        [keep, recv],
-    )
-    got = [xor_move(a, "seq", bits) for a, bits in ((sx, 2), (sy, 4), (sd, 6))]
+        [((rows, chans), F32), ((4, rows, chans), BF16)],
+        [where, keep, recv],
+    )
+    got = lax.all_to_all(out, ("y", "x"), 0, 0)
     part = rows // n_dp
-    outs = call(
+    mine, out = call(
         plane_sum_kernel,
-        [((part, chans), F32)] + [((2 * part, width), BF16)] * (n_dp - 1),
-        [where, own, *got],
+        [((part, chans), F32), ((n_dp, 2 * part, width), BF16)],
+        [where, own, got],
         scratch=[pltpu.VMEM((rows, chans), F32)],
     )
-    far = [xor_move(a, "dp", rel + 1) for rel, a in enumerate(outs[1:])]
+    got = lax.all_to_all(out, "dp", 0, 0)
     scale = 1.0 / math.sqrt(8 * n_dp * cap)
     (grad,) = call(
-        functools.partial(last_sum_kernel, scale), [((part, chans), F32)], [outs[0], *far]
+        functools.partial(last_sum_kernel, scale),
+        [((part * chans // 128, 128), F32)],
+        [where, mine, got],
     )
     return sal[None], grad.reshape(-1)
 
 
-def plain_shards(bases, where, cot, c1, p1, c2, p2, embed):
+def plain_shards(bases, lengths, cotangent, c1, p1, c2, p2, embed):
+    cot = cotangent[0]
+    where = jnp.stack(
+        [
+            lax.axis_index("seq").astype(jnp.int32),
+            lax.axis_index("dp").astype(jnp.int32),
+            lengths[0, 0],
+        ]
+    )
     cap, chans = cot.shape
     width = c1.shape[2]
     me, count = where[0], where[2]
@@ -546,40 +563,22 @@
     return sal[None], grad
 
 
-def shards(
-    bases,
-    lengths,
-    cotangent,
-    first_conv_taps,
-    first_projection,
-    second_conv_taps,
-    second_projection,
-    embed,
-):
-    where = jnp.stack(
-        [
-            lax.axis_index("seq").astype(jnp.int32),
-            lax.axis_index("dp").astype(jnp.int32),
-            lengths[0, 0],
-        ]
-    )
-    run = fast_shards if lax.axis_size("seq") == 8 and lax.axis_size("dp") == 4 else plain_shards
-    return run(
-        bases, where, cotangent[0], first_conv_taps, first_projection, second_conv_taps,
-        second_projection, embed,
-    )
-
-
 def solution(mesh):
+    run, seq = plain_shards, "seq"
+    if mesh.shape["seq"] == 8:
+        run, seq = fast_shards, ("y", "x", "core")
+        count = mesh.shape["dp"]
+        mesh = jax.sharding.Mesh(mesh.devices.reshape(2, 2, 2, count), (*seq, "dp"))
+    every = seq if isinstance(seq, tuple) else (seq,)
     in_specs = (
-        P("dp", "seq"),
-        P("dp", "seq"),
-        P("dp", "seq", None),
-        P(None, "seq", None),
-        P("seq", None),
-        P(None, "seq", None),
-        P("seq", None),
+        P("dp", seq),
+        P("dp", seq),
+        P("dp", seq, None),
+        P(None, seq, None),
+        P(seq, None),
+        P(None, seq, None),
+        P(seq, None),
         P(),
     )
-    out_specs = (P("dp", None, "seq"), P(("seq", "dp")))
-    return jax.shard_map(shards, mesh=mesh, in_specs=in_specs, out_specs=out_specs, check_vma=False)
+    out_specs = (P("dp", None, seq), P((*every, "dp")))
+    return jax.shard_map(run, mesh=mesh, in_specs=in_specs, out_specs=out_specs, check_vma=False)

time: 91 us -> 77.7 us (0.85)
  starting transfers between devices: 34 us -> 5.2 us
  blocking collectives: 0 us -> 23.7 us
  waiting for transfers between devices: 36.6 us -> 29 us
  local copies, waits for them, and re-layouts: 8.21 us -> 5.93 us
  Pallas kernels: 10.1 us -> 12.1 us
    ppermute x25 -> x8, starting transfers between devices: 34 us -> 5.2 us  [flip_move(): return lax.ppermute(array, axes, [(i, size - 1 - i) for i in range(size)])]
    all_to_all x0 -> x2, blocking collectives: none -> 23.7 us  [the longest x1 12.4 us: fast_shards(): got = lax.all_to_all(out, ('y', 'x'), 0, 0)]
    ppermute x25 -> x8, waiting for transfers between devices: 36.6 us -> 29 us  [flip_move(): return lax.ppermute(array, axes, [(i, size - 1 - i) for i in range(size)])]
    pallas_call x6 -> x5, Pallas kernels: 10.1 us -> 12.1 us  [call(): pl.pallas_call(body, out_shape=[jax.ShapeDtypeStruct(s, d) for s, d in ou...]
    unnamed x22 -> x14, local copies, waits for them, and re-layouts: 7.57 us -> 5.93 us
  transfers between devices with their start and end apart: 25 -> 8, of which waited for: 13 -> 5; matrix products, arithmetic and copies ran while one was open for 0% -> 0% of each run, Pallas kernels for 2% -> 0%
where the time goes in v2:
time: 77.7 us; the launch traced here: 77.3 us
  waiting for transfers between devices  29 us (37%)
  blocking collectives  23.7 us (31%)
  Pallas kernels  12.1 us (16%)
  local copies, waits for them, and re-layouts  5.93 us (8%)
  starting transfers between devices  5.2 us (7%)
  between operations  1.32 us (2%)
    ppermute x8, waiting for transfers between devices, flip_move(): return lax.ppermute(array, axes, [(i, size - 1 - i) for i in range(size)])  29 us
    all_to_all x1, blocking collectives, fast_shards(): got = lax.all_to_all(out, ('y', 'x'), 0, 0)  12.4 us
    pallas_call x5, Pallas kernels, call(): pl.pallas_call(body, out_shape=[jax.ShapeDtypeStruct(s, d) for s, d in ou...  12.1 us
    all_to_all x1, blocking collectives, fast_shards(): got = lax.all_to_all(out, 'dp', 0, 0)  11.4 us
    unnamed x14, local copies, waits for them, and re-layouts  5.93 us
    ppermute x8, starting transfers between devices, flip_move(): return lax.ppermute(array, axes, [(i, size - 1 - i) for i in range(size)])  5.2 us
  transfers between devices with their start and end apart: 8, of which 5 were waited for; matrix products, arithmetic and copies ran while one was open for 0% of the time, Pallas kernels for 0%

profile of v2, /device:TPU:0, one launch (start us, length us, event | category | flops | bytes accessed | tf_op | source)
XLA Modules:
  0.0 77.3 jit_solution(8008511341000847065)
XLA Ops:
  1.3 0.1 pad_add_fusion.where_ref
  1.4 0.0 copy-start
  1.4 0.9 %copy-done = bf16[3,96,384]{2,1,0:T(8,128)(2,1)S(1)} copy-done((bf16[3,96,384]{2,1,0:T(8,128)(2,1)S(1)}, bf16[3,96,384]{2,1,0:T(8,128)(2,1)}, u32[]{:S(2)}) %copy-start) | copy-done | bytes 221208
  2.3 0.0 copy-start.1
  2.3 0.9 %copy-done.1 = bf16[3,96,384]{2,1,0:T(8,128)(2,1)S(1)} copy-done((bf16[3,96,384]{2,1,0:T(8,128)(2,1)S(1)}, bf16[3,96,384]{2,1,0:T(8,128)(2,1)}, u32[]{:S(2)}) %copy-start.1) | copy-done | bytes 221208
  3.2 0.0 copy-start.2
  3.2 0.9 %copy-done.2 = bf16[1,128,768]{2,1,0:T(8,128)(2,1)S(1)} copy-done((bf16[1,128,768]{2,1,0:T(8,128)(2,1)S(1)}, bf16[1,128,768]{2,1,0:T(8,128)(2,1)}, u32[]{:S(2)}) %copy-start.2) | copy-done | bytes 196632
  4.2 0.0 copy-start.3
  4.2 0.9 %copy-done.3 = bf16[48,768]{1,0:T(8,128)(2,1)S(1)} copy-done((bf16[48,768]{1,0:T(8,128)(2,1)S(1)}, bf16[48,768]{1,0:T(8,128)(2,1)}, u32[]{:S(2)}) %copy-start.3) | copy-done | bytes 73752
  5.0 0.0 copy-start.4
  5.0 0.9 %copy-done.4 = bf16[48,768]{1,0:T(8,128)(2,1)S(1)} copy-done((bf16[48,768]{1,0:T(8,128)(2,1)S(1)}, bf16[48,768]{1,0:T(8,128)(2,1)}, u32[]{:S(2)}) %copy-start.4) | copy-done | bytes 73752
  5.9 0.0 copy-start.5
  5.9 0.7 copy-done.5
  6.6 0.0 copy-start.6
  6.6 0.7 copy-done.6
  7.3 2.2 %shard_map.95 = (bf16[368,768]{1,0:T(8,128)(2,1)S(1)}, bf16[368,768]{1,0:T(8,128)(2,1)S(1)}, bf16[368,768]{1,0:T(8,128)(2,1)S(1)}, bf16[368,768]{1,0:T(8,128)(2,...) custom-call(s32[3]{0:T(128)S(1)} %pad_add_fusion.where_ref, ...), custom_call_target="tpu_custom_call" | custom-call | tf_op jit(solution)/shard_map/pallas_call | solution.py:62
  9.5 3.0 %collective-permute-start = (bf16[368,768]{1,0:T(8,128)(2,1)S(1)}, bf16[368,768]{1,0:T(8,128)(2,1)S(1)}, u32[]{:S(2)}, u32[]{:S(2)}) collective-permute-start(bf16[368,768]{1,0:T(8,128)(2,1)S(1)} %get-tuple-element.17), channel_id=1, source_target_pairs={{0,8},{8,0},{1,9},{9,1},{2,10},{10,2},{3,11},{11,3},{4,12},{12,4},... | collective-permute-start | bytes 1695752 | tf_op jit(solution)/shard_map/ppermute | solution.py:423
  12.5 1.5 %collective-permute-start.1 = (bf16[368,768]{1,0:T(8,128)(2,1)S(1)}, bf16[368,768]{1,0:T(8,128)(2,1)S(1)}, u32[]{:S(2)}, u32[]{:S(2)}) collective-permute-start(bf16[368,768]{1,0:T(8,128)(2,1)S(1)} %get-tuple-element.18), channel_id=1, source_target_pairs={{0,16},{16,0},{1,17},{17,1},{2,18},{18,2},{3,19},{19,3},{4,20},{20... | collective-permute-start | bytes 1695752 | tf_op jit(solution)/shard_map/ppermute | solution.py:423
  14.0 0.0 collective-permute-start.2
  14.0 0.0 collective-permute-start.3
  14.0 12.1 %collective-permute-done.refs_1_ = bf16[368,768]{1,0:T(8,128)(2,1)S(1)} collective-permute-done((bf16[368,768]{1,0:T(8,128)(2,1)S(1)}, bf16[368,768]{1,0:T(8,128)(2,1)S(1)}, u32[]{:S(2)}, u32[]{:S(2)}) %collective-permute-start) | collective-permute-done | bytes 565280 | tf_op jit(solution)/shard_map/ppermute | solution.py:423
  26.1 0.0 collective-permute-start.4
  26.1 12.7 %collective-permute-done.1.refs_2_ = bf16[368,768]{1,0:T(8,128)(2,1)S(1)} collective-permute-done((bf16[368,768]{1,0:T(8,128)(2,1)S(1)}, bf16[368,768]{1,0:T(8,128)(2,1)S(1)}, u32[]{:S(2)}, u32[]{:S(2)}) %collective-permute-start.1) | collective-permute-done | bytes 565280 | tf_op jit(solution)/shard_map/ppermute | solution.py:423
  38.8 0.0 collective-permute-start.5
  38.8 0.0 collective-permute-done.2.refs_3_
  38.9 0.5 collective-permute-start.6
  39.4 0.0 collective-permute-done.3.refs_4_
  39.4 0.0 collective-permute-done.4.refs_5_
  39.4 1.4 %collective-permute-done.5.refs_6_ = bf16[368,768]{1,0:T(8,128)(2,1)S(1)} collective-permute-done((bf16[368,768]{1,0:T(8,128)(2,1)S(1)}, bf16[368,768]{1,0:T(8,128)(2,1)S(1)}, u32[]{:S(2)}, u32[]{:S(2)}) %collective-permute-start.5) | collective-permute-done | bytes 565280 | tf_op jit(solution)/shard_map/ppermute | solution.py:423
  40.8 0.8 %collective-permute-done.6.refs_7_ = bf16[368,768]{1,0:T(8,128)(2,1)S(1)} collective-permute-done((bf16[368,768]{1,0:T(8,128)(2,1)S(1)}, bf16[368,768]{1,0:T(8,128)(2,1)S(1)}, u32[]{:S(2)}, u32[]{:S(2)}) %collective-permute-start.6) | collective-permute-done | bytes 565280 | tf_op jit(solution)/shard_map/ppermute | solution.py:423
  41.6 7.3 %shard_map.96 = (f32[4,128]{1,0:T(4,128)}, f32[4,96,768]{2,1,0:T(8,128)S(1)}, bf16[4,96,768]{2,1,0:T(8,128)(2,1)S(1)}) custom-call(s32[3]{0:T(128)S(1)} %pad_add_fusion.where_ref, bf16[368,768]{1,0:T(8,128)(2,1)S(1)} %get-tuple-element.16.refs_0_, bf16[368,768]{1,0:T(8,128)(2,1)S(1)} %collective-permute-done.refs_1_, ...), custom_call_target="tpu_custom_call" | custom-call | tf_op jit(solution)/shard_map/pallas_call | solution.py:62
  49.0 0.1 collective-permute-start.7
  49.1 1.9 %collective-permute-done.7.recv_ref = bf16[4,96,768]{2,1,0:T(8,128)(2,1)S(1)} collective-permute-done((bf16[4,96,768]{2,1,0:T(8,128)(2,1)S(1)}, bf16[4,96,768]{2,1,0:T(8,128)(2,1)S(1)}, u32[]{:S(2)}, u32[]{:S(2)}) %collective-permute-start.7) | collective-permute-done | bytes 589856 | tf_op jit(solution)/shard_map/ppermute | solution.py:423
  51.0 0.7 shard_map.97
  51.6 12.4 %all_to_all.10.got_ref = bf16[4,96,768]{2,1,0:T(8,128)(2,1)S(1)} all-to-all(bf16[4,96,768]{2,1,0:T(8,128)(2,1)S(1)} %get-tuple-element.27), channel_id=1, replica_groups=mesh['y'=2,'x'=2,'core'=2,'dp'=4] {'y','x'}, dimensions={0} | all-to-all | bytes 1179648 | tf_op jit(solution)/shard_map/all_to_all | solution.py:490
  64.0 0.7 shard_map.98
  64.7 11.4 %all_to_all.11.got_ref = bf16[4,48,384]{2,1,0:T(8,128)(2,1)S(1)} all-to-all(bf16[4,48,384]{2,1,0:T(8,128)(2,1)S(1)} %get-tuple-element.29), channel_id=1, replica_groups=mesh['y'=2,'x'=2,'core'=2,'dp'=4] {'dp'}, dimensions={0} | all-to-all | bytes 294912 | tf_op jit(solution)/shard_map/all_to_all | solution.py:498
  76.1 1.2 %shard_map.99 = f32[144,128]{1,0:T(8,128)} custom-call(s32[3]{0:T(128)S(1)} %pad_add_fusion.where_ref, f32[24,768]{1,0:T(8,128)S(1)} %get-tuple-element.28.mine_ref, bf16[4,48,384]{2,1,0:T(8,128)(2,1)S(1)} %all_to_all.11.got_ref), custom_call_target="tpu_custom_call" | custom-call | tf_op jit(solution)/shard_map/pallas_call | solution.py:62
Async XLA Ops:
  1.4 0.9 %copy-start = (bf16[3,96,384]{2,1,0:T(8,128)(2,1)S(1)}, bf16[3,96,384]{2,1,0:T(8,128)(2,1)}, u32[]{:S(2)}) copy-start(bf16[3,96,384]{2,1,0:T(8,128)(2,1)} %refs_1_.1) | copy-start | bytes 663556
  2.3 0.9 %copy-start.1 = (bf16[3,96,384]{2,1,0:T(8,128)(2,1)S(1)}, bf16[3,96,384]{2,1,0:T(8,128)(2,1)}, u32[]{:S(2)}) copy-start(bf16[3,96,384]{2,1,0:T(8,128)(2,1)} %refs_4_.1) | copy-start | bytes 663556
  3.2 0.9 %copy-start.2 = (bf16[1,128,768]{2,1,0:T(8,128)(2,1)S(1)}, bf16[1,128,768]{2,1,0:T(8,128)(2,1)}, u32[]{:S(2)}) copy-start(bf16[1,128,768]{2,1,0:T(8,128)(2,1)} %param.10) | copy-start | bytes 589828
  4.2 0.9 %copy-start.3 = (bf16[48,768]{1,0:T(8,128)(2,1)S(1)}, bf16[48,768]{1,0:T(8,128)(2,1)}, u32[]{:S(2)}) copy-start(bf16[48,768]{1,0:T(8,128)(2,1)} %refs_5_.1) | copy-start | bytes 221188
  5.0 0.9 %copy-start.4 = (bf16[48,768]{1,0:T(8,128)(2,1)S(1)}, bf16[48,768]{1,0:T(8,128)(2,1)}, u32[]{:S(2)}) copy-start(bf16[48,768]{1,0:T(8,128)(2,1)} %refs_6_.1) | copy-start | bytes 221188
  5.9 0.7 copy-start.5
  6.6 0.7 copy-start.6
  9.5 16.6 %collective-permute-start = (bf16[368,768]{1,0:T(8,128)(2,1)S(1)}, bf16[368,768]{1,0:T(8,128)(2,1)S(1)}, u32[]{:S(2)}, u32[]{:S(2)}) collective-permute-start(bf16[368,768]{1,0:T(8,128)(2,1)S(1)} %get-tuple-element.17), channel_id=1, source_target_pairs={{0,8},{8,0},{1,9},{9,1},{2,10},{10,2},{3,11},{11,3},{4,12},{12,4},... | collective-permute-start | bytes 1695752 | tf_op jit(solution)/shard_map/ppermute | solution.py:423
  12.5 26.4 %collective-permute-start.1 = (bf16[368,768]{1,0:T(8,128)(2,1)S(1)}, bf16[368,768]{1,0:T(8,128)(2,1)S(1)}, u32[]{:S(2)}, u32[]{:S(2)}) collective-permute-start(bf16[368,768]{1,0:T(8,128)(2,1)S(1)} %get-tuple-element.18), channel_id=1, source_target_pairs={{0,16},{16,0},{1,17},{17,1},{2,18},{18,2},{3,19},{19,3},{4,20},{20... | collective-permute-start | bytes 1695752 | tf_op jit(solution)/shard_map/ppermute | solution.py:423
  14.0 24.9 %collective-permute-start.2 = (bf16[368,768]{1,0:T(8,128)(2,1)S(1)}, bf16[368,768]{1,0:T(8,128)(2,1)S(1)}, u32[]{:S(2)}, u32[]{:S(2)}) collective-permute-start(bf16[368,768]{1,0:T(8,128)(2,1)S(1)} %get-tuple-element.19), channel_id=1, source_target_pairs={{0,24},{8,16},{16,8},{24,0},{1,25},{9,17},{17,9},{25,1},{2,26},{10... | collective-permute-start | bytes 1695752 | tf_op jit(solution)/shard_map/ppermute | solution.py:423
  14.0 25.4 %collective-permute-start.3 = (bf16[368,768]{1,0:T(8,128)(2,1)S(1)}, bf16[368,768]{1,0:T(8,128)(2,1)S(1)}, u32[]{:S(2)}, u32[]{:S(2)}) collective-permute-start(bf16[368,768]{1,0:T(8,128)(2,1)S(1)} %get-tuple-element.16.refs_0_), channel_id=1, source_target_pairs={{0,4},{4,0},{1,5},{5,1},{2,6},{6,2},{3,7},{7,3},{8,12},{12,8},{9,1... | collective-permute-start | bytes 1695752 | tf_op jit(solution)/shard_map/ppermute | solution.py:423
  26.1 13.3 %collective-permute-start.4 = (bf16[368,768]{1,0:T(8,128)(2,1)S(1)}, bf16[368,768]{1,0:T(8,128)(2,1)S(1)}, u32[]{:S(2)}, u32[]{:S(2)}) collective-permute-start(bf16[368,768]{1,0:T(8,128)(2,1)S(1)} %collective-permute-done.refs_1_), channel_id=1, source_target_pairs={{0,4},{4,0},{1,5},{5,1},{2,6},{6,2},{3,7},{7,3},{8,12},{12,8},{9,1... | collective-permute-start | bytes 1695752 | tf_op jit(solution)/shard_map/ppermute | solution.py:423
  38.8 2.0 %collective-permute-start.5 = (bf16[368,768]{1,0:T(8,128)(2,1)S(1)}, bf16[368,768]{1,0:T(8,128)(2,1)S(1)}, u32[]{:S(2)}, u32[]{:S(2)}) collective-permute-start(bf16[368,768]{1,0:T(8,128)(2,1)S(1)} %collective-permute-done.1.refs_2_), channel_id=1, source_target_pairs={{0,4},{4,0},{1,5},{5,1},{2,6},{6,2},{3,7},{7,3},{8,12},{12,8},{9,1... | collective-permute-start | bytes 1695752 | tf_op jit(solution)/shard_map/ppermute | solution.py:423
  38.9 2.8 %collective-permute-start.6 = (bf16[368,768]{1,0:T(8,128)(2,1)S(1)}, bf16[368,768]{1,0:T(8,128)(2,1)S(1)}, u32[]{:S(2)}, u32[]{:S(2)}) collective-permute-start(bf16[368,768]{1,0:T(8,128)(2,1)S(1)} %collective-permute-done.2.refs_3_), channel_id=1, source_target_pairs={{0,4},{4,0},{1,5},{5,1},{2,6},{6,2},{3,7},{7,3},{8,12},{12,8},{9,1... | collective-permute-start | bytes 1695752 | tf_op jit(solution)/shard_map/ppermute | solution.py:423
  49.0 2.0 %collective-permute-start.7 = (bf16[4,96,768]{2,1,0:T(8,128)(2,1)S(1)}, bf16[4,96,768]{2,1,0:T(8,128)(2,1)S(1)}, u32[]{:S(2)}, u32[]{:S(2)}) collective-permute-start(bf16[4,96,768]{2,1,0:T(8,128)(2,1)S(1)} %get-tuple-element.25), channel_id=1, source_target_pairs={{0,4},{4,0},{1,5},{5,1},{2,6},{6,2},{3,7},{7,3},{8,12},{12,8},{9,1... | collective-permute-start | bytes 1769480 | tf_op jit(solution)/shard_map/ppermute | solution.py:423

commit v3 on v2

--- a/solution.py
+++ b/solution.py
@@ -70,16 +70,15 @@
     )(*args)
 
 
-def base_tables(embed_ref, pick, conv, shard):
+def base_tables(emb, pick, conv):
     row = iota((16, 1), 0)
     low, high = row & 3, row >> 2
-    emb = embed_ref[...]
     by_low = spread(emb, low)
     by_high = spread(emb, high)
     act = gelu_pair(by_low)[0].astype(BF16)
     prod_high, prod_low = split(gelu_pair(by_high)[1] * by_low)
     own = mm(jnp.concatenate([act, prod_high, prod_low], axis=0), pick).astype(BF16)
-    first = jnp.zeros((16, conv.shape[2]), F32)
+    first = jnp.zeros((16, conv[0].shape[1]), F32)
     second = []
     for k in range(3):
         res = mm(own, conv[k])
@@ -88,32 +87,27 @@
     return first, jnp.concatenate(second, axis=0)
 
 
-def prep_kernel(where_ref, *refs):
-    sources = refs[:7]
-    own_ref, x_ref, y_ref, d_ref, cot_out, embed_out, bases_out = refs[7:14]
-    held = refs[14:21]
-    sems = refs[21]
-    moves = [
-        pltpu.make_async_copy(src, dst, sems.at[n])
-        for n, (src, dst) in enumerate(zip(sources, held))
-    ]
-    for move in moves:
-        move.start()
-    for move in moves:
-        move.wait()
-    embed_ref, c1_ref, cot_ref, bases_ref, c2_ref, p2_ref, p1_ref = held
+def prep_kernel(
+    where_ref, narrow_ref, broad_ref, small_ref,
+    own_ref, half_ref, r1_ref, r2_ref, l1_ref, l2_ref,
+):
     me, count = where_ref[0], where_ref[2]
-    shard = c1_ref.shape[1]
-    chans = embed_ref.shape[1]
-    width = c1_ref.shape[2]
-    cap = bases_ref.shape[1]
-    prows = p1_ref.shape[0]
+    width = narrow_ref.shape[1]
+    chans = 2 * width
+    shard = narrow_ref.shape[0] // 6
+    prows = width // 8
+    cap = broad_ref.shape[0] - 2 * prows
+    half = 3 * shard // 2
+    cut = half - 16
+    flat = narrow_ref.at[3 * shard : 6 * shard]
+    cot = broad_ref[2 * prows :]
     pick = (iota((chans, shard), 0) == iota((chans, shard), 1) + me * shard).astype(BF16)
-    first, second = base_tables(embed_ref, pick, c1_ref, shard)
+    taps = [narrow_ref[k * shard : (k + 1) * shard] for k in range(3)]
+    first, second = base_tables(small_ref[0:4], pick, taps)
     f_high, f_low = split(first)
     info = jnp.concatenate(
         [
-            bases_ref[...].astype(F32),
+            small_ref[4:5, 0:cap],
             jnp.full((1, 128), count, jnp.int32).astype(F32),
             jnp.zeros((1, chans - cap - 128), F32),
         ],
@@ -122,31 +116,28 @@
     tail = jnp.concatenate([f_high.astype(F32), f_low.astype(F32)], axis=1)
     tail = jnp.where(iota((16, 1), 0) == 12, info, tail)
     wide = jnp.concatenate([second[0:24], second[24:48]], axis=1)
-    tail = jnp.concatenate([wide, tail, jnp.zeros((8, chans), F32)], axis=0).astype(BF16)
-    half = 3 * shard // 2
-    flat = c2_ref[...].reshape(3 * shard, width)
-    cot = cot_ref[...]
+    extra = jnp.concatenate([info, jnp.zeros((7, chans), F32)], axis=0)
+    own_ref[0:cut, 0:width] = flat[0:cut]
+    own_ref[0:cut, width:chans] = flat[half : half + cut]
+    own_ref[cut:half] = tail.astype(BF16)
+    own_ref[half : half + 16, 0:width] = flat[cut:half]
+    own_ref[half : half + 16, width:chans] = flat[half + cut : 2 * half]
+    own_ref[half + 16 : half + 16 + 2 * prows] = broad_ref[0 : 2 * prows]
+    own_ref[2 * half - 32 :] = jnp.concatenate([wide, extra], axis=0).astype(BF16)
+    half_ref[...] = own_ref[pl.ds(pl.multiple_of((where_ref[1] & 1) * half, 16), half), :]
     take = (iota((HALO, cap), 1) == iota((HALO, cap), 0) + (count - HALO)).astype(BF16)
     last = mm(take, cot).astype(BF16)
-    chip = me >> 1
-    for rel, out in enumerate((own_ref, x_ref, y_ref, d_ref)):
-        out[0:half, 0:width] = flat[0:half]
-        out[0:half, width : 2 * width] = flat[half : 2 * half]
-        out[half : half + prows] = p2_ref[...]
-        out[half + prows : half + 2 * prows] = p1_ref[...]
-        out[half + 2 * prows : half + 2 * prows + 48] = tail
-        upward = (me & 1) == 0 if rel == 0 else (chip ^ rel) > chip
-        out[half + 2 * prows + 48 :] = jnp.where(upward, last, cot[0:HALO])
-    cot_out[...] = cot
-    embed_out[...] = embed_ref[...]
-    bases_out[...] = bases_ref[...]
+    r1_ref[...] = last
+    r2_ref[...] = last[HALO - SPILL :]
+    l1_ref[...] = cot[0:HALO]
+    l2_ref[...] = cot[0:SPILL]
 
 
 def table_body(
-    first, project, info_at, cot_ref, r1, r2, l1, l2, embed_ref,
+    first, project, info_at, cot, r1, r2, l1, l2, emb,
     b1_ref, s1_ref, a2_ref, s2_ref, hot_f_ref, hot_r_ref, cx_ref,
 ):
-    cap = cot_ref.shape[0]
+    cap = cot.shape[0]
     outer = HALO + SECOND_DILATION + FIRST_DILATION
     span = cap + 2 * outer
     counts = [info_at(o)[0:1, cap : cap + 128] for o in range(-REACH, REACH + 1)]
@@ -191,7 +182,7 @@
     high, low = split(slope)
     s1_ref[0:TABLE] = high
     s1_ref[TABLE : 2 * TABLE] = low
-    stream = spread(embed_ref[...], by25) + mm(b1, project)
+    stream = spread(emb, by25) + mm(b1, project)
     value, slope = gelu_pair(stream)
     a2_ref[...] = value.astype(BF16)
     high, low = split(slope)
@@ -207,7 +198,7 @@
     row_s = (iota((grow, SPILL), 0) - HALO).astype(F32)
     row_o = (iota((grow, cap), 0) - HALO).astype(F32)
     own_pos = jnp.where(lane < own_n, lane, FAR)
-    acc = mm((row_o == own_pos).astype(BF16), cot_ref[...])
+    acc = mm((row_o == own_pos).astype(BF16), cot)
     pos = jnp.where(lane_h >= HALO - before_n[:, 0:HALO], lane_h - HALO, FAR)
     acc = acc + mm((row_h == pos).astype(BF16), r1)
     pos = jnp.where(
@@ -229,16 +220,16 @@
     first_ref, project_ref, info_ref, cot_ref, r1_ref, r2_ref, l1_ref, l2_ref, embed_ref, *outs
 ):
     table_body(
-        first_ref[...], project_ref[...], lambda o: info_ref[REACH + o], cot_ref, r1_ref[...],
-        r2_ref[...], l1_ref[...], l2_ref[...], embed_ref, *outs
+        first_ref[...], project_ref[...], lambda o: info_ref[REACH + o], cot_ref[...], r1_ref[...],
+        r2_ref[...], l1_ref[...], l2_ref[...], embed_ref[...], *outs
     )
 
 
 def tower_body(
-    conv, p2, second, p1, count, bases_ref, cx_ref, b1_ref, s1_ref, a2_ref, s2_ref,
-    hot_f_ref, hot_r_ref, embed_ref, sal_ref, put,
+    conv, p2, second, p1, count, bases, cx_ref, b1_ref, s1_ref, a2_ref, s2_ref,
+    hot_f_ref, hot_r_ref, emb, sal_ref, put,
 ):
-    cap = bases_ref.shape[1]
+    cap = bases.shape[1]
     grow = cap + 2 * HALO
     inner = cap + 2 * FIRST_DILATION
     d, D = FIRST_DILATION, SECOND_DILATION
@@ -269,13 +260,11 @@
     s1 = s1_ref[...]
     s2 = s2_ref[...]
     sal = jnp.zeros((8, cap), F32)
-    emb = embed_ref[...]
     emb8 = jnp.concatenate([emb, emb], axis=0)
     flipped = jnp.concatenate(
         [emb[3 - c : 4 - c] for c in range(4)] * 2, axis=0
     )
     sec_high, sec_low = split(second)
-    bases = bases_ref[...]
     dproj1 = None
     for pass_idx, (hot_ref, order) in enumerate(((hot_f_ref, (0, 1, 2)), (hot_r_ref, (2, 1, 0)))):
         grad = grads[pass_idx]
@@ -313,45 +302,76 @@
 
 
 def tower_kernel_packed(where_ref, *refs):
-    parts = refs[:8]
-    cot_ref, embed_ref, bases_ref, sal_ref, keep_ref, send_ref = refs[8:14]
-    tables = refs[14:21]
-    conv_ref, p1_ref, p2_ref, info_ref, halo_ref, all_ref = refs[21:]
+    own_parts, plane_parts, dp_parts = refs[0:2], refs[2:8], refs[8:14]
+    broad_ref, small_ref, r1_ref, r2_ref, l1_ref, l2_ref = refs[14:20]
+    sal_ref, keep_ref, send_ref = refs[20:23]
+    tables = refs[23:30]
+    conv_ref, p1_ref, p2_ref, info_ref, first_ref, second_ref, all_ref = refs[30:]
     me, count = where_ref[0], where_ref[2]
-    chip, core = me >> 1, me & 1
-    chans = cot_ref.shape[1]
+    core, odd = me & 1, where_ref[1] & 1
+    chans = broad_ref.shape[1]
     width = chans // 2
     shard = chans // 8
     prow = width // 8
+    cap = broad_ref.shape[0] - 2 * prow
     half = 3 * shard // 2
+    cut = half - 16
     info_ref[0:REACH] = jnp.zeros((REACH, 8, 256), F32)
     info_ref[REACH + 8 :] = jnp.zeros((REACH, 8, 256), F32)
-    first = jnp.zeros((16, width), F32)
-    wide = jnp.zeros((24, chans), F32)
-    for n, part in enumerate(parts):
-        rel = 2 * (n & 3) + (n >> 2)
-        peer = me ^ rel
-        at = pl.multiple_of(peer * shard, 16)
-        conv_ref[0, pl.ds(at, shard), :] = part[0:shard, 0:width]
-        conv_ref[1, pl.ds(at, half - shard), :] = part[shard:half, 0:width]
-        at_half = pl.multiple_of(peer * shard + (half - shard), 16)
-        conv_ref[1, pl.ds(at_half, half - shard), :] = part[0 : half - shard, width : 2 * width]
-        conv_ref[2, pl.ds(at, shard), :] = part[half - shard : half, width : 2 * width]
-        at = pl.multiple_of(peer * prow, 16)
-        p2_ref[pl.ds(at, prow), :] = part[half : half + prow]
-        p1_ref[pl.ds(at, prow), :] = part[half + prow : half + 2 * prow]
-        tail = part[half + 2 * prow : half + 2 * prow + 48].astype(F32)
-        wide = wide + tail[0:24]
-        first = first + tail[24:40, 0:width] + tail[24:40, width : 2 * width]
-        info_ref[REACH + peer] = jnp.broadcast_to(tail[36:37, 0:256], (8, 256))
-        halo_ref[(n >> 2) * 4 + (peer >> 1)] = part[half + 2 * prow + 48 :]
-    r1 = halo_ref[4 + jnp.maximum(chip + core - 1, 0)]
-    l1 = halo_ref[4 + jnp.minimum(chip + core, 3)]
-    r2 = halo_ref[jnp.maximum(chip - 1, 0)]
-    l2 = halo_ref[jnp.minimum(chip + 1, 3)]
+
+    def place(side, rows, peer, told):
+        at = peer * shard
+
+        def lay(k, start, size, source, lane):
+            conv_ref[k, pl.ds(pl.multiple_of(at + start, 16), size), :] = rows(
+                source, size
+            )[:, lane : lane + width]
+
+        if side == 0:
+            lay(0, 0, shard, 0, 0)
+            lay(1, 0, cut - shard, shard, 0)
+            lay(1, shard // 2, shard // 2, 0, width)
+            lay(2, 0, cut - shard // 2, shard // 2, width)
+            tail = rows(cut, 16).astype(F32)
+            first_ref[peer] = tail[:, 0:width] + tail[:, width:]
+            line = tail[12:13, 0:256]
+        else:
+            lay(1, cut - shard, 16, 0, 0)
+            lay(2, shard - 16, 16, 0, width)
+            to = pl.ds(pl.multiple_of(peer * prow, 16), prow)
+            p2_ref[to, :] = rows(16, prow)
+            p1_ref[to, :] = rows(16 + prow, prow)
+            tail = rows(half - 32, 32).astype(F32)
+            second_ref[peer] = tail[0:24]
+            line = tail[24:25, 0:256]
+        if told:
+            info_ref[REACH + peer] = jnp.broadcast_to(line, (8, 256))
+
+    for n in range(2):
+        for side in range(2):
+            rows = lambda a, size, n=n, side=side: own_parts[n][
+                side * half + a : side * half + a + size
+            ]
+            place(side, rows, me ^ n, side == 0)
+    for parity in range(2):
+
+        @pl.when(odd == parity)
+        def _():
+            for n in range(6):
+                peer = me ^ (2 * (n % 3 + 1) + n // 3)
+                for side, part in ((parity, plane_parts[n]), (1 - parity, dp_parts[n])):
+                    rows = lambda a, size, part=part: part[a : a + size]
+                    place(side, rows, peer, side == parity)
+
+    first = first_ref[0]
+    wide = second_ref[0]
+    for peer in range(1, 8):
+        first = first + first_ref[peer]
+        wide = wide + second_ref[peer]
+    emb = small_ref[0:4]
     table_body(
-        first, p1_ref[...], lambda o: info_ref[me + (REACH + o)], cot_ref, r1,
-        r2[HALO - SPILL :], l1, l2[0:SPILL], embed_ref, *tables,
+        first, p1_ref[...], lambda o: info_ref[me + (REACH + o)], broad_ref[2 * prow :],
+        r1_ref[...], r2_ref[...], l1_ref[...], l2_ref[...], emb, *tables,
     )
     second = jnp.concatenate([wide[:, 0:width], wide[:, width : 2 * width]], axis=0)
 
@@ -363,8 +383,8 @@
 
     b1, s1, a2, s2, hf, hr, cx = tables
     tower_body(
-        lambda k: conv_ref[k], p2_ref[...], second, p1_ref[...], count, bases_ref, cx,
-        b1, s1, a2, s2, hf, hr, embed_ref, sal_ref, put,
+        lambda k: conv_ref[k], p2_ref[...], second, p1_ref[...], count, small_ref[4:5, 0:cap],
+        cx, b1, s1, a2, s2, hf, hr, emb, sal_ref, put,
     )
     keep_ref[...] = all_ref[0:4]
     send_ref[...] = all_ref[4:8].astype(BF16)
@@ -380,41 +400,39 @@
 
     tower_body(
         lambda k: conv_ref[k], p2_ref[...], second_ref[...], p1_ref[...], where_ref[2],
-        bases_ref, cx_ref, b1_ref, s1_ref, a2_ref, s2_ref, hf, hr, emb, sal_ref, put,
-    )
-
-
-def core_sum_kernel(where_ref, keep_ref, recv_ref, own_ref, out_ref):
-    out_ref[...] = (keep_ref[...] + recv_ref[...].astype(F32)).astype(BF16)
+        bases_ref[...], cx_ref, b1_ref, s1_ref, a2_ref, s2_ref, hf, hr, emb[...], sal_ref, put,
+    )
+
+
+def fold(value):
+    width = value.shape[1] // 2
+    return jnp.concatenate([value[:, 0:width], value[:, width:]], axis=0)
+
+
+def core_sum_kernel(where_ref, keep_ref, recv_ref, mine_ref, out_ref, sum_ref):
+    rows = mine_ref.shape[0] // 2
+    per = keep_ref.shape[1] // rows
+    for c in range(keep_ref.shape[0]):
+        total = keep_ref[c] + recv_ref[c].astype(F32)
+        sum_ref[c] = total
+        for n in range(per):
+            out_ref[per * c + n] = fold(total[n * rows : (n + 1) * rows]).astype(BF16)
     chip = where_ref[0] >> 1
-    own_ref[...] = keep_ref[chip] + recv_ref[chip].astype(F32)
-
-
-def plane_sum_kernel(where_ref, own_ref, got_ref, mine_ref, out_ref, sum_ref):
-    chip, z = where_ref[0] >> 1, where_ref[1]
-    total = own_ref[...]
-    for c in range(got_ref.shape[0]):
-        total = total + jnp.where(chip == c, 0.0, got_ref[c].astype(F32))
-    sum_ref[...] = total
-    count, rows = out_ref.shape[0], mine_ref.shape[0]
-    width = own_ref.shape[1] // 2
-    for c in range(count):
-        value = total[c * rows : (c + 1) * rows]
-        out_ref[c] = jnp.concatenate([value[:, 0:width], value[:, width:]], axis=0).astype(BF16)
-    mine_ref[...] = sum_ref[pl.ds(pl.multiple_of(z * rows, 8), rows), :]
+    at = pl.ds(pl.multiple_of(where_ref[1] * rows, 8), rows)
+    mine_ref[...] = fold(sum_ref[chip, at, :])
 
 
 def last_sum_kernel(scale, where_ref, mine_ref, got_ref, out_ref):
     total = mine_ref[...]
-    rows, chans = total.shape
+    me = (where_ref[0] >> 1) * (got_ref.shape[0] // 4) + where_ref[1]
     for c in range(got_ref.shape[0]):
-        value = got_ref[c].astype(F32)
-        value = jnp.concatenate([value[0:rows], value[rows : 2 * rows]], axis=1)
-        total = total + jnp.where(where_ref[1] == c, 0.0, value)
+        total = total + jnp.where(me == c, 0.0, got_ref[c].astype(F32))
     total = total * scale
-    parts = chans // 128
-    for n in range(parts):
-        out_ref[pl.ds(n, rows, stride=parts), :] = total[:, 128 * n : 128 * n + 128]
+    rows, half = total.shape[0] // 2, total.shape[1] // 128
+    for n in range(2 * half):
+        at = rows * (n // half)
+        lane = 128 * (n % half)
+        out_ref[pl.ds(n, rows, stride=2 * half), :] = total[at : at + rows, lane : lane + 128]
 
 
 def flip_move(array, *axes):
@@ -423,9 +441,9 @@
     return lax.ppermute(array, axes, [(i, size - 1 - i) for i in range(size)])
 
 
-def shift_move(array, axis, by):
-    size = lax.axis_size(axis)
-    return lax.ppermute(array, axis, [(i, i + by) for i in range(size) if 0 <= i + by < size])
+def shift_move(array, by, axes=("y", "x", "core")):
+    size = math.prod(lax.axis_size(a) for a in axes)
+    return lax.ppermute(array, axes, [(i, i + by) for i in range(size) if 0 <= i + by < size])
 
 
 def table_shapes(cap, chans, width):
@@ -450,52 +468,51 @@
     cap, chans = cot.shape
     width = c1.shape[2]
     n_dp = lax.axis_size("dp")
-    height = 3 * c2.shape[1] // 2 + 2 * p1.shape[0] + 48 + HALO
-    sources = [embed, c1, cot, bases, c2, p2, p1]
-    outs = call(
+    half = 3 * c2.shape[1] // 2
+    narrow = jnp.concatenate([c1.reshape(-1, width), c2.reshape(-1, width)], axis=0)
+    broad = jnp.concatenate([p2, p1, cot], axis=0)
+    small = jnp.concatenate(
+        [embed, jnp.pad(bases.astype(F32), ((0, 3), (0, chans - cap)))], axis=0
+    )
+    own, part, r1, r2, l1, l2 = call(
         prep_kernel,
-        [((height, chans), BF16)] * 4
-        + [(cot.shape, BF16), (embed.shape, F32), (bases.shape, jnp.int32)],
-        [where, *sources],
-        scratch=[pltpu.VMEM(a.shape, a.dtype) for a in sources]
-        + [pltpu.SemaphoreType.DMA((len(sources),))],
-        space=pl.ANY,
-    )
-    near = list(outs[:4])
-    for n, axes in ((1, ("x",)), (2, ("y",)), (3, ("y", "x"))):
-        near[n] = flip_move(near[n], *axes)
-    across = [flip_move(a, "core") for a in near]
+        [((r, chans), BF16) for r in (2 * half, half, HALO, SPILL, HALO, SPILL)],
+        [where, narrow, broad, small],
+    )
+    plane = [flip_move(part, *axes) for axes in (("x",), ("y",), ("y", "x"))]
+    pairs = [(i, i ^ 1) for i in range(n_dp)]
+    other = [lax.ppermute(a, "dp", pairs) for a in plane]
+    halos = [shift_move(r1, 1), shift_move(r2, 2), shift_move(l1, -1), shift_move(l2, -2)]
+    across = lambda arrays: [flip_move(a, "core") for a in arrays]
     rows = chans // 8
     sal, keep, send = call(
         tower_kernel_packed,
         [((4, cap), F32), ((4, rows, chans), F32), ((4, rows, chans), BF16)],
-        [where, outs[0], *near[1:], *across, *outs[4:]],
+        [
+            where, own, *across([own]), *plane, *across(plane), *other, *across(other),
+            broad, small, *halos,
+        ],
         scratch=[pltpu.VMEM(s, d) for s, d in table_shapes(cap, chans, width)]
         + [
             pltpu.VMEM((3, chans, width), BF16),
             pltpu.VMEM((width, chans), BF16),
             pltpu.VMEM((width, chans), BF16),
             pltpu.VMEM((8 + 2 * REACH, 8, 256), F32),
-            pltpu.VMEM((8, HALO, chans), BF16),
+            pltpu.VMEM((8, 16, width), F32),
+            pltpu.VMEM((8, 24, chans), F32),
             pltpu.VMEM((8, rows, chans), F32),
         ],
         limit=40,
     )
     recv = flip_move(send, "core")
-    own, out = call(
-        core_sum_kernel,
-        [((rows, chans), F32), ((4, rows, chans), BF16)],
-        [where, keep, recv],
-    )
-    got = lax.all_to_all(out, ("y", "x"), 0, 0)
     part = rows // n_dp
     mine, out = call(
-        plane_sum_kernel,
-        [((part, chans), F32), ((n_dp, 2 * part, width), BF16)],
-        [where, own, got],
-        scratch=[pltpu.VMEM((rows, chans), F32)],
-    )
-    got = lax.all_to_all(out, "dp", 0, 0)
+        core_sum_kernel,
+        [((2 * part, width), F32), ((4 * n_dp, 2 * part, width), BF16)],
+        [where, keep, recv],
+        scratch=[pltpu.VMEM((4, rows, chans), F32)],
+    )
+    got = lax.all_to_all(out, ("y", "x", "dp"), 0, 0)
     scale = 1.0 / math.sqrt(8 * n_dp * cap)
     (grad,) = call(
         functools.partial(last_sum_kernel, scale),
@@ -540,10 +557,10 @@
     padded = jnp.pad(cot, ((HALO, 0), (0, 0)))
     last = lax.dynamic_slice_in_dim(padded, count, HALO, 0)
     halos = [
-        shift_move(last, "seq", 1),
-        shift_move(last[HALO - SPILL :], "seq", 2),
-        shift_move(cot[:HALO], "seq", -1),
-        shift_move(cot[:SPILL], "seq", -2),
+        shift_move(last, 1, ("seq",)),
+        shift_move(last[HALO - SPILL :], 2, ("seq",)),
+        shift_move(cot[:HALO], -1, ("seq",)),
+        shift_move(cot[:SPILL], -2, ("seq",)),
     ]
     b1, s1, a2, s2, hf, hr, cx = call(
         table_kernel_plain,
@@ -565,7 +582,7 @@
 
 def solution(mesh):
     run, seq = plain_shards, "seq"
-    if mesh.shape["seq"] == 8:
+    if mesh.shape["seq"] == 8 and mesh.shape["dp"] == 4:
         run, seq = fast_shards, ("y", "x", "core")
         count = mesh.shape["dp"]
         mesh = jax.sharding.Mesh(mesh.devices.reshape(2, 2, 2, count), (*seq, "dp"))

time: 77.7 us -> 83.7 us (1.077)
  starting transfers between devices: 5.2 us -> 21.8 us
  waiting for transfers between devices: 29 us -> 22.1 us
  local copies, waits for them, and re-layouts: 5.93 us -> 0 us
  other arithmetic: 0.08 us -> 3.58 us
  Pallas kernels: 12.1 us -> 10.6 us
    ppermute x8 -> x11, waiting for transfers between devices: 29 us -> 8.99 us  [flip_move(): return lax.ppermute(array, axes, [(i, size - 1 - i) for i in range(size)])]
    ppermute x0 -> x7, waiting for transfers between devices: none -> 13.2 us  [the longest x3 9.3 us: fast_shards(): other = [lax.ppermute(a, 'dp', pairs) for a in plane]]
    ppermute x0 -> x7, starting transfers between devices: none -> 11.4 us  [the longest x4 7.24 us: shift_move(): lax.ppermute(array, axes, [(i, i + by) for i in range(size) if 0 <= i + b...]
    unnamed x14 -> x0, local copies, waits for them, and re-layouts: 5.93 us -> none
    ppermute x8 -> x11, starting transfers between devices: 5.2 us -> 10.4 us  [flip_move(): return lax.ppermute(array, axes, [(i, size - 1 - i) for i in range(size)])]
    concatenate x0 -> x3, other arithmetic: none -> 2.84 us  [the longest x1 1.09 us: fast_shards(): jnp.concatenate([c1.reshape(-1, width), c2.reshape(-1, width)], axis=0)]
    pallas_call x5 -> x4, Pallas kernels: 12.1 us -> 10.6 us  [call(): pl.pallas_call(body, out_shape=[jax.ShapeDtypeStruct(s, d) for s, d in ou...]
    all_to_all x2 -> x1, blocking collectives: 23.7 us -> 23.9 us  [fast_shards(): got = lax.all_to_all(out, ('y', 'x', 'dp'), 0, 0)]
  transfers between devices with their start and end apart: 8 -> 18, of which waited for: 5 -> 8; matrix products, arithmetic and copies ran while one was open for 0% -> 0% of each run, Pallas kernels for 0% -> 0%
where the time goes in v3:
time: 83.7 us; the launch traced here: 83.3 us
  blocking collectives  23.9 us (29%)
  waiting for transfers between devices  22.1 us (26%)
  starting transfers between devices  21.8 us (26%)
  Pallas kernels  10.6 us (13%)
  other arithmetic  3.58 us (4%)
  between operations  1.38 us (2%)
    all_to_all x1, blocking collectives, fast_shards(): got = lax.all_to_all(out, ('y', 'x', 'dp'), 0, 0)  23.9 us
    pallas_call x4, Pallas kernels, call(): pl.pallas_call(body, out_shape=[jax.ShapeDtypeStruct(s, d) for s, d in ou...  10.6 us
    ppermute x11, starting transfers between devices, flip_move(): return lax.ppermute(array, axes, [(i, size - 1 - i) for i in range(size)])  10.4 us
    ppermute x3, waiting for transfers between devices, fast_shards(): other = [lax.ppermute(a, 'dp', pairs) for a in plane]  9.3 us
    ppermute x11, waiting for transfers between devices, flip_move(): return lax.ppermute(array, axes, [(i, size - 1 - i) for i in range(size)])  8.99 us
    ppermute x4, starting transfers between devices, shift_move(): lax.ppermute(array, axes, [(i, i + by) for i in range(size) if 0 <= i + b...  7.24 us
    ppermute x3, starting transfers between devices, fast_shards(): other = [lax.ppermute(a, 'dp', pairs) for a in plane]  4.18 us
    ppermute x4, waiting for transfers between devices, shift_move(): lax.ppermute(array, axes, [(i, i + by) for i in range(size) if 0 <= i + b...  3.86 us
  transfers between devices with their start and end apart: 18, of which 8 were waited for; matrix products, arithmetic and copies ran while one was open for 0% of the time, Pallas kernels for 0%

profile of v3, /device:TPU:0, one launch (start us, length us, event | category | flops | bytes accessed | tf_op | source)
XLA Modules:
  0.0 83.3 jit_solution(3401853730644548012)
XLA Ops:
  1.3 0.7 convert_element_type.5
  1.9 0.7 select_maximum_fusion.small_ref.refs_15_
  2.7 1.1 %pad_maximum_fusion.narrow_ref = bf16[576,384]{1,0:T(8,128)(2,1)S(1)} fusion(bf16[288,384]{1,0:T(8,128)(2,1)} %bitcast.9, bf16[288,384]{1,0:T(8,128)(2,1)} %bitcast.10), kind=kLoop, calls=%fused_computation | loop fusion | flops 884736 | bytes 884736 | tf_op jit(solution)/shard_map/concatenate | solution.py:472
  3.7 0.1 pad_add_fusion.where_ref
  3.8 1.0 %pad_maximum_fusion.1.broad_ref.refs_14_ = bf16[224,768]{1,0:T(8,128)(2,1)S(1)} fusion(bf16[128,768]{1,0:T(8,128)(2,1)} %bitcast.11, bf16[48,768]{1,0:T(8,128)(2,1)} %param.12, bf16[48,768]{1,0:T(8,128)(2,1)} %param.14), kind=kLoop, calls=%fused_computation.1 | loop fusion | flops 1032192 | bytes 688128 | tf_op jit(solution)/shard_map/concatenate | solution.py:473
  4.9 0.9 %shard_map.95 = (bf16[288,768]{1,0:T(8,128)(2,1)S(1)}, bf16[144,768]{1,0:T(8,128)(2,1)S(1)}, bf16[80,768]{1,0:T(8,128)(2,1)S(1)}, bf16[16,768]{1,0:T(8,128)(2,1)...) custom-call(s32[3]{0:T(128)S(1)} %pad_add_fusion.where_ref, ...), custom_call_target="tpu_custom_call" | custom-call | tf_op jit(solution)/shard_map/pallas_call | solution.py:62
  5.8 4.0 %collective-permute-start.3 = (bf16[144,768]{1,0:T(8,128)(2,1)S(1)}, bf16[144,768]{1,0:T(8,128)(2,1)S(1)}, u32[]{:S(2)}, u32[]{:S(2)}) collective-permute-start(bf16[144,768]{1,0:T(8,128)(2,1)S(1)} %get-tuple-element.14), channel_id=1, source_target_pairs={{0,24},{8,16},{16,8},{24,0},{1,25},{9,17},{17,9},{25,1},{2,26},{10... | collective-permute-start | bytes 663560 | tf_op jit(solution)/shard_map/ppermute | solution.py:441
  9.8 0.5 collective-permute-start.2
  10.3 0.1 collective-permute-start.1
  10.4 5.7 %collective-permute-done.3.refs_4_ = bf16[144,768]{1,0:T(8,128)(2,1)S(1)} collective-permute-done((bf16[144,768]{1,0:T(8,128)(2,1)S(1)}, bf16[144,768]{1,0:T(8,128)(2,1)S(1)}, u32[]{:S(2)}, u32[]{:S(2)}) %collective-permute-start.3) | collective-permute-done | bytes 221216 | tf_op jit(solution)/shard_map/ppermute | solution.py:441
  16.1 2.1 %collective-permute-start.9 = (bf16[144,768]{1,0:T(8,128)(2,1)S(1)}, bf16[144,768]{1,0:T(8,128)(2,1)S(1)}, u32[]{:S(2)}, u32[]{:S(2)}) collective-permute-start(bf16[144,768]{1,0:T(8,128)(2,1)S(1)} %collective-permute-done.3.refs_4_), channel_id=1, source_target_pairs={{0,1},{1,0},{2,3},{3,2},{4,5},{5,4},{6,7},{7,6},{8,9},{9,8},{10,11... | collective-permute-start | bytes 663560 | tf_op jit(solution)/shard_map/ppermute | solution.py:484
  18.2 3.4 %collective-permute-start.14 = (bf16[16,768]{1,0:T(8,128)(2,1)S(1)}, bf16[16,768]{1,0:T(8,128)(2,1)S(1)}, u32[]{:S(2)}, u32[]{:S(2)}) collective-permute-start(bf16[16,768]{1,0:T(8,128)(2,1)S(1)} %get-tuple-element.16), channel_id=1, source_target_pairs={{0,8},{4,12},{8,16},{12,20},{16,24},{20,28},{1,9},{5,13},{9,17},{1... | collective-permute-start | bytes 73736 | tf_op jit(solution)/shard_map/ppermute | solution.py:446
  21.6 1.3 %collective-permute-start.16 = (bf16[16,768]{1,0:T(8,128)(2,1)S(1)}, bf16[16,768]{1,0:T(8,128)(2,1)S(1)}, u32[]{:S(2)}, u32[]{:S(2)}) collective-permute-start(bf16[16,768]{1,0:T(8,128)(2,1)S(1)} %get-tuple-element.18), channel_id=1, source_target_pairs={{8,0},{12,4},{16,8},{20,12},{24,16},{28,20},{9,1},{13,5},{17,9},{2... | collective-permute-start | bytes 73736 | tf_op jit(solution)/shard_map/ppermute | solution.py:446
  22.9 0.2 collective-permute-done.14.refs_17_
  23.1 1.3 %collective-permute-start.13 = (bf16[80,768]{1,0:T(8,128)(2,1)S(1)}, bf16[80,768]{1,0:T(8,128)(2,1)S(1)}, u32[]{:S(2)}, u32[]{:S(2)}) collective-permute-start(bf16[80,768]{1,0:T(8,128)(2,1)S(1)} %get-tuple-element.15), channel_id=1, source_target_pairs={{0,4},{4,8},{8,12},{12,16},{16,20},{20,24},{24,28},{1,5},{5,9},{9,... | collective-permute-start | bytes 368648 | tf_op jit(solution)/shard_map/ppermute | solution.py:446
  24.4 2.9 %collective-permute-done.16.refs_19_ = bf16[16,768]{1,0:T(8,128)(2,1)S(1)} collective-permute-done((bf16[16,768]{1,0:T(8,128)(2,1)S(1)}, bf16[16,768]{1,0:T(8,128)(2,1)S(1)}, u32[]{:S(2)}, u32[]{:S(2)}) %collective-permute-start.16) | collective-permute-done | bytes 24608 | tf_op jit(solution)/shard_map/ppermute | solution.py:446
  27.3 1.3 %collective-permute-start.15 = (bf16[80,768]{1,0:T(8,128)(2,1)S(1)}, bf16[80,768]{1,0:T(8,128)(2,1)S(1)}, u32[]{:S(2)}, u32[]{:S(2)}) collective-permute-start(bf16[80,768]{1,0:T(8,128)(2,1)S(1)} %get-tuple-element.17), channel_id=1, source_target_pairs={{4,0},{8,4},{12,8},{16,12},{20,16},{24,20},{28,24},{5,1},{9,5},{13... | collective-permute-start | bytes 368648 | tf_op jit(solution)/shard_map/ppermute | solution.py:446
  28.6 0.0 collective-permute-done.13.refs_16_
  28.6 1.2 %collective-permute-start = (bf16[288,768]{1,0:T(8,128)(2,1)S(1)}, bf16[288,768]{1,0:T(8,128)(2,1)S(1)}, u32[]{:S(2)}, u32[]{:S(2)}) collective-permute-start(bf16[288,768]{1,0:T(8,128)(2,1)S(1)} %get-tuple-element.13.refs_0_), channel_id=1, source_target_pairs={{0,4},{4,0},{1,5},{5,1},{2,6},{6,2},{3,7},{7,3},{8,12},{12,8},{9,1... | collective-permute-start | bytes 1327112 | tf_op jit(solution)/shard_map/ppermute | solution.py:441
  29.8 0.7 collective-permute-done.15.refs_18_
  30.5 3.7 %collective-permute-start.6 = (bf16[144,768]{1,0:T(8,128)(2,1)S(1)}, bf16[144,768]{1,0:T(8,128)(2,1)S(1)}, u32[]{:S(2)}, u32[]{:S(2)}) collective-permute-start(bf16[144,768]{1,0:T(8,128)(2,1)S(1)} %collective-permute-done.3.refs_4_), channel_id=1, source_target_pairs={{0,4},{4,0},{1,5},{5,1},{2,6},{6,2},{3,7},{7,3},{8,12},{12,8},{9,1... | collective-permute-start | bytes 663560 | tf_op jit(solution)/shard_map/ppermute | solution.py:441
  34.3 0.0 collective-permute-done.2.refs_3_
  34.3 0.4 collective-permute-start.8
  34.7 0.0 collective-permute-done.1.refs_2_
  34.7 0.0 collective-permute-start.5
  34.7 0.0 collective-permute-done.9.refs_10_
  34.7 1.6 %collective-permute-start.7 = (bf16[144,768]{1,0:T(8,128)(2,1)S(1)}, bf16[144,768]{1,0:T(8,128)(2,1)S(1)}, u32[]{:S(2)}, u32[]{:S(2)}) collective-permute-start(bf16[144,768]{1,0:T(8,128)(2,1)S(1)} %collective-permute-done.1.refs_2_), channel_id=1, source_target_pairs={{0,1},{1,0},{2,3},{3,2},{4,5},{5,4},{6,7},{7,6},{8,9},{9,8},{10,11... | collective-permute-start | bytes 663560 | tf_op jit(solution)/shard_map/ppermute | solution.py:484
  36.4 0.0 collective-permute-done.6.refs_7_
  36.4 0.2 collective-permute-start.4
  36.5 6.0 %collective-permute-done.8.refs_9_ = bf16[144,768]{1,0:T(8,128)(2,1)S(1)} collective-permute-done((bf16[144,768]{1,0:T(8,128)(2,1)S(1)}, bf16[144,768]{1,0:T(8,128)(2,1)S(1)}, u32[]{:S(2)}, u32[]{:S(2)}) %collective-permute-start.8) | collective-permute-done | bytes 221216 | tf_op jit(solution)/shard_map/ppermute | solution.py:484
  42.6 0.0 collective-permute-start.12
  42.6 0.0 collective-permute-done.5.refs_6_
  42.6 0.5 collective-permute-start.11
  43.1 3.3 %collective-permute-done.7.refs_8_ = bf16[144,768]{1,0:T(8,128)(2,1)S(1)} collective-permute-done((bf16[144,768]{1,0:T(8,128)(2,1)S(1)}, bf16[144,768]{1,0:T(8,128)(2,1)S(1)}, u32[]{:S(2)}, u32[]{:S(2)}) %collective-permute-start.7) | collective-permute-done | bytes 221216 | tf_op jit(solution)/shard_map/ppermute | solution.py:484
  46.3 0.0 collective-permute-start.10
  46.3 0.0 collective-permute-done.4.refs_5_
  46.3 0.0 collective-permute-done.refs_1_
  46.3 0.0 collective-permute-done.12.refs_13_
  46.4 0.0 collective-permute-done.11.refs_12_
  46.4 1.4 %collective-permute-done.10.refs_11_ = bf16[144,768]{1,0:T(8,128)(2,1)S(1)} collective-permute-done((bf16[144,768]{1,0:T(8,128)(2,1)S(1)}, bf16[144,768]{1,0:T(8,128)(2,1)S(1)}, u32[]{:S(2)}, u32[]{:S(2)}) %collective-permute-start.10) | collective-permute-done | bytes 221216 | tf_op jit(solution)/shard_map/ppermute | solution.py:441
  47.8 7.6 %shard_map.96 = (f32[4,128]{1,0:T(4,128)}, f32[4,96,768]{2,1,0:T(8,128)S(1)}, bf16[4,96,768]{2,1,0:T(8,128)(2,1)S(1)}) custom-call(s32[3]{0:T(128)S(1)} %pad_add_fusion.where_ref, bf16[288,768]{1,0:T(8,128)(2,1)S(1)} %get-tuple-element.13.refs_0_, bf16[288,768]{1,0:T(8,128)(2,1)S(1)} %collective-permute-done.refs_1_, ...), custom_call_target="tpu_custom_call" | custom-call | tf_op jit(solution)/shard_map/pallas_call | solution.py:62
  55.4 0.1 collective-permute-start.17
  55.5 1.9 %collective-permute-done.17.recv_ref = bf16[4,96,768]{2,1,0:T(8,128)(2,1)S(1)} collective-permute-done((bf16[4,96,768]{2,1,0:T(8,128)(2,1)S(1)}, bf16[4,96,768]{2,1,0:T(8,128)(2,1)S(1)}, u32[]{:S(2)}, u32[]{:S(2)}) %collective-permute-start.17) | collective-permute-done | bytes 589856 | tf_op jit(solution)/shard_map/ppermute | solution.py:441
  57.4 0.7 shard_map.97
  58.1 23.9 %all_to_all.5.got_ref = bf16[16,48,384]{2,1,0:T(8,128)(2,1)S(1)} all-to-all(bf16[16,48,384]{2,1,0:T(8,128)(2,1)S(1)} %get-tuple-element.23), channel_id=1, replica_groups=mesh['y'=2,'x'=2,'core'=2,'dp'=4] {'y','x','dp'}, dimensions={0} | all-to-all | bytes 1179648 | tf_op jit(solution)/shard_map/all_to_all | solution.py:515
  82.0 1.3 %shard_map.98 = f32[144,128]{1,0:T(8,128)} custom-call(s32[3]{0:T(128)S(1)} %pad_add_fusion.where_ref, f32[48,384]{1,0:T(8,128)S(1)} %get-tuple-element.22.mine_ref, bf16[16,48,384]{2,1,0:T(8,128)(2,1)S(1)} %all_to_all.5.got_ref), custom_call_target="tpu_custom_call" | custom-call | tf_op jit(solution)/shard_map/pallas_call | solution.py:62
Async XLA Ops:
  5.8 10.3 %collective-permute-start.3 = (bf16[144,768]{1,0:T(8,128)(2,1)S(1)}, bf16[144,768]{1,0:T(8,128)(2,1)S(1)}, u32[]{:S(2)}, u32[]{:S(2)}) collective-permute-start(bf16[144,768]{1,0:T(8,128)(2,1)S(1)} %get-tuple-element.14), channel_id=1, source_target_pairs={{0,24},{8,16},{16,8},{24,0},{1,25},{9,17},{17,9},{25,1},{2,26},{10... | collective-permute-start | bytes 663560 | tf_op jit(solution)/shard_map/ppermute | solution.py:441
  9.8 24.5 %collective-permute-start.2 = (bf16[144,768]{1,0:T(8,128)(2,1)S(1)}, bf16[144,768]{1,0:T(8,128)(2,1)S(1)}, u32[]{:S(2)}, u32[]{:S(2)}) collective-permute-start(bf16[144,768]{1,0:T(8,128)(2,1)S(1)} %get-tuple-element.14), channel_id=1, source_target_pairs={{0,16},{16,0},{1,17},{17,1},{2,18},{18,2},{3,19},{19,3},{4,20},{20... | collective-permute-start | bytes 663560 | tf_op jit(solution)/shard_map/ppermute | solution.py:441
  10.3 24.4 %collective-permute-start.1 = (bf16[144,768]{1,0:T(8,128)(2,1)S(1)}, bf16[144,768]{1,0:T(8,128)(2,1)S(1)}, u32[]{:S(2)}, u32[]{:S(2)}) collective-permute-start(bf16[144,768]{1,0:T(8,128)(2,1)S(1)} %get-tuple-element.14), channel_id=1, source_target_pairs={{0,8},{8,0},{1,9},{9,1},{2,10},{10,2},{3,11},{11,3},{4,12},{12,4},... | collective-permute-start | bytes 663560 | tf_op jit(solution)/shard_map/ppermute | solution.py:441
  16.1 18.6 %collective-permute-start.9 = (bf16[144,768]{1,0:T(8,128)(2,1)S(1)}, bf16[144,768]{1,0:T(8,128)(2,1)S(1)}, u32[]{:S(2)}, u32[]{:S(2)}) collective-permute-start(bf16[144,768]{1,0:T(8,128)(2,1)S(1)} %collective-permute-done.3.refs_4_), channel_id=1, source_target_pairs={{0,1},{1,0},{2,3},{3,2},{4,5},{5,4},{6,7},{7,6},{8,9},{9,8},{10,11... | collective-permute-start | bytes 663560 | tf_op jit(solution)/shard_map/ppermute | solution.py:484
  18.2 4.9 %collective-permute-start.14 = (bf16[16,768]{1,0:T(8,128)(2,1)S(1)}, bf16[16,768]{1,0:T(8,128)(2,1)S(1)}, u32[]{:S(2)}, u32[]{:S(2)}) collective-permute-start(bf16[16,768]{1,0:T(8,128)(2,1)S(1)} %get-tuple-element.16), channel_id=1, source_target_pairs={{0,8},{4,12},{8,16},{12,20},{16,24},{20,28},{1,9},{5,13},{9,17},{1... | collective-permute-start | bytes 73736 | tf_op jit(solution)/shard_map/ppermute | solution.py:446
  21.6 5.7 %collective-permute-start.16 = (bf16[16,768]{1,0:T(8,128)(2,1)S(1)}, bf16[16,768]{1,0:T(8,128)(2,1)S(1)}, u32[]{:S(2)}, u32[]{:S(2)}) collective-permute-start(bf16[16,768]{1,0:T(8,128)(2,1)S(1)} %get-tuple-element.18), channel_id=1, source_target_pairs={{8,0},{12,4},{16,8},{20,12},{24,16},{28,20},{9,1},{13,5},{17,9},{2... | collective-permute-start | bytes 73736 | tf_op jit(solution)/shard_map/ppermute | solution.py:446
  23.1 5.5 %collective-permute-start.13 = (bf16[80,768]{1,0:T(8,128)(2,1)S(1)}, bf16[80,768]{1,0:T(8,128)(2,1)S(1)}, u32[]{:S(2)}, u32[]{:S(2)}) collective-permute-start(bf16[80,768]{1,0:T(8,128)(2,1)S(1)} %get-tuple-element.15), channel_id=1, source_target_pairs={{0,4},{4,8},{8,12},{12,16},{16,20},{20,24},{24,28},{1,5},{5,9},{9,... | collective-permute-start | bytes 368648 | tf_op jit(solution)/shard_map/ppermute | solution.py:446
  27.3 3.2 %collective-permute-start.15 = (bf16[80,768]{1,0:T(8,128)(2,1)S(1)}, bf16[80,768]{1,0:T(8,128)(2,1)S(1)}, u32[]{:S(2)}, u32[]{:S(2)}) collective-permute-start(bf16[80,768]{1,0:T(8,128)(2,1)S(1)} %get-tuple-element.17), channel_id=1, source_target_pairs={{4,0},{8,4},{12,8},{16,12},{20,16},{24,20},{28,24},{5,1},{9,5},{13... | collective-permute-start | bytes 368648 | tf_op jit(solution)/shard_map/ppermute | solution.py:446
  28.6 17.8 %collective-permute-start = (bf16[288,768]{1,0:T(8,128)(2,1)S(1)}, bf16[288,768]{1,0:T(8,128)(2,1)S(1)}, u32[]{:S(2)}, u32[]{:S(2)}) collective-permute-start(bf16[288,768]{1,0:T(8,128)(2,1)S(1)} %get-tuple-element.13.refs_0_), channel_id=1, source_target_pairs={{0,4},{4,0},{1,5},{5,1},{2,6},{6,2},{3,7},{7,3},{8,12},{12,8},{9,1... | collective-permute-start | bytes 1327112 | tf_op jit(solution)/shard_map/ppermute | solution.py:441
  30.5 5.9 %collective-permute-start.6 = (bf16[144,768]{1,0:T(8,128)(2,1)S(1)}, bf16[144,768]{1,0:T(8,128)(2,1)S(1)}, u32[]{:S(2)}, u32[]{:S(2)}) collective-permute-start(bf16[144,768]{1,0:T(8,128)(2,1)S(1)} %collective-permute-done.3.refs_4_), channel_id=1, source_target_pairs={{0,4},{4,0},{1,5},{5,1},{2,6},{6,2},{3,7},{7,3},{8,12},{12,8},{9,1... | collective-permute-start | bytes 663560 | tf_op jit(solution)/shard_map/ppermute | solution.py:441
  34.3 8.3 %collective-permute-start.8 = (bf16[144,768]{1,0:T(8,128)(2,1)S(1)}, bf16[144,768]{1,0:T(8,128)(2,1)S(1)}, u32[]{:S(2)}, u32[]{:S(2)}) collective-permute-start(bf16[144,768]{1,0:T(8,128)(2,1)S(1)} %collective-permute-done.2.refs_3_), channel_id=1, source_target_pairs={{0,1},{1,0},{2,3},{3,2},{4,5},{5,4},{6,7},{7,6},{8,9},{9,8},{10,11... | collective-permute-start | bytes 663560 | tf_op jit(solution)/shard_map/ppermute | solution.py:484
  34.7 7.9 %collective-permute-start.5 = (bf16[144,768]{1,0:T(8,128)(2,1)S(1)}, bf16[144,768]{1,0:T(8,128)(2,1)S(1)}, u32[]{:S(2)}, u32[]{:S(2)}) collective-permute-start(bf16[144,768]{1,0:T(8,128)(2,1)S(1)} %collective-permute-done.2.refs_3_), channel_id=1, source_target_pairs={{0,4},{4,0},{1,5},{5,1},{2,6},{6,2},{3,7},{7,3},{8,12},{12,8},{9,1... | collective-permute-start | bytes 663560 | tf_op jit(solution)/shard_map/ppermute | solution.py:441
  34.7 11.6 %collective-permute-start.7 = (bf16[144,768]{1,0:T(8,128)(2,1)S(1)}, bf16[144,768]{1,0:T(8,128)(2,1)S(1)}, u32[]{:S(2)}, u32[]{:S(2)}) collective-permute-start(bf16[144,768]{1,0:T(8,128)(2,1)S(1)} %collective-permute-done.1.refs_2_), channel_id=1, source_target_pairs={{0,1},{1,0},{2,3},{3,2},{4,5},{5,4},{6,7},{7,6},{8,9},{9,8},{10,11... | collective-permute-start | bytes 663560 | tf_op jit(solution)/shard_map/ppermute | solution.py:484
  36.4 10.0 %collective-permute-start.4 = (bf16[144,768]{1,0:T(8,128)(2,1)S(1)}, bf16[144,768]{1,0:T(8,128)(2,1)S(1)}, u32[]{:S(2)}, u32[]{:S(2)}) collective-permute-start(bf16[144,768]{1,0:T(8,128)(2,1)S(1)} %collective-permute-done.1.refs_2_), channel_id=1, source_target_pairs={{0,4},{4,0},{1,5},{5,1},{2,6},{6,2},{3,7},{7,3},{8,12},{12,8},{9,1... | collective-permute-start | bytes 663560 | tf_op jit(solution)/shard_map/ppermute | solution.py:441
  42.6 3.8 %collective-permute-start.12 = (bf16[144,768]{1,0:T(8,128)(2,1)S(1)}, bf16[144,768]{1,0:T(8,128)(2,1)S(1)}, u32[]{:S(2)}, u32[]{:S(2)}) collective-permute-start(bf16[144,768]{1,0:T(8,128)(2,1)S(1)} %collective-permute-done.9.refs_10_), channel_id=1, source_target_pairs={{0,4},{4,0},{1,5},{5,1},{2,6},{6,2},{3,7},{7,3},{8,12},{12,8},{9,1... | collective-permute-start | bytes 663560 | tf_op jit(solution)/shard_map/ppermute | solution.py:441
  42.6 3.8 %collective-permute-start.11 = (bf16[144,768]{1,0:T(8,128)(2,1)S(1)}, bf16[144,768]{1,0:T(8,128)(2,1)S(1)}, u32[]{:S(2)}, u32[]{:S(2)}) collective-permute-start(bf16[144,768]{1,0:T(8,128)(2,1)S(1)} %collective-permute-done.8.refs_9_), channel_id=1, source_target_pairs={{0,4},{4,0},{1,5},{5,1},{2,6},{6,2},{3,7},{7,3},{8,12},{12,8},{9,1... | collective-permute-start | bytes 663560 | tf_op jit(solution)/shard_map/ppermute | solution.py:441
  46.3 1.5 %collective-permute-start.10 = (bf16[144,768]{1,0:T(8,128)(2,1)S(1)}, bf16[144,768]{1,0:T(8,128)(2,1)S(1)}, u32[]{:S(2)}, u32[]{:S(2)}) collective-permute-start(bf16[144,768]{1,0:T(8,128)(2,1)S(1)} %collective-permute-done.7.refs_8_), channel_id=1, source_target_pairs={{0,4},{4,0},{1,5},{5,1},{2,6},{6,2},{3,7},{7,3},{8,12},{12,8},{9,1... | collective-permute-start | bytes 663560 | tf_op jit(solution)/shard_map/ppermute | solution.py:441
  55.4 2.0 %collective-permute-start.17 = (bf16[4,96,768]{2,1,0:T(8,128)(2,1)S(1)}, bf16[4,96,768]{2,1,0:T(8,128)(2,1)S(1)}, u32[]{:S(2)}, u32[]{:S(2)}) collective-permute-start(bf16[4,96,768]{2,1,0:T(8,128)(2,1)S(1)} %get-tuple-element.21), channel_id=1, source_target_pairs={{0,4},{4,0},{1,5},{5,1},{2,6},{6,2},{3,7},{7,3},{8,12},{12,8},{9,1... | collective-permute-start | bytes 1769480 | tf_op jit(solution)/shard_map/ppermute | solution.py:441

commit v4 on v3

--- a/solution.py
+++ b/solution.py
@@ -89,7 +89,7 @@
 
 def prep_kernel(
     where_ref, narrow_ref, broad_ref, small_ref,
-    own_ref, half_ref, r1_ref, r2_ref, l1_ref, l2_ref,
+    own_ref, x_ref, y_ref, d_ref,
 ):
     me, count = where_ref[0], where_ref[2]
     width = narrow_ref.shape[1]
@@ -123,14 +123,16 @@
     own_ref[half : half + 16, 0:width] = flat[cut:half]
     own_ref[half : half + 16, width:chans] = flat[half + cut : 2 * half]
     own_ref[half + 16 : half + 16 + 2 * prows] = broad_ref[0 : 2 * prows]
-    own_ref[2 * half - 32 :] = jnp.concatenate([wide, extra], axis=0).astype(BF16)
-    half_ref[...] = own_ref[pl.ds(pl.multiple_of((where_ref[1] & 1) * half, 16), half), :]
+    own_ref[2 * half - 32 : 2 * half] = jnp.concatenate([wide, extra], axis=0).astype(BF16)
+    part = own_ref[pl.ds(pl.multiple_of((where_ref[1] & 1) * half, 16), half), :]
+    for out in (x_ref, y_ref, d_ref):
+        out[0:half] = part
     take = (iota((HALO, cap), 1) == iota((HALO, cap), 0) + (count - HALO)).astype(BF16)
     last = mm(take, cot).astype(BF16)
-    r1_ref[...] = last
-    r2_ref[...] = last[HALO - SPILL :]
-    l1_ref[...] = cot[0:HALO]
-    l2_ref[...] = cot[0:SPILL]
+    chip = me >> 1
+    own_ref[2 * half :] = jnp.where((me & 1) == 0, last, cot[0:HALO])
+    x_ref[half:] = jnp.where((chip ^ 1) > chip, last, cot[0:HALO])
+    d_ref[half:] = jnp.where((chip ^ 3) > chip, last, cot[0:HALO])
 
 
 def table_body(
@@ -303,12 +305,11 @@
 
 def tower_kernel_packed(where_ref, *refs):
     own_parts, plane_parts, dp_parts = refs[0:2], refs[2:8], refs[8:14]
-    broad_ref, small_ref, r1_ref, r2_ref, l1_ref, l2_ref = refs[14:20]
-    sal_ref, keep_ref, send_ref = refs[20:23]
-    tables = refs[23:30]
-    conv_ref, p1_ref, p2_ref, info_ref, first_ref, second_ref, all_ref = refs[30:]
+    broad_ref, small_ref, sal_ref, keep_ref, send_ref = refs[14:19]
+    tables = refs[19:26]
+    conv_ref, p1_ref, p2_ref, info_ref, first_ref, second_ref, halo_ref, all_ref = refs[26:]
     me, count = where_ref[0], where_ref[2]
-    core, odd = me & 1, where_ref[1] & 1
+    chip, core, odd = me >> 1, me & 1, where_ref[1] & 1
     chans = broad_ref.shape[1]
     width = chans // 2
     shard = chans // 8
@@ -363,6 +364,14 @@
                     rows = lambda a, size, part=part: part[a : a + size]
                     place(side, rows, peer, side == parity)
 
+    for n in range(2):
+        halo_ref[4 * n + chip] = own_parts[n][2 * half :]
+        halo_ref[4 * n + (chip ^ 1)] = plane_parts[3 * n][half:]
+        halo_ref[4 * n + (chip ^ 3)] = plane_parts[3 * n + 2][half:]
+    r1 = halo_ref[4 + jnp.maximum(chip + core - 1, 0)]
+    l1 = halo_ref[4 + jnp.minimum(chip + core, 3)]
+    r2 = halo_ref[jnp.maximum(chip - 1, 0)]
+    l2 = halo_ref[jnp.minimum(chip + 1, 3)]
     first = first_ref[0]
     wide = second_ref[0]
     for peer in range(1, 8):
@@ -371,7 +380,7 @@
     emb = small_ref[0:4]
     table_body(
         first, p1_ref[...], lambda o: info_ref[me + (REACH + o)], broad_ref[2 * prow :],
-        r1_ref[...], r2_ref[...], l1_ref[...], l2_ref[...], emb, *tables,
+        r1, r2[HALO - SPILL :], l1, l2[0:SPILL], emb, *tables,
     )
     second = jnp.concatenate([wide[:, 0:width], wide[:, width : 2 * width]], axis=0)
 
@@ -409,24 +418,32 @@
     return jnp.concatenate([value[:, 0:width], value[:, width:]], axis=0)
 
 
-def core_sum_kernel(where_ref, keep_ref, recv_ref, mine_ref, out_ref, sum_ref):
+def core_sum_kernel(where_ref, keep_ref, recv_ref, own_ref, *outs):
+    chip = where_ref[0] >> 1
+    own_ref[...] = keep_ref[chip] + recv_ref[chip].astype(F32)
+    for n, out in enumerate(outs):
+        at = chip ^ (n + 1)
+        out[...] = (keep_ref[at] + recv_ref[at].astype(F32)).astype(BF16)
+
+
+def plane_sum_kernel(where_ref, own_ref, x_ref, y_ref, d_ref, mine_ref, *refs):
+    outs, sum_ref = refs[:-1], refs[-1]
+    sum_ref[...] = (
+        own_ref[...] + x_ref[...].astype(F32) + y_ref[...].astype(F32) + d_ref[...].astype(F32)
+    )
+    z = where_ref[1]
     rows = mine_ref.shape[0] // 2
-    per = keep_ref.shape[1] // rows
-    for c in range(keep_ref.shape[0]):
-        total = keep_ref[c] + recv_ref[c].astype(F32)
-        sum_ref[c] = total
-        for n in range(per):
-            out_ref[per * c + n] = fold(total[n * rows : (n + 1) * rows]).astype(BF16)
-    chip = where_ref[0] >> 1
-    at = pl.ds(pl.multiple_of(where_ref[1] * rows, 8), rows)
-    mine_ref[...] = fold(sum_ref[chip, at, :])
-
-
-def last_sum_kernel(scale, where_ref, mine_ref, got_ref, out_ref):
+    mine_ref[...] = fold(sum_ref[pl.ds(pl.multiple_of(z * rows, 8), rows), :])
+    for n, out in enumerate(outs):
+        at = pl.multiple_of((z ^ (n + 1)) * rows, 8)
+        out[...] = fold(sum_ref[pl.ds(at, rows), :]).astype(BF16)
+
+
+def last_sum_kernel(scale, mine_ref, *refs):
+    out_ref = refs[-1]
     total = mine_ref[...]
-    me = (where_ref[0] >> 1) * (got_ref.shape[0] // 4) + where_ref[1]
-    for c in range(got_ref.shape[0]):
-        total = total + jnp.where(me == c, 0.0, got_ref[c].astype(F32))
+    for ref in refs[:-1]:
+        total = total + ref[...].astype(F32)
     total = total * scale
     rows, half = total.shape[0] // 2, total.shape[1] // 128
     for n in range(2 * half):
@@ -441,7 +458,11 @@
     return lax.ppermute(array, axes, [(i, size - 1 - i) for i in range(size)])
 
 
-def shift_move(array, by, axes=("y", "x", "core")):
+def xor_move(array, axis, bits):
+    return lax.ppermute(array, axis, [(i, i ^ bits) for i in range(lax.axis_size(axis))])
+
+
+def shift_move(array, by, axes):
     size = math.prod(lax.axis_size(a) for a in axes)
     return lax.ppermute(array, axes, [(i, i + by) for i in range(size) if 0 <= i + by < size])
 
@@ -474,15 +495,18 @@
     small = jnp.concatenate(
         [embed, jnp.pad(bases.astype(F32), ((0, 3), (0, chans - cap)))], axis=0
     )
-    own, part, r1, r2, l1, l2 = call(
+    own, to_x, to_y, to_d = call(
         prep_kernel,
-        [((r, chans), BF16) for r in (2 * half, half, HALO, SPILL, HALO, SPILL)],
+        [
+            ((2 * half + HALO, chans), BF16),
+            ((half + HALO, chans), BF16),
+            ((half, chans), BF16),
+            ((half + HALO, chans), BF16),
+        ],
         [where, narrow, broad, small],
     )
-    plane = [flip_move(part, *axes) for axes in (("x",), ("y",), ("y", "x"))]
-    pairs = [(i, i ^ 1) for i in range(n_dp)]
-    other = [lax.ppermute(a, "dp", pairs) for a in plane]
-    halos = [shift_move(r1, 1), shift_move(r2, 2), shift_move(l1, -1), shift_move(l2, -2)]
+    plane = [flip_move(to_x, "x"), flip_move(to_y, "y"), flip_move(to_d, "y", "x")]
+    other = [xor_move(a[:half], "dp", 1) for a in plane]
     across = lambda arrays: [flip_move(a, "core") for a in arrays]
     rows = chans // 8
     sal, keep, send = call(
@@ -490,7 +514,7 @@
         [((4, cap), F32), ((4, rows, chans), F32), ((4, rows, chans), BF16)],
         [
             where, own, *across([own]), *plane, *across(plane), *other, *across(other),
-            broad, small, *halos,
+            broad, small,
         ],
         scratch=[pltpu.VMEM(s, d) for s, d in table_shapes(cap, chans, width)]
         + [
@@ -500,24 +524,31 @@
             pltpu.VMEM((8 + 2 * REACH, 8, 256), F32),
             pltpu.VMEM((8, 16, width), F32),
             pltpu.VMEM((8, 24, chans), F32),
+            pltpu.VMEM((8, HALO, chans), BF16),
             pltpu.VMEM((8, rows, chans), F32),
         ],
         limit=40,
     )
     recv = flip_move(send, "core")
+    own, *outs = call(
+        core_sum_kernel,
+        [((rows, chans), F32)] + [((rows, chans), BF16)] * 3,
+        [where, keep, recv],
+    )
+    got = [flip_move(a, *axes) for a, axes in zip(outs, (("x",), ("y",), ("y", "x")))]
     part = rows // n_dp
-    mine, out = call(
-        core_sum_kernel,
-        [((2 * part, width), F32), ((4 * n_dp, 2 * part, width), BF16)],
-        [where, keep, recv],
-        scratch=[pltpu.VMEM((4, rows, chans), F32)],
-    )
-    got = lax.all_to_all(out, ("y", "x", "dp"), 0, 0)
+    mine, *outs = call(
+        plane_sum_kernel,
+        [((2 * part, width), F32)] + [((2 * part, width), BF16)] * (n_dp - 1),
+        [where, own, *got],
+        scratch=[pltpu.VMEM((rows, chans), F32)],
+    )
+    got = [xor_move(a, "dp", n + 1) for n, a in enumerate(outs)]
     scale = 1.0 / math.sqrt(8 * n_dp * cap)
     (grad,) = call(
         functools.partial(last_sum_kernel, scale),
         [((part * chans // 128, 128), F32)],
-        [where, mine, got],
+        [mine, *got],
     )
     return sal[None], grad.reshape(-1)
 

time: 83.7 us -> 65.9 us (0.79)
  blocking collectives: 23.9 us -> 0 us
  waiting for transfers between devices: 22.1 us -> 30.9 us
  starting transfers between devices: 21.8 us -> 19.3 us
    all_to_all x1 -> x0, blocking collectives: 23.9 us -> none  [fast_shards(): got = lax.all_to_all(out, ('y', 'x', 'dp'), 0, 0)]
    ppermute x11 -> x14, waiting for transfers between devices: 8.99 us -> 21.2 us  [flip_move(): return lax.ppermute(array, axes, [(i, size - 1 - i) for i in range(size)])]
    ppermute x7 -> x6, waiting for transfers between devices: 13.2 us -> 9.68 us  [xor_move(): lax.ppermute(array, axis, [(i, i ^ bits) for i in range(lax.axis_size(axi...]
    ppermute x7 -> x6, starting transfers between devices: 11.4 us -> 9.89 us  [xor_move(): lax.ppermute(array, axis, [(i, i ^ bits) for i in range(lax.axis_size(axi...]
    ppermute x11 -> x14, starting transfers between devices: 10.4 us -> 9.39 us  [flip_move(): return lax.ppermute(array, axes, [(i, size - 1 - i) for i in range(size)])]
    pallas_call x4 -> x5, Pallas kernels: 10.6 us -> 10.5 us  [call(): pl.pallas_call(body, out_shape=[jax.ShapeDtypeStruct(s, d) for s, d in ou...]
  transfers between devices with their start and end apart: 18 -> 20, of which waited for: 8 -> 11; matrix products, arithmetic and copies ran while one was open for 0% -> 0% of each run, Pallas kernels for 0% -> 0%
where the time goes in v4:
time: 65.9 us; the launch traced here: 65.6 us
  waiting for transfers between devices  30.9 us (47%)
  starting transfers between devices  19.3 us (29%)
  Pallas kernels  10.5 us (16%)
  other arithmetic  3.58 us (5%)
  between operations  1.34 us (2%)
    ppermute x14, waiting for transfers between devices, flip_move(): return lax.ppermute(array, axes, [(i, size - 1 - i) for i in range(size)])  21.2 us
    pallas_call x5, Pallas kernels, call(): pl.pallas_call(body, out_shape=[jax.ShapeDtypeStruct(s, d) for s, d in ou...  10.5 us
    ppermute x6, starting transfers between devices, xor_move(): lax.ppermute(array, axis, [(i, i ^ bits) for i in range(lax.axis_size(axi...  9.89 us
    ppermute x6, waiting for transfers between devices, xor_move(): lax.ppermute(array, axis, [(i, i ^ bits) for i in range(lax.axis_size(axi...  9.68 us
    ppermute x14, starting transfers between devices, flip_move(): return lax.ppermute(array, axes, [(i, size - 1 - i) for i in range(size)])  9.39 us
  transfers between devices with their start and end apart: 20, of which 11 were waited for; matrix products, arithmetic and copies ran while one was open for 0% of the time, Pallas kernels for 0%

profile of v4, /device:TPU:0, one launch (start us, length us, event | category | flops | bytes accessed | tf_op | source)
XLA Modules:
  0.0 65.6 jit_solution(9720873012140224279)
XLA Ops:
  1.3 0.7 %convert_element_type.5 = f32[1,128]{1,0:T(1,128)S(1)} convert(s32[1,128]{1,0:T(1,128)} %param.8) | non-fusion elementwise | flops 128 | bytes 1024 | tf_op jit(solution)/shard_map/convert_element_type | solution.py:496
  1.9 0.7 %select_maximum_fusion.small_ref.refs_15_ = f32[8,768]{1,0:T(8,128)S(1)} fusion(f32[1,128]{1,0:T(1,128)S(1)} %convert_element_type.5, f32[4,768]{1,0:T(4,128)} %param.15), kind=kLoop, calls=%fused_computation.2 | loop fusion | flops 18432 | bytes 37376 | tf_op jit(solution)/shard_map/concatenate | solution.py:495
  2.7 1.1 %pad_maximum_fusion.narrow_ref = bf16[576,384]{1,0:T(8,128)(2,1)S(1)} fusion(bf16[288,384]{1,0:T(8,128)(2,1)} %bitcast.9, bf16[288,384]{1,0:T(8,128)(2,1)} %bitcast.10), kind=kLoop, calls=%fused_computation | loop fusion | flops 884736 | bytes 884736 | tf_op jit(solution)/shard_map/concatenate | solution.py:493
  3.7 0.1 pad_add_fusion.where_ref
  3.8 1.0 %pad_maximum_fusion.1.broad_ref.refs_14_ = bf16[224,768]{1,0:T(8,128)(2,1)S(1)} fusion(bf16[128,768]{1,0:T(8,128)(2,1)} %bitcast.11, bf16[48,768]{1,0:T(8,128)(2,1)} %param.12, bf16[48,768]{1,0:T(8,128)(2,1)} %param.14), kind=kLoop, calls=%fused_computation.1 | loop fusion | flops 1032192 | bytes 688128 | tf_op jit(solution)/shard_map/concatenate | solution.py:494
  4.9 1.0 %shard_map.95 = (bf16[368,768]{1,0:T(8,128)(2,1)S(1)}, bf16[224,768]{1,0:T(8,128)(2,1)S(1)}, bf16[144,768]{1,0:T(8,128)(2,1)S(1)}, bf16[224,768]{1,0:T(8,128)(2,1)S(1)}) custom-call(s32[3]{0:T(128)S(1)} %pad_add_fusion.where_ref, bf16[576,384]{1,0:T(8,128)(2,1)S(1)} %pad_maximum_fusion.narrow_ref, bf16[224,768]{1,0:T(8,128)(2,1)S(1)} %pad_maximum_fusion.1.broad_ref.refs_14_, ...), custom_call_target="tpu_custom_call" | custom-call | tf_op jit(solution)/shard_map/pallas_call | solution.py:62
  5.8 3.0 %collective-permute-start.1 = (bf16[224,768]{1,0:T(8,128)(2,1)S(1)}, bf16[224,768]{1,0:T(8,128)(2,1)S(1)}, u32[]{:S(2)}, u32[]{:S(2)}) collective-permute-start(bf16[224,768]{1,0:T(8,128)(2,1)S(1)} %get-tuple-element.18), channel_id=1, source_target_pairs={{0,8},{8,0},{1,9},{9,1},{2,10},{10,2},{3,11},{11,3},{4,12},{12,4},... | collective-permute-start | bytes 1032200 | tf_op jit(solution)/shard_map/ppermute | solution.py:458
  8.8 1.5 %collective-permute-start.2 = (bf16[144,768]{1,0:T(8,128)(2,1)S(1)}, bf16[144,768]{1,0:T(8,128)(2,1)S(1)}, u32[]{:S(2)}, u32[]{:S(2)}) collective-permute-start(bf16[144,768]{1,0:T(8,128)(2,1)S(1)} %get-tuple-element.19), channel_id=1, source_target_pairs={{0,16},{16,0},{1,17},{17,1},{2,18},{18,2},{3,19},{19,3},{4,20},{20... | collective-permute-start | bytes 663560 | tf_op jit(solution)/shard_map/ppermute | solution.py:458
  10.4 0.0 collective-permute-start.3
  10.4 0.0 collective-permute-start
  10.4 5.3 %collective-permute-done.2.refs_3_ = bf16[144,768]{1,0:T(8,128)(2,1)S(1)} collective-permute-done((bf16[144,768]{1,0:T(8,128)(2,1)S(1)}, bf16[144,768]{1,0:T(8,128)(2,1)S(1)}, u32[]{:S(2)}, u32[]{:S(2)}) %collective-permute-start.2) | collective-permute-done | bytes 221216 | tf_op jit(solution)/shard_map/ppermute | solution.py:458
  15.7 1.6 %collective-permute-start.8 = (bf16[144,768]{1,0:T(8,128)(2,1)S(1)}, bf16[144,768]{1,0:T(8,128)(2,1)S(1)}, u32[]{:S(2)}, u32[]{:S(2)}) collective-permute-start(bf16[144,768]{1,0:T(8,128)(2,1)S(1)} %collective-permute-done.2.refs_3_), channel_id=1, source_target_pairs={{0,1},{1,0},{2,3},{3,2},{4,5},{5,4},{6,7},{7,6},{8,9},{9,8},{10,11... | collective-permute-start | bytes 663560 | tf_op jit(solution)/shard_map/ppermute | solution.py:462
  17.3 0.0 collective-permute-start.5
  17.3 0.4 collective-permute-done.1.refs_2_
  17.8 2.2 %collective-permute-start.7 = (bf16[144,768]{1,0:T(8,128)(2,1)S(1)}, bf16[144,768]{1,0:T(8,128)(2,1)S(1)}, u32[]{:S(2)}, u32[]{:S(2)}) collective-permute-start(bf16[144,768]{1,0:T(8,128)(2,1)S(1)} %slice.8), channel_id=1, source_target_pairs={{0,1},{1,0},{2,3},{3,2},{4,5},{5,4},{6,7},{7,6},{8,9},{9,8},{10,11... | collective-permute-start | bytes 663560 | tf_op jit(solution)/shard_map/ppermute | solution.py:462
  20.0 5.5 %collective-permute-done.3.refs_4_ = bf16[224,768]{1,0:T(8,128)(2,1)S(1)} collective-permute-done((bf16[224,768]{1,0:T(8,128)(2,1)S(1)}, bf16[224,768]{1,0:T(8,128)(2,1)S(1)}, u32[]{:S(2)}, u32[]{:S(2)}) %collective-permute-start.3) | collective-permute-done | bytes 344096 | tf_op jit(solution)/shard_map/ppermute | solution.py:458
  25.5 1.6 %collective-permute-start.9 = (bf16[144,768]{1,0:T(8,128)(2,1)S(1)}, bf16[144,768]{1,0:T(8,128)(2,1)S(1)}, u32[]{:S(2)}, u32[]{:S(2)}) collective-permute-start(bf16[144,768]{1,0:T(8,128)(2,1)S(1)} %slice.9), channel_id=1, source_target_pairs={{0,1},{1,0},{2,3},{3,2},{4,5},{5,4},{6,7},{7,6},{8,9},{9,8},{10,11... | collective-permute-start | bytes 663560 | tf_op jit(solution)/shard_map/ppermute | solution.py:462
  27.2 0.0 collective-permute-done.8.refs_9_
  27.2 0.0 collective-permute-start.4
  27.2 0.0 collective-permute-done.5.refs_6_
  27.2 0.5 collective-permute-start.6
  27.7 0.0 collective-permute-done.7.refs_8_
  27.7 0.1 collective-permute-start.11
  27.7 4.1 %collective-permute-done.9.refs_10_ = bf16[144,768]{1,0:T(8,128)(2,1)S(1)} collective-permute-done((bf16[144,768]{1,0:T(8,128)(2,1)S(1)}, bf16[144,768]{1,0:T(8,128)(2,1)S(1)}, u32[]{:S(2)}, u32[]{:S(2)}) %collective-permute-start.9) | collective-permute-done | bytes 221216 | tf_op jit(solution)/shard_map/ppermute | solution.py:462
  31.9 0.0 collective-permute-start.10
  31.9 0.0 collective-permute-done.refs_1_
  31.9 0.5 collective-permute-start.12
  32.4 0.0 collective-permute-done.11.refs_12_
  32.4 0.0 collective-permute-done.4.refs_5_
  32.4 0.0 collective-permute-done.6.refs_7_
  32.4 1.0 %collective-permute-done.10.refs_11_ = bf16[144,768]{1,0:T(8,128)(2,1)S(1)} collective-permute-done((bf16[144,768]{1,0:T(8,128)(2,1)S(1)}, bf16[144,768]{1,0:T(8,128)(2,1)S(1)}, u32[]{:S(2)}, u32[]{:S(2)}) %collective-permute-start.10) | collective-permute-done | bytes 221216 | tf_op jit(solution)/shard_map/ppermute | solution.py:458
  33.3 0.3 collective-permute-done.12.refs_13_
  33.7 7.6 %shard_map.96 = (f32[4,128]{1,0:T(4,128)}, f32[4,96,768]{2,1,0:T(8,128)S(1)}, bf16[4,96,768]{2,1,0:T(8,128)(2,1)S(1)}) custom-call(s32[3]{0:T(128)S(1)} %pad_add_fusion.where_ref, bf16[368,768]{1,0:T(8,128)(2,1)S(1)} %get-tuple-element.17.refs_0_, bf16[368,768]{1,0:T(8,128)(2,1)S(1)} %collective-permute-done.refs_1_, ...), custom_call_target="tpu_custom_call" | custom-call | tf_op jit(solution)/shard_map/pallas_call | solution.py:62
  41.2 0.2 collective-permute-start.13
  41.5 1.8 %collective-permute-done.13.recv_ref = bf16[4,96,768]{2,1,0:T(8,128)(2,1)S(1)} collective-permute-done((bf16[4,96,768]{2,1,0:T(8,128)(2,1)S(1)}, bf16[4,96,768]{2,1,0:T(8,128)(2,1)S(1)}, u32[]{:S(2)}, u32[]{:S(2)}) %collective-permute-start.13) | collective-permute-done | bytes 589856 | tf_op jit(solution)/shard_map/ppermute | solution.py:458
  43.3 0.7 %shard_map.97 = (f32[96,768]{1,0:T(8,128)S(1)}, bf16[96,768]{1,0:T(8,128)(2,1)S(1)}, bf16[96,768]{1,0:T(8,128)(2,1)S(1)}, bf16[96,768]{1,0:T(8,128)(2,1)S(1)}) custom-call(s32[3]{0:T(128)S(1)} %pad_add_fusion.where_ref, f32[4,96,768]{2,1,0:T(8,128)S(1)} %get-tuple-element.22.keep_ref, bf16[4,96,768]{2,1,0:T(8,128)(2,1)S(1)} %collective-permute-done.13.recv_ref), custom_call_target="tpu_custom_call" | custom-call | tf_op jit(solution)/shard_map/pallas_call | solution.py:62
  43.9 1.6 %collective-permute-start.14 = (bf16[96,768]{1,0:T(8,128)(2,1)S(1)}, bf16[96,768]{1,0:T(8,128)(2,1)S(1)}, u32[]{:S(2)}, u32[]{:S(2)}) collective-permute-start(bf16[96,768]{1,0:T(8,128)(2,1)S(1)} %get-tuple-element.25), channel_id=1, source_target_pairs={{0,8},{8,0},{1,9},{9,1},{2,10},{10,2},{3,11},{11,3},{4,12},{12,4},... | collective-permute-start | bytes 442376 | tf_op jit(solution)/shard_map/ppermute | solution.py:458
  45.5 0.5 collective-permute-start.15
  46.0 1.5 %collective-permute-start.16 = (bf16[96,768]{1,0:T(8,128)(2,1)S(1)}, bf16[96,768]{1,0:T(8,128)(2,1)S(1)}, u32[]{:S(2)}, u32[]{:S(2)}) collective-permute-start(bf16[96,768]{1,0:T(8,128)(2,1)S(1)} %get-tuple-element.27), channel_id=1, source_target_pairs={{0,24},{8,16},{16,8},{24,0},{1,25},{9,17},{17,9},{25,1},{2,26},{10... | collective-permute-start | bytes 442376 | tf_op jit(solution)/shard_map/ppermute | solution.py:458
  47.5 3.2 %collective-permute-done.14.x_ref = bf16[96,768]{1,0:T(8,128)(2,1)S(1)} collective-permute-done((bf16[96,768]{1,0:T(8,128)(2,1)S(1)}, bf16[96,768]{1,0:T(8,128)(2,1)S(1)}, u32[]{:S(2)}, u32[]{:S(2)}) %collective-permute-start.14) | collective-permute-done | bytes 147488 | tf_op jit(solution)/shard_map/ppermute | solution.py:458
  50.7 3.6 %collective-permute-done.15.y_ref = bf16[96,768]{1,0:T(8,128)(2,1)S(1)} collective-permute-done((bf16[96,768]{1,0:T(8,128)(2,1)S(1)}, bf16[96,768]{1,0:T(8,128)(2,1)S(1)}, u32[]{:S(2)}, u32[]{:S(2)}) %collective-permute-start.15) | collective-permute-done | bytes 147488 | tf_op jit(solution)/shard_map/ppermute | solution.py:458
  54.3 0.6 shard_map.98
  55.0 1.7 %collective-permute-start.17 = (bf16[48,384]{1,0:T(8,128)(2,1)S(1)}, bf16[48,384]{1,0:T(8,128)(2,1)S(1)}, u32[]{:S(2)}, u32[]{:S(2)}) collective-permute-start(bf16[48,384]{1,0:T(8,128)(2,1)S(1)} %get-tuple-element.29), channel_id=1, source_target_pairs={{0,1},{1,0},{2,3},{3,2},{4,5},{5,4},{6,7},{7,6},{8,9},{9,8},{10,11... | collective-permute-start | bytes 110600 | tf_op jit(solution)/shard_map/ppermute | solution.py:462
  56.6 2.6 %collective-permute-start.18 = (bf16[48,384]{1,0:T(8,128)(2,1)S(1)}, bf16[48,384]{1,0:T(8,128)(2,1)S(1)}, u32[]{:S(2)}, u32[]{:S(2)}) collective-permute-start(bf16[48,384]{1,0:T(8,128)(2,1)S(1)} %get-tuple-element.30), channel_id=1, source_target_pairs={{0,2},{1,3},{2,0},{3,1},{4,6},{5,7},{6,4},{7,5},{8,10},{9,11},{10,... | collective-permute-start | bytes 110600 | tf_op jit(solution)/shard_map/ppermute | solution.py:462
  59.2 0.2 collective-permute-start.19
  59.4 2.8 %collective-permute-done.18.refs_1_ = bf16[48,384]{1,0:T(8,128)(2,1)S(1)} collective-permute-done((bf16[48,384]{1,0:T(8,128)(2,1)S(1)}, bf16[48,384]{1,0:T(8,128)(2,1)S(1)}, u32[]{:S(2)}, u32[]{:S(2)}) %collective-permute-start.18) | collective-permute-done | bytes 36896 | tf_op jit(solution)/shard_map/ppermute | solution.py:462
  62.2 2.8 %collective-permute-done.19.refs_2_ = bf16[48,384]{1,0:T(8,128)(2,1)S(1)} collective-permute-done((bf16[48,384]{1,0:T(8,128)(2,1)S(1)}, bf16[48,384]{1,0:T(8,128)(2,1)S(1)}, u32[]{:S(2)}, u32[]{:S(2)}) %collective-permute-start.19) | collective-permute-done | bytes 36896 | tf_op jit(solution)/shard_map/ppermute | solution.py:462
  65.0 0.7 shard_map.99
  (4 shorter events, 0.0 us)
Async XLA Ops:
  5.8 11.9 %collective-permute-start.1 = (bf16[224,768]{1,0:T(8,128)(2,1)S(1)}, bf16[224,768]{1,0:T(8,128)(2,1)S(1)}, u32[]{:S(2)}, u32[]{:S(2)}) collective-permute-start(bf16[224,768]{1,0:T(8,128)(2,1)S(1)} %get-tuple-element.18), channel_id=1, source_target_pairs={{0,8},{8,0},{1,9},{9,1},{2,10},{10,2},{3,11},{11,3},{4,12},{12,4},... | collective-permute-start | bytes 1032200 | tf_op jit(solution)/shard_map/ppermute | solution.py:458
  8.8 6.9 %collective-permute-start.2 = (bf16[144,768]{1,0:T(8,128)(2,1)S(1)}, bf16[144,768]{1,0:T(8,128)(2,1)S(1)}, u32[]{:S(2)}, u32[]{:S(2)}) collective-permute-start(bf16[144,768]{1,0:T(8,128)(2,1)S(1)} %get-tuple-element.19), channel_id=1, source_target_pairs={{0,16},{16,0},{1,17},{17,1},{2,18},{18,2},{3,19},{19,3},{4,20},{20... | collective-permute-start | bytes 663560 | tf_op jit(solution)/shard_map/ppermute | solution.py:458
  10.4 15.1 %collective-permute-start.3 = (bf16[224,768]{1,0:T(8,128)(2,1)S(1)}, bf16[224,768]{1,0:T(8,128)(2,1)S(1)}, u32[]{:S(2)}, u32[]{:S(2)}) collective-permute-start(bf16[224,768]{1,0:T(8,128)(2,1)S(1)} %get-tuple-element.20), channel_id=1, source_target_pairs={{0,24},{8,16},{16,8},{24,0},{1,25},{9,17},{17,9},{25,1},{2,26},{10... | collective-permute-start | bytes 1032200 | tf_op jit(solution)/shard_map/ppermute | solution.py:458
  10.4 21.5 %collective-permute-start = (bf16[368,768]{1,0:T(8,128)(2,1)S(1)}, bf16[368,768]{1,0:T(8,128)(2,1)S(1)}, u32[]{:S(2)}, u32[]{:S(2)}) collective-permute-start(bf16[368,768]{1,0:T(8,128)(2,1)S(1)} %get-tuple-element.17.refs_0_), channel_id=1, source_target_pairs={{0,4},{4,0},{1,5},{5,1},{2,6},{6,2},{3,7},{7,3},{8,12},{12,8},{9,1... | collective-permute-start | bytes 1695752 | tf_op jit(solution)/shard_map/ppermute | solution.py:458
  15.7 11.4 %collective-permute-start.8 = (bf16[144,768]{1,0:T(8,128)(2,1)S(1)}, bf16[144,768]{1,0:T(8,128)(2,1)S(1)}, u32[]{:S(2)}, u32[]{:S(2)}) collective-permute-start(bf16[144,768]{1,0:T(8,128)(2,1)S(1)} %collective-permute-done.2.refs_3_), channel_id=1, source_target_pairs={{0,1},{1,0},{2,3},{3,2},{4,5},{5,4},{6,7},{7,6},{8,9},{9,8},{10,11... | collective-permute-start | bytes 663560 | tf_op jit(solution)/shard_map/ppermute | solution.py:462
  17.3 9.8 %collective-permute-start.5 = (bf16[144,768]{1,0:T(8,128)(2,1)S(1)}, bf16[144,768]{1,0:T(8,128)(2,1)S(1)}, u32[]{:S(2)}, u32[]{:S(2)}) collective-permute-start(bf16[144,768]{1,0:T(8,128)(2,1)S(1)} %collective-permute-done.2.refs_3_), channel_id=1, source_target_pairs={{0,4},{4,0},{1,5},{5,1},{2,6},{6,2},{3,7},{7,3},{8,12},{12,8},{9,1... | collective-permute-start | bytes 663560 | tf_op jit(solution)/shard_map/ppermute | solution.py:458
  17.8 9.9 %collective-permute-start.7 = (bf16[144,768]{1,0:T(8,128)(2,1)S(1)}, bf16[144,768]{1,0:T(8,128)(2,1)S(1)}, u32[]{:S(2)}, u32[]{:S(2)}) collective-permute-start(bf16[144,768]{1,0:T(8,128)(2,1)S(1)} %slice.8), channel_id=1, source_target_pairs={{0,1},{1,0},{2,3},{3,2},{4,5},{5,4},{6,7},{7,6},{8,9},{9,8},{10,11... | collective-permute-start | bytes 663560 | tf_op jit(solution)/shard_map/ppermute | solution.py:462
  25.5 6.4 %collective-permute-start.9 = (bf16[144,768]{1,0:T(8,128)(2,1)S(1)}, bf16[144,768]{1,0:T(8,128)(2,1)S(1)}, u32[]{:S(2)}, u32[]{:S(2)}) collective-permute-start(bf16[144,768]{1,0:T(8,128)(2,1)S(1)} %slice.9), channel_id=1, source_target_pairs={{0,1},{1,0},{2,3},{3,2},{4,5},{5,4},{6,7},{7,6},{8,9},{9,8},{10,11... | collective-permute-start | bytes 663560 | tf_op jit(solution)/shard_map/ppermute | solution.py:462
  27.2 5.2 %collective-permute-start.4 = (bf16[224,768]{1,0:T(8,128)(2,1)S(1)}, bf16[224,768]{1,0:T(8,128)(2,1)S(1)}, u32[]{:S(2)}, u32[]{:S(2)}) collective-permute-start(bf16[224,768]{1,0:T(8,128)(2,1)S(1)} %collective-permute-done.1.refs_2_), channel_id=1, source_target_pairs={{0,4},{4,0},{1,5},{5,1},{2,6},{6,2},{3,7},{7,3},{8,12},{12,8},{9,1... | collective-permute-start | bytes 1032200 | tf_op jit(solution)/shard_map/ppermute | solution.py:458
  27.2 5.2 %collective-permute-start.6 = (bf16[224,768]{1,0:T(8,128)(2,1)S(1)}, bf16[224,768]{1,0:T(8,128)(2,1)S(1)}, u32[]{:S(2)}, u32[]{:S(2)}) collective-permute-start(bf16[224,768]{1,0:T(8,128)(2,1)S(1)} %collective-permute-done.3.refs_4_), channel_id=1, source_target_pairs={{0,4},{4,0},{1,5},{5,1},{2,6},{6,2},{3,7},{7,3},{8,12},{12,8},{9,1... | collective-permute-start | bytes 1032200 | tf_op jit(solution)/shard_map/ppermute | solution.py:458
  27.7 4.7 %collective-permute-start.11 = (bf16[144,768]{1,0:T(8,128)(2,1)S(1)}, bf16[144,768]{1,0:T(8,128)(2,1)S(1)}, u32[]{:S(2)}, u32[]{:S(2)}) collective-permute-start(bf16[144,768]{1,0:T(8,128)(2,1)S(1)} %collective-permute-done.8.refs_9_), channel_id=1, source_target_pairs={{0,4},{4,0},{1,5},{5,1},{2,6},{6,2},{3,7},{7,3},{8,12},{12,8},{9,1... | collective-permute-start | bytes 663560 | tf_op jit(solution)/shard_map/ppermute | solution.py:458
  31.9 1.5 %collective-permute-start.10 = (bf16[144,768]{1,0:T(8,128)(2,1)S(1)}, bf16[144,768]{1,0:T(8,128)(2,1)S(1)}, u32[]{:S(2)}, u32[]{:S(2)}) collective-permute-start(bf16[144,768]{1,0:T(8,128)(2,1)S(1)} %collective-permute-done.7.refs_8_), channel_id=1, source_target_pairs={{0,4},{4,0},{1,5},{5,1},{2,6},{6,2},{3,7},{7,3},{8,12},{12,8},{9,1... | collective-permute-start | bytes 663560 | tf_op jit(solution)/shard_map/ppermute | solution.py:458
  31.9 1.8 %collective-permute-start.12 = (bf16[144,768]{1,0:T(8,128)(2,1)S(1)}, bf16[144,768]{1,0:T(8,128)(2,1)S(1)}, u32[]{:S(2)}, u32[]{:S(2)}) collective-permute-start(bf16[144,768]{1,0:T(8,128)(2,1)S(1)} %collective-permute-done.9.refs_10_), channel_id=1, source_target_pairs={{0,4},{4,0},{1,5},{5,1},{2,6},{6,2},{3,7},{7,3},{8,12},{12,8},{9,1... | collective-permute-start | bytes 663560 | tf_op jit(solution)/shard_map/ppermute | solution.py:458
  41.2 2.0 %collective-permute-start.13 = (bf16[4,96,768]{2,1,0:T(8,128)(2,1)S(1)}, bf16[4,96,768]{2,1,0:T(8,128)(2,1)S(1)}, u32[]{:S(2)}, u32[]{:S(2)}) collective-permute-start(bf16[4,96,768]{2,1,0:T(8,128)(2,1)S(1)} %get-tuple-element.23), channel_id=1, source_target_pairs={{0,4},{4,0},{1,5},{5,1},{2,6},{6,2},{3,7},{7,3},{8,12},{12,8},{9,1... | collective-permute-start | bytes 1769480 | tf_op jit(solution)/shard_map/ppermute | solution.py:458
  43.9 6.8 %collective-permute-start.14 = (bf16[96,768]{1,0:T(8,128)(2,1)S(1)}, bf16[96,768]{1,0:T(8,128)(2,1)S(1)}, u32[]{:S(2)}, u32[]{:S(2)}) collective-permute-start(bf16[96,768]{1,0:T(8,128)(2,1)S(1)} %get-tuple-element.25), channel_id=1, source_target_pairs={{0,8},{8,0},{1,9},{9,1},{2,10},{10,2},{3,11},{11,3},{4,12},{12,4},... | collective-permute-start | bytes 442376 | tf_op jit(solution)/shard_map/ppermute | solution.py:458
  45.5 8.8 %collective-permute-start.15 = (bf16[96,768]{1,0:T(8,128)(2,1)S(1)}, bf16[96,768]{1,0:T(8,128)(2,1)S(1)}, u32[]{:S(2)}, u32[]{:S(2)}) collective-permute-start(bf16[96,768]{1,0:T(8,128)(2,1)S(1)} %get-tuple-element.26), channel_id=1, source_target_pairs={{0,16},{16,0},{1,17},{17,1},{2,18},{18,2},{3,19},{19,3},{4,20},{20... | collective-permute-start | bytes 442376 | tf_op jit(solution)/shard_map/ppermute | solution.py:458
  46.0 8.3 %collective-permute-start.16 = (bf16[96,768]{1,0:T(8,128)(2,1)S(1)}, bf16[96,768]{1,0:T(8,128)(2,1)S(1)}, u32[]{:S(2)}, u32[]{:S(2)}) collective-permute-start(bf16[96,768]{1,0:T(8,128)(2,1)S(1)} %get-tuple-element.27), channel_id=1, source_target_pairs={{0,24},{8,16},{16,8},{24,0},{1,25},{9,17},{17,9},{25,1},{2,26},{10... | collective-permute-start | bytes 442376 | tf_op jit(solution)/shard_map/ppermute | solution.py:458
  55.0 4.5 %collective-permute-start.17 = (bf16[48,384]{1,0:T(8,128)(2,1)S(1)}, bf16[48,384]{1,0:T(8,128)(2,1)S(1)}, u32[]{:S(2)}, u32[]{:S(2)}) collective-permute-start(bf16[48,384]{1,0:T(8,128)(2,1)S(1)} %get-tuple-element.29), channel_id=1, source_target_pairs={{0,1},{1,0},{2,3},{3,2},{4,5},{5,4},{6,7},{7,6},{8,9},{9,8},{10,11... | collective-permute-start | bytes 110600 | tf_op jit(solution)/shard_map/ppermute | solution.py:462
  56.6 5.6 %collective-permute-start.18 = (bf16[48,384]{1,0:T(8,128)(2,1)S(1)}, bf16[48,384]{1,0:T(8,128)(2,1)S(1)}, u32[]{:S(2)}, u32[]{:S(2)}) collective-permute-start(bf16[48,384]{1,0:T(8,128)(2,1)S(1)} %get-tuple-element.30), channel_id=1, source_target_pairs={{0,2},{1,3},{2,0},{3,1},{4,6},{5,7},{6,4},{7,5},{8,10},{9,11},{10,... | collective-permute-start | bytes 110600 | tf_op jit(solution)/shard_map/ppermute | solution.py:462
  59.2 5.8 %collective-permute-start.19 = (bf16[48,384]{1,0:T(8,128)(2,1)S(1)}, bf16[48,384]{1,0:T(8,128)(2,1)S(1)}, u32[]{:S(2)}, u32[]{:S(2)}) collective-permute-start(bf16[48,384]{1,0:T(8,128)(2,1)S(1)} %get-tuple-element.31), channel_id=1, source_target_pairs={{0,3},{1,2},{2,1},{3,0},{4,7},{5,6},{6,5},{7,4},{8,11},{9,10},{10,... | collective-permute-start | bytes 110600 | tf_op jit(solution)/shard_map/ppermute | solution.py:462

commit v5 on v4

--- a/solution.py
+++ b/solution.py
@@ -135,10 +135,7 @@
     d_ref[half:] = jnp.where((chip ^ 3) > chip, last, cot[0:HALO])
 
 
-def table_body(
-    first, project, info_at, cot, r1, r2, l1, l2, emb,
-    b1_ref, s1_ref, a2_ref, s2_ref, hot_f_ref, hot_r_ref, cx_ref,
-):
+def context_body(info_at, cot, r1, r2, l1, l2, hot_f_ref, hot_r_ref, cx_ref):
     cap = cot.shape[0]
     outer = HALO + SECOND_DILATION + FIRST_DILATION
     span = cap + 2 * outer
@@ -166,6 +163,75 @@
     idx = jnp.where(mid == 0.0, -1.0, (4.0 - mid) * 25.0 + flip(right) * 5.0 + flip(left))
     hot_r_ref[...] = (lanes == idx).astype(BF16)
 
+    own_n = counts[REACH]
+    before_n, after_n = counts[REACH - 1], counts[REACH + 1]
+    grow = cap + 2 * HALO
+    lane_h = iota((1, HALO), 1).astype(F32)
+    lane_s = iota((1, SPILL), 1).astype(F32)
+    row_h = (iota((grow, HALO), 0) - HALO).astype(F32)
+    row_s = (iota((grow, SPILL), 0) - HALO).astype(F32)
+    row_o = (iota((grow, cap), 0) - HALO).astype(F32)
+    own_pos = jnp.where(lane < own_n, lane, FAR)
+    acc = mm((row_o == own_pos).astype(BF16), cot)
+    pos = jnp.where(lane_h >= HALO - before_n[:, 0:HALO], lane_h - HALO, FAR)
+    acc = acc + mm((row_h == pos).astype(BF16), r1)
+    pos = jnp.where(
+        counts[REACH - 2][:, 0:SPILL] > 0.0, lane_s - SPILL - before_n[:, 0:SPILL], FAR
+    )
+    acc = acc + mm((row_s == pos).astype(BF16), r2)
+    pos = jnp.where(lane_h < after_n[:, 0:HALO], lane_h + own_n[:, 0:HALO], FAR)
+    acc = acc + mm((row_h == pos).astype(BF16), l1)
+    pos = jnp.where(
+        (counts[REACH + 2][:, 0:SPILL] > 0.0) & (after_n[:, 0:SPILL] < HALO),
+        lane_s + own_n[:, 0:SPILL] + after_n[:, 0:SPILL],
+        FAR,
+    )
+    acc = acc + mm((row_s == pos).astype(BF16), l2)
+    cx_ref[...] = (0.5 * acc).astype(BF16)
+
+
+def context_kernel_plain(info_ref, cot_ref, r1_ref, r2_ref, l1_ref, l2_ref, *outs):
+    context_body(
+        lambda o: info_ref[REACH + o], cot_ref[...], r1_ref[...], r2_ref[...], l1_ref[...],
+        l2_ref[...], *outs,
+    )
+
+
+def context_kernel_packed(where_ref, *refs):
+    parts, broad_ref, outs = refs[0:8], refs[8], refs[9:12]
+    info_ref, halo_ref = refs[12:]
+    me, odd = where_ref[0], where_ref[1] & 1
+    chip, core = me >> 1, me & 1
+    chans = broad_ref.shape[1]
+    prow = chans // 16
+    half = 3 * chans // 16
+    info_ref[0:REACH] = jnp.zeros((REACH, 8, 256), F32)
+    info_ref[REACH + 8 :] = jnp.zeros((REACH, 8, 256), F32)
+    for n, part in enumerate(parts):
+        peer = me ^ (2 * (n % 4) + n // 4)
+        low = part[half - 16 : half].astype(F32)[12:13, 0:256]
+        if n % 4 > 0:
+            high = part[half - 16 : half].astype(F32)[8:9, 0:256]
+            low = jnp.where(odd == 0, low, high)
+        info_ref[REACH + peer] = jnp.broadcast_to(low, (8, 256))
+    for n in range(2):
+        halo_ref[4 * n + chip] = parts[4 * n][2 * half :]
+        halo_ref[4 * n + (chip ^ 1)] = parts[4 * n + 1][half:]
+        halo_ref[4 * n + (chip ^ 3)] = parts[4 * n + 3][half:]
+    r1 = halo_ref[4 + jnp.maximum(chip + core - 1, 0)]
+    l1 = halo_ref[4 + jnp.minimum(chip + core, 3)]
+    r2 = halo_ref[jnp.maximum(chip - 1, 0)]
+    l2 = halo_ref[jnp.minimum(chip + 1, 3)]
+    context_body(
+        lambda o: info_ref[me + (REACH + o)], broad_ref[2 * prow :], r1, r2[HALO - SPILL :], l1,
+        l2[0:SPILL], *outs,
+    )
+
+
+def tower_body(
+    first, project, conv, p2, count, emb, cap, cx_ref, hot_f_ref, hot_r_ref,
+    s1_ref, gb_ref, g_ref, put,
+):
     entry = iota((TABLE, 1), 0)
     by25 = (entry * 1311) >> 15
     by5 = (entry * 6554) >> 15
@@ -180,147 +246,115 @@
         after = jnp.where(in_right == q + 1, first[8 + q : 9 + q], after)
     value, slope = gelu_pair(sums + after)
     b1 = value.astype(BF16)
-    b1_ref[...] = b1
     high, low = split(slope)
     s1_ref[0:TABLE] = high
     s1_ref[TABLE : 2 * TABLE] = low
     stream = spread(emb, by25) + mm(b1, project)
     value, slope = gelu_pair(stream)
-    a2_ref[...] = value.astype(BF16)
-    high, low = split(slope)
-    s2_ref[0:TABLE] = high
-    s2_ref[TABLE : 2 * TABLE] = low
-
-    own_n = counts[REACH]
-    before_n, after_n = counts[REACH - 1], counts[REACH + 1]
-    grow = cap + 2 * HALO
-    lane_h = iota((1, HALO), 1).astype(F32)
-    lane_s = iota((1, SPILL), 1).astype(F32)
-    row_h = (iota((grow, HALO), 0) - HALO).astype(F32)
-    row_s = (iota((grow, SPILL), 0) - HALO).astype(F32)
-    row_o = (iota((grow, cap), 0) - HALO).astype(F32)
-    own_pos = jnp.where(lane < own_n, lane, FAR)
-    acc = mm((row_o == own_pos).astype(BF16), cot)
-    pos = jnp.where(lane_h >= HALO - before_n[:, 0:HALO], lane_h - HALO, FAR)
-    acc = acc + mm((row_h == pos).astype(BF16), r1)
-    pos = jnp.where(
-        counts[REACH - 2][:, 0:SPILL] > 0.0, lane_s - SPILL - before_n[:, 0:SPILL], FAR
-    )
-    acc = acc + mm((row_s == pos).astype(BF16), r2)
-    pos = jnp.where(lane_h < after_n[:, 0:HALO], lane_h + own_n[:, 0:HALO], FAR)
-    acc = acc + mm((row_h == pos).astype(BF16), l1)
-    pos = jnp.where(
-        (counts[REACH + 2][:, 0:SPILL] > 0.0) & (after_n[:, 0:SPILL] < HALO),
-        lane_s + own_n[:, 0:SPILL] + after_n[:, 0:SPILL],
-        FAR,
-    )
-    acc = acc + mm((row_s == pos).astype(BF16), l2)
-    cx_ref[...] = (0.5 * acc).astype(BF16)
-
-
-def table_kernel_plain(
-    first_ref, project_ref, info_ref, cot_ref, r1_ref, r2_ref, l1_ref, l2_ref, embed_ref, *outs
-):
-    table_body(
-        first_ref[...], project_ref[...], lambda o: info_ref[REACH + o], cot_ref[...], r1_ref[...],
-        r2_ref[...], l1_ref[...], l2_ref[...], embed_ref[...], *outs
-    )
-
-
-def tower_body(
-    conv, p2, second, p1, count, bases, cx_ref, b1_ref, s1_ref, a2_ref, s2_ref,
-    hot_f_ref, hot_r_ref, emb, sal_ref, put,
-):
-    cap = bases.shape[1]
+    a2 = value.astype(BF16)
+    s2 = jnp.concatenate(split(slope), axis=0)
+
     grow = cap + 2 * HALO
     inner = cap + 2 * FIRST_DILATION
     d, D = FIRST_DILATION, SECOND_DILATION
     cx = cx_ref[...]
-    a2 = a2_ref[...]
-    taps = []
+    back_mid = mm_nt(cx, p2)
+    before = jnp.zeros((2 * grow, p2.shape[0]), F32)
     for k in range(3):
-        high, low = split(mm(a2, conv(k)))
-        taps.append(jnp.concatenate([high, low], axis=0))
-    back_mid = mm_nt(cx, p2)
+        taps = jnp.concatenate(split(mm(a2, conv(k))), axis=0)
+        hot = jnp.concatenate(
+            [hot_f_ref[k * D : k * D + grow], hot_r_ref[(2 - k) * D : (2 - k) * D + grow]], axis=0
+        )
+        before = before + mm(jnp.concatenate([hot, hot], axis=1), taps)
+    value, slope = gelu_pair(before)
     own_col = (iota((cap, 1), 0) < count).astype(F32)
-    own_cx = cx[HALO : HALO + cap]
-    own_gb = (own_cx.astype(F32) * own_col).astype(BF16)
-    grads = []
-    mids = []
-    for hot_ref, order in ((hot_f_ref, (0, 1, 2)), (hot_r_ref, (2, 1, 0))):
-        before = jnp.zeros((grow, a2_ref.shape[1] // 2), F32)
-        for place in range(3):
-            hot = hot_ref[place * D : place * D + grow]
-            before = before + mm(jnp.concatenate([hot, hot], axis=1), taps[order[place]])
-        value, slope = gelu_pair(before)
-        mids.append(value[HALO : HALO + cap].astype(BF16))
-        grads.append((back_mid * slope).astype(BF16))
-    dproj2 = mm_tn(mids[0], own_gb) + mm_tn(mids[1], own_gb)
-    put(1, dproj2)
+    own_gb = (cx[HALO : HALO + cap].astype(F32) * own_col).astype(BF16)
+    mids = jnp.concatenate(
+        [value[HALO : HALO + cap], value[grow + HALO : grow + HALO + cap]], axis=0
+    ).astype(BF16)
+    put(1, mm_tn(mids, jnp.concatenate([own_gb, own_gb], axis=0)))
+    grad_f = (back_mid * slope[0:grow]).astype(BF16)
+    grad_r = (back_mid * slope[grow:]).astype(BF16)
+    ga = jnp.zeros((2 * inner, cx.shape[1]), F32)
+    for k in range(3):
+        rows = jnp.concatenate(
+            [grad_f[(2 - k) * D : (2 - k) * D + inner], grad_r[k * D : k * D + inner]], axis=0
+        )
+        ga = ga + mm_nt(rows, conv(k))
+    hot = jnp.concatenate(
+        [hot_f_ref[2 * D : 2 * D + inner], hot_r_ref[2 * D : 2 * D + inner]], axis=0
+    )
     base_g = cx[D : D + inner].astype(F32)
-    b1 = b1_ref[...]
-    s1 = s1_ref[...]
-    s2 = s2_ref[...]
-    sal = jnp.zeros((8, cap), F32)
-    emb8 = jnp.concatenate([emb, emb], axis=0)
-    flipped = jnp.concatenate(
-        [emb[3 - c : 4 - c] for c in range(4)] * 2, axis=0
-    )
-    sec_high, sec_low = split(second)
-    dproj1 = None
-    for pass_idx, (hot_ref, order) in enumerate(((hot_f_ref, (0, 1, 2)), (hot_r_ref, (2, 1, 0)))):
-        grad = grads[pass_idx]
-        ga = jnp.zeros((inner, cx.shape[1]), F32)
-        for place in range(3):
-            ga = ga + mm_nt(grad[place * D : place * D + inner], conv(order[2 - place]))
-        hot = hot_ref[2 * D : 2 * D + inner]
-        hot2 = jnp.concatenate([hot, hot], axis=1)
-        g = base_g + ga * mm(hot2, s2)
-        gb = g.astype(BF16)
-        own_hot = (hot[d : d + cap].astype(F32) * own_col).astype(BF16)
-        own_b1 = mm(own_hot, b1).astype(BF16)
-        piece = mm_tn(own_b1, gb[d : d + cap])
-        dproj1 = piece if dproj1 is None else dproj1 + piece
-        gh = (mm_nt(gb, p1) * mm(hot2, s1)).astype(BF16)
-        g_high, g_low = split(g[d : d + cap])
-        e_high, e_low = split(emb8 if pass_idx == 0 else flipped)
-        sal = sal + mm_nt(e_high, g_high) + mm_nt(e_high, g_low) + mm_nt(e_low, g_high)
+    g = jnp.concatenate([base_g, base_g], axis=0) + ga * mm(
+        jnp.concatenate([hot, hot], axis=1), s2
+    )
+    gb = g.astype(BF16)
+    gb_ref[...] = gb
+    g_ref[0:cap] = g[d : d + cap]
+    g_ref[cap : 2 * cap] = g[inner + d : inner + d + cap]
+    col = jnp.concatenate([own_col, own_col], axis=0)
+    own_hot = jnp.concatenate([hot[d : d + cap], hot[inner + d : inner + d + cap]], axis=0)
+    own_b1 = mm((own_hot.astype(F32) * col).astype(BF16), b1).astype(BF16)
+    own_g = jnp.concatenate([gb[d : d + cap], gb[inner + d : inner + d + cap]], axis=0)
+    put(0, mm_tn(own_b1, own_g))
+
+
+def saliency_kernel(
+    where_ref, small_ref, hot_f_ref, hot_r_ref, s1_ref, gb_ref, g_ref, second_ref, p1_ref, sal_ref
+):
+    count = where_ref[2]
+    cap = g_ref.shape[0] // 2
+    inner = cap + 2 * FIRST_DILATION
+    d, D = FIRST_DILATION, SECOND_DILATION
+    hot = jnp.concatenate(
+        [hot_f_ref[2 * D : 2 * D + inner], hot_r_ref[2 * D : 2 * D + inner]], axis=0
+    )
+    slope = mm(jnp.concatenate([hot, hot], axis=1), s1_ref[...])
+    gh = (mm_nt(gb_ref[...], p1_ref[...]) * slope).astype(BF16)
+    emb = small_ref[0:4]
+    bases = small_ref[4:5, 0:cap]
+    wide = jnp.concatenate(split(second_ref[...]), axis=0)
+    total = jnp.zeros((4, cap), F32)
+    e_high, e_low = split(jnp.concatenate([emb, emb], axis=0))
+    for turn in range(2):
+        g_high, g_low = split(g_ref[turn * cap : (turn + 1) * cap])
+        got = mm_nt(e_high, g_high) + mm_nt(e_high, g_low) + mm_nt(e_low, g_high)
+        got = got[0:4]
         table = jnp.zeros((16, cap), F32)
-        for place in range(3):
-            k = order[2 - place]
-            rows = gh[place * d : place * d + cap]
-            table = table + mm_nt(sec_high[16 * k : 16 * k + 16], rows)
-            table = table + mm_nt(sec_low[16 * k : 16 * k + 16], rows)
-        got = jnp.zeros((4, cap), F32)
+        for k in range(3):
+            place = 2 - k if turn == 0 else k
+            at = turn * inner + place * d
+            both = mm_nt(
+                jnp.concatenate(
+                    [wide[16 * k : 16 * k + 16], wide[48 + 16 * k : 64 + 16 * k]], axis=0
+                ),
+                gh[at : at + cap],
+            )
+            table = table + both[0:16] + both[16:32]
         for q in range(4):
-            match = bases == (q if pass_idx == 0 else 3 - q)
-            got = got + jnp.where(match, table[4 * q : 4 * q + 4], 0.0)
-        if pass_idx == 1:
+            code = float(q if turn == 0 else 3 - q)
+            got = got + jnp.where(bases == code, table[4 * q : 4 * q + 4], 0.0)
+        if turn == 1:
             got = jnp.concatenate([got[3 - c : 4 - c] for c in range(4)], axis=0)
-        sal = sal + jnp.concatenate([got, got], axis=0)
-    put(0, dproj1)
+        total = total + got
     live = iota((1, cap), 1) < count
-    sal_ref[...] = jnp.where(live, sal[0:4] * (1.0 / math.sqrt(cx.shape[1])), 0.0)
+    sal_ref[...] = jnp.where(live, total * (1.0 / math.sqrt(emb.shape[1])), 0.0)
 
 
 def tower_kernel_packed(where_ref, *refs):
     own_parts, plane_parts, dp_parts = refs[0:2], refs[2:8], refs[8:14]
-    broad_ref, small_ref, sal_ref, keep_ref, send_ref = refs[14:19]
-    tables = refs[19:26]
-    conv_ref, p1_ref, p2_ref, info_ref, first_ref, second_ref, halo_ref, all_ref = refs[26:]
+    small_ref, cx_ref, hf_ref, hr_ref = refs[14:18]
+    keep_ref, send_ref, s1_ref, gb_ref, g_ref, wide_ref, p1_ref = refs[18:25]
+    conv_ref, p2_ref, first_ref, second_ref = refs[25:]
     me, count = where_ref[0], where_ref[2]
-    chip, core, odd = me >> 1, me & 1, where_ref[1] & 1
-    chans = broad_ref.shape[1]
-    width = chans // 2
+    core, odd = me & 1, where_ref[1] & 1
+    width, chans = p1_ref.shape
     shard = chans // 8
     prow = width // 8
-    cap = broad_ref.shape[0] - 2 * prow
     half = 3 * shard // 2
     cut = half - 16
-    info_ref[0:REACH] = jnp.zeros((REACH, 8, 256), F32)
-    info_ref[REACH + 8 :] = jnp.zeros((REACH, 8, 256), F32)
-
-    def place(side, rows, peer, told):
+
+    def place(side, rows, peer):
         at = peer * shard
 
         def lay(k, start, size, source, lane):
@@ -335,25 +369,20 @@
             lay(2, 0, cut - shard // 2, shard // 2, width)
             tail = rows(cut, 16).astype(F32)
             first_ref[peer] = tail[:, 0:width] + tail[:, width:]
-            line = tail[12:13, 0:256]
         else:
             lay(1, cut - shard, 16, 0, 0)
             lay(2, shard - 16, 16, 0, width)
             to = pl.ds(pl.multiple_of(peer * prow, 16), prow)
             p2_ref[to, :] = rows(16, prow)
             p1_ref[to, :] = rows(16 + prow, prow)
-            tail = rows(half - 32, 32).astype(F32)
-            second_ref[peer] = tail[0:24]
-            line = tail[24:25, 0:256]
-        if told:
-            info_ref[REACH + peer] = jnp.broadcast_to(line, (8, 256))
+            second_ref[peer] = rows(half - 32, 32).astype(F32)[0:24]
 
     for n in range(2):
         for side in range(2):
             rows = lambda a, size, n=n, side=side: own_parts[n][
                 side * half + a : side * half + a + size
             ]
-            place(side, rows, me ^ n, side == 0)
+            place(side, rows, me ^ n)
     for parity in range(2):
 
         @pl.when(odd == parity)
@@ -362,54 +391,40 @@
                 peer = me ^ (2 * (n % 3 + 1) + n // 3)
                 for side, part in ((parity, plane_parts[n]), (1 - parity, dp_parts[n])):
                     rows = lambda a, size, part=part: part[a : a + size]
-                    place(side, rows, peer, side == parity)
-
-    for n in range(2):
-        halo_ref[4 * n + chip] = own_parts[n][2 * half :]
-        halo_ref[4 * n + (chip ^ 1)] = plane_parts[3 * n][half:]
-        halo_ref[4 * n + (chip ^ 3)] = plane_parts[3 * n + 2][half:]
-    r1 = halo_ref[4 + jnp.maximum(chip + core - 1, 0)]
-    l1 = halo_ref[4 + jnp.minimum(chip + core, 3)]
-    r2 = halo_ref[jnp.maximum(chip - 1, 0)]
-    l2 = halo_ref[jnp.minimum(chip + 1, 3)]
+                    place(side, rows, peer)
+
     first = first_ref[0]
     wide = second_ref[0]
     for peer in range(1, 8):
         first = first + first_ref[peer]
         wide = wide + second_ref[peer]
-    emb = small_ref[0:4]
-    table_body(
-        first, p1_ref[...], lambda o: info_ref[me + (REACH + o)], broad_ref[2 * prow :],
-        r1, r2[HALO - SPILL :], l1, l2[0:SPILL], emb, *tables,
-    )
-    second = jnp.concatenate([wide[:, 0:width], wide[:, width : 2 * width]], axis=0)
+    wide_ref[...] = jnp.concatenate([wide[:, 0:width], wide[:, width : 2 * width]], axis=0)
 
     def put(block, value):
         rows = value.shape[0] // 4
-        for c in range(4):
-            peer = 4 * block + c
-            all_ref[((core ^ (peer & 1)) << 2) + (peer >> 1)] = value[c * rows : (c + 1) * rows]
-
-    b1, s1, a2, s2, hf, hr, cx = tables
+        for c in range(2):
+            even = value[2 * c * rows : (2 * c + 1) * rows]
+            uneven = value[(2 * c + 1) * rows : (2 * c + 2) * rows]
+            keep_ref[2 * block + c] = jnp.where(core == 0, even, uneven)
+            send_ref[2 * block + c] = jnp.where(core == 0, uneven, even).astype(BF16)
+
     tower_body(
-        lambda k: conv_ref[k], p2_ref[...], second, p1_ref[...], count, small_ref[4:5, 0:cap],
-        cx, b1, s1, a2, s2, hf, hr, emb, sal_ref, put,
-    )
-    keep_ref[...] = all_ref[0:4]
-    send_ref[...] = all_ref[4:8].astype(BF16)
+        first, p1_ref[...], lambda k: conv_ref[k], p2_ref[...], count, small_ref[0:4],
+        g_ref.shape[0] // 2, cx_ref, hf_ref, hr_ref, s1_ref, gb_ref, g_ref, put,
+    )
 
 
 def tower_kernel_plain(
-    where_ref, conv_ref, p2_ref, second_ref, p1_ref, bases_ref, cx_ref, b1_ref, s1_ref,
-    a2_ref, s2_ref, hf, hr, emb, sal_ref, grad_ref,
+    where_ref, first_ref, p1_ref, conv_ref, p2_ref, small_ref, cx_ref, hf_ref, hr_ref,
+    grad_ref, s1_ref, gb_ref, g_ref,
 ):
     def put(block, value):
         rows = value.shape[0]
         grad_ref[block * rows : (block + 1) * rows] = value
 
     tower_body(
-        lambda k: conv_ref[k], p2_ref[...], second_ref[...], p1_ref[...], where_ref[2],
-        bases_ref[...], cx_ref, b1_ref, s1_ref, a2_ref, s2_ref, hf, hr, emb[...], sal_ref, put,
+        first_ref[...], p1_ref[...], lambda k: conv_ref[k], p2_ref[...], where_ref[2],
+        small_ref[0:4], g_ref.shape[0] // 2, cx_ref, hf_ref, hr_ref, s1_ref, gb_ref, g_ref, put,
     )
 
 
@@ -467,17 +482,24 @@
     return lax.ppermute(array, axes, [(i, i + by) for i in range(size) if 0 <= i + by < size])
 
 
-def table_shapes(cap, chans, width):
+def context_shapes(cap, chans):
     rows = cap + 2 * (HALO + SECOND_DILATION)
-    return [
-        ((TABLE, width), BF16),
-        ((2 * TABLE, width), BF16),
-        ((TABLE, chans), BF16),
-        ((2 * TABLE, chans), BF16),
-        ((rows, TABLE), BF16),
-        ((rows, TABLE), BF16),
-        ((cap + 2 * HALO, chans), BF16),
-    ]
+    return [((rows, TABLE), BF16), ((rows, TABLE), BF16), ((cap + 2 * HALO, chans), BF16)]
+
+
+def pass_shapes(cap, chans, width):
+    inner = cap + 2 * FIRST_DILATION
+    return [((2 * TABLE, width), BF16), ((2 * inner, chans), BF16), ((2 * cap, chans), F32)]
+
+
+def lines(embed, bases):
+    cap, chans = bases.shape[1], embed.shape[1]
+    extra = jnp.pad(bases.astype(F32), ((0, 3), (0, chans - cap)))
+    return jnp.concatenate([embed, extra], axis=0)
+
+
+def weight(flops):
+    return pl.CostEstimate(flops=flops, bytes_accessed=10**6, transcendentals=0)
 
 
 def fast_shards(
@@ -492,9 +514,7 @@
     half = 3 * c2.shape[1] // 2
     narrow = jnp.concatenate([c1.reshape(-1, width), c2.reshape(-1, width)], axis=0)
     broad = jnp.concatenate([p2, p1, cot], axis=0)
-    small = jnp.concatenate(
-        [embed, jnp.pad(bases.astype(F32), ((0, 3), (0, chans - cap)))], axis=0
-    )
+    small = lines(embed, bases)
     own, to_x, to_y, to_d = call(
         prep_kernel,
         [
@@ -509,27 +529,41 @@
     other = [xor_move(a[:half], "dp", 1) for a in plane]
     across = lambda arrays: [flip_move(a, "core") for a in arrays]
     rows = chans // 8
-    sal, keep, send = call(
+    swapped = across([own, *plane])
+    hf, hr, cx = call(
+        context_kernel_packed,
+        context_shapes(cap, chans),
+        [where, own, *plane, *swapped, broad],
+        scratch=[
+            pltpu.VMEM((8 + 2 * REACH, 8, 256), F32),
+            pltpu.VMEM((8, HALO, chans), BF16),
+        ],
+        cost=weight(10**9),
+    )
+    keep, send, s1, gb, g, second, p1_full = call(
         tower_kernel_packed,
-        [((4, cap), F32), ((4, rows, chans), F32), ((4, rows, chans), BF16)],
+        [((4, rows, chans), F32), ((4, rows, chans), BF16), *pass_shapes(cap, chans, width)]
+        + [((48, width), F32), ((width, chans), BF16)],
         [
-            where, own, *across([own]), *plane, *across(plane), *other, *across(other),
-            broad, small,
+            where, own, swapped[0], *plane, *swapped[1:], *other, *across(other),
+            small, cx, hf, hr,
         ],
-        scratch=[pltpu.VMEM(s, d) for s, d in table_shapes(cap, chans, width)]
-        + [
+        scratch=[
             pltpu.VMEM((3, chans, width), BF16),
             pltpu.VMEM((width, chans), BF16),
-            pltpu.VMEM((width, chans), BF16),
-            pltpu.VMEM((8 + 2 * REACH, 8, 256), F32),
             pltpu.VMEM((8, 16, width), F32),
             pltpu.VMEM((8, 24, chans), F32),
-            pltpu.VMEM((8, HALO, chans), BF16),
-            pltpu.VMEM((8, rows, chans), F32),
         ],
         limit=40,
+        cost=weight(4 * 10**9),
     )
     recv = flip_move(send, "core")
+    (sal,) = call(
+        saliency_kernel,
+        [((4, cap), F32)],
+        [where, small, hf, hr, s1, gb, g, second, p1_full],
+        cost=weight(10**9),
+    )
     own, *outs = call(
         core_sum_kernel,
         [((rows, chans), F32)] + [((rows, chans), BF16)] * 3,
@@ -593,16 +627,20 @@
         shift_move(cot[:HALO], -1, ("seq",)),
         shift_move(cot[:SPILL], -2, ("seq",)),
     ]
-    b1, s1, a2, s2, hf, hr, cx = call(
-        table_kernel_plain,
-        table_shapes(cap, chans, width),
-        [first, p1_full, info, cot, *halos, embed],
-    )
-    sal, grad = call(
+    small = lines(embed, bases)
+    hf, hr, cx = call(
+        context_kernel_plain, context_shapes(cap, chans), [info, cot, *halos]
+    )
+    grad, s1, gb, g = call(
         tower_kernel_plain,
-        [((4, cap), F32), ((2 * width, chans), F32)],
-        [where, conv, p2_full, second, p1_full, bases, cx, b1, s1, a2, s2, hf, hr, embed],
+        [((2 * width, chans), F32), *pass_shapes(cap, chans, width)],
+        [where, first, p1_full, conv, p2_full, small, cx, hf, hr],
         limit=40,
+    )
+    (sal,) = call(
+        saliency_kernel,
+        [((4, cap), F32)],
+        [where, small, hf, hr, s1, gb, g, second, p1_full],
     )
     scale = 1.0 / math.sqrt(lax.axis_size("seq") * lax.axis_size("dp") * cap)
     grad = lax.psum_scatter(

time: 65.9 us -> 62.8 us (0.953)
  waiting for transfers between devices: 30.9 us -> 27.7 us
    ppermute x6, waiting for transfers between devices: 9.68 us -> 7.37 us  [xor_move(): lax.ppermute(array, axis, [(i, i ^ bits) for i in range(lax.axis_size(axi...]
    ppermute x14, waiting for transfers between devices: 21.2 us -> 20.3 us  [flip_move(): return lax.ppermute(array, axes, [(i, size - 1 - i) for i in range(size)])]
    pallas_call x5 -> x7, Pallas kernels: 10.5 us -> 10.9 us  [call(): pl.pallas_call(body, out_shape=[jax.ShapeDtypeStruct(s, d) for s, d in ou...]
  transfers between devices with their start and end apart: 20 -> 20, of which waited for: 11 -> 9; matrix products, arithmetic and copies ran while one was open for 0% -> 0% of each run, Pallas kernels for 0% -> 6%
where the time goes in v5:
time: 62.8 us; the launch traced here: 62.5 us
  waiting for transfers between devices  27.7 us (44%)
  starting transfers between devices  19 us (30%)
  Pallas kernels  10.9 us (17%)
  other arithmetic  3.58 us (6%)
  between operations  1.37 us (2%)
    ppermute x14, waiting for transfers between devices, flip_move(): return lax.ppermute(array, axes, [(i, size - 1 - i) for i in range(size)])  20.3 us
    pallas_call x7, Pallas kernels, call(): pl.pallas_call(body, out_shape=[jax.ShapeDtypeStruct(s, d) for s, d in ou...  10.9 us
    ppermute x6, starting transfers between devices, xor_move(): lax.ppermute(array, axis, [(i, i ^ bits) for i in range(lax.axis_size(axi...  9.69 us
    ppermute x14, starting transfers between devices, flip_move(): return lax.ppermute(array, axes, [(i, size - 1 - i) for i in range(size)])  9.3 us
    ppermute x6, waiting for transfers between devices, xor_move(): lax.ppermute(array, axis, [(i, i ^ bits) for i in range(lax.axis_size(axi...  7.37 us
  transfers between devices with their start and end apart: 20, of which 9 were waited for; matrix products, arithmetic and copies ran while one was open for 0% of the time, Pallas kernels for 6%

profile of v5, /device:TPU:0, one launch (start us, length us, event | category | flops | bytes accessed | tf_op | source)
XLA Modules:
  0.0 62.5 jit_solution(12048380006657042688)
XLA Ops:
  1.3 0.7 %convert_element_type.5 = f32[1,128]{1,0:T(1,128)S(1)} convert(s32[1,128]{1,0:T(1,128)} %param.8) | non-fusion elementwise | flops 128 | bytes 1024 | tf_op jit(solution)/shard_map/convert_element_type | solution.py:497
  1.9 0.7 %select_maximum_fusion.small_ref.refs_14_ = f32[8,768]{1,0:T(8,128)S(1)} fusion(f32[1,128]{1,0:T(1,128)S(1)} %convert_element_type.5, f32[4,768]{1,0:T(4,128)} %param.15), kind=kLoop, calls=%fused_computation.2 | loop fusion | flops 18432 | bytes 37376 | tf_op jit(solution)/shard_map/concatenate | solution.py:498
  2.7 1.1 %pad_maximum_fusion.narrow_ref = bf16[576,384]{1,0:T(8,128)(2,1)S(1)} fusion(bf16[288,384]{1,0:T(8,128)(2,1)} %bitcast.9, bf16[288,384]{1,0:T(8,128)(2,1)} %bitcast.10), kind=kLoop, calls=%fused_computation | loop fusion | flops 884736 | bytes 884736 | tf_op jit(solution)/shard_map/concatenate | solution.py:515
  3.7 0.1 pad_add_fusion.where_ref
  3.8 1.0 %pad_maximum_fusion.1.broad_ref.refs_8_ = bf16[224,768]{1,0:T(8,128)(2,1)S(1)} fusion(bf16[128,768]{1,0:T(8,128)(2,1)} %bitcast.11, bf16[48,768]{1,0:T(8,128)(2,1)} %param.12, bf16[48,768]{1,0:T(8,128)(2,1)} %param.14), kind=kLoop, calls=%fused_computation.1 | loop fusion | flops 1032192 | bytes 688128 | tf_op jit(solution)/shard_map/concatenate | solution.py:516
  4.9 1.0 %shard_map.95 = (bf16[368,768]{1,0:T(8,128)(2,1)S(1)}, bf16[224,768]{1,0:T(8,128)(2,1)S(1)}, bf16[144,768]{1,0:T(8,128)(2,1)S(1)}, bf16[224,768]{1,0:T(8,128)(2,1)S(1)}) custom-call(s32[3]{0:T(128)S(1)} %pad_add_fusion.where_ref, bf16[576,384]{1,0:T(8,128)(2,1)S(1)} %pad_maximum_fusion.narrow_ref, bf16[224,768]{1,0:T(8,128)(2,1)S(1)} %pad_maximum_fusion.1.broad_ref.refs_8_, ...), custom_call_target="tpu_custom_call" | custom-call | tf_op jit(solution)/shard_map/pallas_call | solution.py:62
  5.8 3.0 %collective-permute-start.1 = (bf16[144,768]{1,0:T(8,128)(2,1)S(1)}, bf16[144,768]{1,0:T(8,128)(2,1)S(1)}, u32[]{:S(2)}, u32[]{:S(2)}) collective-permute-start(bf16[144,768]{1,0:T(8,128)(2,1)S(1)} %get-tuple-element.26), channel_id=1, source_target_pairs={{0,16},{16,0},{1,17},{17,1},{2,18},{18,2},{3,19},{19,3},{4,20},{20... | collective-permute-start | bytes 663560 | tf_op jit(solution)/shard_map/ppermute | solution.py:473
  8.9 1.5 %collective-permute-start = (bf16[224,768]{1,0:T(8,128)(2,1)S(1)}, bf16[224,768]{1,0:T(8,128)(2,1)S(1)}, u32[]{:S(2)}, u32[]{:S(2)}) collective-permute-start(bf16[224,768]{1,0:T(8,128)(2,1)S(1)} %get-tuple-element.25), channel_id=1, source_target_pairs={{0,8},{8,0},{1,9},{9,1},{2,10},{10,2},{3,11},{11,3},{4,12},{12,4},... | collective-permute-start | bytes 1032200 | tf_op jit(solution)/shard_map/ppermute | solution.py:473
  10.4 0.1 collective-permute-start.2
  10.4 0.0 collective-permute-start.3
  10.4 3.9 %collective-permute-done.1.refs_2_.refs_3_ = bf16[144,768]{1,0:T(8,128)(2,1)S(1)} collective-permute-done((bf16[144,768]{1,0:T(8,128)(2,1)S(1)}, bf16[144,768]{1,0:T(8,128)(2,1)S(1)}, u32[]{:S(2)}, u32[]{:S(2)}) %collective-permute-start.1) | collective-permute-done | bytes 221216 | tf_op jit(solution)/shard_map/ppermute | solution.py:473
  14.3 1.8 %collective-permute-start.8 = (bf16[144,768]{1,0:T(8,128)(2,1)S(1)}, bf16[144,768]{1,0:T(8,128)(2,1)S(1)}, u32[]{:S(2)}, u32[]{:S(2)}) collective-permute-start(bf16[144,768]{1,0:T(8,128)(2,1)S(1)} %collective-permute-done.1.refs_2_.refs_3_), channel_id=1, source_target_pairs={{0,1},{1,0},{2,3},{3,2},{4,5},{5,4},{6,7},{7,6},{8,9},{9,8},{10,11... | collective-permute-start | bytes 663560 | tf_op jit(solution)/shard_map/ppermute | solution.py:477
  16.1 0.0 collective-permute-start.5
  16.1 3.8 %collective-permute-done.refs_1_.refs_2_ = bf16[224,768]{1,0:T(8,128)(2,1)S(1)} collective-permute-done((bf16[224,768]{1,0:T(8,128)(2,1)S(1)}, bf16[224,768]{1,0:T(8,128)(2,1)S(1)}, u32[]{:S(2)}, u32[]{:S(2)}) %collective-permute-start) | collective-permute-done | bytes 344096 | tf_op jit(solution)/shard_map/ppermute | solution.py:473
  19.9 1.7 %collective-permute-start.7 = (bf16[144,768]{1,0:T(8,128)(2,1)S(1)}, bf16[144,768]{1,0:T(8,128)(2,1)S(1)}, u32[]{:S(2)}, u32[]{:S(2)}) collective-permute-start(bf16[144,768]{1,0:T(8,128)(2,1)S(1)} %slice.8), channel_id=1, source_target_pairs={{0,1},{1,0},{2,3},{3,2},{4,5},{5,4},{6,7},{7,6},{8,9},{9,8},{10,11... | collective-permute-start | bytes 663560 | tf_op jit(solution)/shard_map/ppermute | solution.py:477
  21.5 4.0 %collective-permute-done.2.refs_3_.refs_4_ = bf16[224,768]{1,0:T(8,128)(2,1)S(1)} collective-permute-done((bf16[224,768]{1,0:T(8,128)(2,1)S(1)}, bf16[224,768]{1,0:T(8,128)(2,1)S(1)}, u32[]{:S(2)}, u32[]{:S(2)}) %collective-permute-start.2) | collective-permute-done | bytes 344096 | tf_op jit(solution)/shard_map/ppermute | solution.py:473
  25.6 1.8 %collective-permute-start.9 = (bf16[144,768]{1,0:T(8,128)(2,1)S(1)}, bf16[144,768]{1,0:T(8,128)(2,1)S(1)}, u32[]{:S(2)}, u32[]{:S(2)}) collective-permute-start(bf16[144,768]{1,0:T(8,128)(2,1)S(1)} %slice.9), channel_id=1, source_target_pairs={{0,1},{1,0},{2,3},{3,2},{4,5},{5,4},{6,7},{7,6},{8,9},{9,8},{10,11... | collective-permute-start | bytes 663560 | tf_op jit(solution)/shard_map/ppermute | solution.py:477
  27.4 0.0 collective-permute-done.8.refs_9_
  27.4 0.0 collective-permute-start.4
  27.4 0.0 collective-permute-done.5.refs_6_
  27.4 0.5 collective-permute-start.6
  27.9 0.0 collective-permute-done.7.refs_8_
  27.9 0.1 collective-permute-start.11
  27.9 4.0 %collective-permute-done.9.refs_10_ = bf16[144,768]{1,0:T(8,128)(2,1)S(1)} collective-permute-done((bf16[144,768]{1,0:T(8,128)(2,1)S(1)}, bf16[144,768]{1,0:T(8,128)(2,1)S(1)}, u32[]{:S(2)}, u32[]{:S(2)}) %collective-permute-start.9) | collective-permute-done | bytes 221216 | tf_op jit(solution)/shard_map/ppermute | solution.py:477
  31.9 0.0 collective-permute-start.10
  31.9 0.0 collective-permute-done.3.refs_4_.refs_1_
  31.9 0.5 collective-permute-start.12
  32.4 0.0 collective-permute-done.4.refs_5_
  32.4 0.0 collective-permute-done.6.refs_7_
  32.4 1.4 %shard_map.96 = (bf16[416,128]{1,0:T(8,128)(2,1)S(1)}, bf16[416,128]{1,0:T(8,128)(2,1)S(1)}, bf16[288,768]{1,0:T(8,128)(2,1)S(1)}) custom-call(s32[3]{0:T(128)S(1)} %pad_add_fusion.where_ref, bf16[368,768]{1,0:T(8,128)(2,1)S(1)} %get-tuple-element.24.refs_0_, bf16[224,768]{1,0:T(8,128)(2,1)S(1)} %collective-permute-done.refs_1_.refs_2_, ...), custom_call_target="tpu_custom_call" | custom-call | flops 1000000000 | bytes 1000000 | tf_op jit(solution)/shard_map/pallas_call | solution.py:62
  33.9 0.0 collective-permute-done.11.refs_12_
  33.9 4.4 %shard_map.97 = (f32[4,96,768]{2,1,0:T(8,128)S(1)}, bf16[4,96,768]{2,1,0:T(8,128)(2,1)S(1)}, bf16[256,384]{1,0:T(8,128)(2,1)S(1)}, bf16[320,768]{1,0:T(8,128)(2,...) custom-call(s32[3]{0:T(128)S(1)} %pad_add_fusion.where_ref, ...), custom_call_target="tpu_custom_call" | custom-call | flops 4000000000 | bytes 1000000 | tf_op jit(solution)/shard_map/pallas_call | solution.py:62
  38.3 0.1 collective-permute-start.13
  38.4 2.0 %collective-permute-done.13.recv_ref = bf16[4,96,768]{2,1,0:T(8,128)(2,1)S(1)} collective-permute-done((bf16[4,96,768]{2,1,0:T(8,128)(2,1)S(1)}, bf16[4,96,768]{2,1,0:T(8,128)(2,1)S(1)}, u32[]{:S(2)}, u32[]{:S(2)}) %collective-permute-start.13) | collective-permute-done | bytes 589856 | tf_op jit(solution)/shard_map/ppermute | solution.py:473
  40.4 0.7 %shard_map.99 = (f32[96,768]{1,0:T(8,128)S(1)}, bf16[96,768]{1,0:T(8,128)(2,1)S(1)}, bf16[96,768]{1,0:T(8,128)(2,1)S(1)}, bf16[96,768]{1,0:T(8,128)(2,1)S(1)}) custom-call(s32[3]{0:T(128)S(1)} %pad_add_fusion.where_ref, f32[4,96,768]{2,1,0:T(8,128)S(1)} %get-tuple-element.36.keep_ref, bf16[4,96,768]{2,1,0:T(8,128)(2,1)S(1)} %collective-permute-done.13.recv_ref), custom_call_target="tpu_custom_call" | custom-call | tf_op jit(solution)/shard_map/pallas_call | solution.py:62
  41.1 1.4 %collective-permute-start.14 = (bf16[96,768]{1,0:T(8,128)(2,1)S(1)}, bf16[96,768]{1,0:T(8,128)(2,1)S(1)}, u32[]{:S(2)}, u32[]{:S(2)}) collective-permute-start(bf16[96,768]{1,0:T(8,128)(2,1)S(1)} %get-tuple-element.39), channel_id=1, source_target_pairs={{0,8},{8,0},{1,9},{9,1},{2,10},{10,2},{3,11},{11,3},{4,12},{12,4},... | collective-permute-start | bytes 442376 | tf_op jit(solution)/shard_map/ppermute | solution.py:473
  42.5 1.5 %collective-permute-start.15 = (bf16[96,768]{1,0:T(8,128)(2,1)S(1)}, bf16[96,768]{1,0:T(8,128)(2,1)S(1)}, u32[]{:S(2)}, u32[]{:S(2)}) collective-permute-start(bf16[96,768]{1,0:T(8,128)(2,1)S(1)} %get-tuple-element.40), channel_id=1, source_target_pairs={{0,16},{16,0},{1,17},{17,1},{2,18},{18,2},{3,19},{19,3},{4,20},{20... | collective-permute-start | bytes 442376 | tf_op jit(solution)/shard_map/ppermute | solution.py:473
  44.0 0.6 collective-permute-start.16
  44.6 3.2 %collective-permute-done.14.x_ref = bf16[96,768]{1,0:T(8,128)(2,1)S(1)} collective-permute-done((bf16[96,768]{1,0:T(8,128)(2,1)S(1)}, bf16[96,768]{1,0:T(8,128)(2,1)S(1)}, u32[]{:S(2)}, u32[]{:S(2)}) %collective-permute-start.14) | collective-permute-done | bytes 147488 | tf_op jit(solution)/shard_map/ppermute | solution.py:473
  47.8 3.4 %collective-permute-done.15.y_ref = bf16[96,768]{1,0:T(8,128)(2,1)S(1)} collective-permute-done((bf16[96,768]{1,0:T(8,128)(2,1)S(1)}, bf16[96,768]{1,0:T(8,128)(2,1)S(1)}, u32[]{:S(2)}, u32[]{:S(2)}) %collective-permute-start.15) | collective-permute-done | bytes 147488 | tf_op jit(solution)/shard_map/ppermute | solution.py:473
  51.3 0.6 %shard_map.100 = (f32[48,384]{1,0:T(8,128)S(1)}, bf16[48,384]{1,0:T(8,128)(2,1)S(1)}, bf16[48,384]{1,0:T(8,128)(2,1)S(1)}, bf16[48,384]{1,0:T(8,128)(2,1)S(1)}) custom-call(s32[3]{0:T(128)S(1)} %pad_add_fusion.where_ref, f32[96,768]{1,0:T(8,128)S(1)} %get-tuple-element.38.own_ref, bf16[96,768]{1,0:T(8,128)(2,1)S(1)} %collective-permute-done.14.x_ref, ...), custom_call_target="tpu_custom_call" | custom-call | tf_op jit(solution)/shard_map/pallas_call | solution.py:62
  51.9 1.6 %collective-permute-start.17 = (bf16[48,384]{1,0:T(8,128)(2,1)S(1)}, bf16[48,384]{1,0:T(8,128)(2,1)S(1)}, u32[]{:S(2)}, u32[]{:S(2)}) collective-permute-start(bf16[48,384]{1,0:T(8,128)(2,1)S(1)} %get-tuple-element.43), channel_id=1, source_target_pairs={{0,1},{1,0},{2,3},{3,2},{4,5},{5,4},{6,7},{7,6},{8,9},{9,8},{10,11... | collective-permute-start | bytes 110600 | tf_op jit(solution)/shard_map/ppermute | solution.py:477
  53.5 2.6 %collective-permute-start.18 = (bf16[48,384]{1,0:T(8,128)(2,1)S(1)}, bf16[48,384]{1,0:T(8,128)(2,1)S(1)}, u32[]{:S(2)}, u32[]{:S(2)}) collective-permute-start(bf16[48,384]{1,0:T(8,128)(2,1)S(1)} %get-tuple-element.44), channel_id=1, source_target_pairs={{0,2},{1,3},{2,0},{3,1},{4,6},{5,7},{6,4},{7,5},{8,10},{9,11},{10,... | collective-permute-start | bytes 110600 | tf_op jit(solution)/shard_map/ppermute | solution.py:477
  56.1 0.2 collective-permute-start.19
  56.4 2.1 %shard_map.98 = f32[4,128]{1,0:T(4,128)} custom-call(s32[3]{0:T(128)S(1)} %pad_add_fusion.where_ref, f32[8,768]{1,0:T(8,128)S(1)} %select_maximum_fusion.small_ref.refs_14_, bf16[416,128]{1,0:T(8,128)(2,1)S(1)} %get-tuple-element.28.refs_16_.hot_f_ref, bf16[416,128]{1,0:T(8,128)(2,1)S(1)} %get-tuple-element.29.refs_17_.hot_r_ref, ...), custom_call_target="tpu_custom_call" | custom-call | flops 1000000000 | bytes 1000000 | tf_op jit(solution)/shard_map/pallas_call | solution.py:62
  58.5 0.2 collective-permute-done.18.refs_1_
  58.7 3.2 %collective-permute-done.19.refs_2_ = bf16[48,384]{1,0:T(8,128)(2,1)S(1)} collective-permute-done((bf16[48,384]{1,0:T(8,128)(2,1)S(1)}, bf16[48,384]{1,0:T(8,128)(2,1)S(1)}, u32[]{:S(2)}, u32[]{:S(2)}) %collective-permute-start.19) | collective-permute-done | bytes 36896 | tf_op jit(solution)/shard_map/ppermute | solution.py:477
  61.9 0.7 %shard_map.101 = f32[144,128]{1,0:T(8,128)} custom-call(f32[48,384]{1,0:T(8,128)S(1)} %get-tuple-element.42.mine_ref, bf16[48,384]{1,0:T(8,128)(2,1)S(1)} %collective-permute-done.17.refs_0_, bf16[48,384]{1,0:T(8,128)(2,1)S(1)} %collective-permute-done.18.refs_1_, bf16[48,384]{1,0:T(8,128)(2,1)S(1)} %collective-permute-done.19.refs_2_), custom_call_target="tpu_custom_call" | custom-call | tf_op jit(solution)/shard_map/pallas_call | solution.py:62
  (6 shorter events, 0.0 us)
Async XLA Ops:
  5.8 8.5 %collective-permute-start.1 = (bf16[144,768]{1,0:T(8,128)(2,1)S(1)}, bf16[144,768]{1,0:T(8,128)(2,1)S(1)}, u32[]{:S(2)}, u32[]{:S(2)}) collective-permute-start(bf16[144,768]{1,0:T(8,128)(2,1)S(1)} %get-tuple-element.26), channel_id=1, source_target_pairs={{0,16},{16,0},{1,17},{17,1},{2,18},{18,2},{3,19},{19,3},{4,20},{20... | collective-permute-start | bytes 663560 | tf_op jit(solution)/shard_map/ppermute | solution.py:473
  8.9 11.0 %collective-permute-start = (bf16[224,768]{1,0:T(8,128)(2,1)S(1)}, bf16[224,768]{1,0:T(8,128)(2,1)S(1)}, u32[]{:S(2)}, u32[]{:S(2)}) collective-permute-start(bf16[224,768]{1,0:T(8,128)(2,1)S(1)} %get-tuple-element.25), channel_id=1, source_target_pairs={{0,8},{8,0},{1,9},{9,1},{2,10},{10,2},{3,11},{11,3},{4,12},{12,4},... | collective-permute-start | bytes 1032200 | tf_op jit(solution)/shard_map/ppermute | solution.py:473
  10.4 15.2 %collective-permute-start.2 = (bf16[224,768]{1,0:T(8,128)(2,1)S(1)}, bf16[224,768]{1,0:T(8,128)(2,1)S(1)}, u32[]{:S(2)}, u32[]{:S(2)}) collective-permute-start(bf16[224,768]{1,0:T(8,128)(2,1)S(1)} %get-tuple-element.27), channel_id=1, source_target_pairs={{0,24},{8,16},{16,8},{24,0},{1,25},{9,17},{17,9},{25,1},{2,26},{10... | collective-permute-start | bytes 1032200 | tf_op jit(solution)/shard_map/ppermute | solution.py:473
  10.4 21.5 %collective-permute-start.3 = (bf16[368,768]{1,0:T(8,128)(2,1)S(1)}, bf16[368,768]{1,0:T(8,128)(2,1)S(1)}, u32[]{:S(2)}, u32[]{:S(2)}) collective-permute-start(bf16[368,768]{1,0:T(8,128)(2,1)S(1)} %get-tuple-element.24.refs_0_), channel_id=1, source_target_pairs={{0,4},{4,0},{1,5},{5,1},{2,6},{6,2},{3,7},{7,3},{8,12},{12,8},{9,1... | collective-permute-start | bytes 1695752 | tf_op jit(solution)/shard_map/ppermute | solution.py:473
  14.3 13.1 %collective-permute-start.8 = (bf16[144,768]{1,0:T(8,128)(2,1)S(1)}, bf16[144,768]{1,0:T(8,128)(2,1)S(1)}, u32[]{:S(2)}, u32[]{:S(2)}) collective-permute-start(bf16[144,768]{1,0:T(8,128)(2,1)S(1)} %collective-permute-done.1.refs_2_.refs_3_), channel_id=1, source_target_pairs={{0,1},{1,0},{2,3},{3,2},{4,5},{5,4},{6,7},{7,6},{8,9},{9,8},{10,11... | collective-permute-start | bytes 663560 | tf_op jit(solution)/shard_map/ppermute | solution.py:477
  16.1 11.3 %collective-permute-start.5 = (bf16[144,768]{1,0:T(8,128)(2,1)S(1)}, bf16[144,768]{1,0:T(8,128)(2,1)S(1)}, u32[]{:S(2)}, u32[]{:S(2)}) collective-permute-start(bf16[144,768]{1,0:T(8,128)(2,1)S(1)} %collective-permute-done.1.refs_2_.refs_3_), channel_id=1, source_target_pairs={{0,4},{4,0},{1,5},{5,1},{2,6},{6,2},{3,7},{7,3},{8,12},{12,8},{9,1... | collective-permute-start | bytes 663560 | tf_op jit(solution)/shard_map/ppermute | solution.py:473
  19.9 8.0 %collective-permute-start.7 = (bf16[144,768]{1,0:T(8,128)(2,1)S(1)}, bf16[144,768]{1,0:T(8,128)(2,1)S(1)}, u32[]{:S(2)}, u32[]{:S(2)}) collective-permute-start(bf16[144,768]{1,0:T(8,128)(2,1)S(1)} %slice.8), channel_id=1, source_target_pairs={{0,1},{1,0},{2,3},{3,2},{4,5},{5,4},{6,7},{7,6},{8,9},{9,8},{10,11... | collective-permute-start | bytes 663560 | tf_op jit(solution)/shard_map/ppermute | solution.py:477
  25.6 6.4 %collective-permute-start.9 = (bf16[144,768]{1,0:T(8,128)(2,1)S(1)}, bf16[144,768]{1,0:T(8,128)(2,1)S(1)}, u32[]{:S(2)}, u32[]{:S(2)}) collective-permute-start(bf16[144,768]{1,0:T(8,128)(2,1)S(1)} %slice.9), channel_id=1, source_target_pairs={{0,1},{1,0},{2,3},{3,2},{4,5},{5,4},{6,7},{7,6},{8,9},{9,8},{10,11... | collective-permute-start | bytes 663560 | tf_op jit(solution)/shard_map/ppermute | solution.py:477
  27.4 5.1 %collective-permute-start.4 = (bf16[224,768]{1,0:T(8,128)(2,1)S(1)}, bf16[224,768]{1,0:T(8,128)(2,1)S(1)}, u32[]{:S(2)}, u32[]{:S(2)}) collective-permute-start(bf16[224,768]{1,0:T(8,128)(2,1)S(1)} %collective-permute-done.refs_1_.refs_2_), channel_id=1, source_target_pairs={{0,4},{4,0},{1,5},{5,1},{2,6},{6,2},{3,7},{7,3},{8,12},{12,8},{9,1... | collective-permute-start | bytes 1032200 | tf_op jit(solution)/shard_map/ppermute | solution.py:473
  27.4 5.1 %collective-permute-start.6 = (bf16[224,768]{1,0:T(8,128)(2,1)S(1)}, bf16[224,768]{1,0:T(8,128)(2,1)S(1)}, u32[]{:S(2)}, u32[]{:S(2)}) collective-permute-start(bf16[224,768]{1,0:T(8,128)(2,1)S(1)} %collective-permute-done.2.refs_3_.refs_4_), channel_id=1, source_target_pairs={{0,4},{4,0},{1,5},{5,1},{2,6},{6,2},{3,7},{7,3},{8,12},{12,8},{9,1... | collective-permute-start | bytes 1032200 | tf_op jit(solution)/shard_map/ppermute | solution.py:473
  27.9 6.0 %collective-permute-start.11 = (bf16[144,768]{1,0:T(8,128)(2,1)S(1)}, bf16[144,768]{1,0:T(8,128)(2,1)S(1)}, u32[]{:S(2)}, u32[]{:S(2)}) collective-permute-start(bf16[144,768]{1,0:T(8,128)(2,1)S(1)} %collective-permute-done.8.refs_9_), channel_id=1, source_target_pairs={{0,4},{4,0},{1,5},{5,1},{2,6},{6,2},{3,7},{7,3},{8,12},{12,8},{9,1... | collective-permute-start | bytes 663560 | tf_op jit(solution)/shard_map/ppermute | solution.py:473
  31.9 2.0 %collective-permute-start.10 = (bf16[144,768]{1,0:T(8,128)(2,1)S(1)}, bf16[144,768]{1,0:T(8,128)(2,1)S(1)}, u32[]{:S(2)}, u32[]{:S(2)}) collective-permute-start(bf16[144,768]{1,0:T(8,128)(2,1)S(1)} %collective-permute-done.7.refs_8_), channel_id=1, source_target_pairs={{0,4},{4,0},{1,5},{5,1},{2,6},{6,2},{3,7},{7,3},{8,12},{12,8},{9,1... | collective-permute-start | bytes 663560 | tf_op jit(solution)/shard_map/ppermute | solution.py:473
  31.9 2.0 %collective-permute-start.12 = (bf16[144,768]{1,0:T(8,128)(2,1)S(1)}, bf16[144,768]{1,0:T(8,128)(2,1)S(1)}, u32[]{:S(2)}, u32[]{:S(2)}) collective-permute-start(bf16[144,768]{1,0:T(8,128)(2,1)S(1)} %collective-permute-done.9.refs_10_), channel_id=1, source_target_pairs={{0,4},{4,0},{1,5},{5,1},{2,6},{6,2},{3,7},{7,3},{8,12},{12,8},{9,1... | collective-permute-start | bytes 663560 | tf_op jit(solution)/shard_map/ppermute | solution.py:473
  38.3 2.1 %collective-permute-start.13 = (bf16[4,96,768]{2,1,0:T(8,128)(2,1)S(1)}, bf16[4,96,768]{2,1,0:T(8,128)(2,1)S(1)}, u32[]{:S(2)}, u32[]{:S(2)}) collective-permute-start(bf16[4,96,768]{2,1,0:T(8,128)(2,1)S(1)} %get-tuple-element.37), channel_id=1, source_target_pairs={{0,4},{4,0},{1,5},{5,1},{2,6},{6,2},{3,7},{7,3},{8,12},{12,8},{9,1... | collective-permute-start | bytes 1769480 | tf_op jit(solution)/shard_map/ppermute | solution.py:473
  41.1 6.8 %collective-permute-start.14 = (bf16[96,768]{1,0:T(8,128)(2,1)S(1)}, bf16[96,768]{1,0:T(8,128)(2,1)S(1)}, u32[]{:S(2)}, u32[]{:S(2)}) collective-permute-start(bf16[96,768]{1,0:T(8,128)(2,1)S(1)} %get-tuple-element.39), channel_id=1, source_target_pairs={{0,8},{8,0},{1,9},{9,1},{2,10},{10,2},{3,11},{11,3},{4,12},{12,4},... | collective-permute-start | bytes 442376 | tf_op jit(solution)/shard_map/ppermute | solution.py:473
  42.5 8.8 %collective-permute-start.15 = (bf16[96,768]{1,0:T(8,128)(2,1)S(1)}, bf16[96,768]{1,0:T(8,128)(2,1)S(1)}, u32[]{:S(2)}, u32[]{:S(2)}) collective-permute-start(bf16[96,768]{1,0:T(8,128)(2,1)S(1)} %get-tuple-element.40), channel_id=1, source_target_pairs={{0,16},{16,0},{1,17},{17,1},{2,18},{18,2},{3,19},{19,3},{4,20},{20... | collective-permute-start | bytes 442376 | tf_op jit(solution)/shard_map/ppermute | solution.py:473
  44.0 7.3 %collective-permute-start.16 = (bf16[96,768]{1,0:T(8,128)(2,1)S(1)}, bf16[96,768]{1,0:T(8,128)(2,1)S(1)}, u32[]{:S(2)}, u32[]{:S(2)}) collective-permute-start(bf16[96,768]{1,0:T(8,128)(2,1)S(1)} %get-tuple-element.41), channel_id=1, source_target_pairs={{0,24},{8,16},{16,8},{24,0},{1,25},{9,17},{17,9},{25,1},{2,26},{10... | collective-permute-start | bytes 442376 | tf_op jit(solution)/shard_map/ppermute | solution.py:473
  51.9 6.6 %collective-permute-start.17 = (bf16[48,384]{1,0:T(8,128)(2,1)S(1)}, bf16[48,384]{1,0:T(8,128)(2,1)S(1)}, u32[]{:S(2)}, u32[]{:S(2)}) collective-permute-start(bf16[48,384]{1,0:T(8,128)(2,1)S(1)} %get-tuple-element.43), channel_id=1, source_target_pairs={{0,1},{1,0},{2,3},{3,2},{4,5},{5,4},{6,7},{7,6},{8,9},{9,8},{10,11... | collective-permute-start | bytes 110600 | tf_op jit(solution)/shard_map/ppermute | solution.py:477
  53.5 5.2 %collective-permute-start.18 = (bf16[48,384]{1,0:T(8,128)(2,1)S(1)}, bf16[48,384]{1,0:T(8,128)(2,1)S(1)}, u32[]{:S(2)}, u32[]{:S(2)}) collective-permute-start(bf16[48,384]{1,0:T(8,128)(2,1)S(1)} %get-tuple-element.44), channel_id=1, source_target_pairs={{0,2},{1,3},{2,0},{3,1},{4,6},{5,7},{6,4},{7,5},{8,10},{9,11},{10,... | collective-permute-start | bytes 110600 | tf_op jit(solution)/shard_map/ppermute | solution.py:477
  56.1 5.8 %collective-permute-start.19 = (bf16[48,384]{1,0:T(8,128)(2,1)S(1)}, bf16[48,384]{1,0:T(8,128)(2,1)S(1)}, u32[]{:S(2)}, u32[]{:S(2)}) collective-permute-start(bf16[48,384]{1,0:T(8,128)(2,1)S(1)} %get-tuple-element.45), channel_id=1, source_target_pairs={{0,3},{1,2},{2,1},{3,0},{4,7},{5,6},{6,5},{7,4},{8,11},{9,10},{10,... | collective-permute-start | bytes 110600 | tf_op jit(solution)/shard_map/ppermute | solution.py:477

commit v6 on v5

--- a/solution.py
+++ b/solution.py
@@ -89,7 +89,7 @@
 
 def prep_kernel(
     where_ref, narrow_ref, broad_ref, small_ref,
-    own_ref, x_ref, y_ref, d_ref,
+    own_ref, half_ref,
 ):
     me, count = where_ref[0], where_ref[2]
     width = narrow_ref.shape[1]
@@ -124,15 +124,23 @@
     own_ref[half : half + 16, width:chans] = flat[half + cut : 2 * half]
     own_ref[half + 16 : half + 16 + 2 * prows] = broad_ref[0 : 2 * prows]
     own_ref[2 * half - 32 : 2 * half] = jnp.concatenate([wide, extra], axis=0).astype(BF16)
-    part = own_ref[pl.ds(pl.multiple_of((where_ref[1] & 1) * half, 16), half), :]
-    for out in (x_ref, y_ref, d_ref):
-        out[0:half] = part
+    half_ref[...] = own_ref[pl.ds(pl.multiple_of((where_ref[1] & 1) * half, 16), half), :]
+    first, last = edges(cot, count)
+    own_ref[2 * half :] = jnp.where((me & 1) == 0, last, first)
+
+
+def edges(cot, count):
+    cap = cot.shape[0]
     take = (iota((HALO, cap), 1) == iota((HALO, cap), 0) + (count - HALO)).astype(BF16)
-    last = mm(take, cot).astype(BF16)
-    chip = me >> 1
-    own_ref[2 * half :] = jnp.where((me & 1) == 0, last, cot[0:HALO])
-    x_ref[half:] = jnp.where((chip ^ 1) > chip, last, cot[0:HALO])
-    d_ref[half:] = jnp.where((chip ^ 3) > chip, last, cot[0:HALO])
+    return cot[0:HALO], mm(take, cot).astype(BF16)
+
+
+def halo_kernel(where_ref, broad_ref, after_ref, x_ref, d_ref):
+    del after_ref
+    chip = where_ref[0] >> 1
+    first, last = edges(broad_ref[broad_ref.shape[1] // 8 :], where_ref[2])
+    x_ref[...] = jnp.where((chip ^ 1) > chip, last, first)
+    d_ref[...] = jnp.where((chip ^ 3) > chip, last, first)
 
 
 def context_body(info_at, cot, r1, r2, l1, l2, hot_f_ref, hot_r_ref, cx_ref):
@@ -198,8 +206,8 @@
 
 
 def context_kernel_packed(where_ref, *refs):
-    parts, broad_ref, outs = refs[0:8], refs[8], refs[9:12]
-    info_ref, halo_ref = refs[12:]
+    parts, far_parts, broad_ref, outs = refs[0:8], refs[8:12], refs[12], refs[13:16]
+    info_ref, halo_ref = refs[16:]
     me, odd = where_ref[0], where_ref[1] & 1
     chip, core = me >> 1, me & 1
     chans = broad_ref.shape[1]
@@ -216,8 +224,8 @@
         info_ref[REACH + peer] = jnp.broadcast_to(low, (8, 256))
     for n in range(2):
         halo_ref[4 * n + chip] = parts[4 * n][2 * half :]
-        halo_ref[4 * n + (chip ^ 1)] = parts[4 * n + 1][half:]
-        halo_ref[4 * n + (chip ^ 3)] = parts[4 * n + 3][half:]
+        halo_ref[4 * n + (chip ^ 1)] = far_parts[2 * n][...]
+        halo_ref[4 * n + (chip ^ 3)] = far_parts[2 * n + 1][...]
     r1 = halo_ref[4 + jnp.maximum(chip + core - 1, 0)]
     l1 = halo_ref[4 + jnp.minimum(chip + core, 3)]
     r2 = halo_ref[jnp.maximum(chip - 1, 0)]
@@ -433,20 +441,20 @@
     return jnp.concatenate([value[:, 0:width], value[:, width:]], axis=0)
 
 
-def core_sum_kernel(where_ref, keep_ref, recv_ref, own_ref, *outs):
-    chip = where_ref[0] >> 1
+def core_sum_kernel(keep_ref, recv_ref, own_ref, *outs):
+    chip = 2 * lax.axis_index("y") + lax.axis_index("x")
     own_ref[...] = keep_ref[chip] + recv_ref[chip].astype(F32)
     for n, out in enumerate(outs):
         at = chip ^ (n + 1)
         out[...] = (keep_ref[at] + recv_ref[at].astype(F32)).astype(BF16)
 
 
-def plane_sum_kernel(where_ref, own_ref, x_ref, y_ref, d_ref, mine_ref, *refs):
+def plane_sum_kernel(own_ref, d_ref, y_ref, x_ref, mine_ref, *refs):
     outs, sum_ref = refs[:-1], refs[-1]
     sum_ref[...] = (
         own_ref[...] + x_ref[...].astype(F32) + y_ref[...].astype(F32) + d_ref[...].astype(F32)
     )
-    z = where_ref[1]
+    z = lax.axis_index("dp")
     rows = mine_ref.shape[0] // 2
     mine_ref[...] = fold(sum_ref[pl.ds(pl.multiple_of(z * rows, 8), rows), :])
     for n, out in enumerate(outs):
@@ -494,8 +502,9 @@
 
 def lines(embed, bases):
     cap, chans = bases.shape[1], embed.shape[1]
-    extra = jnp.pad(bases.astype(F32), ((0, 3), (0, chans - cap)))
-    return jnp.concatenate([embed, extra], axis=0)
+    row = lax.broadcasted_iota(jnp.int32, (8, chans), 0)
+    line = jnp.pad(bases, ((0, 0), (0, chans - cap))).astype(F32)
+    return jnp.where(row == 4, line, jnp.pad(embed, ((0, 4), (0, 0))))
 
 
 def weight(flops):
@@ -515,30 +524,31 @@
     narrow = jnp.concatenate([c1.reshape(-1, width), c2.reshape(-1, width)], axis=0)
     broad = jnp.concatenate([p2, p1, cot], axis=0)
     small = lines(embed, bases)
-    own, to_x, to_y, to_d = call(
+    own, part = call(
         prep_kernel,
-        [
-            ((2 * half + HALO, chans), BF16),
-            ((half + HALO, chans), BF16),
-            ((half, chans), BF16),
-            ((half + HALO, chans), BF16),
-        ],
+        [((2 * half + HALO, chans), BF16), ((half, chans), BF16)],
         [where, narrow, broad, small],
     )
-    plane = [flip_move(to_x, "x"), flip_move(to_y, "y"), flip_move(to_d, "y", "x")]
-    other = [xor_move(a[:half], "dp", 1) for a in plane]
+    from_x, from_y, from_d = [flip_move(part, *axes) for axes in (("x",), ("y",), ("y", "x"))]
+    plane = [from_x, from_y, from_d]
+    other = [xor_move(a, "dp", 1) for a in plane]
+    edge_x, edge_d = call(
+        halo_kernel, [((HALO, chans), BF16)] * 2, [where, broad, other[1]], cost=weight(10**6)
+    )
+    edge_d = flip_move(edge_d, "y", "x")
+    edge_x = flip_move(edge_x, "x")
     across = lambda arrays: [flip_move(a, "core") for a in arrays]
     rows = chans // 8
     swapped = across([own, *plane])
     hf, hr, cx = call(
         context_kernel_packed,
         context_shapes(cap, chans),
-        [where, own, *plane, *swapped, broad],
+        [where, own, *plane, *swapped, edge_x, edge_d, *across([edge_x, edge_d]), broad],
         scratch=[
             pltpu.VMEM((8 + 2 * REACH, 8, 256), F32),
             pltpu.VMEM((8, HALO, chans), BF16),
         ],
-        cost=weight(10**9),
+        cost=weight(10**6),
     )
     keep, send, s1, gb, g, second, p1_full = call(
         tower_kernel_packed,
@@ -567,17 +577,18 @@
     own, *outs = call(
         core_sum_kernel,
         [((rows, chans), F32)] + [((rows, chans), BF16)] * 3,
-        [where, keep, recv],
-    )
-    got = [flip_move(a, *axes) for a, axes in zip(outs, (("x",), ("y",), ("y", "x")))]
+        [keep, recv],
+    )
+    ways = (("x",), ("y",), ("y", "x"))
+    got = [flip_move(outs[n], *ways[n]) for n in (2, 1, 0)]
     part = rows // n_dp
     mine, *outs = call(
         plane_sum_kernel,
         [((2 * part, width), F32)] + [((2 * part, width), BF16)] * (n_dp - 1),
-        [where, own, *got],
+        [own, *got],
         scratch=[pltpu.VMEM((rows, chans), F32)],
     )
-    got = [xor_move(a, "dp", n + 1) for n, a in enumerate(outs)]
+    got = [xor_move(outs[n], "dp", n + 1) for n in reversed(range(n_dp - 1))]
     scale = 1.0 / math.sqrt(8 * n_dp * cap)
     (grad,) = call(
         functools.partial(last_sum_kernel, scale),

time: 62.8 us -> 68 us (1.083)
  starting transfers between devices: 19 us -> 23.5 us
  waiting for transfers between devices: 27.7 us -> 28.7 us
    ppermute x14 -> x18, starting transfers between devices: 9.3 us -> 13.3 us  [flip_move(): return lax.ppermute(array, axes, [(i, size - 1 - i) for i in range(size)])]
    ppermute x14 -> x18, waiting for transfers between devices: 20.3 us -> 22.6 us  [flip_move(): return lax.ppermute(array, axes, [(i, size - 1 - i) for i in range(size)])]
    ppermute x6, waiting for transfers between devices: 7.37 us -> 6.1 us  [xor_move(): lax.ppermute(array, axis, [(i, i ^ bits) for i in range(lax.axis_size(axi...]
    select_n x0 -> x1, other arithmetic: none -> 0.78 us  [lines(): return jnp.where(row == 4, line, jnp.pad(embed, ((0, 4), (0, 0))))]
    concatenate x1 -> x0, other arithmetic: 0.71 us -> none  [lines(): return jnp.concatenate([embed, extra], axis=0)]
    pallas_call x7 -> x8, Pallas kernels: 10.9 us -> 10.5 us  [call(): pl.pallas_call(body, out_shape=[jax.ShapeDtypeStruct(s, d) for s, d in ou...]
  transfers between devices with their start and end apart: 20 -> 24, of which waited for: 9 -> 11; matrix products, arithmetic and copies ran while one was open for 0% -> 0% of each run, Pallas kernels for 6% -> 6%
where the time goes in v6:
time: 68 us; the launch traced here: 67.7 us
  waiting for transfers between devices  28.7 us (42%)
  starting transfers between devices  23.5 us (35%)
  Pallas kernels  10.5 us (15%)
  other arithmetic  3.67 us (5%)
  between operations  1.4 us (2%)
    ppermute x18, waiting for transfers between devices, flip_move(): return lax.ppermute(array, axes, [(i, size - 1 - i) for i in range(size)])  22.6 us
    ppermute x18, starting transfers between devices, flip_move(): return lax.ppermute(array, axes, [(i, size - 1 - i) for i in range(size)])  13.3 us
    pallas_call x8, Pallas kernels, call(): pl.pallas_call(body, out_shape=[jax.ShapeDtypeStruct(s, d) for s, d in ou...  10.5 us
    ppermute x6, starting transfers between devices, xor_move(): lax.ppermute(array, axis, [(i, i ^ bits) for i in range(lax.axis_size(axi...  10.2 us
    ppermute x6, waiting for transfers between devices, xor_move(): lax.ppermute(array, axis, [(i, i ^ bits) for i in range(lax.axis_size(axi...  6.1 us
  transfers between devices with their start and end apart: 24, of which 11 were waited for; matrix products, arithmetic and copies ran while one was open for 0% of the time, Pallas kernels for 6%

profile of v6, /device:TPU:0, one launch (start us, length us, event | category | flops | bytes accessed | tf_op | source)
XLA Modules:
  0.0 67.7 jit_solution(3110540867472033187)
XLA Ops:
  1.3 0.7 convert_reduce_fusion
  2.0 1.1 %pad_maximum_fusion.narrow_ref = bf16[576,384]{1,0:T(8,128)(2,1)S(1)} fusion(bf16[288,384]{1,0:T(8,128)(2,1)} %bitcast.9, bf16[288,384]{1,0:T(8,128)(2,1)} %bitcast.10), kind=kLoop, calls=%fused_computation | loop fusion | flops 884736 | bytes 884736 | tf_op jit(solution)/shard_map/concatenate | solution.py:524
  3.1 0.1 pad_add_fusion.where_ref
  3.1 0.8 %pad_select_fusion.small_ref.refs_14_ = f32[8,768]{1,0:T(8,128)S(1)} fusion(f32[4,768]{1,0:T(4,128)} %param.15, f32[768]{0:T(1024)S(1)} %convert_reduce_fusion, pred[8]{0:T(512)(128)(4,1)S(1)} %iota_compare_fusion), kind=kLoop, calls=%fused_computation.2 | loop fusion | flops 6144 | bytes 39944 | tf_op jit(solution)/shard_map/jit(_where)/select_n | solution.py:507
  3.9 1.0 %pad_maximum_fusion.1.broad_ref.refs_12_ = bf16[224,768]{1,0:T(8,128)(2,1)S(1)} fusion(bf16[128,768]{1,0:T(8,128)(2,1)} %bitcast.11, bf16[48,768]{1,0:T(8,128)(2,1)} %param.12, bf16[48,768]{1,0:T(8,128)(2,1)} %param.14), kind=kLoop, calls=%fused_computation.1 | loop fusion | flops 1032192 | bytes 688128 | tf_op jit(solution)/shard_map/concatenate | solution.py:525
  5.0 1.0 %shard_map.95 = (bf16[368,768]{1,0:T(8,128)(2,1)S(1)}, bf16[144,768]{1,0:T(8,128)(2,1)S(1)}) custom-call(s32[3]{0:T(128)S(1)} %pad_add_fusion.where_ref, bf16[576,384]{1,0:T(8,128)(2,1)S(1)} %pad_maximum_fusion.narrow_ref, bf16[224,768]{1,0:T(8,128)(2,1)S(1)} %pad_maximum_fusion.1.broad_ref.refs_12_, f32[8,768]{1,0:T(8,128)S(1)} %pad_select_fusion.small_ref.refs_14_), custom_call_target="tpu_custom_call" | custom-call | tf_op jit(solution)/shard_map/pallas_call | solution.py:62
  5.9 4.0 %collective-permute-start.2 = (bf16[144,768]{1,0:T(8,128)(2,1)S(1)}, bf16[144,768]{1,0:T(8,128)(2,1)S(1)}, u32[]{:S(2)}, u32[]{:S(2)}) collective-permute-start(bf16[144,768]{1,0:T(8,128)(2,1)S(1)} %get-tuple-element.25), channel_id=1, source_target_pairs={{0,24},{8,16},{16,8},{24,0},{1,25},{9,17},{17,9},{25,1},{2,26},{10... | collective-permute-start | bytes 663560 | tf_op jit(solution)/shard_map/ppermute | solution.py:481
  9.9 0.5 collective-permute-start.1
  10.4 0.1 collective-permute-start
  10.5 5.7 %collective-permute-done.2.refs_3_.refs_4_ = bf16[144,768]{1,0:T(8,128)(2,1)S(1)} collective-permute-done((bf16[144,768]{1,0:T(8,128)(2,1)S(1)}, bf16[144,768]{1,0:T(8,128)(2,1)S(1)}, u32[]{:S(2)}, u32[]{:S(2)}) %collective-permute-start.2) | collective-permute-done | bytes 221216 | tf_op jit(solution)/shard_map/ppermute | solution.py:481
  16.2 2.1 %collective-permute-start.13 = (bf16[144,768]{1,0:T(8,128)(2,1)S(1)}, bf16[144,768]{1,0:T(8,128)(2,1)S(1)}, u32[]{:S(2)}, u32[]{:S(2)}) collective-permute-start(bf16[144,768]{1,0:T(8,128)(2,1)S(1)} %collective-permute-done.2.refs_3_.refs_4_), channel_id=1, source_target_pairs={{0,1},{1,0},{2,3},{3,2},{4,5},{5,4},{6,7},{7,6},{8,9},{9,8},{10,11... | collective-permute-start | bytes 663560 | tf_op jit(solution)/shard_map/ppermute | solution.py:485
  18.3 1.8 %collective-permute-done.1.refs_2_.refs_3_ = bf16[144,768]{1,0:T(8,128)(2,1)S(1)} collective-permute-done((bf16[144,768]{1,0:T(8,128)(2,1)S(1)}, bf16[144,768]{1,0:T(8,128)(2,1)S(1)}, u32[]{:S(2)}, u32[]{:S(2)}) %collective-permute-start.1) | collective-permute-done | bytes 221216 | tf_op jit(solution)/shard_map/ppermute | solution.py:481
  20.1 1.8 %collective-permute-start.7 = (bf16[144,768]{1,0:T(8,128)(2,1)S(1)}, bf16[144,768]{1,0:T(8,128)(2,1)S(1)}, u32[]{:S(2)}, u32[]{:S(2)}) collective-permute-start(bf16[144,768]{1,0:T(8,128)(2,1)S(1)} %collective-permute-done.1.refs_2_.refs_3_), channel_id=1, source_target_pairs={{0,1},{1,0},{2,3},{3,2},{4,5},{5,4},{6,7},{7,6},{8,9},{9,8},{10,11... | collective-permute-start | bytes 663560 | tf_op jit(solution)/shard_map/ppermute | solution.py:485
  21.8 0.0 collective-permute-start.6
  21.8 0.5 collective-permute-start.5
  22.3 1.9 %collective-permute-start.12 = (bf16[144,768]{1,0:T(8,128)(2,1)S(1)}, bf16[144,768]{1,0:T(8,128)(2,1)S(1)}, u32[]{:S(2)}, u32[]{:S(2)}) collective-permute-start(bf16[144,768]{1,0:T(8,128)(2,1)S(1)} %collective-permute-done.refs_1_.refs_2_), channel_id=1, source_target_pairs={{0,1},{1,0},{2,3},{3,2},{4,5},{5,4},{6,7},{7,6},{8,9},{9,8},{10,11... | collective-permute-start | bytes 663560 | tf_op jit(solution)/shard_map/ppermute | solution.py:485
  24.2 4.1 %collective-permute-done.7.after_ref.refs_9_ = bf16[144,768]{1,0:T(8,128)(2,1)S(1)} collective-permute-done((bf16[144,768]{1,0:T(8,128)(2,1)S(1)}, bf16[144,768]{1,0:T(8,128)(2,1)S(1)}, u32[]{:S(2)}, u32[]{:S(2)}) %collective-permute-start.7) | collective-permute-done | bytes 221216 | tf_op jit(solution)/shard_map/ppermute | solution.py:485
  28.4 0.7 %shard_map.96 = (bf16[80,768]{1,0:T(8,128)(2,1)S(1)}, bf16[80,768]{1,0:T(8,128)(2,1)S(1)}) custom-call(s32[3]{0:T(128)S(1)} %pad_add_fusion.where_ref, bf16[224,768]{1,0:T(8,128)(2,1)S(1)} %pad_maximum_fusion.1.broad_ref.refs_12_, bf16[144,768]{1,0:T(8,128)(2,1)S(1)} %collective-permute-done.7.after_ref.refs_9_), custom_call_target="tpu_custom_call" | custom-call | flops 1000000 | bytes 1000000 | tf_op jit(solution)/shard_map/pallas_call | solution.py:62
  29.1 0.0 collective-permute-done.6.refs_7_
  29.1 1.7 %collective-permute-start.8 = (bf16[80,768]{1,0:T(8,128)(2,1)S(1)}, bf16[80,768]{1,0:T(8,128)(2,1)S(1)}, u32[]{:S(2)}, u32[]{:S(2)}) collective-permute-start(bf16[80,768]{1,0:T(8,128)(2,1)S(1)} %get-tuple-element.26), channel_id=1, source_target_pairs={{0,8},{8,0},{1,9},{9,1},{2,10},{10,2},{3,11},{11,3},{4,12},{12,4},... | collective-permute-start | bytes 368648 | tf_op jit(solution)/shard_map/ppermute | solution.py:481
  30.8 0.0 collective-permute-done.5.refs_6_
  30.8 1.5 %collective-permute-start.9 = (bf16[80,768]{1,0:T(8,128)(2,1)S(1)}, bf16[80,768]{1,0:T(8,128)(2,1)S(1)}, u32[]{:S(2)}, u32[]{:S(2)}) collective-permute-start(bf16[80,768]{1,0:T(8,128)(2,1)S(1)} %get-tuple-element.27), channel_id=1, source_target_pairs={{0,24},{8,16},{16,8},{24,0},{1,25},{9,17},{17,9},{25,1},{2,26},{10... | collective-permute-start | bytes 368648 | tf_op jit(solution)/shard_map/ppermute | solution.py:481
  32.3 0.0 collective-permute-done.12.refs_8_
  32.3 0.0 collective-permute-start.15
  32.3 0.5 collective-permute-start.16
  32.8 2.1 %collective-permute-done.8.refs_8_ = bf16[80,768]{1,0:T(8,128)(2,1)S(1)} collective-permute-done((bf16[80,768]{1,0:T(8,128)(2,1)S(1)}, bf16[80,768]{1,0:T(8,128)(2,1)S(1)}, u32[]{:S(2)}, u32[]{:S(2)}) %collective-permute-start.8) | collective-permute-done | bytes 122912 | tf_op jit(solution)/shard_map/ppermute | solution.py:481
  34.9 0.0 collective-permute-start.14
  34.9 3.7 %collective-permute-done.9.refs_9_ = bf16[80,768]{1,0:T(8,128)(2,1)S(1)} collective-permute-done((bf16[80,768]{1,0:T(8,128)(2,1)S(1)}, bf16[80,768]{1,0:T(8,128)(2,1)S(1)}, u32[]{:S(2)}, u32[]{:S(2)}) %collective-permute-start.9) | collective-permute-done | bytes 122912 | tf_op jit(solution)/shard_map/ppermute | solution.py:481
  38.7 0.0 collective-permute-done.3.refs_4_.refs_1_
  38.7 0.5 collective-permute-start.11
  39.2 0.8 %collective-permute-done.10.refs_10_ = bf16[80,768]{1,0:T(8,128)(2,1)S(1)} collective-permute-done((bf16[80,768]{1,0:T(8,128)(2,1)S(1)}, bf16[80,768]{1,0:T(8,128)(2,1)S(1)}, u32[]{:S(2)}, u32[]{:S(2)}) %collective-permute-start.10) | collective-permute-done | bytes 122912 | tf_op jit(solution)/shard_map/ppermute | solution.py:481
  40.0 0.2 collective-permute-done.11.refs_11_
  40.2 1.4 %shard_map.97 = (bf16[416,128]{1,0:T(8,128)(2,1)S(1)}, bf16[416,128]{1,0:T(8,128)(2,1)S(1)}, bf16[288,768]{1,0:T(8,128)(2,1)S(1)}) custom-call(s32[3]{0:T(128)S(1)} %pad_add_fusion.where_ref, bf16[368,768]{1,0:T(8,128)(2,1)S(1)} %get-tuple-element.24.refs_0_, bf16[144,768]{1,0:T(8,128)(2,1)S(1)} %collective-permute-done.refs_1_.refs_2_, ...), custom_call_target="tpu_custom_call" | custom-call | flops 1000000 | bytes 1000000 | tf_op jit(solution)/shard_map/pallas_call | solution.py:62
  41.6 4.4 %shard_map.98 = (f32[4,96,768]{2,1,0:T(8,128)S(1)}, bf16[4,96,768]{2,1,0:T(8,128)(2,1)S(1)}, bf16[256,384]{1,0:T(8,128)(2,1)S(1)}, bf16[320,768]{1,0:T(8,128)(2,...) custom-call(s32[3]{0:T(128)S(1)} %pad_add_fusion.where_ref, ...), custom_call_target="tpu_custom_call" | custom-call | flops 4000000000 | bytes 1000000 | tf_op jit(solution)/shard_map/pallas_call | solution.py:62
  46.0 0.4 collective-permute-start.17
  46.4 1.7 %collective-permute-done.17.recv_ref = bf16[4,96,768]{2,1,0:T(8,128)(2,1)S(1)} collective-permute-done((bf16[4,96,768]{2,1,0:T(8,128)(2,1)S(1)}, bf16[4,96,768]{2,1,0:T(8,128)(2,1)S(1)}, u32[]{:S(2)}, u32[]{:S(2)}) %collective-permute-start.17) | collective-permute-done | bytes 589856 | tf_op jit(solution)/shard_map/ppermute | solution.py:481
  48.1 0.1 shard_map.100
  48.2 1.5 %collective-permute-start.18 = (bf16[96,768]{1,0:T(8,128)(2,1)S(1)}, bf16[96,768]{1,0:T(8,128)(2,1)S(1)}, u32[]{:S(2)}, u32[]{:S(2)}) collective-permute-start(bf16[96,768]{1,0:T(8,128)(2,1)S(1)} %get-tuple-element.39), channel_id=1, source_target_pairs={{0,24},{8,16},{16,8},{24,0},{1,25},{9,17},{17,9},{25,1},{2,26},{10... | collective-permute-start | bytes 442376 | tf_op jit(solution)/shard_map/ppermute | solution.py:481
  49.7 1.7 %collective-permute-start.19 = (bf16[96,768]{1,0:T(8,128)(2,1)S(1)}, bf16[96,768]{1,0:T(8,128)(2,1)S(1)}, u32[]{:S(2)}, u32[]{:S(2)}) collective-permute-start(bf16[96,768]{1,0:T(8,128)(2,1)S(1)} %get-tuple-element.40), channel_id=1, source_target_pairs={{0,16},{16,0},{1,17},{17,1},{2,18},{18,2},{3,19},{19,3},{4,20},{20... | collective-permute-start | bytes 442376 | tf_op jit(solution)/shard_map/ppermute | solution.py:481
  51.4 0.4 collective-permute-start.20
  51.8 4.1 %collective-permute-done.18.d_ref = bf16[96,768]{1,0:T(8,128)(2,1)S(1)} collective-permute-done((bf16[96,768]{1,0:T(8,128)(2,1)S(1)}, bf16[96,768]{1,0:T(8,128)(2,1)S(1)}, u32[]{:S(2)}, u32[]{:S(2)}) %collective-permute-start.18) | collective-permute-done | bytes 147488 | tf_op jit(solution)/shard_map/ppermute | solution.py:481
  55.9 2.5 %collective-permute-done.19.y_ref = bf16[96,768]{1,0:T(8,128)(2,1)S(1)} collective-permute-done((bf16[96,768]{1,0:T(8,128)(2,1)S(1)}, bf16[96,768]{1,0:T(8,128)(2,1)S(1)}, u32[]{:S(2)}, u32[]{:S(2)}) %collective-permute-start.19) | collective-permute-done | bytes 147488 | tf_op jit(solution)/shard_map/ppermute | solution.py:481
  58.4 0.1 shard_map.101
  58.5 3.7 %collective-permute-start.21 = (bf16[48,384]{1,0:T(8,128)(2,1)S(1)}, bf16[48,384]{1,0:T(8,128)(2,1)S(1)}, u32[]{:S(2)}, u32[]{:S(2)}) collective-permute-start(bf16[48,384]{1,0:T(8,128)(2,1)S(1)} %get-tuple-element.43), channel_id=1, source_target_pairs={{0,3},{1,2},{2,1},{3,0},{4,7},{5,6},{6,5},{7,4},{8,11},{9,10},{10,... | collective-permute-start | bytes 110600 | tf_op jit(solution)/shard_map/ppermute | solution.py:485
  62.2 0.8 %collective-permute-start.23 = (bf16[48,384]{1,0:T(8,128)(2,1)S(1)}, bf16[48,384]{1,0:T(8,128)(2,1)S(1)}, u32[]{:S(2)}, u32[]{:S(2)}) collective-permute-start(bf16[48,384]{1,0:T(8,128)(2,1)S(1)} %get-tuple-element.45), channel_id=1, source_target_pairs={{0,1},{1,0},{2,3},{3,2},{4,5},{5,4},{6,7},{7,6},{8,9},{9,8},{10,11... | collective-permute-start | bytes 110600 | tf_op jit(solution)/shard_map/ppermute | solution.py:485
  63.0 2.1 %shard_map.99 = f32[4,128]{1,0:T(4,128)} custom-call(s32[3]{0:T(128)S(1)} %pad_add_fusion.where_ref, f32[8,768]{1,0:T(8,128)S(1)} %pad_select_fusion.small_ref.refs_14_, bf16[416,128]{1,0:T(8,128)(2,1)S(1)} %get-tuple-element.28.refs_16_.hot_f_ref, bf16[416,128]{1,0:T(8,128)(2,1)S(1)} %get-tuple-element.29.refs_17_.hot_r_ref, ...), custom_call_target="tpu_custom_call" | custom-call | flops 1000000000 | bytes 1000000 | tf_op jit(solution)/shard_map/pallas_call | solution.py:62
  65.1 1.9 %collective-permute-done.22.refs_1_ = bf16[48,384]{1,0:T(8,128)(2,1)S(1)} collective-permute-done((bf16[48,384]{1,0:T(8,128)(2,1)S(1)}, bf16[48,384]{1,0:T(8,128)(2,1)S(1)}, u32[]{:S(2)}, u32[]{:S(2)}) %collective-permute-start.22) | collective-permute-done | bytes 36896 | tf_op jit(solution)/shard_map/ppermute | solution.py:485
  67.1 0.7 shard_map.102
  (14 shorter events, 0.0 us)
Async XLA Ops:
  5.9 10.3 %collective-permute-start.2 = (bf16[144,768]{1,0:T(8,128)(2,1)S(1)}, bf16[144,768]{1,0:T(8,128)(2,1)S(1)}, u32[]{:S(2)}, u32[]{:S(2)}) collective-permute-start(bf16[144,768]{1,0:T(8,128)(2,1)S(1)} %get-tuple-element.25), channel_id=1, source_target_pairs={{0,24},{8,16},{16,8},{24,0},{1,25},{9,17},{17,9},{25,1},{2,26},{10... | collective-permute-start | bytes 663560 | tf_op jit(solution)/shard_map/ppermute | solution.py:481
  9.9 10.2 %collective-permute-start.1 = (bf16[144,768]{1,0:T(8,128)(2,1)S(1)}, bf16[144,768]{1,0:T(8,128)(2,1)S(1)}, u32[]{:S(2)}, u32[]{:S(2)}) collective-permute-start(bf16[144,768]{1,0:T(8,128)(2,1)S(1)} %get-tuple-element.25), channel_id=1, source_target_pairs={{0,16},{16,0},{1,17},{17,1},{2,18},{18,2},{3,19},{19,3},{4,20},{20... | collective-permute-start | bytes 663560 | tf_op jit(solution)/shard_map/ppermute | solution.py:481
  10.4 11.4 %collective-permute-start = (bf16[144,768]{1,0:T(8,128)(2,1)S(1)}, bf16[144,768]{1,0:T(8,128)(2,1)S(1)}, u32[]{:S(2)}, u32[]{:S(2)}) collective-permute-start(bf16[144,768]{1,0:T(8,128)(2,1)S(1)} %get-tuple-element.25), channel_id=1, source_target_pairs={{0,8},{8,0},{1,9},{9,1},{2,10},{10,2},{3,11},{11,3},{4,12},{12,4},... | collective-permute-start | bytes 663560 | tf_op jit(solution)/shard_map/ppermute | solution.py:481
  10.5 28.1 %collective-permute-start.3 = (bf16[368,768]{1,0:T(8,128)(2,1)S(1)}, bf16[368,768]{1,0:T(8,128)(2,1)S(1)}, u32[]{:S(2)}, u32[]{:S(2)}) collective-permute-start(bf16[368,768]{1,0:T(8,128)(2,1)S(1)} %get-tuple-element.24.refs_0_), channel_id=1, source_target_pairs={{0,4},{4,0},{1,5},{5,1},{2,6},{6,2},{3,7},{7,3},{8,12},{12,8},{9,1... | collective-permute-start | bytes 1695752 | tf_op jit(solution)/shard_map/ppermute | solution.py:481
  16.2 6.1 %collective-permute-start.13 = (bf16[144,768]{1,0:T(8,128)(2,1)S(1)}, bf16[144,768]{1,0:T(8,128)(2,1)S(1)}, u32[]{:S(2)}, u32[]{:S(2)}) collective-permute-start(bf16[144,768]{1,0:T(8,128)(2,1)S(1)} %collective-permute-done.2.refs_3_.refs_4_), channel_id=1, source_target_pairs={{0,1},{1,0},{2,3},{3,2},{4,5},{5,4},{6,7},{7,6},{8,9},{9,8},{10,11... | collective-permute-start | bytes 663560 | tf_op jit(solution)/shard_map/ppermute | solution.py:485
  20.1 8.3 %collective-permute-start.7 = (bf16[144,768]{1,0:T(8,128)(2,1)S(1)}, bf16[144,768]{1,0:T(8,128)(2,1)S(1)}, u32[]{:S(2)}, u32[]{:S(2)}) collective-permute-start(bf16[144,768]{1,0:T(8,128)(2,1)S(1)} %collective-permute-done.1.refs_2_.refs_3_), channel_id=1, source_target_pairs={{0,1},{1,0},{2,3},{3,2},{4,5},{5,4},{6,7},{7,6},{8,9},{9,8},{10,11... | collective-permute-start | bytes 663560 | tf_op jit(solution)/shard_map/ppermute | solution.py:485
  21.8 7.3 %collective-permute-start.6 = (bf16[144,768]{1,0:T(8,128)(2,1)S(1)}, bf16[144,768]{1,0:T(8,128)(2,1)S(1)}, u32[]{:S(2)}, u32[]{:S(2)}) collective-permute-start(bf16[144,768]{1,0:T(8,128)(2,1)S(1)} %collective-permute-done.2.refs_3_.refs_4_), channel_id=1, source_target_pairs={{0,4},{4,0},{1,5},{5,1},{2,6},{6,2},{3,7},{7,3},{8,12},{12,8},{9,1... | collective-permute-start | bytes 663560 | tf_op jit(solution)/shard_map/ppermute | solution.py:481
  21.8 9.0 %collective-permute-start.5 = (bf16[144,768]{1,0:T(8,128)(2,1)S(1)}, bf16[144,768]{1,0:T(8,128)(2,1)S(1)}, u32[]{:S(2)}, u32[]{:S(2)}) collective-permute-start(bf16[144,768]{1,0:T(8,128)(2,1)S(1)} %collective-permute-done.1.refs_2_.refs_3_), channel_id=1, source_target_pairs={{0,4},{4,0},{1,5},{5,1},{2,6},{6,2},{3,7},{7,3},{8,12},{12,8},{9,1... | collective-permute-start | bytes 663560 | tf_op jit(solution)/shard_map/ppermute | solution.py:481
  22.3 10.0 %collective-permute-start.12 = (bf16[144,768]{1,0:T(8,128)(2,1)S(1)}, bf16[144,768]{1,0:T(8,128)(2,1)S(1)}, u32[]{:S(2)}, u32[]{:S(2)}) collective-permute-start(bf16[144,768]{1,0:T(8,128)(2,1)S(1)} %collective-permute-done.refs_1_.refs_2_), channel_id=1, source_target_pairs={{0,1},{1,0},{2,3},{3,2},{4,5},{5,4},{6,7},{7,6},{8,9},{9,8},{10,11... | collective-permute-start | bytes 663560 | tf_op jit(solution)/shard_map/ppermute | solution.py:485
  28.4 4.0 %collective-permute-start.4 = (bf16[144,768]{1,0:T(8,128)(2,1)S(1)}, bf16[144,768]{1,0:T(8,128)(2,1)S(1)}, u32[]{:S(2)}, u32[]{:S(2)}) collective-permute-start(bf16[144,768]{1,0:T(8,128)(2,1)S(1)} %collective-permute-done.refs_1_.refs_2_), channel_id=1, source_target_pairs={{0,4},{4,0},{1,5},{5,1},{2,6},{6,2},{3,7},{7,3},{8,12},{12,8},{9,1... | collective-permute-start | bytes 663560 | tf_op jit(solution)/shard_map/ppermute | solution.py:481
  29.1 5.8 %collective-permute-start.8 = (bf16[80,768]{1,0:T(8,128)(2,1)S(1)}, bf16[80,768]{1,0:T(8,128)(2,1)S(1)}, u32[]{:S(2)}, u32[]{:S(2)}) collective-permute-start(bf16[80,768]{1,0:T(8,128)(2,1)S(1)} %get-tuple-element.26), channel_id=1, source_target_pairs={{0,8},{8,0},{1,9},{9,1},{2,10},{10,2},{3,11},{11,3},{4,12},{12,4},... | collective-permute-start | bytes 368648 | tf_op jit(solution)/shard_map/ppermute | solution.py:481
  30.8 7.8 %collective-permute-start.9 = (bf16[80,768]{1,0:T(8,128)(2,1)S(1)}, bf16[80,768]{1,0:T(8,128)(2,1)S(1)}, u32[]{:S(2)}, u32[]{:S(2)}) collective-permute-start(bf16[80,768]{1,0:T(8,128)(2,1)S(1)} %get-tuple-element.27), channel_id=1, source_target_pairs={{0,24},{8,16},{16,8},{24,0},{1,25},{9,17},{17,9},{25,1},{2,26},{10... | collective-permute-start | bytes 368648 | tf_op jit(solution)/shard_map/ppermute | solution.py:481
  32.3 9.3 %collective-permute-start.15 = (bf16[144,768]{1,0:T(8,128)(2,1)S(1)}, bf16[144,768]{1,0:T(8,128)(2,1)S(1)}, u32[]{:S(2)}, u32[]{:S(2)}) collective-permute-start(bf16[144,768]{1,0:T(8,128)(2,1)S(1)} %collective-permute-done.7.after_ref.refs_9_), channel_id=1, source_target_pairs={{0,4},{4,0},{1,5},{5,1},{2,6},{6,2},{3,7},{7,3},{8,12},{12,8},{9,1... | collective-permute-start | bytes 663560 | tf_op jit(solution)/shard_map/ppermute | solution.py:481
  32.3 9.3 %collective-permute-start.16 = (bf16[144,768]{1,0:T(8,128)(2,1)S(1)}, bf16[144,768]{1,0:T(8,128)(2,1)S(1)}, u32[]{:S(2)}, u32[]{:S(2)}) collective-permute-start(bf16[144,768]{1,0:T(8,128)(2,1)S(1)} %collective-permute-done.13.refs_10_), channel_id=1, source_target_pairs={{0,4},{4,0},{1,5},{5,1},{2,6},{6,2},{3,7},{7,3},{8,12},{12,8},{9,1... | collective-permute-start | bytes 663560 | tf_op jit(solution)/shard_map/ppermute | solution.py:481
  34.9 6.7 %collective-permute-start.14 = (bf16[144,768]{1,0:T(8,128)(2,1)S(1)}, bf16[144,768]{1,0:T(8,128)(2,1)S(1)}, u32[]{:S(2)}, u32[]{:S(2)}) collective-permute-start(bf16[144,768]{1,0:T(8,128)(2,1)S(1)} %collective-permute-done.12.refs_8_), channel_id=1, source_target_pairs={{0,4},{4,0},{1,5},{5,1},{2,6},{6,2},{3,7},{7,3},{8,12},{12,8},{9,1... | collective-permute-start | bytes 663560 | tf_op jit(solution)/shard_map/ppermute | solution.py:481
  38.7 1.3 %collective-permute-start.10 = (bf16[80,768]{1,0:T(8,128)(2,1)S(1)}, bf16[80,768]{1,0:T(8,128)(2,1)S(1)}, u32[]{:S(2)}, u32[]{:S(2)}) collective-permute-start(bf16[80,768]{1,0:T(8,128)(2,1)S(1)} %collective-permute-done.8.refs_8_), channel_id=1, source_target_pairs={{0,4},{4,0},{1,5},{5,1},{2,6},{6,2},{3,7},{7,3},{8,12},{12,8},{9,1... | collective-permute-start | bytes 368648 | tf_op jit(solution)/shard_map/ppermute | solution.py:481
  38.7 1.5 %collective-permute-start.11 = (bf16[80,768]{1,0:T(8,128)(2,1)S(1)}, bf16[80,768]{1,0:T(8,128)(2,1)S(1)}, u32[]{:S(2)}, u32[]{:S(2)}) collective-permute-start(bf16[80,768]{1,0:T(8,128)(2,1)S(1)} %collective-permute-done.9.refs_9_), channel_id=1, source_target_pairs={{0,4},{4,0},{1,5},{5,1},{2,6},{6,2},{3,7},{7,3},{8,12},{12,8},{9,1... | collective-permute-start | bytes 368648 | tf_op jit(solution)/shard_map/ppermute | solution.py:481
  46.0 2.1 %collective-permute-start.17 = (bf16[4,96,768]{2,1,0:T(8,128)(2,1)S(1)}, bf16[4,96,768]{2,1,0:T(8,128)(2,1)S(1)}, u32[]{:S(2)}, u32[]{:S(2)}) collective-permute-start(bf16[4,96,768]{2,1,0:T(8,128)(2,1)S(1)} %get-tuple-element.37), channel_id=1, source_target_pairs={{0,4},{4,0},{1,5},{5,1},{2,6},{6,2},{3,7},{7,3},{8,12},{12,8},{9,1... | collective-permute-start | bytes 1769480 | tf_op jit(solution)/shard_map/ppermute | solution.py:481
  48.2 7.7 %collective-permute-start.18 = (bf16[96,768]{1,0:T(8,128)(2,1)S(1)}, bf16[96,768]{1,0:T(8,128)(2,1)S(1)}, u32[]{:S(2)}, u32[]{:S(2)}) collective-permute-start(bf16[96,768]{1,0:T(8,128)(2,1)S(1)} %get-tuple-element.39), channel_id=1, source_target_pairs={{0,24},{8,16},{16,8},{24,0},{1,25},{9,17},{17,9},{25,1},{2,26},{10... | collective-permute-start | bytes 442376 | tf_op jit(solution)/shard_map/ppermute | solution.py:481
  49.7 8.7 %collective-permute-start.19 = (bf16[96,768]{1,0:T(8,128)(2,1)S(1)}, bf16[96,768]{1,0:T(8,128)(2,1)S(1)}, u32[]{:S(2)}, u32[]{:S(2)}) collective-permute-start(bf16[96,768]{1,0:T(8,128)(2,1)S(1)} %get-tuple-element.40), channel_id=1, source_target_pairs={{0,16},{16,0},{1,17},{17,1},{2,18},{18,2},{3,19},{19,3},{4,20},{20... | collective-permute-start | bytes 442376 | tf_op jit(solution)/shard_map/ppermute | solution.py:481
  51.4 7.0 %collective-permute-start.20 = (bf16[96,768]{1,0:T(8,128)(2,1)S(1)}, bf16[96,768]{1,0:T(8,128)(2,1)S(1)}, u32[]{:S(2)}, u32[]{:S(2)}) collective-permute-start(bf16[96,768]{1,0:T(8,128)(2,1)S(1)} %get-tuple-element.41), channel_id=1, source_target_pairs={{0,8},{8,0},{1,9},{9,1},{2,10},{10,2},{3,11},{11,3},{4,12},{12,4},... | collective-permute-start | bytes 442376 | tf_op jit(solution)/shard_map/ppermute | solution.py:481
  58.5 6.6 %collective-permute-start.21 = (bf16[48,384]{1,0:T(8,128)(2,1)S(1)}, bf16[48,384]{1,0:T(8,128)(2,1)S(1)}, u32[]{:S(2)}, u32[]{:S(2)}) collective-permute-start(bf16[48,384]{1,0:T(8,128)(2,1)S(1)} %get-tuple-element.43), channel_id=1, source_target_pairs={{0,3},{1,2},{2,1},{3,0},{4,7},{5,6},{6,5},{7,4},{8,11},{9,10},{10,... | collective-permute-start | bytes 110600 | tf_op jit(solution)/shard_map/ppermute | solution.py:485
  62.2 4.9 %collective-permute-start.22 = (bf16[48,384]{1,0:T(8,128)(2,1)S(1)}, bf16[48,384]{1,0:T(8,128)(2,1)S(1)}, u32[]{:S(2)}, u32[]{:S(2)}) collective-permute-start(bf16[48,384]{1,0:T(8,128)(2,1)S(1)} %get-tuple-element.44), channel_id=1, source_target_pairs={{0,2},{1,3},{2,0},{3,1},{4,6},{5,7},{6,4},{7,5},{8,10},{9,11},{10,... | collective-permute-start | bytes 110600 | tf_op jit(solution)/shard_map/ppermute | solution.py:485
  62.2 4.9 %collective-permute-start.23 = (bf16[48,384]{1,0:T(8,128)(2,1)S(1)}, bf16[48,384]{1,0:T(8,128)(2,1)S(1)}, u32[]{:S(2)}, u32[]{:S(2)}) collective-permute-start(bf16[48,384]{1,0:T(8,128)(2,1)S(1)} %get-tuple-element.45), channel_id=1, source_target_pairs={{0,1},{1,0},{2,3},{3,2},{4,5},{5,4},{6,7},{7,6},{8,9},{9,8},{10,11... | collective-permute-start | bytes 110600 | tf_op jit(solution)/shard_map/ppermute | solution.py:485

commit v7 on v5

--- a/solution.py
+++ b/solution.py
@@ -54,10 +54,9 @@
     return out
 
 
-def call(body, out_shapes, args, scratch=(), limit=24, cost=None, space=pltpu.VMEM):
+def call(body, out_shapes, args, scratch=(), limit=24, cost=None):
     in_specs = [
-        pl.BlockSpec(memory_space=pltpu.SMEM if a.dtype == jnp.int32 and a.ndim == 1 else space)
-        for a in args
+        pl.BlockSpec(memory_space=pltpu.VMEM) for _ in args
     ]
     return pl.pallas_call(
         body,
@@ -87,11 +86,16 @@
     return first, jnp.concatenate(second, axis=0)
 
 
+def position():
+    return (2 * lax.axis_index("y") + lax.axis_index("x")) * 2 + lax.axis_index("core")
+
+
 def prep_kernel(
-    where_ref, narrow_ref, broad_ref, small_ref,
+    narrow_ref, broad_ref, small_ref,
     own_ref, x_ref, y_ref, d_ref,
 ):
-    me, count = where_ref[0], where_ref[2]
+    me, odd = position(), lax.axis_index("dp") & 1
+    count = small_ref[5:6, 0:128]
     width = narrow_ref.shape[1]
     chans = 2 * width
     shard = narrow_ref.shape[0] // 6
@@ -108,7 +112,7 @@
     info = jnp.concatenate(
         [
             small_ref[4:5, 0:cap],
-            jnp.full((1, 128), count, jnp.int32).astype(F32),
+            count,
             jnp.zeros((1, chans - cap - 128), F32),
         ],
         axis=1,
@@ -124,10 +128,11 @@
     own_ref[half : half + 16, width:chans] = flat[half + cut : 2 * half]
     own_ref[half + 16 : half + 16 + 2 * prows] = broad_ref[0 : 2 * prows]
     own_ref[2 * half - 32 : 2 * half] = jnp.concatenate([wide, extra], axis=0).astype(BF16)
-    part = own_ref[pl.ds(pl.multiple_of((where_ref[1] & 1) * half, 16), half), :]
+    part = own_ref[pl.ds(pl.multiple_of(odd * half, 16), half), :]
     for out in (x_ref, y_ref, d_ref):
         out[0:half] = part
-    take = (iota((HALO, cap), 1) == iota((HALO, cap), 0) + (count - HALO)).astype(BF16)
+    ahead = (iota((HALO, cap), 1) - iota((HALO, cap), 0) + HALO).astype(F32)
+    take = (ahead == count).astype(BF16)
     last = mm(take, cot).astype(BF16)
     chip = me >> 1
     own_ref[2 * half :] = jnp.where((me & 1) == 0, last, cot[0:HALO])
@@ -197,10 +202,10 @@
     )
 
 
-def context_kernel_packed(where_ref, *refs):
+def context_kernel_packed(*refs):
     parts, broad_ref, outs = refs[0:8], refs[8], refs[9:12]
     info_ref, halo_ref = refs[12:]
-    me, odd = where_ref[0], where_ref[1] & 1
+    me, odd = position(), lax.axis_index("dp") & 1
     chip, core = me >> 1, me & 1
     chans = broad_ref.shape[1]
     prow = chans // 16
@@ -267,7 +272,7 @@
         )
         before = before + mm(jnp.concatenate([hot, hot], axis=1), taps)
     value, slope = gelu_pair(before)
-    own_col = (iota((cap, 1), 0) < count).astype(F32)
+    own_col = (iota((cap, 1), 0).astype(F32) < count).astype(F32)
     own_gb = (cx[HALO : HALO + cap].astype(F32) * own_col).astype(BF16)
     mids = jnp.concatenate(
         [value[HALO : HALO + cap], value[grow + HALO : grow + HALO + cap]], axis=0
@@ -300,9 +305,8 @@
 
 
 def saliency_kernel(
-    where_ref, small_ref, hot_f_ref, hot_r_ref, s1_ref, gb_ref, g_ref, second_ref, p1_ref, sal_ref
+    small_ref, hot_f_ref, hot_r_ref, s1_ref, gb_ref, g_ref, second_ref, p1_ref, sal_ref
 ):
-    count = where_ref[2]
     cap = g_ref.shape[0] // 2
     inner = cap + 2 * FIRST_DILATION
     d, D = FIRST_DILATION, SECOND_DILATION
@@ -337,17 +341,18 @@
         if turn == 1:
             got = jnp.concatenate([got[3 - c : 4 - c] for c in range(4)], axis=0)
         total = total + got
-    live = iota((1, cap), 1) < count
+    live = iota((1, cap), 1).astype(F32) < small_ref[5:6, 0:cap]
     sal_ref[...] = jnp.where(live, total * (1.0 / math.sqrt(emb.shape[1])), 0.0)
 
 
-def tower_kernel_packed(where_ref, *refs):
+def tower_kernel_packed(*refs):
     own_parts, plane_parts, dp_parts = refs[0:2], refs[2:8], refs[8:14]
     small_ref, cx_ref, hf_ref, hr_ref = refs[14:18]
     keep_ref, send_ref, s1_ref, gb_ref, g_ref, wide_ref, p1_ref = refs[18:25]
     conv_ref, p2_ref, first_ref, second_ref = refs[25:]
-    me, count = where_ref[0], where_ref[2]
-    core, odd = me & 1, where_ref[1] & 1
+    me = position()
+    core, odd = me & 1, lax.axis_index("dp") & 1
+    count = small_ref[5:6, 0:1]
     width, chans = p1_ref.shape
     shard = chans // 8
     prow = width // 8
@@ -415,7 +420,7 @@
 
 
 def tower_kernel_plain(
-    where_ref, first_ref, p1_ref, conv_ref, p2_ref, small_ref, cx_ref, hf_ref, hr_ref,
+    first_ref, p1_ref, conv_ref, p2_ref, small_ref, cx_ref, hf_ref, hr_ref,
     grad_ref, s1_ref, gb_ref, g_ref,
 ):
     def put(block, value):
@@ -423,7 +428,7 @@
         grad_ref[block * rows : (block + 1) * rows] = value
 
     tower_body(
-        first_ref[...], p1_ref[...], lambda k: conv_ref[k], p2_ref[...], where_ref[2],
+        first_ref[...], p1_ref[...], lambda k: conv_ref[k], p2_ref[...], small_ref[5:6, 0:1],
         small_ref[0:4], g_ref.shape[0] // 2, cx_ref, hf_ref, hr_ref, s1_ref, gb_ref, g_ref, put,
     )
 
@@ -433,20 +438,20 @@
     return jnp.concatenate([value[:, 0:width], value[:, width:]], axis=0)
 
 
-def core_sum_kernel(where_ref, keep_ref, recv_ref, own_ref, *outs):
-    chip = where_ref[0] >> 1
+def core_sum_kernel(keep_ref, recv_ref, own_ref, *outs):
+    chip = 2 * lax.axis_index("y") + lax.axis_index("x")
     own_ref[...] = keep_ref[chip] + recv_ref[chip].astype(F32)
     for n, out in enumerate(outs):
         at = chip ^ (n + 1)
         out[...] = (keep_ref[at] + recv_ref[at].astype(F32)).astype(BF16)
 
 
-def plane_sum_kernel(where_ref, own_ref, x_ref, y_ref, d_ref, mine_ref, *refs):
+def plane_sum_kernel(own_ref, d_ref, y_ref, x_ref, mine_ref, *refs):
     outs, sum_ref = refs[:-1], refs[-1]
     sum_ref[...] = (
         own_ref[...] + x_ref[...].astype(F32) + y_ref[...].astype(F32) + d_ref[...].astype(F32)
     )
-    z = where_ref[1]
+    z = lax.axis_index("dp")
     rows = mine_ref.shape[0] // 2
     mine_ref[...] = fold(sum_ref[pl.ds(pl.multiple_of(z * rows, 8), rows), :])
     for n, out in enumerate(outs):
@@ -492,10 +497,12 @@
     return [((2 * TABLE, width), BF16), ((2 * inner, chans), BF16), ((2 * cap, chans), F32)]
 
 
-def lines(embed, bases):
+def lines(embed, bases, lengths):
     cap, chans = bases.shape[1], embed.shape[1]
-    extra = jnp.pad(bases.astype(F32), ((0, 3), (0, chans - cap)))
-    return jnp.concatenate([embed, extra], axis=0)
+    row = lax.broadcasted_iota(jnp.int32, (8, chans), 0)
+    line = jnp.pad(bases, ((0, 0), (0, chans - cap)))
+    extra = jnp.where(row == 4, line, jnp.where(row == 5, lengths, 0)).astype(F32)
+    return jnp.where(row < 4, jnp.pad(embed, ((0, 4), (0, 0))), extra)
 
 
 def weight(flops):
@@ -506,15 +513,13 @@
     bases, lengths, cotangent, c1, p1, c2, p2, embed
 ):
     cot = cotangent[0]
-    me = (lax.axis_index("y") * 2 + lax.axis_index("x")) * 2 + lax.axis_index("core")
-    where = jnp.stack([me.astype(jnp.int32), lax.axis_index("dp").astype(jnp.int32), lengths[0, 0]])
     cap, chans = cot.shape
     width = c1.shape[2]
     n_dp = lax.axis_size("dp")
     half = 3 * c2.shape[1] // 2
     narrow = jnp.concatenate([c1.reshape(-1, width), c2.reshape(-1, width)], axis=0)
     broad = jnp.concatenate([p2, p1, cot], axis=0)
-    small = lines(embed, bases)
+    small = lines(embed, bases, lengths)
     own, to_x, to_y, to_d = call(
         prep_kernel,
         [
@@ -523,7 +528,7 @@
             ((half, chans), BF16),
             ((half + HALO, chans), BF16),
         ],
-        [where, narrow, broad, small],
+        [narrow, broad, small],
     )
     plane = [flip_move(to_x, "x"), flip_move(to_y, "y"), flip_move(to_d, "y", "x")]
     other = [xor_move(a[:half], "dp", 1) for a in plane]
@@ -533,7 +538,7 @@
     hf, hr, cx = call(
         context_kernel_packed,
         context_shapes(cap, chans),
-        [where, own, *plane, *swapped, broad],
+        [own, *plane, *swapped, broad],
         scratch=[
             pltpu.VMEM((8 + 2 * REACH, 8, 256), F32),
             pltpu.VMEM((8, HALO, chans), BF16),
@@ -545,7 +550,7 @@
         [((4, rows, chans), F32), ((4, rows, chans), BF16), *pass_shapes(cap, chans, width)]
         + [((48, width), F32), ((width, chans), BF16)],
         [
-            where, own, swapped[0], *plane, *swapped[1:], *other, *across(other),
+            own, swapped[0], *plane, *swapped[1:], *other, *across(other),
             small, cx, hf, hr,
         ],
         scratch=[
@@ -561,23 +566,24 @@
     (sal,) = call(
         saliency_kernel,
         [((4, cap), F32)],
-        [where, small, hf, hr, s1, gb, g, second, p1_full],
+        [small, hf, hr, s1, gb, g, second, p1_full],
         cost=weight(10**9),
     )
     own, *outs = call(
         core_sum_kernel,
         [((rows, chans), F32)] + [((rows, chans), BF16)] * 3,
-        [where, keep, recv],
-    )
-    got = [flip_move(a, *axes) for a, axes in zip(outs, (("x",), ("y",), ("y", "x")))]
+        [keep, recv],
+    )
+    ways = (("x",), ("y",), ("y", "x"))
+    got = [flip_move(outs[n], *ways[n]) for n in (2, 1, 0)]
     part = rows // n_dp
     mine, *outs = call(
         plane_sum_kernel,
         [((2 * part, width), F32)] + [((2 * part, width), BF16)] * (n_dp - 1),
-        [where, own, *got],
+        [own, *got],
         scratch=[pltpu.VMEM((rows, chans), F32)],
     )
-    got = [xor_move(a, "dp", n + 1) for n, a in enumerate(outs)]
+    got = [xor_move(outs[n], "dp", n + 1) for n in reversed(range(n_dp - 1))]
     scale = 1.0 / math.sqrt(8 * n_dp * cap)
     (grad,) = call(
         functools.partial(last_sum_kernel, scale),
@@ -589,16 +595,9 @@
 
 def plain_shards(bases, lengths, cotangent, c1, p1, c2, p2, embed):
     cot = cotangent[0]
-    where = jnp.stack(
-        [
-            lax.axis_index("seq").astype(jnp.int32),
-            lax.axis_index("dp").astype(jnp.int32),
-            lengths[0, 0],
-        ]
-    )
     cap, chans = cot.shape
     width = c1.shape[2]
-    me, count = where[0], where[2]
+    me, count = lax.axis_index("seq"), lengths[0, 0]
     shard = c1.shape[1]
     own = lax.dynamic_slice_in_dim(embed, me * shard, shard, 1)
     act, slope = gelu_pair(own)
@@ -627,20 +626,20 @@
         shift_move(cot[:HALO], -1, ("seq",)),
         shift_move(cot[:SPILL], -2, ("seq",)),
     ]
-    small = lines(embed, bases)
+    small = lines(embed, bases, lengths)
     hf, hr, cx = call(
         context_kernel_plain, context_shapes(cap, chans), [info, cot, *halos]
     )
     grad, s1, gb, g = call(
         tower_kernel_plain,
         [((2 * width, chans), F32), *pass_shapes(cap, chans, width)],
-        [where, first, p1_full, conv, p2_full, small, cx, hf, hr],
+        [first, p1_full, conv, p2_full, small, cx, hf, hr],
         limit=40,
     )
     (sal,) = call(
         saliency_kernel,
         [((4, cap), F32)],
-        [where, small, hf, hr, s1, gb, g, second, p1_full],
+        [small, hf, hr, s1, gb, g, second, p1_full],
     )
     scale = 1.0 / math.sqrt(lax.axis_size("seq") * lax.axis_size("dp") * cap)
     grad = lax.psum_scatter(

time: 62.8 us -> 58.1 us (0.925)
  Pallas kernels: 10.9 us -> 7.63 us
  other arithmetic: 3.58 us -> 2.22 us
  waiting for transfers between devices: 27.7 us -> 26.8 us
  local copies, waits for them, and re-layouts: 0.03 us -> 0.7 us
    pallas_call x7, Pallas kernels: 10.9 us -> 7.63 us  [call(): pl.pallas_call(body, out_shape=[jax.ShapeDtypeStruct(s, d) for s, d in ou...]
    ppermute x6, waiting for transfers between devices: 7.37 us -> 6.4 us  [xor_move(): lax.ppermute(array, axis, [(i, i ^ bits) for i in range(lax.axis_size(axi...]
    concatenate x1 -> x0, other arithmetic: 0.71 us -> none  [lines(): return jnp.concatenate([embed, extra], axis=0)]
    pad x0 -> x1, local copies, waits for them, and re-layouts: none -> 0.67 us  [lines(): line = jnp.pad(bases, ((0, 0), (0, chans - cap)))]
    convert_element_type x1 -> x0, other arithmetic: 0.66 us -> none  [lines(): extra = jnp.pad(bases.astype(F32), ((0, 3), (0, chans - cap)))]
  transfers between devices with their start and end apart: 20 -> 20, of which waited for: 9 -> 9; matrix products, arithmetic and copies ran while one was open for 0% -> 0% of each run, Pallas kernels for 6% -> 4%
where the time goes in v7:
time: 58.1 us; the launch traced here: 57.8 us
  waiting for transfers between devices  26.8 us (46%)
  starting transfers between devices  19.2 us (33%)
  Pallas kernels  7.63 us (13%)
  other arithmetic  2.22 us (4%)
  between operations  1.38 us (2%)
  local copies, waits for them, and re-layouts  0.7 us (1%)
    ppermute x14, waiting for transfers between devices, flip_move(): return lax.ppermute(array, axes, [(i, size - 1 - i) for i in range(size)])  20.4 us
    ppermute x6, starting transfers between devices, xor_move(): lax.ppermute(array, axis, [(i, i ^ bits) for i in range(lax.axis_size(axi...  9.67 us
    ppermute x14, starting transfers between devices, flip_move(): return lax.ppermute(array, axes, [(i, size - 1 - i) for i in range(size)])  9.48 us
    pallas_call x7, Pallas kernels, call(): pl.pallas_call(body, out_shape=[jax.ShapeDtypeStruct(s, d) for s, d in ou...  7.63 us
    ppermute x6, waiting for transfers between devices, xor_move(): lax.ppermute(array, axis, [(i, i ^ bits) for i in range(lax.axis_size(axi...  6.4 us
  transfers between devices with their start and end apart: 20, of which 9 were waited for; matrix products, arithmetic and copies ran while one was open for 0% of the time, Pallas kernels for 4%

profile of v7, /device:TPU:0, one launch (start us, length us, event | category | flops | bytes accessed | tf_op | source)
XLA Modules:
  0.0 57.8 jit_solution(1622639395289926112)
XLA Ops:
  1.3 0.7 %pad_reduce_fusion = s32[768]{0:T(1024)S(1)} fusion(s32[1,128]{1,0:T(1,128)} %param.8), kind=kLoop, calls=%fused_computation.3 | loop fusion | bytes 3584 | tf_op jit(solution)/shard_map/jit(_pad)/pad | solution.py:503
  2.0 1.1 %pad_maximum_fusion.narrow_ref = bf16[576,384]{1,0:T(8,128)(2,1)S(1)} fusion(bf16[288,384]{1,0:T(8,128)(2,1)} %bitcast.7, bf16[288,384]{1,0:T(8,128)(2,1)} %bitcast.8), kind=kLoop, calls=%fused_computation | loop fusion | flops 884736 | bytes 884736 | tf_op jit(solution)/shard_map/concatenate | solution.py:520
  3.1 1.0 %pad_maximum_fusion.1.broad_ref.refs_8_ = bf16[224,768]{1,0:T(8,128)(2,1)S(1)} fusion(bf16[128,768]{1,0:T(8,128)(2,1)} %bitcast.9, bf16[48,768]{1,0:T(8,128)(2,1)} %param.12, bf16[48,768]{1,0:T(8,128)(2,1)} %param.14), kind=kLoop, calls=%fused_computation.1 | loop fusion | flops 1032192 | bytes 688128 | tf_op jit(solution)/shard_map/concatenate | solution.py:521
  4.1 0.1 convert_select_fusion.small_ref.refs_14_
  4.2 0.4 shard_map.95
  4.6 3.0 %collective-permute-start.1 = (bf16[144,768]{1,0:T(8,128)(2,1)S(1)}, bf16[144,768]{1,0:T(8,128)(2,1)S(1)}, u32[]{:S(2)}, u32[]{:S(2)}) collective-permute-start(bf16[144,768]{1,0:T(8,128)(2,1)S(1)} %get-tuple-element.26), channel_id=1, source_target_pairs={{0,16},{16,0},{1,17},{17,1},{2,18},{18,2},{3,19},{19,3},{4,20},{20... | collective-permute-start | bytes 663560 | tf_op jit(solution)/shard_map/ppermute | solution.py:478
  7.7 1.5 %collective-permute-start = (bf16[224,768]{1,0:T(8,128)(2,1)S(1)}, bf16[224,768]{1,0:T(8,128)(2,1)S(1)}, u32[]{:S(2)}, u32[]{:S(2)}) collective-permute-start(bf16[224,768]{1,0:T(8,128)(2,1)S(1)} %get-tuple-element.25), channel_id=1, source_target_pairs={{0,8},{8,0},{1,9},{9,1},{2,10},{10,2},{3,11},{11,3},{4,12},{12,4},... | collective-permute-start | bytes 1032200 | tf_op jit(solution)/shard_map/ppermute | solution.py:478
  9.2 0.1 collective-permute-start.2
  9.2 0.0 collective-permute-start.3
  9.2 3.9 %collective-permute-done.1.refs_2_.refs_3_ = bf16[144,768]{1,0:T(8,128)(2,1)S(1)} collective-permute-done((bf16[144,768]{1,0:T(8,128)(2,1)S(1)}, bf16[144,768]{1,0:T(8,128)(2,1)S(1)}, u32[]{:S(2)}, u32[]{:S(2)}) %collective-permute-start.1) | collective-permute-done | bytes 221216 | tf_op jit(solution)/shard_map/ppermute | solution.py:478
  13.1 1.8 %collective-permute-start.8 = (bf16[144,768]{1,0:T(8,128)(2,1)S(1)}, bf16[144,768]{1,0:T(8,128)(2,1)S(1)}, u32[]{:S(2)}, u32[]{:S(2)}) collective-permute-start(bf16[144,768]{1,0:T(8,128)(2,1)S(1)} %collective-permute-done.1.refs_2_.refs_3_), channel_id=1, source_target_pairs={{0,1},{1,0},{2,3},{3,2},{4,5},{5,4},{6,7},{7,6},{8,9},{9,8},{10,11... | collective-permute-start | bytes 663560 | tf_op jit(solution)/shard_map/ppermute | solution.py:482
  14.9 0.0 collective-permute-start.5
  14.9 3.8 %collective-permute-done.refs_1_.refs_2_ = bf16[224,768]{1,0:T(8,128)(2,1)S(1)} collective-permute-done((bf16[224,768]{1,0:T(8,128)(2,1)S(1)}, bf16[224,768]{1,0:T(8,128)(2,1)S(1)}, u32[]{:S(2)}, u32[]{:S(2)}) %collective-permute-start) | collective-permute-done | bytes 344096 | tf_op jit(solution)/shard_map/ppermute | solution.py:478
  18.7 1.6 %collective-permute-start.7 = (bf16[144,768]{1,0:T(8,128)(2,1)S(1)}, bf16[144,768]{1,0:T(8,128)(2,1)S(1)}, u32[]{:S(2)}, u32[]{:S(2)}) collective-permute-start(bf16[144,768]{1,0:T(8,128)(2,1)S(1)} %slice.8), channel_id=1, source_target_pairs={{0,1},{1,0},{2,3},{3,2},{4,5},{5,4},{6,7},{7,6},{8,9},{9,8},{10,11... | collective-permute-start | bytes 663560 | tf_op jit(solution)/shard_map/ppermute | solution.py:482
  20.3 4.0 %collective-permute-done.2.refs_3_.refs_4_ = bf16[224,768]{1,0:T(8,128)(2,1)S(1)} collective-permute-done((bf16[224,768]{1,0:T(8,128)(2,1)S(1)}, bf16[224,768]{1,0:T(8,128)(2,1)S(1)}, u32[]{:S(2)}, u32[]{:S(2)}) %collective-permute-start.2) | collective-permute-done | bytes 344096 | tf_op jit(solution)/shard_map/ppermute | solution.py:478
  24.4 1.8 %collective-permute-start.9 = (bf16[144,768]{1,0:T(8,128)(2,1)S(1)}, bf16[144,768]{1,0:T(8,128)(2,1)S(1)}, u32[]{:S(2)}, u32[]{:S(2)}) collective-permute-start(bf16[144,768]{1,0:T(8,128)(2,1)S(1)} %slice.9), channel_id=1, source_target_pairs={{0,1},{1,0},{2,3},{3,2},{4,5},{5,4},{6,7},{7,6},{8,9},{9,8},{10,11... | collective-permute-start | bytes 663560 | tf_op jit(solution)/shard_map/ppermute | solution.py:482
  26.2 0.0 collective-permute-done.8.refs_9_
  26.2 0.0 collective-permute-start.4
  26.2 0.0 collective-permute-done.5.refs_6_
  26.2 0.5 collective-permute-start.6
  26.7 0.0 collective-permute-done.7.refs_8_
  26.7 0.1 collective-permute-start.11
  26.8 4.0 %collective-permute-done.9.refs_10_ = bf16[144,768]{1,0:T(8,128)(2,1)S(1)} collective-permute-done((bf16[144,768]{1,0:T(8,128)(2,1)S(1)}, bf16[144,768]{1,0:T(8,128)(2,1)S(1)}, u32[]{:S(2)}, u32[]{:S(2)}) %collective-permute-start.9) | collective-permute-done | bytes 221216 | tf_op jit(solution)/shard_map/ppermute | solution.py:482
  30.7 0.0 collective-permute-start.10
  30.7 0.0 collective-permute-done.3.refs_4_.refs_1_
  30.7 0.5 collective-permute-start.12
  31.2 0.0 collective-permute-done.4.refs_5_
  31.2 0.0 collective-permute-done.6.refs_7_
  31.2 0.9 %shard_map.96 = (bf16[416,128]{1,0:T(8,128)(2,1)S(1)}, bf16[416,128]{1,0:T(8,128)(2,1)S(1)}, bf16[288,768]{1,0:T(8,128)(2,1)S(1)}) custom-call(bf16[368,768]{1,0:T(8,128)(2,1)S(1)} %get-tuple-element.24.refs_0_, bf16[224,768]{1,0:T(8,128)(2,1)S(1)} %collective-permute-done.refs_1_.refs_2_, bf16[144,768]{1,0:T(8,128)(2,1)S(1)} %collective-permute-done.1.refs_2_.refs_3_, ...), custom_call_target="tpu_custom_call" | custom-call | flops 1000000000 | bytes 1000000 | tf_op jit(solution)/shard_map/pallas_call | solution.py:61
  32.2 0.0 collective-permute-done.11.refs_12_
  32.2 0.0 collective-permute-done.10.refs_11_
  32.2 0.3 collective-permute-done.12.refs_13_
  32.5 3.8 %shard_map.97 = (f32[4,96,768]{2,1,0:T(8,128)S(1)}, bf16[4,96,768]{2,1,0:T(8,128)(2,1)S(1)}, bf16[256,384]{1,0:T(8,128)(2,1)S(1)}, bf16[320,768]{1,0:T(8,128)(2,...) custom-call(bf16[368,768]{1,0:T(8,128)(2,1)S(1)} %get-tuple-element.24.refs_0_, ...), custom_call_target="tpu_custom_call" | custom-call | flops 4000000000 | bytes 1000000 | tf_op jit(solution)/shard_map/pallas_call | solution.py:61
  36.3 0.3 collective-permute-start.13
  36.6 1.8 %collective-permute-done.13.recv_ref = bf16[4,96,768]{2,1,0:T(8,128)(2,1)S(1)} collective-permute-done((bf16[4,96,768]{2,1,0:T(8,128)(2,1)S(1)}, bf16[4,96,768]{2,1,0:T(8,128)(2,1)S(1)}, u32[]{:S(2)}, u32[]{:S(2)}) %collective-permute-start.13) | collective-permute-done | bytes 589856 | tf_op jit(solution)/shard_map/ppermute | solution.py:478
  38.4 0.1 shard_map.99
  38.5 2.4 %collective-permute-start.14 = (bf16[96,768]{1,0:T(8,128)(2,1)S(1)}, bf16[96,768]{1,0:T(8,128)(2,1)S(1)}, u32[]{:S(2)}, u32[]{:S(2)}) collective-permute-start(bf16[96,768]{1,0:T(8,128)(2,1)S(1)} %get-tuple-element.39), channel_id=1, source_target_pairs={{0,24},{8,16},{16,8},{24,0},{1,25},{9,17},{17,9},{25,1},{2,26},{10... | collective-permute-start | bytes 442376 | tf_op jit(solution)/shard_map/ppermute | solution.py:478
  40.9 0.5 collective-permute-start.15
  41.4 0.7 %collective-permute-start.16 = (bf16[96,768]{1,0:T(8,128)(2,1)S(1)}, bf16[96,768]{1,0:T(8,128)(2,1)S(1)}, u32[]{:S(2)}, u32[]{:S(2)}) collective-permute-start(bf16[96,768]{1,0:T(8,128)(2,1)S(1)} %get-tuple-element.41), channel_id=1, source_target_pairs={{0,8},{8,0},{1,9},{9,1},{2,10},{10,2},{3,11},{11,3},{4,12},{12,4},... | collective-permute-start | bytes 442376 | tf_op jit(solution)/shard_map/ppermute | solution.py:478
  42.1 4.1 %collective-permute-done.14.d_ref = bf16[96,768]{1,0:T(8,128)(2,1)S(1)} collective-permute-done((bf16[96,768]{1,0:T(8,128)(2,1)S(1)}, bf16[96,768]{1,0:T(8,128)(2,1)S(1)}, u32[]{:S(2)}, u32[]{:S(2)}) %collective-permute-start.14) | collective-permute-done | bytes 147488 | tf_op jit(solution)/shard_map/ppermute | solution.py:478
  46.2 2.4 %collective-permute-done.15.y_ref = bf16[96,768]{1,0:T(8,128)(2,1)S(1)} collective-permute-done((bf16[96,768]{1,0:T(8,128)(2,1)S(1)}, bf16[96,768]{1,0:T(8,128)(2,1)S(1)}, u32[]{:S(2)}, u32[]{:S(2)}) %collective-permute-start.15) | collective-permute-done | bytes 147488 | tf_op jit(solution)/shard_map/ppermute | solution.py:478
  48.6 0.1 shard_map.100
  48.7 3.6 %collective-permute-start.17 = (bf16[48,384]{1,0:T(8,128)(2,1)S(1)}, bf16[48,384]{1,0:T(8,128)(2,1)S(1)}, u32[]{:S(2)}, u32[]{:S(2)}) collective-permute-start(bf16[48,384]{1,0:T(8,128)(2,1)S(1)} %get-tuple-element.43), channel_id=1, source_target_pairs={{0,3},{1,2},{2,1},{3,0},{4,7},{5,6},{6,5},{7,4},{8,11},{9,10},{10,... | collective-permute-start | bytes 110600 | tf_op jit(solution)/shard_map/ppermute | solution.py:482
  52.3 0.8 %collective-permute-start.19 = (bf16[48,384]{1,0:T(8,128)(2,1)S(1)}, bf16[48,384]{1,0:T(8,128)(2,1)S(1)}, u32[]{:S(2)}, u32[]{:S(2)}) collective-permute-start(bf16[48,384]{1,0:T(8,128)(2,1)S(1)} %get-tuple-element.45), channel_id=1, source_target_pairs={{0,1},{1,0},{2,3},{3,2},{4,5},{5,4},{6,7},{7,6},{8,9},{9,8},{10,11... | collective-permute-start | bytes 110600 | tf_op jit(solution)/shard_map/ppermute | solution.py:482
  53.2 1.6 %shard_map.98 = f32[4,128]{1,0:T(4,128)} custom-call(f32[8,768]{1,0:T(8,128)S(1)} %convert_select_fusion.small_ref.refs_14_, bf16[416,128]{1,0:T(8,128)(2,1)S(1)} %get-tuple-element.28.refs_16_.hot_f_ref, bf16[416,128]{1,0:T(8,128)(2,1)S(1)} %get-tuple-element.29.refs_17_.hot_r_ref, bf16[256,384]{1,0:T(8,128)(2,1)S(1)} %get-tuple-element.31.s1_ref, ...), custom_call_target="tpu_custom_call" | custom-call | flops 1000000000 | bytes 1000000 | tf_op jit(solution)/shard_map/pallas_call | solution.py:61
  54.8 2.4 %collective-permute-done.18.refs_1_ = bf16[48,384]{1,0:T(8,128)(2,1)S(1)} collective-permute-done((bf16[48,384]{1,0:T(8,128)(2,1)S(1)}, bf16[48,384]{1,0:T(8,128)(2,1)S(1)}, u32[]{:S(2)}, u32[]{:S(2)}) %collective-permute-start.18) | collective-permute-done | bytes 36896 | tf_op jit(solution)/shard_map/ppermute | solution.py:482
  57.2 0.0 collective-permute-done.19.refs_2_
  57.2 0.7 %shard_map.101 = f32[144,128]{1,0:T(8,128)} custom-call(f32[48,384]{1,0:T(8,128)S(1)} %get-tuple-element.42.mine_ref, bf16[48,384]{1,0:T(8,128)(2,1)S(1)} %collective-permute-done.17.refs_0_, bf16[48,384]{1,0:T(8,128)(2,1)S(1)} %collective-permute-done.18.refs_1_, bf16[48,384]{1,0:T(8,128)(2,1)S(1)} %collective-permute-done.19.refs_2_), custom_call_target="tpu_custom_call" | custom-call | tf_op jit(solution)/shard_map/pallas_call | solution.py:61
  (9 shorter events, 0.1 us)
Async XLA Ops:
  0.6 3.5 %copy-start = (f32[4,768]{1,0:T(4,128)S(1)}, f32[4,768]{1,0:T(4,128)}, u32[]{:S(2)}) copy-start(f32[4,768]{1,0:T(4,128)} %param.15) | copy-start | bytes 36868
  4.6 8.5 %collective-permute-start.1 = (bf16[144,768]{1,0:T(8,128)(2,1)S(1)}, bf16[144,768]{1,0:T(8,128)(2,1)S(1)}, u32[]{:S(2)}, u32[]{:S(2)}) collective-permute-start(bf16[144,768]{1,0:T(8,128)(2,1)S(1)} %get-tuple-element.26), channel_id=1, source_target_pairs={{0,16},{16,0},{1,17},{17,1},{2,18},{18,2},{3,19},{19,3},{4,20},{20... | collective-permute-start | bytes 663560 | tf_op jit(solution)/shard_map/ppermute | solution.py:478
  7.7 11.0 %collective-permute-start = (bf16[224,768]{1,0:T(8,128)(2,1)S(1)}, bf16[224,768]{1,0:T(8,128)(2,1)S(1)}, u32[]{:S(2)}, u32[]{:S(2)}) collective-permute-start(bf16[224,768]{1,0:T(8,128)(2,1)S(1)} %get-tuple-element.25), channel_id=1, source_target_pairs={{0,8},{8,0},{1,9},{9,1},{2,10},{10,2},{3,11},{11,3},{4,12},{12,4},... | collective-permute-start | bytes 1032200 | tf_op jit(solution)/shard_map/ppermute | solution.py:478
  9.2 15.2 %collective-permute-start.2 = (bf16[224,768]{1,0:T(8,128)(2,1)S(1)}, bf16[224,768]{1,0:T(8,128)(2,1)S(1)}, u32[]{:S(2)}, u32[]{:S(2)}) collective-permute-start(bf16[224,768]{1,0:T(8,128)(2,1)S(1)} %get-tuple-element.27), channel_id=1, source_target_pairs={{0,24},{8,16},{16,8},{24,0},{1,25},{9,17},{17,9},{25,1},{2,26},{10... | collective-permute-start | bytes 1032200 | tf_op jit(solution)/shard_map/ppermute | solution.py:478
  9.2 21.5 %collective-permute-start.3 = (bf16[368,768]{1,0:T(8,128)(2,1)S(1)}, bf16[368,768]{1,0:T(8,128)(2,1)S(1)}, u32[]{:S(2)}, u32[]{:S(2)}) collective-permute-start(bf16[368,768]{1,0:T(8,128)(2,1)S(1)} %get-tuple-element.24.refs_0_), channel_id=1, source_target_pairs={{0,4},{4,0},{1,5},{5,1},{2,6},{6,2},{3,7},{7,3},{8,12},{12,8},{9,1... | collective-permute-start | bytes 1695752 | tf_op jit(solution)/shard_map/ppermute | solution.py:478
  13.1 13.1 %collective-permute-start.8 = (bf16[144,768]{1,0:T(8,128)(2,1)S(1)}, bf16[144,768]{1,0:T(8,128)(2,1)S(1)}, u32[]{:S(2)}, u32[]{:S(2)}) collective-permute-start(bf16[144,768]{1,0:T(8,128)(2,1)S(1)} %collective-permute-done.1.refs_2_.refs_3_), channel_id=1, source_target_pairs={{0,1},{1,0},{2,3},{3,2},{4,5},{5,4},{6,7},{7,6},{8,9},{9,8},{10,11... | collective-permute-start | bytes 663560 | tf_op jit(solution)/shard_map/ppermute | solution.py:482
  14.9 11.3 %collective-permute-start.5 = (bf16[144,768]{1,0:T(8,128)(2,1)S(1)}, bf16[144,768]{1,0:T(8,128)(2,1)S(1)}, u32[]{:S(2)}, u32[]{:S(2)}) collective-permute-start(bf16[144,768]{1,0:T(8,128)(2,1)S(1)} %collective-permute-done.1.refs_2_.refs_3_), channel_id=1, source_target_pairs={{0,4},{4,0},{1,5},{5,1},{2,6},{6,2},{3,7},{7,3},{8,12},{12,8},{9,1... | collective-permute-start | bytes 663560 | tf_op jit(solution)/shard_map/ppermute | solution.py:478
  18.7 8.0 %collective-permute-start.7 = (bf16[144,768]{1,0:T(8,128)(2,1)S(1)}, bf16[144,768]{1,0:T(8,128)(2,1)S(1)}, u32[]{:S(2)}, u32[]{:S(2)}) collective-permute-start(bf16[144,768]{1,0:T(8,128)(2,1)S(1)} %slice.8), channel_id=1, source_target_pairs={{0,1},{1,0},{2,3},{3,2},{4,5},{5,4},{6,7},{7,6},{8,9},{9,8},{10,11... | collective-permute-start | bytes 663560 | tf_op jit(solution)/shard_map/ppermute | solution.py:482
  24.4 6.4 %collective-permute-start.9 = (bf16[144,768]{1,0:T(8,128)(2,1)S(1)}, bf16[144,768]{1,0:T(8,128)(2,1)S(1)}, u32[]{:S(2)}, u32[]{:S(2)}) collective-permute-start(bf16[144,768]{1,0:T(8,128)(2,1)S(1)} %slice.9), channel_id=1, source_target_pairs={{0,1},{1,0},{2,3},{3,2},{4,5},{5,4},{6,7},{7,6},{8,9},{9,8},{10,11... | collective-permute-start | bytes 663560 | tf_op jit(solution)/shard_map/ppermute | solution.py:482
  26.2 5.1 %collective-permute-start.4 = (bf16[224,768]{1,0:T(8,128)(2,1)S(1)}, bf16[224,768]{1,0:T(8,128)(2,1)S(1)}, u32[]{:S(2)}, u32[]{:S(2)}) collective-permute-start(bf16[224,768]{1,0:T(8,128)(2,1)S(1)} %collective-permute-done.refs_1_.refs_2_), channel_id=1, source_target_pairs={{0,4},{4,0},{1,5},{5,1},{2,6},{6,2},{3,7},{7,3},{8,12},{12,8},{9,1... | collective-permute-start | bytes 1032200 | tf_op jit(solution)/shard_map/ppermute | solution.py:478
  26.2 5.1 %collective-permute-start.6 = (bf16[224,768]{1,0:T(8,128)(2,1)S(1)}, bf16[224,768]{1,0:T(8,128)(2,1)S(1)}, u32[]{:S(2)}, u32[]{:S(2)}) collective-permute-start(bf16[224,768]{1,0:T(8,128)(2,1)S(1)} %collective-permute-done.2.refs_3_.refs_4_), channel_id=1, source_target_pairs={{0,4},{4,0},{1,5},{5,1},{2,6},{6,2},{3,7},{7,3},{8,12},{12,8},{9,1... | collective-permute-start | bytes 1032200 | tf_op jit(solution)/shard_map/ppermute | solution.py:478
  26.7 5.5 %collective-permute-start.11 = (bf16[144,768]{1,0:T(8,128)(2,1)S(1)}, bf16[144,768]{1,0:T(8,128)(2,1)S(1)}, u32[]{:S(2)}, u32[]{:S(2)}) collective-permute-start(bf16[144,768]{1,0:T(8,128)(2,1)S(1)} %collective-permute-done.8.refs_9_), channel_id=1, source_target_pairs={{0,4},{4,0},{1,5},{5,1},{2,6},{6,2},{3,7},{7,3},{8,12},{12,8},{9,1... | collective-permute-start | bytes 663560 | tf_op jit(solution)/shard_map/ppermute | solution.py:478
  30.7 1.5 %collective-permute-start.10 = (bf16[144,768]{1,0:T(8,128)(2,1)S(1)}, bf16[144,768]{1,0:T(8,128)(2,1)S(1)}, u32[]{:S(2)}, u32[]{:S(2)}) collective-permute-start(bf16[144,768]{1,0:T(8,128)(2,1)S(1)} %collective-permute-done.7.refs_8_), channel_id=1, source_target_pairs={{0,4},{4,0},{1,5},{5,1},{2,6},{6,2},{3,7},{7,3},{8,12},{12,8},{9,1... | collective-permute-start | bytes 663560 | tf_op jit(solution)/shard_map/ppermute | solution.py:478
  30.7 1.8 %collective-permute-start.12 = (bf16[144,768]{1,0:T(8,128)(2,1)S(1)}, bf16[144,768]{1,0:T(8,128)(2,1)S(1)}, u32[]{:S(2)}, u32[]{:S(2)}) collective-permute-start(bf16[144,768]{1,0:T(8,128)(2,1)S(1)} %collective-permute-done.9.refs_10_), channel_id=1, source_target_pairs={{0,4},{4,0},{1,5},{5,1},{2,6},{6,2},{3,7},{7,3},{8,12},{12,8},{9,1... | collective-permute-start | bytes 663560 | tf_op jit(solution)/shard_map/ppermute | solution.py:478
  36.3 2.1 %collective-permute-start.13 = (bf16[4,96,768]{2,1,0:T(8,128)(2,1)S(1)}, bf16[4,96,768]{2,1,0:T(8,128)(2,1)S(1)}, u32[]{:S(2)}, u32[]{:S(2)}) collective-permute-start(bf16[4,96,768]{2,1,0:T(8,128)(2,1)S(1)} %get-tuple-element.37), channel_id=1, source_target_pairs={{0,4},{4,0},{1,5},{5,1},{2,6},{6,2},{3,7},{7,3},{8,12},{12,8},{9,1... | collective-permute-start | bytes 1769480 | tf_op jit(solution)/shard_map/ppermute | solution.py:478
  38.5 7.7 %collective-permute-start.14 = (bf16[96,768]{1,0:T(8,128)(2,1)S(1)}, bf16[96,768]{1,0:T(8,128)(2,1)S(1)}, u32[]{:S(2)}, u32[]{:S(2)}) collective-permute-start(bf16[96,768]{1,0:T(8,128)(2,1)S(1)} %get-tuple-element.39), channel_id=1, source_target_pairs={{0,24},{8,16},{16,8},{24,0},{1,25},{9,17},{17,9},{25,1},{2,26},{10... | collective-permute-start | bytes 442376 | tf_op jit(solution)/shard_map/ppermute | solution.py:478
  40.9 7.7 %collective-permute-start.15 = (bf16[96,768]{1,0:T(8,128)(2,1)S(1)}, bf16[96,768]{1,0:T(8,128)(2,1)S(1)}, u32[]{:S(2)}, u32[]{:S(2)}) collective-permute-start(bf16[96,768]{1,0:T(8,128)(2,1)S(1)} %get-tuple-element.40), channel_id=1, source_target_pairs={{0,16},{16,0},{1,17},{17,1},{2,18},{18,2},{3,19},{19,3},{4,20},{20... | collective-permute-start | bytes 442376 | tf_op jit(solution)/shard_map/ppermute | solution.py:478
  41.4 7.2 %collective-permute-start.16 = (bf16[96,768]{1,0:T(8,128)(2,1)S(1)}, bf16[96,768]{1,0:T(8,128)(2,1)S(1)}, u32[]{:S(2)}, u32[]{:S(2)}) collective-permute-start(bf16[96,768]{1,0:T(8,128)(2,1)S(1)} %get-tuple-element.41), channel_id=1, source_target_pairs={{0,8},{8,0},{1,9},{9,1},{2,10},{10,2},{3,11},{11,3},{4,12},{12,4},... | collective-permute-start | bytes 442376 | tf_op jit(solution)/shard_map/ppermute | solution.py:478
  48.7 6.0 %collective-permute-start.17 = (bf16[48,384]{1,0:T(8,128)(2,1)S(1)}, bf16[48,384]{1,0:T(8,128)(2,1)S(1)}, u32[]{:S(2)}, u32[]{:S(2)}) collective-permute-start(bf16[48,384]{1,0:T(8,128)(2,1)S(1)} %get-tuple-element.43), channel_id=1, source_target_pairs={{0,3},{1,2},{2,1},{3,0},{4,7},{5,6},{6,5},{7,4},{8,11},{9,10},{10,... | collective-permute-start | bytes 110600 | tf_op jit(solution)/shard_map/ppermute | solution.py:482
  52.3 4.9 %collective-permute-start.18 = (bf16[48,384]{1,0:T(8,128)(2,1)S(1)}, bf16[48,384]{1,0:T(8,128)(2,1)S(1)}, u32[]{:S(2)}, u32[]{:S(2)}) collective-permute-start(bf16[48,384]{1,0:T(8,128)(2,1)S(1)} %get-tuple-element.44), channel_id=1, source_target_pairs={{0,2},{1,3},{2,0},{3,1},{4,6},{5,7},{6,4},{7,5},{8,10},{9,11},{10,... | collective-permute-start | bytes 110600 | tf_op jit(solution)/shard_map/ppermute | solution.py:482
  52.3 4.9 %collective-permute-start.19 = (bf16[48,384]{1,0:T(8,128)(2,1)S(1)}, bf16[48,384]{1,0:T(8,128)(2,1)S(1)}, u32[]{:S(2)}, u32[]{:S(2)}) collective-permute-start(bf16[48,384]{1,0:T(8,128)(2,1)S(1)} %get-tuple-element.45), channel_id=1, source_target_pairs={{0,1},{1,0},{2,3},{3,2},{4,5},{5,4},{6,7},{7,6},{8,9},{9,8},{10,11... | collective-permute-start | bytes 110600 | tf_op jit(solution)/shard_map/ppermute | solution.py:482

commit v8 on v7

--- a/solution.py
+++ b/solution.py
@@ -91,27 +91,30 @@
 
 
 def prep_kernel(
-    narrow_ref, broad_ref, small_ref,
-    own_ref, x_ref, y_ref, d_ref,
+    narrow_ref, broad_ref, embed_ref, bases_ref, lengths_ref,
+    own_ref, x_ref, y_ref, d_ref, small_ref,
 ):
     me, odd = position(), lax.axis_index("dp") & 1
-    count = small_ref[5:6, 0:128]
+    cap = bases_ref.shape[1]
+    count = jnp.broadcast_to(lengths_ref[...], (1, 128)).astype(F32)
+    small_ref[0:4] = embed_ref[...]
+    small_ref[4:5, 0:cap] = bases_ref[...].astype(F32)
+    small_ref[5:6, 0:128] = count
     width = narrow_ref.shape[1]
     chans = 2 * width
     shard = narrow_ref.shape[0] // 6
     prows = width // 8
-    cap = broad_ref.shape[0] - 2 * prows
     half = 3 * shard // 2
     cut = half - 16
     flat = narrow_ref.at[3 * shard : 6 * shard]
     cot = broad_ref[2 * prows :]
     pick = (iota((chans, shard), 0) == iota((chans, shard), 1) + me * shard).astype(BF16)
     taps = [narrow_ref[k * shard : (k + 1) * shard] for k in range(3)]
-    first, second = base_tables(small_ref[0:4], pick, taps)
+    first, second = base_tables(embed_ref[...], pick, taps)
     f_high, f_low = split(first)
     info = jnp.concatenate(
         [
-            small_ref[4:5, 0:cap],
+            bases_ref[...].astype(F32),
             count,
             jnp.zeros((1, chans - cap - 128), F32),
         ],
@@ -519,16 +522,16 @@
     half = 3 * c2.shape[1] // 2
     narrow = jnp.concatenate([c1.reshape(-1, width), c2.reshape(-1, width)], axis=0)
     broad = jnp.concatenate([p2, p1, cot], axis=0)
-    small = lines(embed, bases, lengths)
-    own, to_x, to_y, to_d = call(
+    own, to_x, to_y, to_d, small = call(
         prep_kernel,
         [
             ((2 * half + HALO, chans), BF16),
             ((half + HALO, chans), BF16),
             ((half, chans), BF16),
             ((half + HALO, chans), BF16),
+            ((8, chans), F32),
         ],
-        [narrow, broad, small],
+        [narrow, broad, embed, bases, lengths],
     )
     plane = [flip_move(to_x, "x"), flip_move(to_y, "y"), flip_move(to_d, "y", "x")]
     other = [xor_move(a[:half], "dp", 1) for a in plane]

time: 58.1 us -> 57.3 us (0.986)
  local copies, waits for them, and re-layouts: 0.7 us -> 0.04 us
    pad x1 -> x0, local copies, waits for them, and re-layouts: 0.67 us -> none  [lines(): line = jnp.pad(bases, ((0, 0), (0, chans - cap)))]
where the time goes in v8:
time: 57.3 us; the launch traced here: 57.1 us
  waiting for transfers between devices  26.7 us (47%)
  starting transfers between devices  19.2 us (34%)
  Pallas kernels  7.62 us (13%)
  other arithmetic  2.13 us (4%)
  between operations  1.4 us (2%)
    ppermute x14, waiting for transfers between devices, flip_move(): return lax.ppermute(array, axes, [(i, size - 1 - i) for i in range(size)])  20.4 us
    ppermute x6, starting transfers between devices, xor_move(): lax.ppermute(array, axis, [(i, i ^ bits) for i in range(lax.axis_size(axi...  9.68 us
    ppermute x14, starting transfers between devices, flip_move(): return lax.ppermute(array, axes, [(i, size - 1 - i) for i in range(size)])  9.49 us
    pallas_call x7, Pallas kernels, call(): pl.pallas_call(body, out_shape=[jax.ShapeDtypeStruct(s, d) for s, d in ou...  7.62 us
    ppermute x6, waiting for transfers between devices, xor_move(): lax.ppermute(array, axis, [(i, i ^ bits) for i in range(lax.axis_size(axi...  6.39 us
  transfers between devices with their start and end apart: 20, of which 9 were waited for; matrix products, arithmetic and copies ran while one was open for 0% of the time, Pallas kernels for 4%

profile of v8, /device:TPU:0, one launch (start us, length us, event | category | flops | bytes accessed | tf_op | source)
XLA Modules:
  0.0 57.1 jit_solution(12172187912574298709)
XLA Ops:
  1.3 1.1 %pad_maximum_fusion.narrow_ref = bf16[576,384]{1,0:T(8,128)(2,1)S(1)} fusion(bf16[288,384]{1,0:T(8,128)(2,1)} %bitcast.5, bf16[288,384]{1,0:T(8,128)(2,1)} %bitcast.6), kind=kLoop, calls=%fused_computation | loop fusion | flops 884736 | bytes 884736 | tf_op jit(solution)/shard_map/concatenate | solution.py:523
  2.4 1.0 %pad_maximum_fusion.1.broad_ref.refs_8_ = bf16[224,768]{1,0:T(8,128)(2,1)S(1)} fusion(bf16[128,768]{1,0:T(8,128)(2,1)} %bitcast.7, bf16[48,768]{1,0:T(8,128)(2,1)} %param.12, bf16[48,768]{1,0:T(8,128)(2,1)} %param.14), kind=kLoop, calls=%fused_computation.1 | loop fusion | flops 1032192 | bytes 688128 | tf_op jit(solution)/shard_map/concatenate | solution.py:524
  3.5 0.4 shard_map.95
  3.9 3.0 %collective-permute-start.1 = (bf16[144,768]{1,0:T(8,128)(2,1)S(1)}, bf16[144,768]{1,0:T(8,128)(2,1)S(1)}, u32[]{:S(2)}, u32[]{:S(2)}) collective-permute-start(bf16[144,768]{1,0:T(8,128)(2,1)S(1)} %get-tuple-element.28), channel_id=1, source_target_pairs={{0,16},{16,0},{1,17},{17,1},{2,18},{18,2},{3,19},{19,3},{4,20},{20... | collective-permute-start | bytes 663560 | tf_op jit(solution)/shard_map/ppermute | solution.py:481
  6.9 1.5 %collective-permute-start = (bf16[224,768]{1,0:T(8,128)(2,1)S(1)}, bf16[224,768]{1,0:T(8,128)(2,1)S(1)}, u32[]{:S(2)}, u32[]{:S(2)}) collective-permute-start(bf16[224,768]{1,0:T(8,128)(2,1)S(1)} %get-tuple-element.27), channel_id=1, source_target_pairs={{0,8},{8,0},{1,9},{9,1},{2,10},{10,2},{3,11},{11,3},{4,12},{12,4},... | collective-permute-start | bytes 1032200 | tf_op jit(solution)/shard_map/ppermute | solution.py:481
  8.4 0.0 collective-permute-start.2
  8.5 0.0 collective-permute-start.3
  8.5 3.9 %collective-permute-done.1.refs_2_.refs_3_ = bf16[144,768]{1,0:T(8,128)(2,1)S(1)} collective-permute-done((bf16[144,768]{1,0:T(8,128)(2,1)S(1)}, bf16[144,768]{1,0:T(8,128)(2,1)S(1)}, u32[]{:S(2)}, u32[]{:S(2)}) %collective-permute-start.1) | collective-permute-done | bytes 221216 | tf_op jit(solution)/shard_map/ppermute | solution.py:481
  12.4 1.8 %collective-permute-start.8 = (bf16[144,768]{1,0:T(8,128)(2,1)S(1)}, bf16[144,768]{1,0:T(8,128)(2,1)S(1)}, u32[]{:S(2)}, u32[]{:S(2)}) collective-permute-start(bf16[144,768]{1,0:T(8,128)(2,1)S(1)} %collective-permute-done.1.refs_2_.refs_3_), channel_id=1, source_target_pairs={{0,1},{1,0},{2,3},{3,2},{4,5},{5,4},{6,7},{7,6},{8,9},{9,8},{10,11... | collective-permute-start | bytes 663560 | tf_op jit(solution)/shard_map/ppermute | solution.py:485
  14.2 0.0 collective-permute-start.5
  14.2 3.8 %collective-permute-done.refs_1_.refs_2_ = bf16[224,768]{1,0:T(8,128)(2,1)S(1)} collective-permute-done((bf16[224,768]{1,0:T(8,128)(2,1)S(1)}, bf16[224,768]{1,0:T(8,128)(2,1)S(1)}, u32[]{:S(2)}, u32[]{:S(2)}) %collective-permute-start) | collective-permute-done | bytes 344096 | tf_op jit(solution)/shard_map/ppermute | solution.py:481
  17.9 1.6 %collective-permute-start.7 = (bf16[144,768]{1,0:T(8,128)(2,1)S(1)}, bf16[144,768]{1,0:T(8,128)(2,1)S(1)}, u32[]{:S(2)}, u32[]{:S(2)}) collective-permute-start(bf16[144,768]{1,0:T(8,128)(2,1)S(1)} %slice.8), channel_id=1, source_target_pairs={{0,1},{1,0},{2,3},{3,2},{4,5},{5,4},{6,7},{7,6},{8,9},{9,8},{10,11... | collective-permute-start | bytes 663560 | tf_op jit(solution)/shard_map/ppermute | solution.py:485
  19.6 4.0 %collective-permute-done.2.refs_3_.refs_4_ = bf16[224,768]{1,0:T(8,128)(2,1)S(1)} collective-permute-done((bf16[224,768]{1,0:T(8,128)(2,1)S(1)}, bf16[224,768]{1,0:T(8,128)(2,1)S(1)}, u32[]{:S(2)}, u32[]{:S(2)}) %collective-permute-start.2) | collective-permute-done | bytes 344096 | tf_op jit(solution)/shard_map/ppermute | solution.py:481
  23.6 1.8 %collective-permute-start.9 = (bf16[144,768]{1,0:T(8,128)(2,1)S(1)}, bf16[144,768]{1,0:T(8,128)(2,1)S(1)}, u32[]{:S(2)}, u32[]{:S(2)}) collective-permute-start(bf16[144,768]{1,0:T(8,128)(2,1)S(1)} %slice.9), channel_id=1, source_target_pairs={{0,1},{1,0},{2,3},{3,2},{4,5},{5,4},{6,7},{7,6},{8,9},{9,8},{10,11... | collective-permute-start | bytes 663560 | tf_op jit(solution)/shard_map/ppermute | solution.py:485
  25.4 0.0 collective-permute-done.8.refs_9_
  25.4 0.0 collective-permute-start.4
  25.4 0.0 collective-permute-done.5.refs_6_
  25.4 0.5 collective-permute-start.6
  26.0 0.0 collective-permute-done.7.refs_8_
  26.0 0.1 collective-permute-start.11
  26.0 4.0 %collective-permute-done.9.refs_10_ = bf16[144,768]{1,0:T(8,128)(2,1)S(1)} collective-permute-done((bf16[144,768]{1,0:T(8,128)(2,1)S(1)}, bf16[144,768]{1,0:T(8,128)(2,1)S(1)}, u32[]{:S(2)}, u32[]{:S(2)}) %collective-permute-start.9) | collective-permute-done | bytes 221216 | tf_op jit(solution)/shard_map/ppermute | solution.py:485
  30.0 0.0 collective-permute-start.10
  30.0 0.0 collective-permute-done.3.refs_4_.refs_1_
  30.0 0.5 collective-permute-start.12
  30.5 0.0 collective-permute-done.4.refs_5_
  30.5 0.0 collective-permute-done.6.refs_7_
  30.5 0.9 %shard_map.96 = (bf16[416,128]{1,0:T(8,128)(2,1)S(1)}, bf16[416,128]{1,0:T(8,128)(2,1)S(1)}, bf16[288,768]{1,0:T(8,128)(2,1)S(1)}) custom-call(bf16[368,768]{1,0:T(8,128)(2,1)S(1)} %get-tuple-element.26.refs_0_, bf16[224,768]{1,0:T(8,128)(2,1)S(1)} %collective-permute-done.refs_1_.refs_2_, bf16[144,768]{1,0:T(8,128)(2,1)S(1)} %collective-permute-done.1.refs_2_.refs_3_, ...), custom_call_target="tpu_custom_call" | custom-call | flops 1000000000 | bytes 1000000 | tf_op jit(solution)/shard_map/pallas_call | solution.py:61
  31.4 0.0 collective-permute-done.11.refs_12_
  31.5 0.0 collective-permute-done.10.refs_11_
  31.5 0.3 collective-permute-done.12.refs_13_
  31.8 3.8 %shard_map.97 = (f32[4,96,768]{2,1,0:T(8,128)S(1)}, bf16[4,96,768]{2,1,0:T(8,128)(2,1)S(1)}, bf16[256,384]{1,0:T(8,128)(2,1)S(1)}, bf16[320,768]{1,0:T(8,128)(2,...) custom-call(bf16[368,768]{1,0:T(8,128)(2,1)S(1)} %get-tuple-element.26.refs_0_, ...), custom_call_target="tpu_custom_call" | custom-call | flops 4000000000 | bytes 1000000 | tf_op jit(solution)/shard_map/pallas_call | solution.py:61
  35.6 0.3 collective-permute-start.13
  35.9 1.8 %collective-permute-done.13.recv_ref = bf16[4,96,768]{2,1,0:T(8,128)(2,1)S(1)} collective-permute-done((bf16[4,96,768]{2,1,0:T(8,128)(2,1)S(1)}, bf16[4,96,768]{2,1,0:T(8,128)(2,1)S(1)}, u32[]{:S(2)}, u32[]{:S(2)}) %collective-permute-start.13) | collective-permute-done | bytes 589856 | tf_op jit(solution)/shard_map/ppermute | solution.py:481
  37.7 0.1 shard_map.99
  37.8 2.3 %collective-permute-start.14 = (bf16[96,768]{1,0:T(8,128)(2,1)S(1)}, bf16[96,768]{1,0:T(8,128)(2,1)S(1)}, u32[]{:S(2)}, u32[]{:S(2)}) collective-permute-start(bf16[96,768]{1,0:T(8,128)(2,1)S(1)} %get-tuple-element.41), channel_id=1, source_target_pairs={{0,24},{8,16},{16,8},{24,0},{1,25},{9,17},{17,9},{25,1},{2,26},{10... | collective-permute-start | bytes 442376 | tf_op jit(solution)/shard_map/ppermute | solution.py:481
  40.2 0.5 collective-permute-start.15
  40.7 0.7 %collective-permute-start.16 = (bf16[96,768]{1,0:T(8,128)(2,1)S(1)}, bf16[96,768]{1,0:T(8,128)(2,1)S(1)}, u32[]{:S(2)}, u32[]{:S(2)}) collective-permute-start(bf16[96,768]{1,0:T(8,128)(2,1)S(1)} %get-tuple-element.43), channel_id=1, source_target_pairs={{0,8},{8,0},{1,9},{9,1},{2,10},{10,2},{3,11},{11,3},{4,12},{12,4},... | collective-permute-start | bytes 442376 | tf_op jit(solution)/shard_map/ppermute | solution.py:481
  41.4 4.1 %collective-permute-done.14.d_ref = bf16[96,768]{1,0:T(8,128)(2,1)S(1)} collective-permute-done((bf16[96,768]{1,0:T(8,128)(2,1)S(1)}, bf16[96,768]{1,0:T(8,128)(2,1)S(1)}, u32[]{:S(2)}, u32[]{:S(2)}) %collective-permute-start.14) | collective-permute-done | bytes 147488 | tf_op jit(solution)/shard_map/ppermute | solution.py:481
  45.5 2.4 %collective-permute-done.15.y_ref = bf16[96,768]{1,0:T(8,128)(2,1)S(1)} collective-permute-done((bf16[96,768]{1,0:T(8,128)(2,1)S(1)}, bf16[96,768]{1,0:T(8,128)(2,1)S(1)}, u32[]{:S(2)}, u32[]{:S(2)}) %collective-permute-start.15) | collective-permute-done | bytes 147488 | tf_op jit(solution)/shard_map/ppermute | solution.py:481
  47.9 0.0 collective-permute-done.16.x_ref
  47.9 0.1 shard_map.100
  48.0 3.6 %collective-permute-start.17 = (bf16[48,384]{1,0:T(8,128)(2,1)S(1)}, bf16[48,384]{1,0:T(8,128)(2,1)S(1)}, u32[]{:S(2)}, u32[]{:S(2)}) collective-permute-start(bf16[48,384]{1,0:T(8,128)(2,1)S(1)} %get-tuple-element.45), channel_id=1, source_target_pairs={{0,3},{1,2},{2,1},{3,0},{4,7},{5,6},{6,5},{7,4},{8,11},{9,10},{10,... | collective-permute-start | bytes 110600 | tf_op jit(solution)/shard_map/ppermute | solution.py:485
  51.6 0.0 collective-permute-start.18
  51.6 0.9 %collective-permute-start.19 = (bf16[48,384]{1,0:T(8,128)(2,1)S(1)}, bf16[48,384]{1,0:T(8,128)(2,1)S(1)}, u32[]{:S(2)}, u32[]{:S(2)}) collective-permute-start(bf16[48,384]{1,0:T(8,128)(2,1)S(1)} %get-tuple-element.47), channel_id=1, source_target_pairs={{0,1},{1,0},{2,3},{3,2},{4,5},{5,4},{6,7},{7,6},{8,9},{9,8},{10,11... | collective-permute-start | bytes 110600 | tf_op jit(solution)/shard_map/ppermute | solution.py:485
  52.5 1.6 %shard_map.98 = f32[4,128]{1,0:T(4,128)} custom-call(f32[8,768]{1,0:T(8,128)S(1)} %get-tuple-element.25.refs_14_.small_ref, bf16[416,128]{1,0:T(8,128)(2,1)S(1)} %get-tuple-element.30.refs_16_.hot_f_ref, bf16[416,128]{1,0:T(8,128)(2,1)S(1)} %get-tuple-element.31.refs_17_.hot_r_ref, bf16[256,384]{1,0:T(8,128)(2,1)S(1)} %get-tuple-element.33.s1_ref, ...), custom_call_target="tpu_custom_call" | custom-call | flops 1000000000 | bytes 1000000 | tf_op jit(solution)/shard_map/pallas_call | solution.py:61
  54.1 2.4 %collective-permute-done.18.refs_1_ = bf16[48,384]{1,0:T(8,128)(2,1)S(1)} collective-permute-done((bf16[48,384]{1,0:T(8,128)(2,1)S(1)}, bf16[48,384]{1,0:T(8,128)(2,1)S(1)}, u32[]{:S(2)}, u32[]{:S(2)}) %collective-permute-start.18) | collective-permute-done | bytes 36896 | tf_op jit(solution)/shard_map/ppermute | solution.py:485
  56.5 0.0 collective-permute-done.19.refs_2_
  56.5 0.7 %shard_map.101 = f32[144,128]{1,0:T(8,128)} custom-call(f32[48,384]{1,0:T(8,128)S(1)} %get-tuple-element.44.mine_ref, bf16[48,384]{1,0:T(8,128)(2,1)S(1)} %collective-permute-done.17.refs_0_, bf16[48,384]{1,0:T(8,128)(2,1)S(1)} %collective-permute-done.18.refs_1_, bf16[48,384]{1,0:T(8,128)(2,1)S(1)} %collective-permute-done.19.refs_2_), custom_call_target="tpu_custom_call" | custom-call | tf_op jit(solution)/shard_map/pallas_call | solution.py:61
  (7 shorter events, 0.0 us)
Async XLA Ops:
  0.6 2.8 %copy-start = (f32[4,768]{1,0:T(4,128)S(1)}, f32[4,768]{1,0:T(4,128)}, u32[]{:S(2)}) copy-start(f32[4,768]{1,0:T(4,128)} %embed_ref.1) | copy-start | bytes 36868
  0.6 2.8 %copy-start.1 = (s32[1,128]{1,0:T(1,128)S(1)}, s32[1,128]{1,0:T(1,128)}, u32[]{:S(2)}) copy-start(s32[1,128]{1,0:T(1,128)} %bases_ref.1) | copy-start | bytes 1540
  3.9 8.5 %collective-permute-start.1 = (bf16[144,768]{1,0:T(8,128)(2,1)S(1)}, bf16[144,768]{1,0:T(8,128)(2,1)S(1)}, u32[]{:S(2)}, u32[]{:S(2)}) collective-permute-start(bf16[144,768]{1,0:T(8,128)(2,1)S(1)} %get-tuple-element.28), channel_id=1, source_target_pairs={{0,16},{16,0},{1,17},{17,1},{2,18},{18,2},{3,19},{19,3},{4,20},{20... | collective-permute-start | bytes 663560 | tf_op jit(solution)/shard_map/ppermute | solution.py:481
  6.9 11.0 %collective-permute-start = (bf16[224,768]{1,0:T(8,128)(2,1)S(1)}, bf16[224,768]{1,0:T(8,128)(2,1)S(1)}, u32[]{:S(2)}, u32[]{:S(2)}) collective-permute-start(bf16[224,768]{1,0:T(8,128)(2,1)S(1)} %get-tuple-element.27), channel_id=1, source_target_pairs={{0,8},{8,0},{1,9},{9,1},{2,10},{10,2},{3,11},{11,3},{4,12},{12,4},... | collective-permute-start | bytes 1032200 | tf_op jit(solution)/shard_map/ppermute | solution.py:481
  8.4 15.2 %collective-permute-start.2 = (bf16[224,768]{1,0:T(8,128)(2,1)S(1)}, bf16[224,768]{1,0:T(8,128)(2,1)S(1)}, u32[]{:S(2)}, u32[]{:S(2)}) collective-permute-start(bf16[224,768]{1,0:T(8,128)(2,1)S(1)} %get-tuple-element.29), channel_id=1, source_target_pairs={{0,24},{8,16},{16,8},{24,0},{1,25},{9,17},{17,9},{25,1},{2,26},{10... | collective-permute-start | bytes 1032200 | tf_op jit(solution)/shard_map/ppermute | solution.py:481
  8.5 21.5 %collective-permute-start.3 = (bf16[368,768]{1,0:T(8,128)(2,1)S(1)}, bf16[368,768]{1,0:T(8,128)(2,1)S(1)}, u32[]{:S(2)}, u32[]{:S(2)}) collective-permute-start(bf16[368,768]{1,0:T(8,128)(2,1)S(1)} %get-tuple-element.26.refs_0_), channel_id=1, source_target_pairs={{0,4},{4,0},{1,5},{5,1},{2,6},{6,2},{3,7},{7,3},{8,12},{12,8},{9,1... | collective-permute-start | bytes 1695752 | tf_op jit(solution)/shard_map/ppermute | solution.py:481
  12.4 13.1 %collective-permute-start.8 = (bf16[144,768]{1,0:T(8,128)(2,1)S(1)}, bf16[144,768]{1,0:T(8,128)(2,1)S(1)}, u32[]{:S(2)}, u32[]{:S(2)}) collective-permute-start(bf16[144,768]{1,0:T(8,128)(2,1)S(1)} %collective-permute-done.1.refs_2_.refs_3_), channel_id=1, source_target_pairs={{0,1},{1,0},{2,3},{3,2},{4,5},{5,4},{6,7},{7,6},{8,9},{9,8},{10,11... | collective-permute-start | bytes 663560 | tf_op jit(solution)/shard_map/ppermute | solution.py:485
  14.2 11.3 %collective-permute-start.5 = (bf16[144,768]{1,0:T(8,128)(2,1)S(1)}, bf16[144,768]{1,0:T(8,128)(2,1)S(1)}, u32[]{:S(2)}, u32[]{:S(2)}) collective-permute-start(bf16[144,768]{1,0:T(8,128)(2,1)S(1)} %collective-permute-done.1.refs_2_.refs_3_), channel_id=1, source_target_pairs={{0,4},{4,0},{1,5},{5,1},{2,6},{6,2},{3,7},{7,3},{8,12},{12,8},{9,1... | collective-permute-start | bytes 663560 | tf_op jit(solution)/shard_map/ppermute | solution.py:481
  17.9 8.0 %collective-permute-start.7 = (bf16[144,768]{1,0:T(8,128)(2,1)S(1)}, bf16[144,768]{1,0:T(8,128)(2,1)S(1)}, u32[]{:S(2)}, u32[]{:S(2)}) collective-permute-start(bf16[144,768]{1,0:T(8,128)(2,1)S(1)} %slice.8), channel_id=1, source_target_pairs={{0,1},{1,0},{2,3},{3,2},{4,5},{5,4},{6,7},{7,6},{8,9},{9,8},{10,11... | collective-permute-start | bytes 663560 | tf_op jit(solution)/shard_map/ppermute | solution.py:485
  23.6 6.4 %collective-permute-start.9 = (bf16[144,768]{1,0:T(8,128)(2,1)S(1)}, bf16[144,768]{1,0:T(8,128)(2,1)S(1)}, u32[]{:S(2)}, u32[]{:S(2)}) collective-permute-start(bf16[144,768]{1,0:T(8,128)(2,1)S(1)} %slice.9), channel_id=1, source_target_pairs={{0,1},{1,0},{2,3},{3,2},{4,5},{5,4},{6,7},{7,6},{8,9},{9,8},{10,11... | collective-permute-start | bytes 663560 | tf_op jit(solution)/shard_map/ppermute | solution.py:485
  25.4 5.1 %collective-permute-start.4 = (bf16[224,768]{1,0:T(8,128)(2,1)S(1)}, bf16[224,768]{1,0:T(8,128)(2,1)S(1)}, u32[]{:S(2)}, u32[]{:S(2)}) collective-permute-start(bf16[224,768]{1,0:T(8,128)(2,1)S(1)} %collective-permute-done.refs_1_.refs_2_), channel_id=1, source_target_pairs={{0,4},{4,0},{1,5},{5,1},{2,6},{6,2},{3,7},{7,3},{8,12},{12,8},{9,1... | collective-permute-start | bytes 1032200 | tf_op jit(solution)/shard_map/ppermute | solution.py:481
  25.4 5.1 %collective-permute-start.6 = (bf16[224,768]{1,0:T(8,128)(2,1)S(1)}, bf16[224,768]{1,0:T(8,128)(2,1)S(1)}, u32[]{:S(2)}, u32[]{:S(2)}) collective-permute-start(bf16[224,768]{1,0:T(8,128)(2,1)S(1)} %collective-permute-done.2.refs_3_.refs_4_), channel_id=1, source_target_pairs={{0,4},{4,0},{1,5},{5,1},{2,6},{6,2},{3,7},{7,3},{8,12},{12,8},{9,1... | collective-permute-start | bytes 1032200 | tf_op jit(solution)/shard_map/ppermute | solution.py:481
  26.0 5.5 %collective-permute-start.11 = (bf16[144,768]{1,0:T(8,128)(2,1)S(1)}, bf16[144,768]{1,0:T(8,128)(2,1)S(1)}, u32[]{:S(2)}, u32[]{:S(2)}) collective-permute-start(bf16[144,768]{1,0:T(8,128)(2,1)S(1)} %collective-permute-done.8.refs_9_), channel_id=1, source_target_pairs={{0,4},{4,0},{1,5},{5,1},{2,6},{6,2},{3,7},{7,3},{8,12},{12,8},{9,1... | collective-permute-start | bytes 663560 | tf_op jit(solution)/shard_map/ppermute | solution.py:481
  30.0 1.5 %collective-permute-start.10 = (bf16[144,768]{1,0:T(8,128)(2,1)S(1)}, bf16[144,768]{1,0:T(8,128)(2,1)S(1)}, u32[]{:S(2)}, u32[]{:S(2)}) collective-permute-start(bf16[144,768]{1,0:T(8,128)(2,1)S(1)} %collective-permute-done.7.refs_8_), channel_id=1, source_target_pairs={{0,4},{4,0},{1,5},{5,1},{2,6},{6,2},{3,7},{7,3},{8,12},{12,8},{9,1... | collective-permute-start | bytes 663560 | tf_op jit(solution)/shard_map/ppermute | solution.py:481
  30.0 1.8 %collective-permute-start.12 = (bf16[144,768]{1,0:T(8,128)(2,1)S(1)}, bf16[144,768]{1,0:T(8,128)(2,1)S(1)}, u32[]{:S(2)}, u32[]{:S(2)}) collective-permute-start(bf16[144,768]{1,0:T(8,128)(2,1)S(1)} %collective-permute-done.9.refs_10_), channel_id=1, source_target_pairs={{0,4},{4,0},{1,5},{5,1},{2,6},{6,2},{3,7},{7,3},{8,12},{12,8},{9,1... | collective-permute-start | bytes 663560 | tf_op jit(solution)/shard_map/ppermute | solution.py:481
  35.6 2.1 %collective-permute-start.13 = (bf16[4,96,768]{2,1,0:T(8,128)(2,1)S(1)}, bf16[4,96,768]{2,1,0:T(8,128)(2,1)S(1)}, u32[]{:S(2)}, u32[]{:S(2)}) collective-permute-start(bf16[4,96,768]{2,1,0:T(8,128)(2,1)S(1)} %get-tuple-element.39), channel_id=1, source_target_pairs={{0,4},{4,0},{1,5},{5,1},{2,6},{6,2},{3,7},{7,3},{8,12},{12,8},{9,1... | collective-permute-start | bytes 1769480 | tf_op jit(solution)/shard_map/ppermute | solution.py:481
  37.8 7.7 %collective-permute-start.14 = (bf16[96,768]{1,0:T(8,128)(2,1)S(1)}, bf16[96,768]{1,0:T(8,128)(2,1)S(1)}, u32[]{:S(2)}, u32[]{:S(2)}) collective-permute-start(bf16[96,768]{1,0:T(8,128)(2,1)S(1)} %get-tuple-element.41), channel_id=1, source_target_pairs={{0,24},{8,16},{16,8},{24,0},{1,25},{9,17},{17,9},{25,1},{2,26},{10... | collective-permute-start | bytes 442376 | tf_op jit(solution)/shard_map/ppermute | solution.py:481
  40.2 7.7 %collective-permute-start.15 = (bf16[96,768]{1,0:T(8,128)(2,1)S(1)}, bf16[96,768]{1,0:T(8,128)(2,1)S(1)}, u32[]{:S(2)}, u32[]{:S(2)}) collective-permute-start(bf16[96,768]{1,0:T(8,128)(2,1)S(1)} %get-tuple-element.42), channel_id=1, source_target_pairs={{0,16},{16,0},{1,17},{17,1},{2,18},{18,2},{3,19},{19,3},{4,20},{20... | collective-permute-start | bytes 442376 | tf_op jit(solution)/shard_map/ppermute | solution.py:481
  40.7 7.2 %collective-permute-start.16 = (bf16[96,768]{1,0:T(8,128)(2,1)S(1)}, bf16[96,768]{1,0:T(8,128)(2,1)S(1)}, u32[]{:S(2)}, u32[]{:S(2)}) collective-permute-start(bf16[96,768]{1,0:T(8,128)(2,1)S(1)} %get-tuple-element.43), channel_id=1, source_target_pairs={{0,8},{8,0},{1,9},{9,1},{2,10},{10,2},{3,11},{11,3},{4,12},{12,4},... | collective-permute-start | bytes 442376 | tf_op jit(solution)/shard_map/ppermute | solution.py:481
  48.0 6.0 %collective-permute-start.17 = (bf16[48,384]{1,0:T(8,128)(2,1)S(1)}, bf16[48,384]{1,0:T(8,128)(2,1)S(1)}, u32[]{:S(2)}, u32[]{:S(2)}) collective-permute-start(bf16[48,384]{1,0:T(8,128)(2,1)S(1)} %get-tuple-element.45), channel_id=1, source_target_pairs={{0,3},{1,2},{2,1},{3,0},{4,7},{5,6},{6,5},{7,4},{8,11},{9,10},{10,... | collective-permute-start | bytes 110600 | tf_op jit(solution)/shard_map/ppermute | solution.py:485
  51.6 4.9 %collective-permute-start.18 = (bf16[48,384]{1,0:T(8,128)(2,1)S(1)}, bf16[48,384]{1,0:T(8,128)(2,1)S(1)}, u32[]{:S(2)}, u32[]{:S(2)}) collective-permute-start(bf16[48,384]{1,0:T(8,128)(2,1)S(1)} %get-tuple-element.46), channel_id=1, source_target_pairs={{0,2},{1,3},{2,0},{3,1},{4,6},{5,7},{6,4},{7,5},{8,10},{9,11},{10,... | collective-permute-start | bytes 110600 | tf_op jit(solution)/shard_map/ppermute | solution.py:485
  51.6 4.9 %collective-permute-start.19 = (bf16[48,384]{1,0:T(8,128)(2,1)S(1)}, bf16[48,384]{1,0:T(8,128)(2,1)S(1)}, u32[]{:S(2)}, u32[]{:S(2)}) collective-permute-start(bf16[48,384]{1,0:T(8,128)(2,1)S(1)} %get-tuple-element.47), channel_id=1, source_target_pairs={{0,1},{1,0},{2,3},{3,2},{4,5},{5,4},{6,7},{7,6},{8,9},{9,8},{10,11... | collective-permute-start | bytes 110600 | tf_op jit(solution)/shard_map/ppermute | solution.py:485

commit v9 on v8

--- a/solution.py
+++ b/solution.py
@@ -92,7 +92,7 @@
 
 def prep_kernel(
     narrow_ref, broad_ref, embed_ref, bases_ref, lengths_ref,
-    own_ref, x_ref, y_ref, d_ref, small_ref,
+    own_ref, x_ref, y_ref, d_ref, edge_ref, small_ref,
 ):
     me, odd = position(), lax.axis_index("dp") & 1
     cap = bases_ref.shape[1]
@@ -135,12 +135,13 @@
     for out in (x_ref, y_ref, d_ref):
         out[0:half] = part
     ahead = (iota((HALO, cap), 1) - iota((HALO, cap), 0) + HALO).astype(F32)
-    take = (ahead == count).astype(BF16)
-    last = mm(take, cot).astype(BF16)
-    chip = me >> 1
-    own_ref[2 * half :] = jnp.where((me & 1) == 0, last, cot[0:HALO])
-    x_ref[half:] = jnp.where((chip ^ 1) > chip, last, cot[0:HALO])
-    d_ref[half:] = jnp.where((chip ^ 3) > chip, last, cot[0:HALO])
+    last = mm((ahead == count).astype(BF16), cot).astype(BF16)
+    chip, lower = me >> 1, (me & 1) == 0
+    own_ref[2 * half :] = jnp.where(lower, last, cot[0:HALO])
+    edge_ref[...] = jnp.where(lower, cot[0:HALO], last)
+    for out, bits in ((x_ref, 1), (d_ref, 3)):
+        upward = (chip ^ bits) > chip
+        out[half:] = jnp.where(upward, last[HALO - SPILL :], cot[0:SPILL])
 
 
 def context_body(info_at, cot, r1, r2, l1, l2, hot_f_ref, hot_r_ref, cx_ref):
@@ -206,8 +207,8 @@
 
 
 def context_kernel_packed(*refs):
-    parts, broad_ref, outs = refs[0:8], refs[8], refs[9:12]
-    info_ref, halo_ref = refs[12:]
+    parts, edge_ref, broad_ref, outs = refs[0:8], refs[8], refs[9], refs[10:13]
+    info_ref = refs[13]
     me, odd = position(), lax.axis_index("dp") & 1
     chip, core = me >> 1, me & 1
     chans = broad_ref.shape[1]
@@ -222,17 +223,14 @@
             high = part[half - 16 : half].astype(F32)[8:9, 0:256]
             low = jnp.where(odd == 0, low, high)
         info_ref[REACH + peer] = jnp.broadcast_to(low, (8, 256))
-    for n in range(2):
-        halo_ref[4 * n + chip] = parts[4 * n][2 * half :]
-        halo_ref[4 * n + (chip ^ 1)] = parts[4 * n + 1][half:]
-        halo_ref[4 * n + (chip ^ 3)] = parts[4 * n + 3][half:]
-    r1 = halo_ref[4 + jnp.maximum(chip + core - 1, 0)]
-    l1 = halo_ref[4 + jnp.minimum(chip + core, 3)]
-    r2 = halo_ref[jnp.maximum(chip - 1, 0)]
-    l2 = halo_ref[jnp.minimum(chip + 1, 3)]
+    odd_edge, even_edge = edge_ref[...], parts[4][2 * half :]
+    x_spill, d_spill = parts[1][half:], parts[3][half:]
+    r1 = jnp.where(core == 0, odd_edge, even_edge)
+    l1 = jnp.where(core == 0, even_edge, odd_edge)
+    r2 = jnp.where(chip == 2, d_spill, x_spill)
+    l2 = jnp.where(chip == 1, d_spill, x_spill)
     context_body(
-        lambda o: info_ref[me + (REACH + o)], broad_ref[2 * prow :], r1, r2[HALO - SPILL :], l1,
-        l2[0:SPILL], *outs,
+        lambda o: info_ref[me + (REACH + o)], broad_ref[2 * prow :], r1, r2, l1, l2, *outs,
     )
 
 
@@ -522,30 +520,34 @@
     half = 3 * c2.shape[1] // 2
     narrow = jnp.concatenate([c1.reshape(-1, width), c2.reshape(-1, width)], axis=0)
     broad = jnp.concatenate([p2, p1, cot], axis=0)
-    own, to_x, to_y, to_d, small = call(
+    own, to_x, to_y, to_d, edge, small = call(
         prep_kernel,
         [
             ((2 * half + HALO, chans), BF16),
-            ((half + HALO, chans), BF16),
+            ((half + SPILL, chans), BF16),
             ((half, chans), BF16),
-            ((half + HALO, chans), BF16),
+            ((half + SPILL, chans), BF16),
+            ((HALO, chans), BF16),
             ((8, chans), F32),
         ],
         [narrow, broad, embed, bases, lengths],
     )
     plane = [flip_move(to_x, "x"), flip_move(to_y, "y"), flip_move(to_d, "y", "x")]
-    other = [xor_move(a[:half], "dp", 1) for a in plane]
+    other = [xor_move(a, "dp", 1) for a in plane]
+    edge, _, _ = lax.optimization_barrier((edge, plane[0], plane[2]))
+    edge = lax.ppermute(
+        edge, ("y", "x", "core"), [(i, i + 2 * (i & 1) - 1) for i in range(1, 7)]
+    )
     across = lambda arrays: [flip_move(a, "core") for a in arrays]
     rows = chans // 8
-    swapped = across([own, *plane])
+    late, late_y, _ = lax.optimization_barrier((own, plane[1], other[1]))
+    late_x, late_d, _ = lax.optimization_barrier((plane[0], plane[2], other[0]))
+    swapped = across([late, late_x, late_y, late_d])
     hf, hr, cx = call(
         context_kernel_packed,
         context_shapes(cap, chans),
-        [own, *plane, *swapped, broad],
-        scratch=[
-            pltpu.VMEM((8 + 2 * REACH, 8, 256), F32),
-            pltpu.VMEM((8, HALO, chans), BF16),
-        ],
+        [own, *plane, *swapped, edge, broad],
+        scratch=[pltpu.VMEM((8 + 2 * REACH, 8, 256), F32)],
         cost=weight(10**9),
     )
     keep, send, s1, gb, g, second, p1_full = call(

time: 57.3 us -> 60.5 us (1.056)
  starting transfers between devices: 19.2 us -> 27.1 us
  waiting for transfers between devices: 26.7 us -> 22.1 us
    ppermute x14, starting transfers between devices: 9.49 us -> 18.8 us  [flip_move(): return lax.ppermute(array, axes, [(i, size - 1 - i) for i in range(size)])]
    ppermute x14, waiting for transfers between devices: 20.4 us -> 14.7 us  [flip_move(): return lax.ppermute(array, axes, [(i, size - 1 - i) for i in range(size)])]
    ppermute x6, starting transfers between devices: 9.68 us -> 7.65 us  [xor_move(): lax.ppermute(array, axis, [(i, i ^ bits) for i in range(lax.axis_size(axi...]
    ppermute x6, waiting for transfers between devices: 6.39 us -> 7.32 us  [xor_move(): lax.ppermute(array, axis, [(i, i ^ bits) for i in range(lax.axis_size(axi...]
    ppermute x0 -> x1, starting transfers between devices: none -> 0.66 us  [fast_shards(): lax.ppermute(edge, ('y', 'x', 'core'), [(i, i + 2 * (i & 1) - 1) for i in...]
  transfers between devices with their start and end apart: 20 -> 21, of which waited for: 9 -> 11; matrix products, arithmetic and copies ran while one was open for 0% -> 0% of each run, Pallas kernels for 4% -> 4%
where the time goes in v9:
time: 60.5 us; the launch traced here: 60.3 us
  starting transfers between devices  27.1 us (45%)
  waiting for transfers between devices  22.1 us (37%)
  Pallas kernels  7.58 us (13%)
  other arithmetic  2.13 us (4%)
  between operations  1.4 us (2%)
    ppermute x14, starting transfers between devices, flip_move(): return lax.ppermute(array, axes, [(i, size - 1 - i) for i in range(size)])  18.8 us
    ppermute x14, waiting for transfers between devices, flip_move(): return lax.ppermute(array, axes, [(i, size - 1 - i) for i in range(size)])  14.7 us
    ppermute x6, starting transfers between devices, xor_move(): lax.ppermute(array, axis, [(i, i ^ bits) for i in range(lax.axis_size(axi...  7.65 us
    pallas_call x7, Pallas kernels, call(): pl.pallas_call(body, out_shape=[jax.ShapeDtypeStruct(s, d) for s, d in ou...  7.58 us
    ppermute x6, waiting for transfers between devices, xor_move(): lax.ppermute(array, axis, [(i, i ^ bits) for i in range(lax.axis_size(axi...  7.32 us
  transfers between devices with their start and end apart: 21, of which 11 were waited for; matrix products, arithmetic and copies ran while one was open for 0% of the time, Pallas kernels for 4%

profile of v9, /device:TPU:0, one launch (start us, length us, event | category | flops | bytes accessed | tf_op | source)
XLA Modules:
  0.0 60.3 jit_solution(8995728505071787711)
XLA Ops:
  1.3 1.1 %pad_maximum_fusion.narrow_ref = bf16[576,384]{1,0:T(8,128)(2,1)S(1)} fusion(bf16[288,384]{1,0:T(8,128)(2,1)} %bitcast.5, bf16[288,384]{1,0:T(8,128)(2,1)} %bitcast.6), kind=kLoop, calls=%fused_computation | loop fusion | flops 884736 | bytes 884736 | tf_op jit(solution)/shard_map/concatenate | solution.py:521
  2.4 1.0 %pad_maximum_fusion.1.broad_ref.refs_9_ = bf16[224,768]{1,0:T(8,128)(2,1)S(1)} fusion(bf16[128,768]{1,0:T(8,128)(2,1)} %bitcast.7, bf16[48,768]{1,0:T(8,128)(2,1)} %param.12, bf16[48,768]{1,0:T(8,128)(2,1)} %param.14), kind=kLoop, calls=%fused_computation.1 | loop fusion | flops 1032192 | bytes 688128 | tf_op jit(solution)/shard_map/concatenate | solution.py:522
  3.5 0.4 shard_map.95
  3.9 3.0 %collective-permute-start.1 = (bf16[144,768]{1,0:T(8,128)(2,1)S(1)}, bf16[144,768]{1,0:T(8,128)(2,1)S(1)}, u32[]{:S(2)}, u32[]{:S(2)}) collective-permute-start(bf16[144,768]{1,0:T(8,128)(2,1)S(1)} %get-tuple-element.34), channel_id=1, source_target_pairs={{0,16},{16,0},{1,17},{17,1},{2,18},{18,2},{3,19},{19,3},{4,20},{20... | collective-permute-start | bytes 663560 | tf_op jit(solution)/shard_map/ppermute | solution.py:479
  6.9 1.5 %collective-permute-start = (bf16[160,768]{1,0:T(8,128)(2,1)S(1)}, bf16[160,768]{1,0:T(8,128)(2,1)S(1)}, u32[]{:S(2)}, u32[]{:S(2)}) collective-permute-start(bf16[160,768]{1,0:T(8,128)(2,1)S(1)} %get-tuple-element.33), channel_id=1, source_target_pairs={{0,8},{8,0},{1,9},{9,1},{2,10},{10,2},{3,11},{11,3},{4,12},{12,4},... | collective-permute-start | bytes 737288 | tf_op jit(solution)/shard_map/ppermute | solution.py:479
  8.4 3.9 %collective-permute-done.1.refs_2_.refs_3_ = bf16[144,768]{1,0:T(8,128)(2,1)S(1)} collective-permute-done((bf16[144,768]{1,0:T(8,128)(2,1)S(1)}, bf16[144,768]{1,0:T(8,128)(2,1)S(1)}, u32[]{:S(2)}, u32[]{:S(2)}) %collective-permute-start.1) | collective-permute-done | bytes 221216 | tf_op jit(solution)/shard_map/ppermute | solution.py:479
  12.4 1.8 %collective-permute-start.3 = (bf16[144,768]{1,0:T(8,128)(2,1)S(1)}, bf16[144,768]{1,0:T(8,128)(2,1)S(1)}, u32[]{:S(2)}, u32[]{:S(2)}) collective-permute-start(bf16[144,768]{1,0:T(8,128)(2,1)S(1)} %collective-permute-done.1.refs_2_.refs_3_), channel_id=1, source_target_pairs={{0,1},{1,0},{2,3},{3,2},{4,5},{5,4},{6,7},{7,6},{8,9},{9,8},{10,11... | collective-permute-start | bytes 663560 | tf_op jit(solution)/shard_map/ppermute | solution.py:483
  14.2 2.4 %collective-permute-start.2 = (bf16[160,768]{1,0:T(8,128)(2,1)S(1)}, bf16[160,768]{1,0:T(8,128)(2,1)S(1)}, u32[]{:S(2)}, u32[]{:S(2)}) collective-permute-start(bf16[160,768]{1,0:T(8,128)(2,1)S(1)} %get-tuple-element.35), channel_id=1, source_target_pairs={{0,24},{8,16},{16,8},{24,0},{1,25},{9,17},{17,9},{25,1},{2,26},{10... | collective-permute-start | bytes 737288 | tf_op jit(solution)/shard_map/ppermute | solution.py:479
  16.6 0.0 collective-permute-done.refs_1_.refs_2_
  16.6 0.5 collective-permute-start.5
  17.1 3.2 %collective-permute-done.3.refs_9_ = bf16[144,768]{1,0:T(8,128)(2,1)S(1)} collective-permute-done((bf16[144,768]{1,0:T(8,128)(2,1)S(1)}, bf16[144,768]{1,0:T(8,128)(2,1)S(1)}, u32[]{:S(2)}, u32[]{:S(2)}) %collective-permute-start.3) | collective-permute-done | bytes 221216 | tf_op jit(solution)/shard_map/ppermute | solution.py:483
  20.3 0.0 collective-permute-start.4
  20.3 1.3 %collective-permute-done.2.refs_3_.refs_4_ = bf16[160,768]{1,0:T(8,128)(2,1)S(1)} collective-permute-done((bf16[160,768]{1,0:T(8,128)(2,1)S(1)}, bf16[160,768]{1,0:T(8,128)(2,1)S(1)}, u32[]{:S(2)}, u32[]{:S(2)}) %collective-permute-start.2) | collective-permute-done | bytes 245792 | tf_op jit(solution)/shard_map/ppermute | solution.py:479
  21.6 0.9 %collective-permute-start.10 = (bf16[160,768]{1,0:T(8,128)(2,1)S(1)}, bf16[160,768]{1,0:T(8,128)(2,1)S(1)}, u32[]{:S(2)}, u32[]{:S(2)}) collective-permute-start(bf16[160,768]{1,0:T(8,128)(2,1)S(1)} %collective-permute-done.2.refs_3_.refs_4_), channel_id=1, source_target_pairs={{0,1},{1,0},{2,3},{3,2},{4,5},{5,4},{6,7},{7,6},{8,9},{9,8},{10,11... | collective-permute-start | bytes 737288 | tf_op jit(solution)/shard_map/ppermute | solution.py:483
  22.5 2.0 %collective-permute-done.5.refs_8_ = bf16[160,768]{1,0:T(8,128)(2,1)S(1)} collective-permute-done((bf16[160,768]{1,0:T(8,128)(2,1)S(1)}, bf16[160,768]{1,0:T(8,128)(2,1)S(1)}, u32[]{:S(2)}, u32[]{:S(2)}) %collective-permute-start.5) | collective-permute-done | bytes 245792 | tf_op jit(solution)/shard_map/ppermute | solution.py:483
  24.5 0.0 collective-permute-start.6
  24.5 0.5 collective-permute-start.7
  25.0 0.7 %collective-permute-start.9 = (bf16[80,768]{1,0:T(8,128)(2,1)S(1)}, bf16[80,768]{1,0:T(8,128)(2,1)S(1)}, u32[]{:S(2)}, u32[]{:S(2)}) collective-permute-start(bf16[80,768]{1,0:T(8,128)(2,1)S(1)} %get-tuple-element.41), channel_id=1, source_target_pairs={{4,8},{8,4},{12,16},{16,12},{20,24},{24,20},{5,9},{9,5},{13,17},{1... | collective-permute-start | bytes 368648 | tf_op jit(solution)/shard_map/ppermute | solution.py:538
  25.7 0.0 collective-permute-done.9.refs_8_
  25.7 6.5 %collective-permute-start.8 = (bf16[160,768]{1,0:T(8,128)(2,1)S(1)}, bf16[160,768]{1,0:T(8,128)(2,1)S(1)}, u32[]{:S(2)}, u32[]{:S(2)}) collective-permute-start(bf16[160,768]{1,0:T(8,128)(2,1)S(1)} %collective-permute-done.2.refs_3_.refs_4_), channel_id=1, source_target_pairs={{0,4},{4,0},{1,5},{5,1},{2,6},{6,2},{3,7},{7,3},{8,12},{12,8},{9,1... | collective-permute-start | bytes 737288 | tf_op jit(solution)/shard_map/ppermute | solution.py:479
  32.2 0.0 collective-permute-done.10.refs_10_
  32.2 0.0 collective-permute-start.11
  32.2 0.0 collective-permute-done.7.refs_6_
  32.2 0.5 collective-permute-start.13
  32.7 0.1 collective-permute-start.12
  32.8 0.5 collective-permute-done.8.refs_7_
  33.4 0.0 collective-permute-done.4.refs_4_.refs_1_
  33.4 0.9 %shard_map.96 = (bf16[416,128]{1,0:T(8,128)(2,1)S(1)}, bf16[416,128]{1,0:T(8,128)(2,1)S(1)}, bf16[288,768]{1,0:T(8,128)(2,1)S(1)}) custom-call(bf16[368,768]{1,0:T(8,128)(2,1)S(1)} %get-tuple-element.36.refs_0_, bf16[160,768]{1,0:T(8,128)(2,1)S(1)} %collective-permute-done.refs_1_.refs_2_, bf16[144,768]{1,0:T(8,128)(2,1)S(1)} %collective-permute-done.1.refs_2_.refs_3_, ...), custom_call_target="tpu_custom_call" | custom-call | flops 1000000000 | bytes 1000000 | tf_op jit(solution)/shard_map/pallas_call | solution.py:61
  34.2 0.2 collective-permute-done.12.refs_12_
  34.4 0.0 collective-permute-done.11.refs_11_
  34.4 0.0 collective-permute-done.13.refs_13_
  34.4 3.8 %shard_map.97 = (f32[4,96,768]{2,1,0:T(8,128)S(1)}, bf16[4,96,768]{2,1,0:T(8,128)(2,1)S(1)}, bf16[256,384]{1,0:T(8,128)(2,1)S(1)}, bf16[320,768]{1,0:T(8,128)(2,...) custom-call(bf16[368,768]{1,0:T(8,128)(2,1)S(1)} %get-tuple-element.36.refs_0_, ...), custom_call_target="tpu_custom_call" | custom-call | flops 4000000000 | bytes 1000000 | tf_op jit(solution)/shard_map/pallas_call | solution.py:61
  38.2 0.4 collective-permute-start.14
  38.6 1.7 %collective-permute-done.14.recv_ref = bf16[4,96,768]{2,1,0:T(8,128)(2,1)S(1)} collective-permute-done((bf16[4,96,768]{2,1,0:T(8,128)(2,1)S(1)}, bf16[4,96,768]{2,1,0:T(8,128)(2,1)S(1)}, u32[]{:S(2)}, u32[]{:S(2)}) %collective-permute-start.14) | collective-permute-done | bytes 589856 | tf_op jit(solution)/shard_map/ppermute | solution.py:479
  40.3 0.1 shard_map.99
  40.4 2.8 %collective-permute-start.15 = (bf16[96,768]{1,0:T(8,128)(2,1)S(1)}, bf16[96,768]{1,0:T(8,128)(2,1)S(1)}, u32[]{:S(2)}, u32[]{:S(2)}) collective-permute-start(bf16[96,768]{1,0:T(8,128)(2,1)S(1)} %get-tuple-element.53), channel_id=1, source_target_pairs={{0,24},{8,16},{16,8},{24,0},{1,25},{9,17},{17,9},{25,1},{2,26},{10... | collective-permute-start | bytes 442376 | tf_op jit(solution)/shard_map/ppermute | solution.py:479
  43.2 1.0 %collective-permute-start.16 = (bf16[96,768]{1,0:T(8,128)(2,1)S(1)}, bf16[96,768]{1,0:T(8,128)(2,1)S(1)}, u32[]{:S(2)}, u32[]{:S(2)}) collective-permute-start(bf16[96,768]{1,0:T(8,128)(2,1)S(1)} %get-tuple-element.54), channel_id=1, source_target_pairs={{0,16},{16,0},{1,17},{17,1},{2,18},{18,2},{3,19},{19,3},{4,20},{20... | collective-permute-start | bytes 442376 | tf_op jit(solution)/shard_map/ppermute | solution.py:479
  44.2 0.1 collective-permute-start.17
  44.3 3.8 %collective-permute-done.15.d_ref = bf16[96,768]{1,0:T(8,128)(2,1)S(1)} collective-permute-done((bf16[96,768]{1,0:T(8,128)(2,1)S(1)}, bf16[96,768]{1,0:T(8,128)(2,1)S(1)}, u32[]{:S(2)}, u32[]{:S(2)}) %collective-permute-start.15) | collective-permute-done | bytes 147488 | tf_op jit(solution)/shard_map/ppermute | solution.py:479
  48.1 2.6 %collective-permute-done.16.y_ref = bf16[96,768]{1,0:T(8,128)(2,1)S(1)} collective-permute-done((bf16[96,768]{1,0:T(8,128)(2,1)S(1)}, bf16[96,768]{1,0:T(8,128)(2,1)S(1)}, u32[]{:S(2)}, u32[]{:S(2)}) %collective-permute-start.16) | collective-permute-done | bytes 147488 | tf_op jit(solution)/shard_map/ppermute | solution.py:479
  50.7 0.7 %collective-permute-done.17.x_ref = bf16[96,768]{1,0:T(8,128)(2,1)S(1)} collective-permute-done((bf16[96,768]{1,0:T(8,128)(2,1)S(1)}, bf16[96,768]{1,0:T(8,128)(2,1)S(1)}, u32[]{:S(2)}, u32[]{:S(2)}) %collective-permute-start.17) | collective-permute-done | bytes 147488 | tf_op jit(solution)/shard_map/ppermute | solution.py:479
  51.4 0.1 shard_map.100
  51.5 3.3 %collective-permute-start.18 = (bf16[48,384]{1,0:T(8,128)(2,1)S(1)}, bf16[48,384]{1,0:T(8,128)(2,1)S(1)}, u32[]{:S(2)}, u32[]{:S(2)}) collective-permute-start(bf16[48,384]{1,0:T(8,128)(2,1)S(1)} %get-tuple-element.57), channel_id=1, source_target_pairs={{0,3},{1,2},{2,1},{3,0},{4,7},{5,6},{6,5},{7,4},{8,11},{9,10},{10,... | collective-permute-start | bytes 110600 | tf_op jit(solution)/shard_map/ppermute | solution.py:483
  54.8 0.0 collective-permute-start.19
  54.8 1.2 %collective-permute-start.20 = (bf16[48,384]{1,0:T(8,128)(2,1)S(1)}, bf16[48,384]{1,0:T(8,128)(2,1)S(1)}, u32[]{:S(2)}, u32[]{:S(2)}) collective-permute-start(bf16[48,384]{1,0:T(8,128)(2,1)S(1)} %get-tuple-element.59), channel_id=1, source_target_pairs={{0,1},{1,0},{2,3},{3,2},{4,5},{5,4},{6,7},{7,6},{8,9},{9,8},{10,11... | collective-permute-start | bytes 110600 | tf_op jit(solution)/shard_map/ppermute | solution.py:483
  55.9 1.6 %shard_map.98 = f32[4,128]{1,0:T(4,128)} custom-call(f32[8,768]{1,0:T(8,128)S(1)} %get-tuple-element.31.refs_14_.small_ref, bf16[416,128]{1,0:T(8,128)(2,1)S(1)} %get-tuple-element.42.refs_16_.hot_f_ref, bf16[416,128]{1,0:T(8,128)(2,1)S(1)} %get-tuple-element.43.refs_17_.hot_r_ref, bf16[256,384]{1,0:T(8,128)(2,1)S(1)} %get-tuple-element.45.s1_ref, ...), custom_call_target="tpu_custom_call" | custom-call | flops 1000000000 | bytes 1000000 | tf_op jit(solution)/shard_map/pallas_call | solution.py:61
  57.5 2.1 %collective-permute-done.19.refs_1_ = bf16[48,384]{1,0:T(8,128)(2,1)S(1)} collective-permute-done((bf16[48,384]{1,0:T(8,128)(2,1)S(1)}, bf16[48,384]{1,0:T(8,128)(2,1)S(1)}, u32[]{:S(2)}, u32[]{:S(2)}) %collective-permute-start.19) | collective-permute-done | bytes 36896 | tf_op jit(solution)/shard_map/ppermute | solution.py:483
  59.6 0.7 %shard_map.101 = f32[144,128]{1,0:T(8,128)} custom-call(f32[48,384]{1,0:T(8,128)S(1)} %get-tuple-element.56.mine_ref, bf16[48,384]{1,0:T(8,128)(2,1)S(1)} %collective-permute-done.18.refs_0_, bf16[48,384]{1,0:T(8,128)(2,1)S(1)} %collective-permute-done.19.refs_1_, bf16[48,384]{1,0:T(8,128)(2,1)S(1)} %collective-permute-done.20.refs_2_), custom_call_target="tpu_custom_call" | custom-call | tf_op jit(solution)/shard_map/pallas_call | solution.py:61
  (7 shorter events, 0.0 us)
Async XLA Ops:
  0.6 2.8 %copy-start = (f32[4,768]{1,0:T(4,128)S(1)}, f32[4,768]{1,0:T(4,128)}, u32[]{:S(2)}) copy-start(f32[4,768]{1,0:T(4,128)} %embed_ref.1) | copy-start | bytes 36868
  0.6 2.8 %copy-start.1 = (s32[1,128]{1,0:T(1,128)S(1)}, s32[1,128]{1,0:T(1,128)}, u32[]{:S(2)}) copy-start(s32[1,128]{1,0:T(1,128)} %bases_ref.1) | copy-start | bytes 1540
  3.9 8.5 %collective-permute-start.1 = (bf16[144,768]{1,0:T(8,128)(2,1)S(1)}, bf16[144,768]{1,0:T(8,128)(2,1)S(1)}, u32[]{:S(2)}, u32[]{:S(2)}) collective-permute-start(bf16[144,768]{1,0:T(8,128)(2,1)S(1)} %get-tuple-element.34), channel_id=1, source_target_pairs={{0,16},{16,0},{1,17},{17,1},{2,18},{18,2},{3,19},{19,3},{4,20},{20... | collective-permute-start | bytes 663560 | tf_op jit(solution)/shard_map/ppermute | solution.py:479
  6.9 9.7 %collective-permute-start = (bf16[160,768]{1,0:T(8,128)(2,1)S(1)}, bf16[160,768]{1,0:T(8,128)(2,1)S(1)}, u32[]{:S(2)}, u32[]{:S(2)}) collective-permute-start(bf16[160,768]{1,0:T(8,128)(2,1)S(1)} %get-tuple-element.33), channel_id=1, source_target_pairs={{0,8},{8,0},{1,9},{9,1},{2,10},{10,2},{3,11},{11,3},{4,12},{12,4},... | collective-permute-start | bytes 737288 | tf_op jit(solution)/shard_map/ppermute | solution.py:479
  12.4 7.9 %collective-permute-start.3 = (bf16[144,768]{1,0:T(8,128)(2,1)S(1)}, bf16[144,768]{1,0:T(8,128)(2,1)S(1)}, u32[]{:S(2)}, u32[]{:S(2)}) collective-permute-start(bf16[144,768]{1,0:T(8,128)(2,1)S(1)} %collective-permute-done.1.refs_2_.refs_3_), channel_id=1, source_target_pairs={{0,1},{1,0},{2,3},{3,2},{4,5},{5,4},{6,7},{7,6},{8,9},{9,8},{10,11... | collective-permute-start | bytes 663560 | tf_op jit(solution)/shard_map/ppermute | solution.py:483
  14.2 7.4 %collective-permute-start.2 = (bf16[160,768]{1,0:T(8,128)(2,1)S(1)}, bf16[160,768]{1,0:T(8,128)(2,1)S(1)}, u32[]{:S(2)}, u32[]{:S(2)}) collective-permute-start(bf16[160,768]{1,0:T(8,128)(2,1)S(1)} %get-tuple-element.35), channel_id=1, source_target_pairs={{0,24},{8,16},{16,8},{24,0},{1,25},{9,17},{17,9},{25,1},{2,26},{10... | collective-permute-start | bytes 737288 | tf_op jit(solution)/shard_map/ppermute | solution.py:479
  16.6 7.9 %collective-permute-start.5 = (bf16[160,768]{1,0:T(8,128)(2,1)S(1)}, bf16[160,768]{1,0:T(8,128)(2,1)S(1)}, u32[]{:S(2)}, u32[]{:S(2)}) collective-permute-start(bf16[160,768]{1,0:T(8,128)(2,1)S(1)} %collective-permute-done.refs_1_.refs_2_), channel_id=1, source_target_pairs={{0,1},{1,0},{2,3},{3,2},{4,5},{5,4},{6,7},{7,6},{8,9},{9,8},{10,11... | collective-permute-start | bytes 737288 | tf_op jit(solution)/shard_map/ppermute | solution.py:483
  20.3 13.1 %collective-permute-start.4 = (bf16[368,768]{1,0:T(8,128)(2,1)S(1)}, bf16[368,768]{1,0:T(8,128)(2,1)S(1)}, u32[]{:S(2)}, u32[]{:S(2)}) collective-permute-start(bf16[368,768]{1,0:T(8,128)(2,1)S(1)} %get-tuple-element.36.refs_0_), channel_id=1, source_target_pairs={{0,4},{4,0},{1,5},{5,1},{2,6},{6,2},{3,7},{7,3},{8,12},{12,8},{9,1... | collective-permute-start | bytes 1695752 | tf_op jit(solution)/shard_map/ppermute | solution.py:479
  21.6 10.6 %collective-permute-start.10 = (bf16[160,768]{1,0:T(8,128)(2,1)S(1)}, bf16[160,768]{1,0:T(8,128)(2,1)S(1)}, u32[]{:S(2)}, u32[]{:S(2)}) collective-permute-start(bf16[160,768]{1,0:T(8,128)(2,1)S(1)} %collective-permute-done.2.refs_3_.refs_4_), channel_id=1, source_target_pairs={{0,1},{1,0},{2,3},{3,2},{4,5},{5,4},{6,7},{7,6},{8,9},{9,8},{10,11... | collective-permute-start | bytes 737288 | tf_op jit(solution)/shard_map/ppermute | solution.py:483
  24.5 8.2 %collective-permute-start.6 = (bf16[160,768]{1,0:T(8,128)(2,1)S(1)}, bf16[160,768]{1,0:T(8,128)(2,1)S(1)}, u32[]{:S(2)}, u32[]{:S(2)}) collective-permute-start(bf16[160,768]{1,0:T(8,128)(2,1)S(1)} %collective-permute-done.refs_1_.refs_2_), channel_id=1, source_target_pairs={{0,4},{4,0},{1,5},{5,1},{2,6},{6,2},{3,7},{7,3},{8,12},{12,8},{9,1... | collective-permute-start | bytes 737288 | tf_op jit(solution)/shard_map/ppermute | solution.py:479
  24.5 7.7 %collective-permute-start.7 = (bf16[144,768]{1,0:T(8,128)(2,1)S(1)}, bf16[144,768]{1,0:T(8,128)(2,1)S(1)}, u32[]{:S(2)}, u32[]{:S(2)}) collective-permute-start(bf16[144,768]{1,0:T(8,128)(2,1)S(1)} %collective-permute-done.1.refs_2_.refs_3_), channel_id=1, source_target_pairs={{0,4},{4,0},{1,5},{5,1},{2,6},{6,2},{3,7},{7,3},{8,12},{12,8},{9,1... | collective-permute-start | bytes 663560 | tf_op jit(solution)/shard_map/ppermute | solution.py:479
  25.0 0.7 %collective-permute-start.9 = (bf16[80,768]{1,0:T(8,128)(2,1)S(1)}, bf16[80,768]{1,0:T(8,128)(2,1)S(1)}, u32[]{:S(2)}, u32[]{:S(2)}) collective-permute-start(bf16[80,768]{1,0:T(8,128)(2,1)S(1)} %get-tuple-element.41), channel_id=1, source_target_pairs={{4,8},{8,4},{12,16},{16,12},{20,24},{24,20},{5,9},{9,5},{13,17},{1... | collective-permute-start | bytes 368648 | tf_op jit(solution)/shard_map/ppermute | solution.py:538
  25.7 7.6 %collective-permute-start.8 = (bf16[160,768]{1,0:T(8,128)(2,1)S(1)}, bf16[160,768]{1,0:T(8,128)(2,1)S(1)}, u32[]{:S(2)}, u32[]{:S(2)}) collective-permute-start(bf16[160,768]{1,0:T(8,128)(2,1)S(1)} %collective-permute-done.2.refs_3_.refs_4_), channel_id=1, source_target_pairs={{0,4},{4,0},{1,5},{5,1},{2,6},{6,2},{3,7},{7,3},{8,12},{12,8},{9,1... | collective-permute-start | bytes 737288 | tf_op jit(solution)/shard_map/ppermute | solution.py:479
  32.2 2.2 %collective-permute-start.11 = (bf16[160,768]{1,0:T(8,128)(2,1)S(1)}, bf16[160,768]{1,0:T(8,128)(2,1)S(1)}, u32[]{:S(2)}, u32[]{:S(2)}) collective-permute-start(bf16[160,768]{1,0:T(8,128)(2,1)S(1)} %collective-permute-done.5.refs_8_), channel_id=1, source_target_pairs={{0,4},{4,0},{1,5},{5,1},{2,6},{6,2},{3,7},{7,3},{8,12},{12,8},{9,1... | collective-permute-start | bytes 737288 | tf_op jit(solution)/shard_map/ppermute | solution.py:479
  32.2 2.2 %collective-permute-start.13 = (bf16[160,768]{1,0:T(8,128)(2,1)S(1)}, bf16[160,768]{1,0:T(8,128)(2,1)S(1)}, u32[]{:S(2)}, u32[]{:S(2)}) collective-permute-start(bf16[160,768]{1,0:T(8,128)(2,1)S(1)} %collective-permute-done.10.refs_10_), channel_id=1, source_target_pairs={{0,4},{4,0},{1,5},{5,1},{2,6},{6,2},{3,7},{7,3},{8,12},{12,8},{9,1... | collective-permute-start | bytes 737288 | tf_op jit(solution)/shard_map/ppermute | solution.py:479
  32.7 1.7 %collective-permute-start.12 = (bf16[144,768]{1,0:T(8,128)(2,1)S(1)}, bf16[144,768]{1,0:T(8,128)(2,1)S(1)}, u32[]{:S(2)}, u32[]{:S(2)}) collective-permute-start(bf16[144,768]{1,0:T(8,128)(2,1)S(1)} %collective-permute-done.3.refs_9_), channel_id=1, source_target_pairs={{0,4},{4,0},{1,5},{5,1},{2,6},{6,2},{3,7},{7,3},{8,12},{12,8},{9,1... | collective-permute-start | bytes 663560 | tf_op jit(solution)/shard_map/ppermute | solution.py:479
  38.2 2.1 %collective-permute-start.14 = (bf16[4,96,768]{2,1,0:T(8,128)(2,1)S(1)}, bf16[4,96,768]{2,1,0:T(8,128)(2,1)S(1)}, u32[]{:S(2)}, u32[]{:S(2)}) collective-permute-start(bf16[4,96,768]{2,1,0:T(8,128)(2,1)S(1)} %get-tuple-element.51), channel_id=1, source_target_pairs={{0,4},{4,0},{1,5},{5,1},{2,6},{6,2},{3,7},{7,3},{8,12},{12,8},{9,1... | collective-permute-start | bytes 1769480 | tf_op jit(solution)/shard_map/ppermute | solution.py:479
  40.4 7.6 %collective-permute-start.15 = (bf16[96,768]{1,0:T(8,128)(2,1)S(1)}, bf16[96,768]{1,0:T(8,128)(2,1)S(1)}, u32[]{:S(2)}, u32[]{:S(2)}) collective-permute-start(bf16[96,768]{1,0:T(8,128)(2,1)S(1)} %get-tuple-element.53), channel_id=1, source_target_pairs={{0,24},{8,16},{16,8},{24,0},{1,25},{9,17},{17,9},{25,1},{2,26},{10... | collective-permute-start | bytes 442376 | tf_op jit(solution)/shard_map/ppermute | solution.py:479
  43.2 7.4 %collective-permute-start.16 = (bf16[96,768]{1,0:T(8,128)(2,1)S(1)}, bf16[96,768]{1,0:T(8,128)(2,1)S(1)}, u32[]{:S(2)}, u32[]{:S(2)}) collective-permute-start(bf16[96,768]{1,0:T(8,128)(2,1)S(1)} %get-tuple-element.54), channel_id=1, source_target_pairs={{0,16},{16,0},{1,17},{17,1},{2,18},{18,2},{3,19},{19,3},{4,20},{20... | collective-permute-start | bytes 442376 | tf_op jit(solution)/shard_map/ppermute | solution.py:479
  44.2 7.2 %collective-permute-start.17 = (bf16[96,768]{1,0:T(8,128)(2,1)S(1)}, bf16[96,768]{1,0:T(8,128)(2,1)S(1)}, u32[]{:S(2)}, u32[]{:S(2)}) collective-permute-start(bf16[96,768]{1,0:T(8,128)(2,1)S(1)} %get-tuple-element.55), channel_id=1, source_target_pairs={{0,8},{8,0},{1,9},{9,1},{2,10},{10,2},{3,11},{11,3},{4,12},{12,4},... | collective-permute-start | bytes 442376 | tf_op jit(solution)/shard_map/ppermute | solution.py:479
  51.5 6.0 %collective-permute-start.18 = (bf16[48,384]{1,0:T(8,128)(2,1)S(1)}, bf16[48,384]{1,0:T(8,128)(2,1)S(1)}, u32[]{:S(2)}, u32[]{:S(2)}) collective-permute-start(bf16[48,384]{1,0:T(8,128)(2,1)S(1)} %get-tuple-element.57), channel_id=1, source_target_pairs={{0,3},{1,2},{2,1},{3,0},{4,7},{5,6},{6,5},{7,4},{8,11},{9,10},{10,... | collective-permute-start | bytes 110600 | tf_op jit(solution)/shard_map/ppermute | solution.py:483
  54.8 4.9 %collective-permute-start.19 = (bf16[48,384]{1,0:T(8,128)(2,1)S(1)}, bf16[48,384]{1,0:T(8,128)(2,1)S(1)}, u32[]{:S(2)}, u32[]{:S(2)}) collective-permute-start(bf16[48,384]{1,0:T(8,128)(2,1)S(1)} %get-tuple-element.58), channel_id=1, source_target_pairs={{0,2},{1,3},{2,0},{3,1},{4,6},{5,7},{6,4},{7,5},{8,10},{9,11},{10,... | collective-permute-start | bytes 110600 | tf_op jit(solution)/shard_map/ppermute | solution.py:483
  54.8 4.9 %collective-permute-start.20 = (bf16[48,384]{1,0:T(8,128)(2,1)S(1)}, bf16[48,384]{1,0:T(8,128)(2,1)S(1)}, u32[]{:S(2)}, u32[]{:S(2)}) collective-permute-start(bf16[48,384]{1,0:T(8,128)(2,1)S(1)} %get-tuple-element.59), channel_id=1, source_target_pairs={{0,1},{1,0},{2,3},{3,2},{4,5},{5,4},{6,7},{7,6},{8,9},{9,8},{10,11... | collective-permute-start | bytes 110600 | tf_op jit(solution)/shard_map/ppermute | solution.py:483

commit v10 on v8

--- a/solution.py
+++ b/solution.py
@@ -91,8 +91,8 @@
 
 
 def prep_kernel(
-    narrow_ref, broad_ref, embed_ref, bases_ref, lengths_ref,
-    own_ref, x_ref, y_ref, d_ref, small_ref,
+    narrow_ref, broad_ref, cot_ref, embed_ref, bases_ref, lengths_ref,
+    own_ref, x_ref, y_ref, d_ref, small_ref, cot_out,
 ):
     me, odd = position(), lax.axis_index("dp") & 1
     cap = bases_ref.shape[1]
@@ -107,7 +107,8 @@
     half = 3 * shard // 2
     cut = half - 16
     flat = narrow_ref.at[3 * shard : 6 * shard]
-    cot = broad_ref[2 * prows :]
+    cot = cot_ref[...]
+    cot_out[...] = cot
     pick = (iota((chans, shard), 0) == iota((chans, shard), 1) + me * shard).astype(BF16)
     taps = [narrow_ref[k * shard : (k + 1) * shard] for k in range(3)]
     first, second = base_tables(embed_ref[...], pick, taps)
@@ -206,13 +207,11 @@
 
 
 def context_kernel_packed(*refs):
-    parts, broad_ref, outs = refs[0:8], refs[8], refs[9:12]
+    parts, cot_ref, outs = refs[0:8], refs[8], refs[9:12]
     info_ref, halo_ref = refs[12:]
     me, odd = position(), lax.axis_index("dp") & 1
     chip, core = me >> 1, me & 1
-    chans = broad_ref.shape[1]
-    prow = chans // 16
-    half = 3 * chans // 16
+    half = 3 * cot_ref.shape[1] // 16
     info_ref[0:REACH] = jnp.zeros((REACH, 8, 256), F32)
     info_ref[REACH + 8 :] = jnp.zeros((REACH, 8, 256), F32)
     for n, part in enumerate(parts):
@@ -231,7 +230,7 @@
     r2 = halo_ref[jnp.maximum(chip - 1, 0)]
     l2 = halo_ref[jnp.minimum(chip + 1, 3)]
     context_body(
-        lambda o: info_ref[me + (REACH + o)], broad_ref[2 * prow :], r1, r2[HALO - SPILL :], l1,
+        lambda o: info_ref[me + (REACH + o)], cot_ref[...], r1, r2[HALO - SPILL :], l1,
         l2[0:SPILL], *outs,
     )
 
@@ -521,8 +520,8 @@
     n_dp = lax.axis_size("dp")
     half = 3 * c2.shape[1] // 2
     narrow = jnp.concatenate([c1.reshape(-1, width), c2.reshape(-1, width)], axis=0)
-    broad = jnp.concatenate([p2, p1, cot], axis=0)
-    own, to_x, to_y, to_d, small = call(
+    broad = jnp.concatenate([p2, p1], axis=0)
+    own, to_x, to_y, to_d, small, cot = call(
         prep_kernel,
         [
             ((2 * half + HALO, chans), BF16),
@@ -530,8 +529,9 @@
             ((half, chans), BF16),
             ((half + HALO, chans), BF16),
             ((8, chans), F32),
+            ((cap, chans), BF16),
         ],
-        [narrow, broad, embed, bases, lengths],
+        [narrow, broad, cot, embed, bases, lengths],
     )
     plane = [flip_move(to_x, "x"), flip_move(to_y, "y"), flip_move(to_d, "y", "x")]
     other = [xor_move(a[:half], "dp", 1) for a in plane]
@@ -541,7 +541,7 @@
     hf, hr, cx = call(
         context_kernel_packed,
         context_shapes(cap, chans),
-        [own, *plane, *swapped, broad],
+        [own, *plane, *swapped, cot],
         scratch=[
             pltpu.VMEM((8 + 2 * REACH, 8, 256), F32),
             pltpu.VMEM((8, HALO, chans), BF16),

time: 57.3 us -> 57.2 us (level)
  no operation moved by 1% of the time
where the time goes in v10:
time: 57.2 us; the launch traced here: 57 us
  waiting for transfers between devices  26.8 us (47%)
  starting transfers between devices  19.2 us (34%)
  Pallas kernels  7.62 us (13%)
  other arithmetic  2.02 us (4%)
  between operations  1.44 us (3%)
    ppermute x14, waiting for transfers between devices, flip_move(): return lax.ppermute(array, axes, [(i, size - 1 - i) for i in range(size)])  20.4 us
    ppermute x6, starting transfers between devices, xor_move(): lax.ppermute(array, axis, [(i, i ^ bits) for i in range(lax.axis_size(axi...  9.68 us
    ppermute x14, starting transfers between devices, flip_move(): return lax.ppermute(array, axes, [(i, size - 1 - i) for i in range(size)])  9.48 us
    pallas_call x7, Pallas kernels, call(): pl.pallas_call(body, out_shape=[jax.ShapeDtypeStruct(s, d) for s, d in ou...  7.62 us
    ppermute x6, waiting for transfers between devices, xor_move(): lax.ppermute(array, axis, [(i, i ^ bits) for i in range(lax.axis_size(axi...  6.39 us
  transfers between devices with their start and end apart: 20, of which 9 were waited for; matrix products, arithmetic and copies ran while one was open for 0% of the time, Pallas kernels for 4%

profile of v10, /device:TPU:0, one launch (start us, length us, event | category | flops | bytes accessed | tf_op | source)
XLA Modules:
  0.0 57.0 jit_solution(14970127982152698079)
XLA Ops:
  1.3 0.9 %pad_maximum_fusion.1.broad_ref = bf16[96,768]{1,0:T(8,128)(2,1)S(1)} fusion(bf16[48,768]{1,0:T(8,128)(2,1)} %param.12, bf16[48,768]{1,0:T(8,128)(2,1)} %param.14), kind=kLoop, calls=%fused_computation.1 | loop fusion | flops 294912 | bytes 294912 | tf_op jit(solution)/shard_map/concatenate | solution.py:523
  2.3 1.1 %pad_maximum_fusion.narrow_ref = bf16[576,384]{1,0:T(8,128)(2,1)S(1)} fusion(bf16[288,384]{1,0:T(8,128)(2,1)} %bitcast.6, bf16[288,384]{1,0:T(8,128)(2,1)} %bitcast.7), kind=kLoop, calls=%fused_computation | loop fusion | flops 884736 | bytes 884736 | tf_op jit(solution)/shard_map/concatenate | solution.py:522
  3.4 0.4 shard_map.95
  3.8 3.0 %collective-permute-start.1 = (bf16[144,768]{1,0:T(8,128)(2,1)S(1)}, bf16[144,768]{1,0:T(8,128)(2,1)S(1)}, u32[]{:S(2)}, u32[]{:S(2)}) collective-permute-start(bf16[144,768]{1,0:T(8,128)(2,1)S(1)} %get-tuple-element.29), channel_id=1, source_target_pairs={{0,16},{16,0},{1,17},{17,1},{2,18},{18,2},{3,19},{19,3},{4,20},{20... | collective-permute-start | bytes 663560 | tf_op jit(solution)/shard_map/ppermute | solution.py:480
  6.9 1.5 %collective-permute-start = (bf16[224,768]{1,0:T(8,128)(2,1)S(1)}, bf16[224,768]{1,0:T(8,128)(2,1)S(1)}, u32[]{:S(2)}, u32[]{:S(2)}) collective-permute-start(bf16[224,768]{1,0:T(8,128)(2,1)S(1)} %get-tuple-element.28), channel_id=1, source_target_pairs={{0,8},{8,0},{1,9},{9,1},{2,10},{10,2},{3,11},{11,3},{4,12},{12,4},... | collective-permute-start | bytes 1032200 | tf_op jit(solution)/shard_map/ppermute | solution.py:480
  8.4 0.0 collective-permute-start.2
  8.4 0.0 collective-permute-start.3
  8.4 3.9 %collective-permute-done.1.refs_2_.refs_3_ = bf16[144,768]{1,0:T(8,128)(2,1)S(1)} collective-permute-done((bf16[144,768]{1,0:T(8,128)(2,1)S(1)}, bf16[144,768]{1,0:T(8,128)(2,1)S(1)}, u32[]{:S(2)}, u32[]{:S(2)}) %collective-permute-start.1) | collective-permute-done | bytes 221216 | tf_op jit(solution)/shard_map/ppermute | solution.py:480
  12.3 1.8 %collective-permute-start.8 = (bf16[144,768]{1,0:T(8,128)(2,1)S(1)}, bf16[144,768]{1,0:T(8,128)(2,1)S(1)}, u32[]{:S(2)}, u32[]{:S(2)}) collective-permute-start(bf16[144,768]{1,0:T(8,128)(2,1)S(1)} %collective-permute-done.1.refs_2_.refs_3_), channel_id=1, source_target_pairs={{0,1},{1,0},{2,3},{3,2},{4,5},{5,4},{6,7},{7,6},{8,9},{9,8},{10,11... | collective-permute-start | bytes 663560 | tf_op jit(solution)/shard_map/ppermute | solution.py:484
  14.1 0.0 collective-permute-start.5
  14.1 3.8 %collective-permute-done.refs_1_.refs_2_ = bf16[224,768]{1,0:T(8,128)(2,1)S(1)} collective-permute-done((bf16[224,768]{1,0:T(8,128)(2,1)S(1)}, bf16[224,768]{1,0:T(8,128)(2,1)S(1)}, u32[]{:S(2)}, u32[]{:S(2)}) %collective-permute-start) | collective-permute-done | bytes 344096 | tf_op jit(solution)/shard_map/ppermute | solution.py:480
  17.9 1.6 %collective-permute-start.7 = (bf16[144,768]{1,0:T(8,128)(2,1)S(1)}, bf16[144,768]{1,0:T(8,128)(2,1)S(1)}, u32[]{:S(2)}, u32[]{:S(2)}) collective-permute-start(bf16[144,768]{1,0:T(8,128)(2,1)S(1)} %slice.8), channel_id=1, source_target_pairs={{0,1},{1,0},{2,3},{3,2},{4,5},{5,4},{6,7},{7,6},{8,9},{9,8},{10,11... | collective-permute-start | bytes 663560 | tf_op jit(solution)/shard_map/ppermute | solution.py:484
  19.5 4.0 %collective-permute-done.2.refs_3_.refs_4_ = bf16[224,768]{1,0:T(8,128)(2,1)S(1)} collective-permute-done((bf16[224,768]{1,0:T(8,128)(2,1)S(1)}, bf16[224,768]{1,0:T(8,128)(2,1)S(1)}, u32[]{:S(2)}, u32[]{:S(2)}) %collective-permute-start.2) | collective-permute-done | bytes 344096 | tf_op jit(solution)/shard_map/ppermute | solution.py:480
  23.6 1.8 %collective-permute-start.9 = (bf16[144,768]{1,0:T(8,128)(2,1)S(1)}, bf16[144,768]{1,0:T(8,128)(2,1)S(1)}, u32[]{:S(2)}, u32[]{:S(2)}) collective-permute-start(bf16[144,768]{1,0:T(8,128)(2,1)S(1)} %slice.9), channel_id=1, source_target_pairs={{0,1},{1,0},{2,3},{3,2},{4,5},{5,4},{6,7},{7,6},{8,9},{9,8},{10,11... | collective-permute-start | bytes 663560 | tf_op jit(solution)/shard_map/ppermute | solution.py:484
  25.4 0.0 collective-permute-done.8.refs_9_
  25.4 0.0 collective-permute-start.4
  25.4 0.0 collective-permute-done.5.refs_6_
  25.4 0.5 collective-permute-start.6
  25.9 0.0 collective-permute-done.7.refs_8_
  25.9 0.1 collective-permute-start.11
  26.0 4.0 %collective-permute-done.9.refs_10_ = bf16[144,768]{1,0:T(8,128)(2,1)S(1)} collective-permute-done((bf16[144,768]{1,0:T(8,128)(2,1)S(1)}, bf16[144,768]{1,0:T(8,128)(2,1)S(1)}, u32[]{:S(2)}, u32[]{:S(2)}) %collective-permute-start.9) | collective-permute-done | bytes 221216 | tf_op jit(solution)/shard_map/ppermute | solution.py:484
  29.9 0.0 collective-permute-start.10
  29.9 0.0 collective-permute-done.3.refs_4_.refs_1_
  29.9 0.5 collective-permute-start.12
  30.5 0.0 collective-permute-done.4.refs_5_
  30.5 0.0 collective-permute-done.6.refs_7_
  30.5 0.9 %shard_map.96 = (bf16[416,128]{1,0:T(8,128)(2,1)S(1)}, bf16[416,128]{1,0:T(8,128)(2,1)S(1)}, bf16[288,768]{1,0:T(8,128)(2,1)S(1)}) custom-call(bf16[368,768]{1,0:T(8,128)(2,1)S(1)} %get-tuple-element.27.refs_0_, bf16[224,768]{1,0:T(8,128)(2,1)S(1)} %collective-permute-done.refs_1_.refs_2_, bf16[144,768]{1,0:T(8,128)(2,1)S(1)} %collective-permute-done.1.refs_2_.refs_3_, ...), custom_call_target="tpu_custom_call" | custom-call | flops 1000000000 | bytes 1000000 | tf_op jit(solution)/shard_map/pallas_call | solution.py:61
  31.4 0.0 collective-permute-done.11.refs_12_
  31.4 0.0 collective-permute-done.10.refs_11_
  31.4 0.3 collective-permute-done.12.refs_13_
  31.7 3.8 %shard_map.97 = (f32[4,96,768]{2,1,0:T(8,128)S(1)}, bf16[4,96,768]{2,1,0:T(8,128)(2,1)S(1)}, bf16[256,384]{1,0:T(8,128)(2,1)S(1)}, bf16[320,768]{1,0:T(8,128)(2,...) custom-call(bf16[368,768]{1,0:T(8,128)(2,1)S(1)} %get-tuple-element.27.refs_0_, ...), custom_call_target="tpu_custom_call" | custom-call | flops 4000000000 | bytes 1000000 | tf_op jit(solution)/shard_map/pallas_call | solution.py:61
  35.5 0.3 collective-permute-start.13
  35.8 1.8 %collective-permute-done.13.recv_ref = bf16[4,96,768]{2,1,0:T(8,128)(2,1)S(1)} collective-permute-done((bf16[4,96,768]{2,1,0:T(8,128)(2,1)S(1)}, bf16[4,96,768]{2,1,0:T(8,128)(2,1)S(1)}, u32[]{:S(2)}, u32[]{:S(2)}) %collective-permute-start.13) | collective-permute-done | bytes 589856 | tf_op jit(solution)/shard_map/ppermute | solution.py:480
  37.6 0.1 shard_map.99
  37.8 2.3 %collective-permute-start.14 = (bf16[96,768]{1,0:T(8,128)(2,1)S(1)}, bf16[96,768]{1,0:T(8,128)(2,1)S(1)}, u32[]{:S(2)}, u32[]{:S(2)}) collective-permute-start(bf16[96,768]{1,0:T(8,128)(2,1)S(1)} %get-tuple-element.43), channel_id=1, source_target_pairs={{0,24},{8,16},{16,8},{24,0},{1,25},{9,17},{17,9},{25,1},{2,26},{10... | collective-permute-start | bytes 442376 | tf_op jit(solution)/shard_map/ppermute | solution.py:480
  40.1 0.5 collective-permute-start.15
  40.6 0.7 %collective-permute-start.16 = (bf16[96,768]{1,0:T(8,128)(2,1)S(1)}, bf16[96,768]{1,0:T(8,128)(2,1)S(1)}, u32[]{:S(2)}, u32[]{:S(2)}) collective-permute-start(bf16[96,768]{1,0:T(8,128)(2,1)S(1)} %get-tuple-element.45), channel_id=1, source_target_pairs={{0,8},{8,0},{1,9},{9,1},{2,10},{10,2},{3,11},{11,3},{4,12},{12,4},... | collective-permute-start | bytes 442376 | tf_op jit(solution)/shard_map/ppermute | solution.py:480
  41.3 4.1 %collective-permute-done.14.d_ref = bf16[96,768]{1,0:T(8,128)(2,1)S(1)} collective-permute-done((bf16[96,768]{1,0:T(8,128)(2,1)S(1)}, bf16[96,768]{1,0:T(8,128)(2,1)S(1)}, u32[]{:S(2)}, u32[]{:S(2)}) %collective-permute-start.14) | collective-permute-done | bytes 147488 | tf_op jit(solution)/shard_map/ppermute | solution.py:480
  45.4 2.4 %collective-permute-done.15.y_ref = bf16[96,768]{1,0:T(8,128)(2,1)S(1)} collective-permute-done((bf16[96,768]{1,0:T(8,128)(2,1)S(1)}, bf16[96,768]{1,0:T(8,128)(2,1)S(1)}, u32[]{:S(2)}, u32[]{:S(2)}) %collective-permute-start.15) | collective-permute-done | bytes 147488 | tf_op jit(solution)/shard_map/ppermute | solution.py:480
  47.8 0.0 collective-permute-done.16.x_ref
  47.8 0.1 shard_map.100
  47.9 3.6 %collective-permute-start.17 = (bf16[48,384]{1,0:T(8,128)(2,1)S(1)}, bf16[48,384]{1,0:T(8,128)(2,1)S(1)}, u32[]{:S(2)}, u32[]{:S(2)}) collective-permute-start(bf16[48,384]{1,0:T(8,128)(2,1)S(1)} %get-tuple-element.47), channel_id=1, source_target_pairs={{0,3},{1,2},{2,1},{3,0},{4,7},{5,6},{6,5},{7,4},{8,11},{9,10},{10,... | collective-permute-start | bytes 110600 | tf_op jit(solution)/shard_map/ppermute | solution.py:484
  51.5 0.9 %collective-permute-start.19 = (bf16[48,384]{1,0:T(8,128)(2,1)S(1)}, bf16[48,384]{1,0:T(8,128)(2,1)S(1)}, u32[]{:S(2)}, u32[]{:S(2)}) collective-permute-start(bf16[48,384]{1,0:T(8,128)(2,1)S(1)} %get-tuple-element.49), channel_id=1, source_target_pairs={{0,1},{1,0},{2,3},{3,2},{4,5},{5,4},{6,7},{7,6},{8,9},{9,8},{10,11... | collective-permute-start | bytes 110600 | tf_op jit(solution)/shard_map/ppermute | solution.py:484
  52.4 1.6 %shard_map.98 = f32[4,128]{1,0:T(4,128)} custom-call(f32[8,768]{1,0:T(8,128)S(1)} %get-tuple-element.26.refs_14_.small_ref, bf16[416,128]{1,0:T(8,128)(2,1)S(1)} %get-tuple-element.32.refs_16_.hot_f_ref, bf16[416,128]{1,0:T(8,128)(2,1)S(1)} %get-tuple-element.33.refs_17_.hot_r_ref, bf16[256,384]{1,0:T(8,128)(2,1)S(1)} %get-tuple-element.35.s1_ref, ...), custom_call_target="tpu_custom_call" | custom-call | flops 1000000000 | bytes 1000000 | tf_op jit(solution)/shard_map/pallas_call | solution.py:61
  54.0 0.0 collective-permute-done.17.refs_0_
  54.0 2.4 %collective-permute-done.18.refs_1_ = bf16[48,384]{1,0:T(8,128)(2,1)S(1)} collective-permute-done((bf16[48,384]{1,0:T(8,128)(2,1)S(1)}, bf16[48,384]{1,0:T(8,128)(2,1)S(1)}, u32[]{:S(2)}, u32[]{:S(2)}) %collective-permute-start.18) | collective-permute-done | bytes 36896 | tf_op jit(solution)/shard_map/ppermute | solution.py:484
  56.4 0.0 collective-permute-done.19.refs_2_
  56.4 0.7 %shard_map.101 = f32[144,128]{1,0:T(8,128)} custom-call(f32[48,384]{1,0:T(8,128)S(1)} %get-tuple-element.46.mine_ref, bf16[48,384]{1,0:T(8,128)(2,1)S(1)} %collective-permute-done.17.refs_0_, bf16[48,384]{1,0:T(8,128)(2,1)S(1)} %collective-permute-done.18.refs_1_, bf16[48,384]{1,0:T(8,128)(2,1)S(1)} %collective-permute-done.19.refs_2_), custom_call_target="tpu_custom_call" | custom-call | tf_op jit(solution)/shard_map/pallas_call | solution.py:61
  (9 shorter events, 0.0 us)
Async XLA Ops:
  0.6 2.7 %copy-start.1 = (f32[4,768]{1,0:T(4,128)S(1)}, f32[4,768]{1,0:T(4,128)}, u32[]{:S(2)}) copy-start(f32[4,768]{1,0:T(4,128)} %embed_ref.1) | copy-start | bytes 36868
  0.6 2.7 %copy-start = (bf16[1,128,768]{2,1,0:T(8,128)(2,1)S(1)}, bf16[1,128,768]{2,1,0:T(8,128)(2,1)}, u32[]{:S(2)}) copy-start(bf16[1,128,768]{2,1,0:T(8,128)(2,1)} %param.10) | copy-start | bytes 589828
  0.7 2.7 %copy-start.2 = (s32[1,128]{1,0:T(1,128)S(1)}, s32[1,128]{1,0:T(1,128)}, u32[]{:S(2)}) copy-start(s32[1,128]{1,0:T(1,128)} %bases_ref.1) | copy-start | bytes 1540
  3.8 8.5 %collective-permute-start.1 = (bf16[144,768]{1,0:T(8,128)(2,1)S(1)}, bf16[144,768]{1,0:T(8,128)(2,1)S(1)}, u32[]{:S(2)}, u32[]{:S(2)}) collective-permute-start(bf16[144,768]{1,0:T(8,128)(2,1)S(1)} %get-tuple-element.29), channel_id=1, source_target_pairs={{0,16},{16,0},{1,17},{17,1},{2,18},{18,2},{3,19},{19,3},{4,20},{20... | collective-permute-start | bytes 663560 | tf_op jit(solution)/shard_map/ppermute | solution.py:480
  6.9 11.0 %collective-permute-start = (bf16[224,768]{1,0:T(8,128)(2,1)S(1)}, bf16[224,768]{1,0:T(8,128)(2,1)S(1)}, u32[]{:S(2)}, u32[]{:S(2)}) collective-permute-start(bf16[224,768]{1,0:T(8,128)(2,1)S(1)} %get-tuple-element.28), channel_id=1, source_target_pairs={{0,8},{8,0},{1,9},{9,1},{2,10},{10,2},{3,11},{11,3},{4,12},{12,4},... | collective-permute-start | bytes 1032200 | tf_op jit(solution)/shard_map/ppermute | solution.py:480
  8.4 15.2 %collective-permute-start.2 = (bf16[224,768]{1,0:T(8,128)(2,1)S(1)}, bf16[224,768]{1,0:T(8,128)(2,1)S(1)}, u32[]{:S(2)}, u32[]{:S(2)}) collective-permute-start(bf16[224,768]{1,0:T(8,128)(2,1)S(1)} %get-tuple-element.30), channel_id=1, source_target_pairs={{0,24},{8,16},{16,8},{24,0},{1,25},{9,17},{17,9},{25,1},{2,26},{10... | collective-permute-start | bytes 1032200 | tf_op jit(solution)/shard_map/ppermute | solution.py:480
  8.4 21.5 %collective-permute-start.3 = (bf16[368,768]{1,0:T(8,128)(2,1)S(1)}, bf16[368,768]{1,0:T(8,128)(2,1)S(1)}, u32[]{:S(2)}, u32[]{:S(2)}) collective-permute-start(bf16[368,768]{1,0:T(8,128)(2,1)S(1)} %get-tuple-element.27.refs_0_), channel_id=1, source_target_pairs={{0,4},{4,0},{1,5},{5,1},{2,6},{6,2},{3,7},{7,3},{8,12},{12,8},{9,1... | collective-permute-start | bytes 1695752 | tf_op jit(solution)/shard_map/ppermute | solution.py:480
  12.3 13.1 %collective-permute-start.8 = (bf16[144,768]{1,0:T(8,128)(2,1)S(1)}, bf16[144,768]{1,0:T(8,128)(2,1)S(1)}, u32[]{:S(2)}, u32[]{:S(2)}) collective-permute-start(bf16[144,768]{1,0:T(8,128)(2,1)S(1)} %collective-permute-done.1.refs_2_.refs_3_), channel_id=1, source_target_pairs={{0,1},{1,0},{2,3},{3,2},{4,5},{5,4},{6,7},{7,6},{8,9},{9,8},{10,11... | collective-permute-start | bytes 663560 | tf_op jit(solution)/shard_map/ppermute | solution.py:484
  14.1 11.3 %collective-permute-start.5 = (bf16[144,768]{1,0:T(8,128)(2,1)S(1)}, bf16[144,768]{1,0:T(8,128)(2,1)S(1)}, u32[]{:S(2)}, u32[]{:S(2)}) collective-permute-start(bf16[144,768]{1,0:T(8,128)(2,1)S(1)} %collective-permute-done.1.refs_2_.refs_3_), channel_id=1, source_target_pairs={{0,4},{4,0},{1,5},{5,1},{2,6},{6,2},{3,7},{7,3},{8,12},{12,8},{9,1... | collective-permute-start | bytes 663560 | tf_op jit(solution)/shard_map/ppermute | solution.py:480
  17.9 8.0 %collective-permute-start.7 = (bf16[144,768]{1,0:T(8,128)(2,1)S(1)}, bf16[144,768]{1,0:T(8,128)(2,1)S(1)}, u32[]{:S(2)}, u32[]{:S(2)}) collective-permute-start(bf16[144,768]{1,0:T(8,128)(2,1)S(1)} %slice.8), channel_id=1, source_target_pairs={{0,1},{1,0},{2,3},{3,2},{4,5},{5,4},{6,7},{7,6},{8,9},{9,8},{10,11... | collective-permute-start | bytes 663560 | tf_op jit(solution)/shard_map/ppermute | solution.py:484
  23.6 6.4 %collective-permute-start.9 = (bf16[144,768]{1,0:T(8,128)(2,1)S(1)}, bf16[144,768]{1,0:T(8,128)(2,1)S(1)}, u32[]{:S(2)}, u32[]{:S(2)}) collective-permute-start(bf16[144,768]{1,0:T(8,128)(2,1)S(1)} %slice.9), channel_id=1, source_target_pairs={{0,1},{1,0},{2,3},{3,2},{4,5},{5,4},{6,7},{7,6},{8,9},{9,8},{10,11... | collective-permute-start | bytes 663560 | tf_op jit(solution)/shard_map/ppermute | solution.py:484
  25.4 5.1 %collective-permute-start.4 = (bf16[224,768]{1,0:T(8,128)(2,1)S(1)}, bf16[224,768]{1,0:T(8,128)(2,1)S(1)}, u32[]{:S(2)}, u32[]{:S(2)}) collective-permute-start(bf16[224,768]{1,0:T(8,128)(2,1)S(1)} %collective-permute-done.refs_1_.refs_2_), channel_id=1, source_target_pairs={{0,4},{4,0},{1,5},{5,1},{2,6},{6,2},{3,7},{7,3},{8,12},{12,8},{9,1... | collective-permute-start | bytes 1032200 | tf_op jit(solution)/shard_map/ppermute | solution.py:480
  25.4 5.1 %collective-permute-start.6 = (bf16[224,768]{1,0:T(8,128)(2,1)S(1)}, bf16[224,768]{1,0:T(8,128)(2,1)S(1)}, u32[]{:S(2)}, u32[]{:S(2)}) collective-permute-start(bf16[224,768]{1,0:T(8,128)(2,1)S(1)} %collective-permute-done.2.refs_3_.refs_4_), channel_id=1, source_target_pairs={{0,4},{4,0},{1,5},{5,1},{2,6},{6,2},{3,7},{7,3},{8,12},{12,8},{9,1... | collective-permute-start | bytes 1032200 | tf_op jit(solution)/shard_map/ppermute | solution.py:480
  25.9 5.5 %collective-permute-start.11 = (bf16[144,768]{1,0:T(8,128)(2,1)S(1)}, bf16[144,768]{1,0:T(8,128)(2,1)S(1)}, u32[]{:S(2)}, u32[]{:S(2)}) collective-permute-start(bf16[144,768]{1,0:T(8,128)(2,1)S(1)} %collective-permute-done.8.refs_9_), channel_id=1, source_target_pairs={{0,4},{4,0},{1,5},{5,1},{2,6},{6,2},{3,7},{7,3},{8,12},{12,8},{9,1... | collective-permute-start | bytes 663560 | tf_op jit(solution)/shard_map/ppermute | solution.py:480
  29.9 1.5 %collective-permute-start.10 = (bf16[144,768]{1,0:T(8,128)(2,1)S(1)}, bf16[144,768]{1,0:T(8,128)(2,1)S(1)}, u32[]{:S(2)}, u32[]{:S(2)}) collective-permute-start(bf16[144,768]{1,0:T(8,128)(2,1)S(1)} %collective-permute-done.7.refs_8_), channel_id=1, source_target_pairs={{0,4},{4,0},{1,5},{5,1},{2,6},{6,2},{3,7},{7,3},{8,12},{12,8},{9,1... | collective-permute-start | bytes 663560 | tf_op jit(solution)/shard_map/ppermute | solution.py:480
  29.9 1.8 %collective-permute-start.12 = (bf16[144,768]{1,0:T(8,128)(2,1)S(1)}, bf16[144,768]{1,0:T(8,128)(2,1)S(1)}, u32[]{:S(2)}, u32[]{:S(2)}) collective-permute-start(bf16[144,768]{1,0:T(8,128)(2,1)S(1)} %collective-permute-done.9.refs_10_), channel_id=1, source_target_pairs={{0,4},{4,0},{1,5},{5,1},{2,6},{6,2},{3,7},{7,3},{8,12},{12,8},{9,1... | collective-permute-start | bytes 663560 | tf_op jit(solution)/shard_map/ppermute | solution.py:480
  35.5 2.1 %collective-permute-start.13 = (bf16[4,96,768]{2,1,0:T(8,128)(2,1)S(1)}, bf16[4,96,768]{2,1,0:T(8,128)(2,1)S(1)}, u32[]{:S(2)}, u32[]{:S(2)}) collective-permute-start(bf16[4,96,768]{2,1,0:T(8,128)(2,1)S(1)} %get-tuple-element.41), channel_id=1, source_target_pairs={{0,4},{4,0},{1,5},{5,1},{2,6},{6,2},{3,7},{7,3},{8,12},{12,8},{9,1... | collective-permute-start | bytes 1769480 | tf_op jit(solution)/shard_map/ppermute | solution.py:480
  37.8 7.6 %collective-permute-start.14 = (bf16[96,768]{1,0:T(8,128)(2,1)S(1)}, bf16[96,768]{1,0:T(8,128)(2,1)S(1)}, u32[]{:S(2)}, u32[]{:S(2)}) collective-permute-start(bf16[96,768]{1,0:T(8,128)(2,1)S(1)} %get-tuple-element.43), channel_id=1, source_target_pairs={{0,24},{8,16},{16,8},{24,0},{1,25},{9,17},{17,9},{25,1},{2,26},{10... | collective-permute-start | bytes 442376 | tf_op jit(solution)/shard_map/ppermute | solution.py:480
  40.1 7.7 %collective-permute-start.15 = (bf16[96,768]{1,0:T(8,128)(2,1)S(1)}, bf16[96,768]{1,0:T(8,128)(2,1)S(1)}, u32[]{:S(2)}, u32[]{:S(2)}) collective-permute-start(bf16[96,768]{1,0:T(8,128)(2,1)S(1)} %get-tuple-element.44), channel_id=1, source_target_pairs={{0,16},{16,0},{1,17},{17,1},{2,18},{18,2},{3,19},{19,3},{4,20},{20... | collective-permute-start | bytes 442376 | tf_op jit(solution)/shard_map/ppermute | solution.py:480
  40.6 7.2 %collective-permute-start.16 = (bf16[96,768]{1,0:T(8,128)(2,1)S(1)}, bf16[96,768]{1,0:T(8,128)(2,1)S(1)}, u32[]{:S(2)}, u32[]{:S(2)}) collective-permute-start(bf16[96,768]{1,0:T(8,128)(2,1)S(1)} %get-tuple-element.45), channel_id=1, source_target_pairs={{0,8},{8,0},{1,9},{9,1},{2,10},{10,2},{3,11},{11,3},{4,12},{12,4},... | collective-permute-start | bytes 442376 | tf_op jit(solution)/shard_map/ppermute | solution.py:480
  47.9 6.0 %collective-permute-start.17 = (bf16[48,384]{1,0:T(8,128)(2,1)S(1)}, bf16[48,384]{1,0:T(8,128)(2,1)S(1)}, u32[]{:S(2)}, u32[]{:S(2)}) collective-permute-start(bf16[48,384]{1,0:T(8,128)(2,1)S(1)} %get-tuple-element.47), channel_id=1, source_target_pairs={{0,3},{1,2},{2,1},{3,0},{4,7},{5,6},{6,5},{7,4},{8,11},{9,10},{10,... | collective-permute-start | bytes 110600 | tf_op jit(solution)/shard_map/ppermute | solution.py:484
  51.5 4.9 %collective-permute-start.18 = (bf16[48,384]{1,0:T(8,128)(2,1)S(1)}, bf16[48,384]{1,0:T(8,128)(2,1)S(1)}, u32[]{:S(2)}, u32[]{:S(2)}) collective-permute-start(bf16[48,384]{1,0:T(8,128)(2,1)S(1)} %get-tuple-element.48), channel_id=1, source_target_pairs={{0,2},{1,3},{2,0},{3,1},{4,6},{5,7},{6,4},{7,5},{8,10},{9,11},{10,... | collective-permute-start | bytes 110600 | tf_op jit(solution)/shard_map/ppermute | solution.py:484
  51.5 4.9 %collective-permute-start.19 = (bf16[48,384]{1,0:T(8,128)(2,1)S(1)}, bf16[48,384]{1,0:T(8,128)(2,1)S(1)}, u32[]{:S(2)}, u32[]{:S(2)}) collective-permute-start(bf16[48,384]{1,0:T(8,128)(2,1)S(1)} %get-tuple-element.49), channel_id=1, source_target_pairs={{0,1},{1,0},{2,3},{3,2},{4,5},{5,4},{6,7},{7,6},{8,9},{9,8},{10,11... | collective-permute-start | bytes 110600 | tf_op jit(solution)/shard_map/ppermute | solution.py:484

commit v11 on v10

--- a/solution.py
+++ b/solution.py
@@ -235,9 +235,8 @@
     )
 
 
-def tower_body(
-    first, project, conv, p2, count, emb, cap, cx_ref, hot_f_ref, hot_r_ref,
-    s1_ref, gb_ref, g_ref, put,
+def tower_front(
+    first, project, conv, p2, count, emb, cap, cx_ref, hot_f_ref, hot_r_ref, s1_ref, put
 ):
     entry = iota((TABLE, 1), 0)
     by25 = (entry * 1311) >> 15
@@ -262,8 +261,7 @@
     s2 = jnp.concatenate(split(slope), axis=0)
 
     grow = cap + 2 * HALO
-    inner = cap + 2 * FIRST_DILATION
-    d, D = FIRST_DILATION, SECOND_DILATION
+    D = SECOND_DILATION
     cx = cx_ref[...]
     back_mid = mm_nt(cx, p2)
     before = jnp.zeros((2 * grow, p2.shape[0]), F32)
@@ -282,6 +280,16 @@
     put(1, mm_tn(mids, jnp.concatenate([own_gb, own_gb], axis=0)))
     grad_f = (back_mid * slope[0:grow]).astype(BF16)
     grad_r = (back_mid * slope[grow:]).astype(BF16)
+    return b1, s2, grad_f, grad_r
+
+
+def tower_back(
+    conv, b1, s2, grad_f, grad_r, count, cap, cx_ref, hot_f_ref, hot_r_ref, gb_ref, g_ref, put
+):
+    inner = cap + 2 * FIRST_DILATION
+    d, D = FIRST_DILATION, SECOND_DILATION
+    cx = cx_ref[...]
+    own_col = (iota((cap, 1), 0).astype(F32) < count).astype(F32)
     ga = jnp.zeros((2 * inner, cx.shape[1]), F32)
     for k in range(3):
         rows = jnp.concatenate(
@@ -350,8 +358,8 @@
 def tower_kernel_packed(*refs):
     own_parts, plane_parts, dp_parts = refs[0:2], refs[2:8], refs[8:14]
     small_ref, cx_ref, hf_ref, hr_ref = refs[14:18]
-    keep_ref, send_ref, s1_ref, gb_ref, g_ref, wide_ref, p1_ref = refs[18:25]
-    conv_ref, p2_ref, first_ref, second_ref = refs[25:]
+    keep_ref, send_ref, s1_ref, wide_ref, p1_ref, conv_ref, *outs = refs[18:28]
+    p2_ref, first_ref, second_ref = refs[28:]
     me = position()
     core, odd = me & 1, lax.axis_index("dp") & 1
     count = small_ref[5:6, 0:1]
@@ -407,17 +415,32 @@
         wide = wide + second_ref[peer]
     wide_ref[...] = jnp.concatenate([wide[:, 0:width], wide[:, width : 2 * width]], axis=0)
 
-    def put(block, value):
-        rows = value.shape[0] // 4
-        for c in range(2):
-            even = value[2 * c * rows : (2 * c + 1) * rows]
-            uneven = value[(2 * c + 1) * rows : (2 * c + 2) * rows]
-            keep_ref[2 * block + c] = jnp.where(core == 0, even, uneven)
-            send_ref[2 * block + c] = jnp.where(core == 0, uneven, even).astype(BF16)
-
-    tower_body(
+    results = tower_front(
         first, p1_ref[...], lambda k: conv_ref[k], p2_ref[...], count, small_ref[0:4],
-        g_ref.shape[0] // 2, cx_ref, hf_ref, hr_ref, s1_ref, gb_ref, g_ref, put,
+        cx_ref.shape[0] - 2 * HALO, cx_ref, hf_ref, hr_ref, s1_ref,
+        functools.partial(share, core, keep_ref, send_ref),
+    )
+    for out, value in zip(outs, results):
+        out[...] = value
+
+
+def share(core, keep_ref, send_ref, block, value):
+    rows = value.shape[0] // 4
+    for c in range(2):
+        even = value[2 * c * rows : (2 * c + 1) * rows]
+        uneven = value[(2 * c + 1) * rows : (2 * c + 2) * rows]
+        keep_ref[c] = jnp.where(core == 0, even, uneven)
+        send_ref[c] = jnp.where(core == 0, uneven, even).astype(BF16)
+
+
+def back_kernel(
+    conv_ref, b1_ref, s2_ref, grad_f_ref, grad_r_ref, small_ref, cx_ref, hf_ref, hr_ref,
+    keep_ref, send_ref, gb_ref, g_ref,
+):
+    tower_back(
+        lambda k: conv_ref[k], b1_ref[...], s2_ref[...], grad_f_ref[...], grad_r_ref[...],
+        small_ref[5:6, 0:1], cx_ref.shape[0] - 2 * HALO, cx_ref, hf_ref, hr_ref, gb_ref, g_ref,
+        functools.partial(share, lax.axis_index("core"), keep_ref, send_ref),
     )
 
 
@@ -429,10 +452,13 @@
         rows = value.shape[0]
         grad_ref[block * rows : (block + 1) * rows] = value
 
-    tower_body(
-        first_ref[...], p1_ref[...], lambda k: conv_ref[k], p2_ref[...], small_ref[5:6, 0:1],
-        small_ref[0:4], g_ref.shape[0] // 2, cx_ref, hf_ref, hr_ref, s1_ref, gb_ref, g_ref, put,
-    )
+    cap, count = g_ref.shape[0] // 2, small_ref[5:6, 0:1]
+    conv = lambda k: conv_ref[k]
+    results = tower_front(
+        first_ref[...], p1_ref[...], conv, p2_ref[...], count, small_ref[0:4], cap, cx_ref,
+        hf_ref, hr_ref, s1_ref, put,
+    )
+    tower_back(conv, *results, count, cap, cx_ref, hf_ref, hr_ref, gb_ref, g_ref, put)
 
 
 def fold(value):
@@ -440,12 +466,16 @@
     return jnp.concatenate([value[:, 0:width], value[:, width:]], axis=0)
 
 
-def core_sum_kernel(keep_ref, recv_ref, own_ref, *outs):
+def core_sum_kernel(keep1_ref, recv1_ref, keep2_ref, recv2_ref, own_ref, *outs):
     chip = 2 * lax.axis_index("y") + lax.axis_index("x")
-    own_ref[...] = keep_ref[chip] + recv_ref[chip].astype(F32)
-    for n, out in enumerate(outs):
-        at = chip ^ (n + 1)
-        out[...] = (keep_ref[at] + recv_ref[at].astype(F32)).astype(BF16)
+    for n, out in enumerate((own_ref, *outs)):
+        at, low = (chip ^ n) & 1, (chip ^ n) < 2
+        total = jnp.where(
+            low,
+            keep1_ref[at] + recv1_ref[at].astype(F32),
+            keep2_ref[at] + recv2_ref[at].astype(F32),
+        )
+        out[...] = total.astype(out.dtype)
 
 
 def plane_sum_kernel(own_ref, d_ref, y_ref, x_ref, mine_ref, *refs):
@@ -548,16 +578,17 @@
         ],
         cost=weight(10**9),
     )
-    keep, send, s1, gb, g, second, p1_full = call(
+    keep2, send2, s1, second, p1_full, conv, *middle = call(
         tower_kernel_packed,
-        [((4, rows, chans), F32), ((4, rows, chans), BF16), *pass_shapes(cap, chans, width)]
-        + [((48, width), F32), ((width, chans), BF16)],
+        [((2, rows, chans), F32), ((2, rows, chans), BF16), ((2 * TABLE, width), BF16)]
+        + [((48, width), F32), ((width, chans), BF16), ((3, chans, width), BF16)]
+        + [((TABLE, width), BF16), ((2 * TABLE, chans), BF16)]
+        + [((cap + 2 * HALO, width), BF16)] * 2,
         [
             own, swapped[0], *plane, *swapped[1:], *other, *across(other),
             small, cx, hf, hr,
         ],
         scratch=[
-            pltpu.VMEM((3, chans, width), BF16),
             pltpu.VMEM((width, chans), BF16),
             pltpu.VMEM((8, 16, width), F32),
             pltpu.VMEM((8, 24, chans), F32),
@@ -565,7 +596,14 @@
         limit=40,
         cost=weight(4 * 10**9),
     )
-    recv = flip_move(send, "core")
+    recv2 = flip_move(send2, "core")
+    keep1, send1, gb, g = call(
+        back_kernel,
+        [((2, rows, chans), F32), ((2, rows, chans), BF16)] + pass_shapes(cap, chans, width)[1:],
+        [conv, *middle, small, cx, hf, hr],
+        cost=weight(2 * 10**9),
+    )
+    recv1 = flip_move(send1, "core")
     (sal,) = call(
         saliency_kernel,
         [((4, cap), F32)],
@@ -575,7 +613,7 @@
     own, *outs = call(
         core_sum_kernel,
         [((rows, chans), F32)] + [((rows, chans), BF16)] * 3,
-        [keep, recv],
+        [keep1, recv1, keep2, recv2],
     )
     ways = (("x",), ("y",), ("y", "x"))
     got = [flip_move(outs[n], *ways[n]) for n in (2, 1, 0)]

time: 57.2 us -> 59.9 us (1.047)
  local copies, waits for them, and re-layouts: 0.04 us -> 2.31 us
    unnamed x6, local copies, waits for them, and re-layouts: 0.01 us -> 2.28 us
    pallas_call x7 -> x8, Pallas kernels: 7.62 us -> 8.08 us  [call(): pl.pallas_call(body, out_shape=[jax.ShapeDtypeStruct(s, d) for s, d in ou...]
    ppermute x14 -> x15, waiting for transfers between devices: 20.4 us -> 19.9 us  [flip_move(): return lax.ppermute(array, axes, [(i, size - 1 - i) for i in range(size)])]
    ppermute x14 -> x15, starting transfers between devices: 9.48 us -> 9.86 us  [flip_move(): return lax.ppermute(array, axes, [(i, size - 1 - i) for i in range(size)])]
  transfers between devices with their start and end apart: 20 -> 21, of which waited for: 9 -> 9; matrix products, arithmetic and copies ran while one was open for 0% -> 0% of each run, Pallas kernels for 4% -> 7%
where the time goes in v11:
time: 59.9 us; the launch traced here: 59.7 us
  waiting for transfers between devices  26.3 us (44%)
  starting transfers between devices  19.6 us (33%)
  Pallas kernels  8.08 us (13%)
  local copies, waits for them, and re-layouts  2.31 us (4%)
  other arithmetic  2.02 us (3%)
  between operations  1.37 us (2%)
    ppermute x15, waiting for transfers between devices, flip_move(): return lax.ppermute(array, axes, [(i, size - 1 - i) for i in range(size)])  19.9 us
    ppermute x15, starting transfers between devices, flip_move(): return lax.ppermute(array, axes, [(i, size - 1 - i) for i in range(size)])  9.86 us
    ppermute x6, starting transfers between devices, xor_move(): lax.ppermute(array, axis, [(i, i ^ bits) for i in range(lax.axis_size(axi...  9.7 us
    pallas_call x8, Pallas kernels, call(): pl.pallas_call(body, out_shape=[jax.ShapeDtypeStruct(s, d) for s, d in ou...  8.08 us
    ppermute x6, waiting for transfers between devices, xor_move(): lax.ppermute(array, axis, [(i, i ^ bits) for i in range(lax.axis_size(axi...  6.39 us
    unnamed x6, local copies, waits for them, and re-layouts  2.28 us
  transfers between devices with their start and end apart: 21, of which 9 were waited for; matrix products, arithmetic and copies ran while one was open for 0% of the time, Pallas kernels for 7%

profile of v11, /device:TPU:0, one launch (start us, length us, event | category | flops | bytes accessed | tf_op | source)
XLA Modules:
  0.0 59.7 jit_solution(14198491256891484512)
XLA Ops:
  1.3 0.9 %pad_maximum_fusion.1.broad_ref = bf16[96,768]{1,0:T(8,128)(2,1)S(1)} fusion(bf16[48,768]{1,0:T(8,128)(2,1)} %param.12, bf16[48,768]{1,0:T(8,128)(2,1)} %param.14), kind=kLoop, calls=%fused_computation.1 | loop fusion | flops 294912 | bytes 294912 | tf_op jit(solution)/shard_map/concatenate | solution.py:553
  2.2 1.1 %pad_maximum_fusion.narrow_ref = bf16[576,384]{1,0:T(8,128)(2,1)S(1)} fusion(bf16[288,384]{1,0:T(8,128)(2,1)} %bitcast.6, bf16[288,384]{1,0:T(8,128)(2,1)} %bitcast.7), kind=kLoop, calls=%fused_computation | loop fusion | flops 884736 | bytes 884736 | tf_op jit(solution)/shard_map/concatenate | solution.py:552
  3.3 0.0 copy-start
  3.3 0.9 %copy-done = bf16[1,128,768]{2,1,0:T(8,128)(2,1)S(1)} copy-done((bf16[1,128,768]{2,1,0:T(8,128)(2,1)S(1)}, bf16[1,128,768]{2,1,0:T(8,128)(2,1)}, u32[]{:S(2)}) %copy-start) | copy-done | bytes 196632
  4.2 0.7 %copy-done.1 = f32[4,768]{1,0:T(4,128)S(1)} copy-done((f32[4,768]{1,0:T(4,128)S(1)}, f32[4,768]{1,0:T(4,128)}, u32[]{:S(2)}) %copy-start.1) | copy-done | bytes 12312
  4.9 0.7 %copy-done.2 = s32[1,128]{1,0:T(1,128)S(1)} copy-done((s32[1,128]{1,0:T(1,128)S(1)}, s32[1,128]{1,0:T(1,128)}, u32[]{:S(2)}) %copy-start.2) | copy-done | bytes 536
  5.6 0.4 shard_map.95
  6.0 3.0 %collective-permute-start.1 = (bf16[144,768]{1,0:T(8,128)(2,1)S(1)}, bf16[144,768]{1,0:T(8,128)(2,1)S(1)}, u32[]{:S(2)}, u32[]{:S(2)}) collective-permute-start(bf16[144,768]{1,0:T(8,128)(2,1)S(1)} %get-tuple-element.36), channel_id=1, source_target_pairs={{0,16},{16,0},{1,17},{17,1},{2,18},{18,2},{3,19},{19,3},{4,20},{20... | collective-permute-start | bytes 663560 | tf_op jit(solution)/shard_map/ppermute | solution.py:510
  9.1 1.5 %collective-permute-start = (bf16[224,768]{1,0:T(8,128)(2,1)S(1)}, bf16[224,768]{1,0:T(8,128)(2,1)S(1)}, u32[]{:S(2)}, u32[]{:S(2)}) collective-permute-start(bf16[224,768]{1,0:T(8,128)(2,1)S(1)} %get-tuple-element.35), channel_id=1, source_target_pairs={{0,8},{8,0},{1,9},{9,1},{2,10},{10,2},{3,11},{11,3},{4,12},{12,4},... | collective-permute-start | bytes 1032200 | tf_op jit(solution)/shard_map/ppermute | solution.py:510
  10.5 0.0 collective-permute-start.2
  10.6 3.9 %collective-permute-done.1.refs_2_.refs_3_ = bf16[144,768]{1,0:T(8,128)(2,1)S(1)} collective-permute-done((bf16[144,768]{1,0:T(8,128)(2,1)S(1)}, bf16[144,768]{1,0:T(8,128)(2,1)S(1)}, u32[]{:S(2)}, u32[]{:S(2)}) %collective-permute-start.1) | collective-permute-done | bytes 221216 | tf_op jit(solution)/shard_map/ppermute | solution.py:510
  14.5 1.8 %collective-permute-start.8 = (bf16[144,768]{1,0:T(8,128)(2,1)S(1)}, bf16[144,768]{1,0:T(8,128)(2,1)S(1)}, u32[]{:S(2)}, u32[]{:S(2)}) collective-permute-start(bf16[144,768]{1,0:T(8,128)(2,1)S(1)} %collective-permute-done.1.refs_2_.refs_3_), channel_id=1, source_target_pairs={{0,1},{1,0},{2,3},{3,2},{4,5},{5,4},{6,7},{7,6},{8,9},{9,8},{10,11... | collective-permute-start | bytes 663560 | tf_op jit(solution)/shard_map/ppermute | solution.py:514
  16.3 0.0 collective-permute-start.5
  16.3 3.7 %collective-permute-done.refs_1_.refs_2_ = bf16[224,768]{1,0:T(8,128)(2,1)S(1)} collective-permute-done((bf16[224,768]{1,0:T(8,128)(2,1)S(1)}, bf16[224,768]{1,0:T(8,128)(2,1)S(1)}, u32[]{:S(2)}, u32[]{:S(2)}) %collective-permute-start) | collective-permute-done | bytes 344096 | tf_op jit(solution)/shard_map/ppermute | solution.py:510
  20.1 1.6 %collective-permute-start.7 = (bf16[144,768]{1,0:T(8,128)(2,1)S(1)}, bf16[144,768]{1,0:T(8,128)(2,1)S(1)}, u32[]{:S(2)}, u32[]{:S(2)}) collective-permute-start(bf16[144,768]{1,0:T(8,128)(2,1)S(1)} %slice.8), channel_id=1, source_target_pairs={{0,1},{1,0},{2,3},{3,2},{4,5},{5,4},{6,7},{7,6},{8,9},{9,8},{10,11... | collective-permute-start | bytes 663560 | tf_op jit(solution)/shard_map/ppermute | solution.py:514
  21.7 4.0 %collective-permute-done.2.refs_3_.refs_4_ = bf16[224,768]{1,0:T(8,128)(2,1)S(1)} collective-permute-done((bf16[224,768]{1,0:T(8,128)(2,1)S(1)}, bf16[224,768]{1,0:T(8,128)(2,1)S(1)}, u32[]{:S(2)}, u32[]{:S(2)}) %collective-permute-start.2) | collective-permute-done | bytes 344096 | tf_op jit(solution)/shard_map/ppermute | solution.py:510
  25.8 1.8 %collective-permute-start.9 = (bf16[144,768]{1,0:T(8,128)(2,1)S(1)}, bf16[144,768]{1,0:T(8,128)(2,1)S(1)}, u32[]{:S(2)}, u32[]{:S(2)}) collective-permute-start(bf16[144,768]{1,0:T(8,128)(2,1)S(1)} %slice.9), channel_id=1, source_target_pairs={{0,1},{1,0},{2,3},{3,2},{4,5},{5,4},{6,7},{7,6},{8,9},{9,8},{10,11... | collective-permute-start | bytes 663560 | tf_op jit(solution)/shard_map/ppermute | solution.py:514
  27.6 0.0 collective-permute-done.5.refs_6_
  27.6 0.5 collective-permute-start.6
  28.1 0.1 collective-permute-start.11
  28.2 4.0 %collective-permute-done.9.refs_10_ = bf16[144,768]{1,0:T(8,128)(2,1)S(1)} collective-permute-done((bf16[144,768]{1,0:T(8,128)(2,1)S(1)}, bf16[144,768]{1,0:T(8,128)(2,1)S(1)}, u32[]{:S(2)}, u32[]{:S(2)}) %collective-permute-start.9) | collective-permute-done | bytes 221216 | tf_op jit(solution)/shard_map/ppermute | solution.py:514
  32.1 0.0 collective-permute-done.3.refs_4_.refs_1_
  32.1 0.5 collective-permute-start.12
  32.6 0.0 collective-permute-done.4.refs_5_
  32.6 0.0 collective-permute-done.6.refs_7_
  32.6 0.9 %shard_map.96 = (bf16[416,128]{1,0:T(8,128)(2,1)S(1)}, bf16[416,128]{1,0:T(8,128)(2,1)S(1)}, bf16[288,768]{1,0:T(8,128)(2,1)S(1)}) custom-call(bf16[368,768]{1,0:T(8,128)(2,1)S(1)} %get-tuple-element.34.refs_0_, bf16[224,768]{1,0:T(8,128)(2,1)S(1)} %collective-permute-done.refs_1_.refs_2_, bf16[144,768]{1,0:T(8,128)(2,1)S(1)} %collective-permute-done.1.refs_2_.refs_3_, ...), custom_call_target="tpu_custom_call" | custom-call | flops 1000000000 | bytes 1000000 | tf_op jit(solution)/shard_map/pallas_call | solution.py:61
  33.6 0.0 collective-permute-done.10.refs_11_
  33.6 0.3 collective-permute-done.12.refs_13_
  33.9 2.7 %shard_map.97 = (f32[2,96,768]{2,1,0:T(8,128)S(1)}, bf16[2,96,768]{2,1,0:T(8,128)(2,1)S(1)}, bf16[256,384]{1,0:T(8,128)(2,1)S(1)}, f32[48,384]{1,0:T(8,128)S(1)}...) custom-call(bf16[368,768]{1,0:T(8,128)(2,1)S(1)} %get-tuple-element., ...), custom_call_target="tpu_custom_call" | custom-call | flops 4000000000 | bytes 1000000 | tf_op jit(solution)/shard_map/pallas_call | solution.py:61
  36.7 0.3 collective-permute-start.14
  36.9 1.4 %shard_map.98 = (f32[2,96,768]{2,1,0:T(8,128)S(1)}, bf16[2,96,768]{2,1,0:T(8,128)(2,1)S(1)}, bf16[320,768]{1,0:T(8,128)(2,1)S(1)}, f32[256,768]{1,0:T(8,128)S(1)}) custom-call(bf16[3,768,384]{2,1,0:T(8,128)(2,1)S(1)} %get-tuple-element.43.conv_ref, bf16[128,384]{1,0:T(8,128)(2,1)S(1)} %get-tuple-element.44.b1_ref, ...), custom_call_target="tpu_custom_call" | custom-call | flops 2000000000 | bytes 1000000 | tf_op jit(solution)/shard_map/pallas_call | solution.py:61
  38.4 0.4 collective-permute-start.13
  38.7 1.3 %collective-permute-done.13.recv1_ref = bf16[2,96,768]{2,1,0:T(8,128)(2,1)S(1)} collective-permute-done((bf16[2,96,768]{2,1,0:T(8,128)(2,1)S(1)}, bf16[2,96,768]{2,1,0:T(8,128)(2,1)S(1)}, u32[]{:S(2)}, u32[]{:S(2)}) %collective-permute-start.13) | collective-permute-done | bytes 294944 | tf_op jit(solution)/shard_map/ppermute | solution.py:510
  40.0 0.3 shard_map.100
  40.3 2.3 %collective-permute-start.15 = (bf16[96,768]{1,0:T(8,128)(2,1)S(1)}, bf16[96,768]{1,0:T(8,128)(2,1)S(1)}, u32[]{:S(2)}, u32[]{:S(2)}) collective-permute-start(bf16[96,768]{1,0:T(8,128)(2,1)S(1)} %get-tuple-element.57), channel_id=1, source_target_pairs={{0,24},{8,16},{16,8},{24,0},{1,25},{9,17},{17,9},{25,1},{2,26},{10... | collective-permute-start | bytes 442376 | tf_op jit(solution)/shard_map/ppermute | solution.py:510
  42.6 0.5 collective-permute-start.16
  43.1 0.7 %collective-permute-start.17 = (bf16[96,768]{1,0:T(8,128)(2,1)S(1)}, bf16[96,768]{1,0:T(8,128)(2,1)S(1)}, u32[]{:S(2)}, u32[]{:S(2)}) collective-permute-start(bf16[96,768]{1,0:T(8,128)(2,1)S(1)} %get-tuple-element.59), channel_id=1, source_target_pairs={{0,8},{8,0},{1,9},{9,1},{2,10},{10,2},{3,11},{11,3},{4,12},{12,4},... | collective-permute-start | bytes 442376 | tf_op jit(solution)/shard_map/ppermute | solution.py:510
  43.8 4.1 %collective-permute-done.15.d_ref = bf16[96,768]{1,0:T(8,128)(2,1)S(1)} collective-permute-done((bf16[96,768]{1,0:T(8,128)(2,1)S(1)}, bf16[96,768]{1,0:T(8,128)(2,1)S(1)}, u32[]{:S(2)}, u32[]{:S(2)}) %collective-permute-start.15) | collective-permute-done | bytes 147488 | tf_op jit(solution)/shard_map/ppermute | solution.py:510
  47.9 2.6 %collective-permute-done.16.y_ref = bf16[96,768]{1,0:T(8,128)(2,1)S(1)} collective-permute-done((bf16[96,768]{1,0:T(8,128)(2,1)S(1)}, bf16[96,768]{1,0:T(8,128)(2,1)S(1)}, u32[]{:S(2)}, u32[]{:S(2)}) %collective-permute-start.16) | collective-permute-done | bytes 147488 | tf_op jit(solution)/shard_map/ppermute | solution.py:510
  50.5 0.0 collective-permute-done.17.x_ref
  50.5 0.1 shard_map.101
  50.6 3.6 %collective-permute-start.18 = (bf16[48,384]{1,0:T(8,128)(2,1)S(1)}, bf16[48,384]{1,0:T(8,128)(2,1)S(1)}, u32[]{:S(2)}, u32[]{:S(2)}) collective-permute-start(bf16[48,384]{1,0:T(8,128)(2,1)S(1)} %get-tuple-element.61), channel_id=1, source_target_pairs={{0,3},{1,2},{2,1},{3,0},{4,7},{5,6},{6,5},{7,4},{8,11},{9,10},{10,... | collective-permute-start | bytes 110600 | tf_op jit(solution)/shard_map/ppermute | solution.py:514
  54.2 0.9 %collective-permute-start.20 = (bf16[48,384]{1,0:T(8,128)(2,1)S(1)}, bf16[48,384]{1,0:T(8,128)(2,1)S(1)}, u32[]{:S(2)}, u32[]{:S(2)}) collective-permute-start(bf16[48,384]{1,0:T(8,128)(2,1)S(1)} %get-tuple-element.63), channel_id=1, source_target_pairs={{0,1},{1,0},{2,3},{3,2},{4,5},{5,4},{6,7},{7,6},{8,9},{9,8},{10,11... | collective-permute-start | bytes 110600 | tf_op jit(solution)/shard_map/ppermute | solution.py:514
  55.0 1.6 %shard_map.99 = f32[4,128]{1,0:T(4,128)} custom-call(f32[8,768]{1,0:T(8,128)S(1)} %get-tuple-element.33.refs_14_.small_ref, bf16[416,128]{1,0:T(8,128)(2,1)S(1)} %get-tuple-element.39.refs_16_.hf_ref.hot_f_ref, bf16[416,128]{1,0:T(8,128)(2,1)S(1)} %get-tuple-element.40.refs_17_.hr_ref.hot_r_ref, bf16[256,384]{1,0:T(8,128)(2,1)S(1)} %get-tuple-element.42.s1_ref, ...), custom_call_target="tpu_custom_call" | custom-call | flops 1000000000 | bytes 1000000 | tf_op jit(solution)/shard_map/pallas_call | solution.py:61
  56.6 0.0 collective-permute-done.18.refs_0_
  56.6 2.4 %collective-permute-done.19.refs_1_ = bf16[48,384]{1,0:T(8,128)(2,1)S(1)} collective-permute-done((bf16[48,384]{1,0:T(8,128)(2,1)S(1)}, bf16[48,384]{1,0:T(8,128)(2,1)S(1)}, u32[]{:S(2)}, u32[]{:S(2)}) %collective-permute-start.19) | collective-permute-done | bytes 36896 | tf_op jit(solution)/shard_map/ppermute | solution.py:514
  59.0 0.0 collective-permute-done.20.refs_2_
  59.0 0.7 %shard_map.102 = f32[144,128]{1,0:T(8,128)} custom-call(f32[48,384]{1,0:T(8,128)S(1)} %get-tuple-element.60.mine_ref, bf16[48,384]{1,0:T(8,128)(2,1)S(1)} %collective-permute-done.18.refs_0_, bf16[48,384]{1,0:T(8,128)(2,1)S(1)} %collective-permute-done.19.refs_1_, bf16[48,384]{1,0:T(8,128)(2,1)S(1)} %collective-permute-done.20.refs_2_), custom_call_target="tpu_custom_call" | custom-call | tf_op jit(solution)/shard_map/pallas_call | solution.py:61
  (12 shorter events, 0.1 us)
Async XLA Ops:
  3.3 0.9 %copy-start = (bf16[1,128,768]{2,1,0:T(8,128)(2,1)S(1)}, bf16[1,128,768]{2,1,0:T(8,128)(2,1)}, u32[]{:S(2)}) copy-start(bf16[1,128,768]{2,1,0:T(8,128)(2,1)} %param.10) | copy-start | bytes 589828
  4.2 0.7 %copy-start.1 = (f32[4,768]{1,0:T(4,128)S(1)}, f32[4,768]{1,0:T(4,128)}, u32[]{:S(2)}) copy-start(f32[4,768]{1,0:T(4,128)} %embed_ref.1) | copy-start | bytes 36868
  4.9 0.7 %copy-start.2 = (s32[1,128]{1,0:T(1,128)S(1)}, s32[1,128]{1,0:T(1,128)}, u32[]{:S(2)}) copy-start(s32[1,128]{1,0:T(1,128)} %bases_ref.1) | copy-start | bytes 1540
  6.0 8.5 %collective-permute-start.1 = (bf16[144,768]{1,0:T(8,128)(2,1)S(1)}, bf16[144,768]{1,0:T(8,128)(2,1)S(1)}, u32[]{:S(2)}, u32[]{:S(2)}) collective-permute-start(bf16[144,768]{1,0:T(8,128)(2,1)S(1)} %get-tuple-element.36), channel_id=1, source_target_pairs={{0,16},{16,0},{1,17},{17,1},{2,18},{18,2},{3,19},{19,3},{4,20},{20... | collective-permute-start | bytes 663560 | tf_op jit(solution)/shard_map/ppermute | solution.py:510
  9.1 11.0 %collective-permute-start = (bf16[224,768]{1,0:T(8,128)(2,1)S(1)}, bf16[224,768]{1,0:T(8,128)(2,1)S(1)}, u32[]{:S(2)}, u32[]{:S(2)}) collective-permute-start(bf16[224,768]{1,0:T(8,128)(2,1)S(1)} %get-tuple-element.35), channel_id=1, source_target_pairs={{0,8},{8,0},{1,9},{9,1},{2,10},{10,2},{3,11},{11,3},{4,12},{12,4},... | collective-permute-start | bytes 1032200 | tf_op jit(solution)/shard_map/ppermute | solution.py:510
  10.5 15.2 %collective-permute-start.2 = (bf16[224,768]{1,0:T(8,128)(2,1)S(1)}, bf16[224,768]{1,0:T(8,128)(2,1)S(1)}, u32[]{:S(2)}, u32[]{:S(2)}) collective-permute-start(bf16[224,768]{1,0:T(8,128)(2,1)S(1)} %get-tuple-element.37), channel_id=1, source_target_pairs={{0,24},{8,16},{16,8},{24,0},{1,25},{9,17},{17,9},{25,1},{2,26},{10... | collective-permute-start | bytes 1032200 | tf_op jit(solution)/shard_map/ppermute | solution.py:510
  10.6 21.5 %collective-permute-start.3 = (bf16[368,768]{1,0:T(8,128)(2,1)S(1)}, bf16[368,768]{1,0:T(8,128)(2,1)S(1)}, u32[]{:S(2)}, u32[]{:S(2)}) collective-permute-start(bf16[368,768]{1,0:T(8,128)(2,1)S(1)} %get-tuple-element.34.refs_0_), channel_id=1, source_target_pairs={{0,4},{4,0},{1,5},{5,1},{2,6},{6,2},{3,7},{7,3},{8,12},{12,8},{9,1... | collective-permute-start | bytes 1695752 | tf_op jit(solution)/shard_map/ppermute | solution.py:510
  14.5 13.1 %collective-permute-start.8 = (bf16[144,768]{1,0:T(8,128)(2,1)S(1)}, bf16[144,768]{1,0:T(8,128)(2,1)S(1)}, u32[]{:S(2)}, u32[]{:S(2)}) collective-permute-start(bf16[144,768]{1,0:T(8,128)(2,1)S(1)} %collective-permute-done.1.refs_2_.refs_3_), channel_id=1, source_target_pairs={{0,1},{1,0},{2,3},{3,2},{4,5},{5,4},{6,7},{7,6},{8,9},{9,8},{10,11... | collective-permute-start | bytes 663560 | tf_op jit(solution)/shard_map/ppermute | solution.py:514
  16.3 11.3 %collective-permute-start.5 = (bf16[144,768]{1,0:T(8,128)(2,1)S(1)}, bf16[144,768]{1,0:T(8,128)(2,1)S(1)}, u32[]{:S(2)}, u32[]{:S(2)}) collective-permute-start(bf16[144,768]{1,0:T(8,128)(2,1)S(1)} %collective-permute-done.1.refs_2_.refs_3_), channel_id=1, source_target_pairs={{0,4},{4,0},{1,5},{5,1},{2,6},{6,2},{3,7},{7,3},{8,12},{12,8},{9,1... | collective-permute-start | bytes 663560 | tf_op jit(solution)/shard_map/ppermute | solution.py:510
  20.1 8.0 %collective-permute-start.7 = (bf16[144,768]{1,0:T(8,128)(2,1)S(1)}, bf16[144,768]{1,0:T(8,128)(2,1)S(1)}, u32[]{:S(2)}, u32[]{:S(2)}) collective-permute-start(bf16[144,768]{1,0:T(8,128)(2,1)S(1)} %slice.8), channel_id=1, source_target_pairs={{0,1},{1,0},{2,3},{3,2},{4,5},{5,4},{6,7},{7,6},{8,9},{9,8},{10,11... | collective-permute-start | bytes 663560 | tf_op jit(solution)/shard_map/ppermute | solution.py:514
  25.8 6.4 %collective-permute-start.9 = (bf16[144,768]{1,0:T(8,128)(2,1)S(1)}, bf16[144,768]{1,0:T(8,128)(2,1)S(1)}, u32[]{:S(2)}, u32[]{:S(2)}) collective-permute-start(bf16[144,768]{1,0:T(8,128)(2,1)S(1)} %slice.9), channel_id=1, source_target_pairs={{0,1},{1,0},{2,3},{3,2},{4,5},{5,4},{6,7},{7,6},{8,9},{9,8},{10,11... | collective-permute-start | bytes 663560 | tf_op jit(solution)/shard_map/ppermute | solution.py:514
  27.6 5.1 %collective-permute-start.4 = (bf16[224,768]{1,0:T(8,128)(2,1)S(1)}, bf16[224,768]{1,0:T(8,128)(2,1)S(1)}, u32[]{:S(2)}, u32[]{:S(2)}) collective-permute-start(bf16[224,768]{1,0:T(8,128)(2,1)S(1)} %collective-permute-done.refs_1_.refs_2_), channel_id=1, source_target_pairs={{0,4},{4,0},{1,5},{5,1},{2,6},{6,2},{3,7},{7,3},{8,12},{12,8},{9,1... | collective-permute-start | bytes 1032200 | tf_op jit(solution)/shard_map/ppermute | solution.py:510
  27.6 5.1 %collective-permute-start.6 = (bf16[224,768]{1,0:T(8,128)(2,1)S(1)}, bf16[224,768]{1,0:T(8,128)(2,1)S(1)}, u32[]{:S(2)}, u32[]{:S(2)}) collective-permute-start(bf16[224,768]{1,0:T(8,128)(2,1)S(1)} %collective-permute-done.2.refs_3_.refs_4_), channel_id=1, source_target_pairs={{0,4},{4,0},{1,5},{5,1},{2,6},{6,2},{3,7},{7,3},{8,12},{12,8},{9,1... | collective-permute-start | bytes 1032200 | tf_op jit(solution)/shard_map/ppermute | solution.py:510
  28.1 5.5 %collective-permute-start.11 = (bf16[144,768]{1,0:T(8,128)(2,1)S(1)}, bf16[144,768]{1,0:T(8,128)(2,1)S(1)}, u32[]{:S(2)}, u32[]{:S(2)}) collective-permute-start(bf16[144,768]{1,0:T(8,128)(2,1)S(1)} %collective-permute-done.8.refs_9_), channel_id=1, source_target_pairs={{0,4},{4,0},{1,5},{5,1},{2,6},{6,2},{3,7},{7,3},{8,12},{12,8},{9,1... | collective-permute-start | bytes 663560 | tf_op jit(solution)/shard_map/ppermute | solution.py:510
  32.1 1.5 %collective-permute-start.10 = (bf16[144,768]{1,0:T(8,128)(2,1)S(1)}, bf16[144,768]{1,0:T(8,128)(2,1)S(1)}, u32[]{:S(2)}, u32[]{:S(2)}) collective-permute-start(bf16[144,768]{1,0:T(8,128)(2,1)S(1)} %collective-permute-done.7.refs_8_), channel_id=1, source_target_pairs={{0,4},{4,0},{1,5},{5,1},{2,6},{6,2},{3,7},{7,3},{8,12},{12,8},{9,1... | collective-permute-start | bytes 663560 | tf_op jit(solution)/shard_map/ppermute | solution.py:510
  32.1 1.8 %collective-permute-start.12 = (bf16[144,768]{1,0:T(8,128)(2,1)S(1)}, bf16[144,768]{1,0:T(8,128)(2,1)S(1)}, u32[]{:S(2)}, u32[]{:S(2)}) collective-permute-start(bf16[144,768]{1,0:T(8,128)(2,1)S(1)} %collective-permute-done.9.refs_10_), channel_id=1, source_target_pairs={{0,4},{4,0},{1,5},{5,1},{2,6},{6,2},{3,7},{7,3},{8,12},{12,8},{9,1... | collective-permute-start | bytes 663560 | tf_op jit(solution)/shard_map/ppermute | solution.py:510
  36.7 2.1 %collective-permute-start.14 = (bf16[2,96,768]{2,1,0:T(8,128)(2,1)S(1)}, bf16[2,96,768]{2,1,0:T(8,128)(2,1)S(1)}, u32[]{:S(2)}, u32[]{:S(2)}) collective-permute-start(bf16[2,96,768]{2,1,0:T(8,128)(2,1)S(1)} %get-tuple-element.55), channel_id=1, source_target_pairs={{0,4},{4,0},{1,5},{5,1},{2,6},{6,2},{3,7},{7,3},{8,12},{12,8},{9,1... | collective-permute-start | bytes 884744 | tf_op jit(solution)/shard_map/ppermute | solution.py:510
  38.4 1.6 %collective-permute-start.13 = (bf16[2,96,768]{2,1,0:T(8,128)(2,1)S(1)}, bf16[2,96,768]{2,1,0:T(8,128)(2,1)S(1)}, u32[]{:S(2)}, u32[]{:S(2)}) collective-permute-start(bf16[2,96,768]{2,1,0:T(8,128)(2,1)S(1)} %get-tuple-element.53), channel_id=1, source_target_pairs={{0,4},{4,0},{1,5},{5,1},{2,6},{6,2},{3,7},{7,3},{8,12},{12,8},{9,1... | collective-permute-start | bytes 884744 | tf_op jit(solution)/shard_map/ppermute | solution.py:510
  40.3 7.6 %collective-permute-start.15 = (bf16[96,768]{1,0:T(8,128)(2,1)S(1)}, bf16[96,768]{1,0:T(8,128)(2,1)S(1)}, u32[]{:S(2)}, u32[]{:S(2)}) collective-permute-start(bf16[96,768]{1,0:T(8,128)(2,1)S(1)} %get-tuple-element.57), channel_id=1, source_target_pairs={{0,24},{8,16},{16,8},{24,0},{1,25},{9,17},{17,9},{25,1},{2,26},{10... | collective-permute-start | bytes 442376 | tf_op jit(solution)/shard_map/ppermute | solution.py:510
  42.6 7.8 %collective-permute-start.16 = (bf16[96,768]{1,0:T(8,128)(2,1)S(1)}, bf16[96,768]{1,0:T(8,128)(2,1)S(1)}, u32[]{:S(2)}, u32[]{:S(2)}) collective-permute-start(bf16[96,768]{1,0:T(8,128)(2,1)S(1)} %get-tuple-element.58), channel_id=1, source_target_pairs={{0,16},{16,0},{1,17},{17,1},{2,18},{18,2},{3,19},{19,3},{4,20},{20... | collective-permute-start | bytes 442376 | tf_op jit(solution)/shard_map/ppermute | solution.py:510
  43.1 7.3 %collective-permute-start.17 = (bf16[96,768]{1,0:T(8,128)(2,1)S(1)}, bf16[96,768]{1,0:T(8,128)(2,1)S(1)}, u32[]{:S(2)}, u32[]{:S(2)}) collective-permute-start(bf16[96,768]{1,0:T(8,128)(2,1)S(1)} %get-tuple-element.59), channel_id=1, source_target_pairs={{0,8},{8,0},{1,9},{9,1},{2,10},{10,2},{3,11},{11,3},{4,12},{12,4},... | collective-permute-start | bytes 442376 | tf_op jit(solution)/shard_map/ppermute | solution.py:510
  50.6 6.0 %collective-permute-start.18 = (bf16[48,384]{1,0:T(8,128)(2,1)S(1)}, bf16[48,384]{1,0:T(8,128)(2,1)S(1)}, u32[]{:S(2)}, u32[]{:S(2)}) collective-permute-start(bf16[48,384]{1,0:T(8,128)(2,1)S(1)} %get-tuple-element.61), channel_id=1, source_target_pairs={{0,3},{1,2},{2,1},{3,0},{4,7},{5,6},{6,5},{7,4},{8,11},{9,10},{10,... | collective-permute-start | bytes 110600 | tf_op jit(solution)/shard_map/ppermute | solution.py:514
  54.2 4.9 %collective-permute-start.19 = (bf16[48,384]{1,0:T(8,128)(2,1)S(1)}, bf16[48,384]{1,0:T(8,128)(2,1)S(1)}, u32[]{:S(2)}, u32[]{:S(2)}) collective-permute-start(bf16[48,384]{1,0:T(8,128)(2,1)S(1)} %get-tuple-element.62), channel_id=1, source_target_pairs={{0,2},{1,3},{2,0},{3,1},{4,6},{5,7},{6,4},{7,5},{8,10},{9,11},{10,... | collective-permute-start | bytes 110600 | tf_op jit(solution)/shard_map/ppermute | solution.py:514
  54.2 4.9 %collective-permute-start.20 = (bf16[48,384]{1,0:T(8,128)(2,1)S(1)}, bf16[48,384]{1,0:T(8,128)(2,1)S(1)}, u32[]{:S(2)}, u32[]{:S(2)}) collective-permute-start(bf16[48,384]{1,0:T(8,128)(2,1)S(1)} %get-tuple-element.63), channel_id=1, source_target_pairs={{0,1},{1,0},{2,3},{3,2},{4,5},{5,4},{6,7},{7,6},{8,9},{9,8},{10,11... | collective-permute-start | bytes 110600 | tf_op jit(solution)/shard_map/ppermute | solution.py:514

commit v12 on v10

--- a/solution.py
+++ b/solution.py
@@ -215,7 +215,7 @@
     info_ref[0:REACH] = jnp.zeros((REACH, 8, 256), F32)
     info_ref[REACH + 8 :] = jnp.zeros((REACH, 8, 256), F32)
     for n, part in enumerate(parts):
-        peer = me ^ (2 * (n % 4) + n // 4)
+        peer = me ^ (2 * (-n % 4) + n // 4)
         low = part[half - 16 : half].astype(F32)[12:13, 0:256]
         if n % 4 > 0:
             high = part[half - 16 : half].astype(F32)[8:9, 0:256]
@@ -223,8 +223,8 @@
         info_ref[REACH + peer] = jnp.broadcast_to(low, (8, 256))
     for n in range(2):
         halo_ref[4 * n + chip] = parts[4 * n][2 * half :]
-        halo_ref[4 * n + (chip ^ 1)] = parts[4 * n + 1][half:]
-        halo_ref[4 * n + (chip ^ 3)] = parts[4 * n + 3][half:]
+        halo_ref[4 * n + (chip ^ 3)] = parts[4 * n + 1][half:]
+        halo_ref[4 * n + (chip ^ 1)] = parts[4 * n + 3][half:]
     r1 = halo_ref[4 + jnp.maximum(chip + core - 1, 0)]
     l1 = halo_ref[4 + jnp.minimum(chip + core, 3)]
     r2 = halo_ref[jnp.maximum(chip - 1, 0)]
@@ -395,7 +395,7 @@
         @pl.when(odd == parity)
         def _():
             for n in range(6):
-                peer = me ^ (2 * (n % 3 + 1) + n // 3)
+                peer = me ^ (2 * (3 - n % 3) + n // 3)
                 for side, part in ((parity, plane_parts[n]), (1 - parity, dp_parts[n])):
                     rows = lambda a, size, part=part: part[a : a + size]
                     place(side, rows, peer)
@@ -533,7 +533,7 @@
         ],
         [narrow, broad, cot, embed, bases, lengths],
     )
-    plane = [flip_move(to_x, "x"), flip_move(to_y, "y"), flip_move(to_d, "y", "x")]
+    plane = [flip_move(to_d, "y", "x"), flip_move(to_y, "y"), flip_move(to_x, "x")]
     other = [xor_move(a[:half], "dp", 1) for a in plane]
     across = lambda arrays: [flip_move(a, "core") for a in arrays]
     rows = chans // 8

time: 57.2 us -> 63.1 us (1.10)
  waiting for transfers between devices: 26.8 us -> 34.1 us
  starting transfers between devices: 19.2 us -> 17.7 us
    ppermute x6, waiting for transfers between devices: 6.39 us -> 12.3 us  [xor_move(): lax.ppermute(array, axis, [(i, i ^ bits) for i in range(lax.axis_size(axi...]
    ppermute x14, waiting for transfers between devices: 20.4 us -> 21.8 us  [flip_move(): return lax.ppermute(array, axes, [(i, size - 1 - i) for i in range(size)])]
    ppermute x6, starting transfers between devices: 9.68 us -> 8.33 us  [xor_move(): lax.ppermute(array, axis, [(i, i ^ bits) for i in range(lax.axis_size(axi...]
  transfers between devices with their start and end apart: 20 -> 20, of which waited for: 9 -> 11; matrix products, arithmetic and copies ran while one was open for 0% -> 0% of each run, Pallas kernels for 4% -> 4%
where the time goes in v12:
time: 63.1 us; the launch traced here: 63 us
  waiting for transfers between devices  34.1 us (54%)
  starting transfers between devices  17.7 us (28%)
  Pallas kernels  7.63 us (12%)
  other arithmetic  2.02 us (3%)
  between operations  1.44 us (2%)
    ppermute x14, waiting for transfers between devices, flip_move(): return lax.ppermute(array, axes, [(i, size - 1 - i) for i in range(size)])  21.8 us
    ppermute x6, waiting for transfers between devices, xor_move(): lax.ppermute(array, axis, [(i, i ^ bits) for i in range(lax.axis_size(axi...  12.3 us
    ppermute x14, starting transfers between devices, flip_move(): return lax.ppermute(array, axes, [(i, size - 1 - i) for i in range(size)])  9.41 us
    ppermute x6, starting transfers between devices, xor_move(): lax.ppermute(array, axis, [(i, i ^ bits) for i in range(lax.axis_size(axi...  8.33 us
    pallas_call x7, Pallas kernels, call(): pl.pallas_call(body, out_shape=[jax.ShapeDtypeStruct(s, d) for s, d in ou...  7.63 us
  transfers between devices with their start and end apart: 20, of which 11 were waited for; matrix products, arithmetic and copies ran while one was open for 0% of the time, Pallas kernels for 4%

profile of v12, /device:TPU:0, one launch (start us, length us, event | category | flops | bytes accessed | tf_op | source)
XLA Modules:
  0.0 63.0 jit_solution(6568865509122493312)
XLA Ops:
  1.3 0.9 %pad_maximum_fusion.1.broad_ref = bf16[96,768]{1,0:T(8,128)(2,1)S(1)} fusion(bf16[48,768]{1,0:T(8,128)(2,1)} %param.12, bf16[48,768]{1,0:T(8,128)(2,1)} %param.14), kind=kLoop, calls=%fused_computation.1 | loop fusion | flops 294912 | bytes 294912 | tf_op jit(solution)/shard_map/concatenate | solution.py:523
  2.3 1.1 %pad_maximum_fusion.narrow_ref = bf16[576,384]{1,0:T(8,128)(2,1)S(1)} fusion(bf16[288,384]{1,0:T(8,128)(2,1)} %bitcast.6, bf16[288,384]{1,0:T(8,128)(2,1)} %bitcast.7), kind=kLoop, calls=%fused_computation | loop fusion | flops 884736 | bytes 884736 | tf_op jit(solution)/shard_map/concatenate | solution.py:522
  3.4 0.4 shard_map.95
  3.8 3.0 %collective-permute-start.1 = (bf16[144,768]{1,0:T(8,128)(2,1)S(1)}, bf16[144,768]{1,0:T(8,128)(2,1)S(1)}, u32[]{:S(2)}, u32[]{:S(2)}) collective-permute-start(bf16[144,768]{1,0:T(8,128)(2,1)S(1)} %get-tuple-element.29), channel_id=1, source_target_pairs={{0,16},{16,0},{1,17},{17,1},{2,18},{18,2},{3,19},{19,3},{4,20},{20... | collective-permute-start | bytes 663560 | tf_op jit(solution)/shard_map/ppermute | solution.py:480
  6.9 1.4 %collective-permute-start = (bf16[224,768]{1,0:T(8,128)(2,1)S(1)}, bf16[224,768]{1,0:T(8,128)(2,1)S(1)}, u32[]{:S(2)}, u32[]{:S(2)}) collective-permute-start(bf16[224,768]{1,0:T(8,128)(2,1)S(1)} %get-tuple-element.28), channel_id=1, source_target_pairs={{0,24},{8,16},{16,8},{24,0},{1,25},{9,17},{17,9},{25,1},{2,26},{10... | collective-permute-start | bytes 1032200 | tf_op jit(solution)/shard_map/ppermute | solution.py:480
  8.3 0.1 collective-permute-start.2
  8.4 0.0 collective-permute-start.3
  8.4 11.3 %collective-permute-done.1.refs_2_.refs_3_ = bf16[144,768]{1,0:T(8,128)(2,1)S(1)} collective-permute-done((bf16[144,768]{1,0:T(8,128)(2,1)S(1)}, bf16[144,768]{1,0:T(8,128)(2,1)S(1)}, u32[]{:S(2)}, u32[]{:S(2)}) %collective-permute-start.1) | collective-permute-done | bytes 221216 | tf_op jit(solution)/shard_map/ppermute | solution.py:480
  19.7 1.8 %collective-permute-start.8 = (bf16[144,768]{1,0:T(8,128)(2,1)S(1)}, bf16[144,768]{1,0:T(8,128)(2,1)S(1)}, u32[]{:S(2)}, u32[]{:S(2)}) collective-permute-start(bf16[144,768]{1,0:T(8,128)(2,1)S(1)} %collective-permute-done.1.refs_2_.refs_3_), channel_id=1, source_target_pairs={{0,1},{1,0},{2,3},{3,2},{4,5},{5,4},{6,7},{7,6},{8,9},{9,8},{10,11... | collective-permute-start | bytes 663560 | tf_op jit(solution)/shard_map/ppermute | solution.py:484
  21.5 0.0 collective-permute-start.5
  21.5 0.0 collective-permute-done.refs_1_.refs_2_
  21.5 0.3 collective-permute-start.7
  21.8 1.8 %collective-permute-done.2.refs_3_.refs_4_ = bf16[224,768]{1,0:T(8,128)(2,1)S(1)} collective-permute-done((bf16[224,768]{1,0:T(8,128)(2,1)S(1)}, bf16[224,768]{1,0:T(8,128)(2,1)S(1)}, u32[]{:S(2)}, u32[]{:S(2)}) %collective-permute-start.2) | collective-permute-done | bytes 344096 | tf_op jit(solution)/shard_map/ppermute | solution.py:480
  23.6 1.8 %collective-permute-start.9 = (bf16[144,768]{1,0:T(8,128)(2,1)S(1)}, bf16[144,768]{1,0:T(8,128)(2,1)S(1)}, u32[]{:S(2)}, u32[]{:S(2)}) collective-permute-start(bf16[144,768]{1,0:T(8,128)(2,1)S(1)} %slice.9), channel_id=1, source_target_pairs={{0,1},{1,0},{2,3},{3,2},{4,5},{5,4},{6,7},{7,6},{8,9},{9,8},{10,11... | collective-permute-start | bytes 663560 | tf_op jit(solution)/shard_map/ppermute | solution.py:484
  25.4 2.4 %collective-permute-done.8.refs_9_ = bf16[144,768]{1,0:T(8,128)(2,1)S(1)} collective-permute-done((bf16[144,768]{1,0:T(8,128)(2,1)S(1)}, bf16[144,768]{1,0:T(8,128)(2,1)S(1)}, u32[]{:S(2)}, u32[]{:S(2)}) %collective-permute-start.8) | collective-permute-done | bytes 221216 | tf_op jit(solution)/shard_map/ppermute | solution.py:484
  27.9 0.0 collective-permute-start.4
  27.9 0.0 collective-permute-done.5.refs_6_
  27.9 0.5 collective-permute-start.6
  28.4 4.2 %collective-permute-done.7.refs_8_ = bf16[144,768]{1,0:T(8,128)(2,1)S(1)} collective-permute-done((bf16[144,768]{1,0:T(8,128)(2,1)S(1)}, bf16[144,768]{1,0:T(8,128)(2,1)S(1)}, u32[]{:S(2)}, u32[]{:S(2)}) %collective-permute-start.7) | collective-permute-done | bytes 221216 | tf_op jit(solution)/shard_map/ppermute | solution.py:484
  32.6 0.0 collective-permute-start.11
  32.6 3.2 %collective-permute-done.9.refs_10_ = bf16[144,768]{1,0:T(8,128)(2,1)S(1)} collective-permute-done((bf16[144,768]{1,0:T(8,128)(2,1)S(1)}, bf16[144,768]{1,0:T(8,128)(2,1)S(1)}, u32[]{:S(2)}, u32[]{:S(2)}) %collective-permute-start.9) | collective-permute-done | bytes 221216 | tf_op jit(solution)/shard_map/ppermute | solution.py:484
  35.8 0.0 collective-permute-start.10
  35.8 0.0 collective-permute-done.3.refs_4_.refs_1_
  35.8 0.5 collective-permute-start.12
  36.3 0.0 collective-permute-done.4.refs_5_
  36.3 0.0 collective-permute-done.6.refs_7_
  36.3 0.9 %shard_map.96 = (bf16[416,128]{1,0:T(8,128)(2,1)S(1)}, bf16[416,128]{1,0:T(8,128)(2,1)S(1)}, bf16[288,768]{1,0:T(8,128)(2,1)S(1)}) custom-call(bf16[368,768]{1,0:T(8,128)(2,1)S(1)} %get-tuple-element.27.refs_0_, bf16[224,768]{1,0:T(8,128)(2,1)S(1)} %collective-permute-done.refs_1_.refs_2_, bf16[144,768]{1,0:T(8,128)(2,1)S(1)} %collective-permute-done.1.refs_2_.refs_3_, ...), custom_call_target="tpu_custom_call" | custom-call | flops 1000000000 | bytes 1000000 | tf_op jit(solution)/shard_map/pallas_call | solution.py:61
  37.2 0.0 collective-permute-done.11.refs_12_
  37.2 0.0 collective-permute-done.10.refs_11_
  37.2 0.3 collective-permute-done.12.refs_13_
  37.6 3.8 %shard_map.97 = (f32[4,96,768]{2,1,0:T(8,128)S(1)}, bf16[4,96,768]{2,1,0:T(8,128)(2,1)S(1)}, bf16[256,384]{1,0:T(8,128)(2,1)S(1)}, bf16[320,768]{1,0:T(8,128)(2,...) custom-call(bf16[368,768]{1,0:T(8,128)(2,1)S(1)} %get-tuple-element.27.refs_0_, ...), custom_call_target="tpu_custom_call" | custom-call | flops 4000000000 | bytes 1000000 | tf_op jit(solution)/shard_map/pallas_call | solution.py:61
  41.4 0.3 collective-permute-start.13
  41.6 1.8 %collective-permute-done.13.recv_ref = bf16[4,96,768]{2,1,0:T(8,128)(2,1)S(1)} collective-permute-done((bf16[4,96,768]{2,1,0:T(8,128)(2,1)S(1)}, bf16[4,96,768]{2,1,0:T(8,128)(2,1)S(1)}, u32[]{:S(2)}, u32[]{:S(2)}) %collective-permute-start.13) | collective-permute-done | bytes 589856 | tf_op jit(solution)/shard_map/ppermute | solution.py:480
  43.4 0.1 shard_map.99
  43.6 2.4 %collective-permute-start.14 = (bf16[96,768]{1,0:T(8,128)(2,1)S(1)}, bf16[96,768]{1,0:T(8,128)(2,1)S(1)}, u32[]{:S(2)}, u32[]{:S(2)}) collective-permute-start(bf16[96,768]{1,0:T(8,128)(2,1)S(1)} %get-tuple-element.43), channel_id=1, source_target_pairs={{0,24},{8,16},{16,8},{24,0},{1,25},{9,17},{17,9},{25,1},{2,26},{10... | collective-permute-start | bytes 442376 | tf_op jit(solution)/shard_map/ppermute | solution.py:480
  46.0 0.5 collective-permute-start.15
  46.5 0.7 %collective-permute-start.16 = (bf16[96,768]{1,0:T(8,128)(2,1)S(1)}, bf16[96,768]{1,0:T(8,128)(2,1)S(1)}, u32[]{:S(2)}, u32[]{:S(2)}) collective-permute-start(bf16[96,768]{1,0:T(8,128)(2,1)S(1)} %get-tuple-element.45), channel_id=1, source_target_pairs={{0,8},{8,0},{1,9},{9,1},{2,10},{10,2},{3,11},{11,3},{4,12},{12,4},... | collective-permute-start | bytes 442376 | tf_op jit(solution)/shard_map/ppermute | solution.py:480
  47.1 4.1 %collective-permute-done.14.d_ref = bf16[96,768]{1,0:T(8,128)(2,1)S(1)} collective-permute-done((bf16[96,768]{1,0:T(8,128)(2,1)S(1)}, bf16[96,768]{1,0:T(8,128)(2,1)S(1)}, u32[]{:S(2)}, u32[]{:S(2)}) %collective-permute-start.14) | collective-permute-done | bytes 147488 | tf_op jit(solution)/shard_map/ppermute | solution.py:480
  51.2 2.4 %collective-permute-done.15.y_ref = bf16[96,768]{1,0:T(8,128)(2,1)S(1)} collective-permute-done((bf16[96,768]{1,0:T(8,128)(2,1)S(1)}, bf16[96,768]{1,0:T(8,128)(2,1)S(1)}, u32[]{:S(2)}, u32[]{:S(2)}) %collective-permute-start.15) | collective-permute-done | bytes 147488 | tf_op jit(solution)/shard_map/ppermute | solution.py:480
  53.7 0.1 collective-permute-done.16.x_ref
  53.7 0.1 shard_map.100
  53.8 3.6 %collective-permute-start.17 = (bf16[48,384]{1,0:T(8,128)(2,1)S(1)}, bf16[48,384]{1,0:T(8,128)(2,1)S(1)}, u32[]{:S(2)}, u32[]{:S(2)}) collective-permute-start(bf16[48,384]{1,0:T(8,128)(2,1)S(1)} %get-tuple-element.47), channel_id=1, source_target_pairs={{0,3},{1,2},{2,1},{3,0},{4,7},{5,6},{6,5},{7,4},{8,11},{9,10},{10,... | collective-permute-start | bytes 110600 | tf_op jit(solution)/shard_map/ppermute | solution.py:484
  57.4 0.0 collective-permute-start.18
  57.4 0.8 %collective-permute-start.19 = (bf16[48,384]{1,0:T(8,128)(2,1)S(1)}, bf16[48,384]{1,0:T(8,128)(2,1)S(1)}, u32[]{:S(2)}, u32[]{:S(2)}) collective-permute-start(bf16[48,384]{1,0:T(8,128)(2,1)S(1)} %get-tuple-element.49), channel_id=1, source_target_pairs={{0,1},{1,0},{2,3},{3,2},{4,5},{5,4},{6,7},{7,6},{8,9},{9,8},{10,11... | collective-permute-start | bytes 110600 | tf_op jit(solution)/shard_map/ppermute | solution.py:484
  58.3 1.6 %shard_map.98 = f32[4,128]{1,0:T(4,128)} custom-call(f32[8,768]{1,0:T(8,128)S(1)} %get-tuple-element.26.refs_14_.small_ref, bf16[416,128]{1,0:T(8,128)(2,1)S(1)} %get-tuple-element.32.refs_16_.hot_f_ref, bf16[416,128]{1,0:T(8,128)(2,1)S(1)} %get-tuple-element.33.refs_17_.hot_r_ref, bf16[256,384]{1,0:T(8,128)(2,1)S(1)} %get-tuple-element.35.s1_ref, ...), custom_call_target="tpu_custom_call" | custom-call | flops 1000000000 | bytes 1000000 | tf_op jit(solution)/shard_map/pallas_call | solution.py:61
  59.9 0.0 collective-permute-done.17.refs_0_
  59.9 2.4 %collective-permute-done.18.refs_1_ = bf16[48,384]{1,0:T(8,128)(2,1)S(1)} collective-permute-done((bf16[48,384]{1,0:T(8,128)(2,1)S(1)}, bf16[48,384]{1,0:T(8,128)(2,1)S(1)}, u32[]{:S(2)}, u32[]{:S(2)}) %collective-permute-start.18) | collective-permute-done | bytes 36896 | tf_op jit(solution)/shard_map/ppermute | solution.py:484
  62.3 0.7 %shard_map.101 = f32[144,128]{1,0:T(8,128)} custom-call(f32[48,384]{1,0:T(8,128)S(1)} %get-tuple-element.46.mine_ref, bf16[48,384]{1,0:T(8,128)(2,1)S(1)} %collective-permute-done.17.refs_0_, bf16[48,384]{1,0:T(8,128)(2,1)S(1)} %collective-permute-done.18.refs_1_, bf16[48,384]{1,0:T(8,128)(2,1)S(1)} %collective-permute-done.19.refs_2_), custom_call_target="tpu_custom_call" | custom-call | tf_op jit(solution)/shard_map/pallas_call | solution.py:61
  (9 shorter events, 0.0 us)
Async XLA Ops:
  0.6 2.7 %copy-start.1 = (f32[4,768]{1,0:T(4,128)S(1)}, f32[4,768]{1,0:T(4,128)}, u32[]{:S(2)}) copy-start(f32[4,768]{1,0:T(4,128)} %embed_ref.1) | copy-start | bytes 36868
  0.6 2.7 %copy-start = (bf16[1,128,768]{2,1,0:T(8,128)(2,1)S(1)}, bf16[1,128,768]{2,1,0:T(8,128)(2,1)}, u32[]{:S(2)}) copy-start(bf16[1,128,768]{2,1,0:T(8,128)(2,1)} %param.10) | copy-start | bytes 589828
  0.7 2.7 %copy-start.2 = (s32[1,128]{1,0:T(1,128)S(1)}, s32[1,128]{1,0:T(1,128)}, u32[]{:S(2)}) copy-start(s32[1,128]{1,0:T(1,128)} %bases_ref.1) | copy-start | bytes 1540
  3.8 15.8 %collective-permute-start.1 = (bf16[144,768]{1,0:T(8,128)(2,1)S(1)}, bf16[144,768]{1,0:T(8,128)(2,1)S(1)}, u32[]{:S(2)}, u32[]{:S(2)}) collective-permute-start(bf16[144,768]{1,0:T(8,128)(2,1)S(1)} %get-tuple-element.29), channel_id=1, source_target_pairs={{0,16},{16,0},{1,17},{17,1},{2,18},{18,2},{3,19},{19,3},{4,20},{20... | collective-permute-start | bytes 663560 | tf_op jit(solution)/shard_map/ppermute | solution.py:480
  6.9 14.6 %collective-permute-start = (bf16[224,768]{1,0:T(8,128)(2,1)S(1)}, bf16[224,768]{1,0:T(8,128)(2,1)S(1)}, u32[]{:S(2)}, u32[]{:S(2)}) collective-permute-start(bf16[224,768]{1,0:T(8,128)(2,1)S(1)} %get-tuple-element.28), channel_id=1, source_target_pairs={{0,24},{8,16},{16,8},{24,0},{1,25},{9,17},{17,9},{25,1},{2,26},{10... | collective-permute-start | bytes 1032200 | tf_op jit(solution)/shard_map/ppermute | solution.py:480
  8.3 15.3 %collective-permute-start.2 = (bf16[224,768]{1,0:T(8,128)(2,1)S(1)}, bf16[224,768]{1,0:T(8,128)(2,1)S(1)}, u32[]{:S(2)}, u32[]{:S(2)}) collective-permute-start(bf16[224,768]{1,0:T(8,128)(2,1)S(1)} %get-tuple-element.30), channel_id=1, source_target_pairs={{0,8},{8,0},{1,9},{9,1},{2,10},{10,2},{3,11},{11,3},{4,12},{12,4},... | collective-permute-start | bytes 1032200 | tf_op jit(solution)/shard_map/ppermute | solution.py:480
  8.4 27.4 %collective-permute-start.3 = (bf16[368,768]{1,0:T(8,128)(2,1)S(1)}, bf16[368,768]{1,0:T(8,128)(2,1)S(1)}, u32[]{:S(2)}, u32[]{:S(2)}) collective-permute-start(bf16[368,768]{1,0:T(8,128)(2,1)S(1)} %get-tuple-element.27.refs_0_), channel_id=1, source_target_pairs={{0,4},{4,0},{1,5},{5,1},{2,6},{6,2},{3,7},{7,3},{8,12},{12,8},{9,1... | collective-permute-start | bytes 1695752 | tf_op jit(solution)/shard_map/ppermute | solution.py:480
  19.7 8.2 %collective-permute-start.8 = (bf16[144,768]{1,0:T(8,128)(2,1)S(1)}, bf16[144,768]{1,0:T(8,128)(2,1)S(1)}, u32[]{:S(2)}, u32[]{:S(2)}) collective-permute-start(bf16[144,768]{1,0:T(8,128)(2,1)S(1)} %collective-permute-done.1.refs_2_.refs_3_), channel_id=1, source_target_pairs={{0,1},{1,0},{2,3},{3,2},{4,5},{5,4},{6,7},{7,6},{8,9},{9,8},{10,11... | collective-permute-start | bytes 663560 | tf_op jit(solution)/shard_map/ppermute | solution.py:484
  21.5 6.4 %collective-permute-start.5 = (bf16[144,768]{1,0:T(8,128)(2,1)S(1)}, bf16[144,768]{1,0:T(8,128)(2,1)S(1)}, u32[]{:S(2)}, u32[]{:S(2)}) collective-permute-start(bf16[144,768]{1,0:T(8,128)(2,1)S(1)} %collective-permute-done.1.refs_2_.refs_3_), channel_id=1, source_target_pairs={{0,4},{4,0},{1,5},{5,1},{2,6},{6,2},{3,7},{7,3},{8,12},{12,8},{9,1... | collective-permute-start | bytes 663560 | tf_op jit(solution)/shard_map/ppermute | solution.py:480
  21.5 11.1 %collective-permute-start.7 = (bf16[144,768]{1,0:T(8,128)(2,1)S(1)}, bf16[144,768]{1,0:T(8,128)(2,1)S(1)}, u32[]{:S(2)}, u32[]{:S(2)}) collective-permute-start(bf16[144,768]{1,0:T(8,128)(2,1)S(1)} %slice.8), channel_id=1, source_target_pairs={{0,1},{1,0},{2,3},{3,2},{4,5},{5,4},{6,7},{7,6},{8,9},{9,8},{10,11... | collective-permute-start | bytes 663560 | tf_op jit(solution)/shard_map/ppermute | solution.py:484
  23.6 12.1 %collective-permute-start.9 = (bf16[144,768]{1,0:T(8,128)(2,1)S(1)}, bf16[144,768]{1,0:T(8,128)(2,1)S(1)}, u32[]{:S(2)}, u32[]{:S(2)}) collective-permute-start(bf16[144,768]{1,0:T(8,128)(2,1)S(1)} %slice.9), channel_id=1, source_target_pairs={{0,1},{1,0},{2,3},{3,2},{4,5},{5,4},{6,7},{7,6},{8,9},{9,8},{10,11... | collective-permute-start | bytes 663560 | tf_op jit(solution)/shard_map/ppermute | solution.py:484
  27.9 8.4 %collective-permute-start.4 = (bf16[224,768]{1,0:T(8,128)(2,1)S(1)}, bf16[224,768]{1,0:T(8,128)(2,1)S(1)}, u32[]{:S(2)}, u32[]{:S(2)}) collective-permute-start(bf16[224,768]{1,0:T(8,128)(2,1)S(1)} %collective-permute-done.refs_1_.refs_2_), channel_id=1, source_target_pairs={{0,4},{4,0},{1,5},{5,1},{2,6},{6,2},{3,7},{7,3},{8,12},{12,8},{9,1... | collective-permute-start | bytes 1032200 | tf_op jit(solution)/shard_map/ppermute | solution.py:480
  27.9 8.4 %collective-permute-start.6 = (bf16[224,768]{1,0:T(8,128)(2,1)S(1)}, bf16[224,768]{1,0:T(8,128)(2,1)S(1)}, u32[]{:S(2)}, u32[]{:S(2)}) collective-permute-start(bf16[224,768]{1,0:T(8,128)(2,1)S(1)} %collective-permute-done.2.refs_3_.refs_4_), channel_id=1, source_target_pairs={{0,4},{4,0},{1,5},{5,1},{2,6},{6,2},{3,7},{7,3},{8,12},{12,8},{9,1... | collective-permute-start | bytes 1032200 | tf_op jit(solution)/shard_map/ppermute | solution.py:480
  32.6 4.6 %collective-permute-start.11 = (bf16[144,768]{1,0:T(8,128)(2,1)S(1)}, bf16[144,768]{1,0:T(8,128)(2,1)S(1)}, u32[]{:S(2)}, u32[]{:S(2)}) collective-permute-start(bf16[144,768]{1,0:T(8,128)(2,1)S(1)} %collective-permute-done.8.refs_9_), channel_id=1, source_target_pairs={{0,4},{4,0},{1,5},{5,1},{2,6},{6,2},{3,7},{7,3},{8,12},{12,8},{9,1... | collective-permute-start | bytes 663560 | tf_op jit(solution)/shard_map/ppermute | solution.py:480
  35.8 1.5 %collective-permute-start.10 = (bf16[144,768]{1,0:T(8,128)(2,1)S(1)}, bf16[144,768]{1,0:T(8,128)(2,1)S(1)}, u32[]{:S(2)}, u32[]{:S(2)}) collective-permute-start(bf16[144,768]{1,0:T(8,128)(2,1)S(1)} %collective-permute-done.7.refs_8_), channel_id=1, source_target_pairs={{0,4},{4,0},{1,5},{5,1},{2,6},{6,2},{3,7},{7,3},{8,12},{12,8},{9,1... | collective-permute-start | bytes 663560 | tf_op jit(solution)/shard_map/ppermute | solution.py:480
  35.8 1.8 %collective-permute-start.12 = (bf16[144,768]{1,0:T(8,128)(2,1)S(1)}, bf16[144,768]{1,0:T(8,128)(2,1)S(1)}, u32[]{:S(2)}, u32[]{:S(2)}) collective-permute-start(bf16[144,768]{1,0:T(8,128)(2,1)S(1)} %collective-permute-done.9.refs_10_), channel_id=1, source_target_pairs={{0,4},{4,0},{1,5},{5,1},{2,6},{6,2},{3,7},{7,3},{8,12},{12,8},{9,1... | collective-permute-start | bytes 663560 | tf_op jit(solution)/shard_map/ppermute | solution.py:480
  41.4 2.1 %collective-permute-start.13 = (bf16[4,96,768]{2,1,0:T(8,128)(2,1)S(1)}, bf16[4,96,768]{2,1,0:T(8,128)(2,1)S(1)}, u32[]{:S(2)}, u32[]{:S(2)}) collective-permute-start(bf16[4,96,768]{2,1,0:T(8,128)(2,1)S(1)} %get-tuple-element.41), channel_id=1, source_target_pairs={{0,4},{4,0},{1,5},{5,1},{2,6},{6,2},{3,7},{7,3},{8,12},{12,8},{9,1... | collective-permute-start | bytes 1769480 | tf_op jit(solution)/shard_map/ppermute | solution.py:480
  43.6 7.6 %collective-permute-start.14 = (bf16[96,768]{1,0:T(8,128)(2,1)S(1)}, bf16[96,768]{1,0:T(8,128)(2,1)S(1)}, u32[]{:S(2)}, u32[]{:S(2)}) collective-permute-start(bf16[96,768]{1,0:T(8,128)(2,1)S(1)} %get-tuple-element.43), channel_id=1, source_target_pairs={{0,24},{8,16},{16,8},{24,0},{1,25},{9,17},{17,9},{25,1},{2,26},{10... | collective-permute-start | bytes 442376 | tf_op jit(solution)/shard_map/ppermute | solution.py:480
  46.0 7.6 %collective-permute-start.15 = (bf16[96,768]{1,0:T(8,128)(2,1)S(1)}, bf16[96,768]{1,0:T(8,128)(2,1)S(1)}, u32[]{:S(2)}, u32[]{:S(2)}) collective-permute-start(bf16[96,768]{1,0:T(8,128)(2,1)S(1)} %get-tuple-element.44), channel_id=1, source_target_pairs={{0,16},{16,0},{1,17},{17,1},{2,18},{18,2},{3,19},{19,3},{4,20},{20... | collective-permute-start | bytes 442376 | tf_op jit(solution)/shard_map/ppermute | solution.py:480
  46.5 7.2 %collective-permute-start.16 = (bf16[96,768]{1,0:T(8,128)(2,1)S(1)}, bf16[96,768]{1,0:T(8,128)(2,1)S(1)}, u32[]{:S(2)}, u32[]{:S(2)}) collective-permute-start(bf16[96,768]{1,0:T(8,128)(2,1)S(1)} %get-tuple-element.45), channel_id=1, source_target_pairs={{0,8},{8,0},{1,9},{9,1},{2,10},{10,2},{3,11},{11,3},{4,12},{12,4},... | collective-permute-start | bytes 442376 | tf_op jit(solution)/shard_map/ppermute | solution.py:480
  53.8 6.0 %collective-permute-start.17 = (bf16[48,384]{1,0:T(8,128)(2,1)S(1)}, bf16[48,384]{1,0:T(8,128)(2,1)S(1)}, u32[]{:S(2)}, u32[]{:S(2)}) collective-permute-start(bf16[48,384]{1,0:T(8,128)(2,1)S(1)} %get-tuple-element.47), channel_id=1, source_target_pairs={{0,3},{1,2},{2,1},{3,0},{4,7},{5,6},{6,5},{7,4},{8,11},{9,10},{10,... | collective-permute-start | bytes 110600 | tf_op jit(solution)/shard_map/ppermute | solution.py:484
  57.4 4.9 %collective-permute-start.18 = (bf16[48,384]{1,0:T(8,128)(2,1)S(1)}, bf16[48,384]{1,0:T(8,128)(2,1)S(1)}, u32[]{:S(2)}, u32[]{:S(2)}) collective-permute-start(bf16[48,384]{1,0:T(8,128)(2,1)S(1)} %get-tuple-element.48), channel_id=1, source_target_pairs={{0,2},{1,3},{2,0},{3,1},{4,6},{5,7},{6,4},{7,5},{8,10},{9,11},{10,... | collective-permute-start | bytes 110600 | tf_op jit(solution)/shard_map/ppermute | solution.py:484
  57.4 4.9 %collective-permute-start.19 = (bf16[48,384]{1,0:T(8,128)(2,1)S(1)}, bf16[48,384]{1,0:T(8,128)(2,1)S(1)}, u32[]{:S(2)}, u32[]{:S(2)}) collective-permute-start(bf16[48,384]{1,0:T(8,128)(2,1)S(1)} %get-tuple-element.49), channel_id=1, source_target_pairs={{0,1},{1,0},{2,3},{3,2},{4,5},{5,4},{6,7},{7,6},{8,9},{9,8},{10,11... | collective-permute-start | bytes 110600 | tf_op jit(solution)/shard_map/ppermute | solution.py:484
